TPU v7x, 32 devices: a whole 2x2x4 slice. The times are simulated.
32 devices in a mesh: ctx: 8 (over z, y), wt: 4 (over x, core).
Axes of the slice: x: 2, y: 2, z: 4, core: 2. Of those that a mesh axis runs over, the one named last changes fastest.
Arguments:
- tokens: bfloat16 [4, 1024, 1536], P('wt', 'ctx'), may hold values from -6 to 6
- cotangent: bfloat16 [4, 1024, 1536], P('wt', 'ctx'), may hold values from -6 to 6
- seq_lengths: int32 [4, 1], P('wt'), may hold values from 1024 to 1024, as said below
- block_deal: int32 [4, 8, 1], P('wt'), may hold values from 0 to 7, as said below
- routes: int32 [2, 4, 1024, 2], P(None, 'wt', 'ctx'), may hold values from 0 to 7, all different within a row; in each aligned block of 128 rows (0 to 127, 128 to 255, ..., all dimensions but the last counted through in order) at most 48 rows name the same one
- attention_gain: bfloat16 [2, 1536], P(None, 'wt'), may hold values from 0.5 to 1.5
- query_weight: bfloat16 [2, 1536, 1536], P(None, 'wt'), may hold values from -0.15625 to 0.15625
- key_weight: bfloat16 [2, 1536, 512], P(None, 'wt'), may hold values from -0.15625 to 0.15625
- value_weight: bfloat16 [2, 1536, 512], P(None, 'wt'), may hold values from -0.15625 to 0.15625
- out_weight: bfloat16 [2, 1536, 1536], P(None, 'wt'), may hold values from -1.25 to 1.25
- mixture_gain: bfloat16 [2, 1536], P(None, 'wt'), may hold values from 0.5 to 1.5
- router_weight: bfloat16 [2, 1536, 8], P(None, 'wt'), may hold values from -0.099609375 to 0.099609375
- gate_weight: bfloat16 [2, 8, 1536, 1024], P(None, 'ctx', None, 'wt'), may hold values from -0.15625 to 0.15625
- up_weight: bfloat16 [2, 8, 1536, 1024], P(None, 'ctx', None, 'wt'), may hold values from -0.15625 to 0.15625
- down_weight: bfloat16 [2, 8, 1024, 1536], P(None, 'ctx', 'wt'), may hold values from -0.375 to 0.375
Outputs:
- block_output: bfloat16 [4, 1024, 1536], P('wt', 'ctx')
- input_grad: float32 [4, 1024, 1536], P('wt', 'ctx')
- attention_gain_grad: float32 [2, 1536], P(None, 'wt')
- query_grad: float32 [2, 1536, 1536], P(None, 'wt')
- key_grad: float32 [2, 1536, 512], P(None, 'wt')
- value_grad: float32 [2, 1536, 512], P(None, 'wt')
- out_grad: float32 [2, 1536, 1536], P(None, 'wt')
- mixture_gain_grad: float32 [2, 1536], P(None, 'wt')
- router_grad: float32 [2, 1536, 8], P(None, 'wt')
- gate_grad: float32 [2, 8, 1536, 1024], P(None, 'ctx', None, 'wt')
- up_grad: float32 [2, 8, 1536, 1024], P(None, 'ctx', None, 'wt')
- down_grad: float32 [2, 8, 1024, 1536], P(None, 'ctx', 'wt')
Inputs may be any that keep to these rules, and one draw needn't show every extreme that they name: `seq_lengths`: a group's lengths sum to 1024, each is at least 1024, and one is exactly 1024. `block_deal`: each group's table is a permutation of the 8 stream blocks; devices 0, 4 and 7 hold blocks 0, 2 and 1 in their first slot. `routes`: each row names two different experts; among the rows of one device no expert is named more than 48 times, a bound that some block reaches.
All inputs are finite; a program needn't handle non-finite values.
Results may differ from a plain program's by a relative error of at most 0.03.
Values may be sent and summed in bfloat16 or wider, within the bound.
No kernel may reach another device: no remote copies, remote signals or barrier semaphores. Data moves between devices by JAX's collectives and lax.ppermute only.
A program may use at most 256 MiB of HBM per device.

v0:
```python
import jax
import jax.numpy as jnp
from jax import lax
from jax.sharding import PartitionSpec as P

HEADS = 24
KV_HEADS = 8
HEAD = 64
BLK = 128


EPS = 1e-05
NEG = -1e30


def rms_scale(rows, gain):
    return rows * lax.rsqrt(jnp.mean(rows * rows, axis=-1, keepdims=True) + EPS) * gain


def stream_positions(table, width):
    offsets = jnp.arange(width, dtype=jnp.int32)
    return (table[:, :, None] * width + offsets[None, None, :]).reshape(-1)


def sequence_ids(positions, seq_row):
    ends = jnp.cumsum(seq_row)
    return jnp.sum((positions[:, None] >= ends[None, :]).astype(jnp.int32), axis=1)


def outer_rows(left, right):
    return lax.dot_general(
        left, right, (((0,), (0,)), ((), ())), preferred_element_type=jnp.float32
    )


def times_transposed(left, right):
    return lax.dot_general(
        left, right, (((1,), (1,)), ((), ())), preferred_element_type=jnp.float32
    )


def unchanged(state):
    return state


def local(
    tokens,
    cotangent,
    seq_lengths,
    block_deal,
    routes,
    attention_gain,
    query_weight,
    key_weight,
    value_weight,
    out_weight,
    mixture_gain,
    router_weight,
    gate_weight,
    up_weight,
    down_weight,
):
    rows_here = tokens.shape[1]
    width = tokens.shape[2]
    layers = query_weight.shape[0]
    experts = router_weight.shape[2]
    capacity = 3 * rows_here // experts
    kv_groups = KV_HEADS
    per_group = HEADS // KV_HEADS
    head_size = HEAD
    kv_width = kv_groups * head_size
    scale = head_size ** (-0.5)
    device = lax.axis_index("ctx")
    everywhere = stream_positions(block_deal[0], BLK)
    every_seq = sequence_ids(everywhere, seq_lengths[0])
    own_pos = lax.dynamic_slice_in_dim(everywhere, device * rows_here, rows_here, 0)
    own_seq = lax.dynamic_slice_in_dim(every_seq, device * rows_here, rows_here, 0)
    choice_rows = jnp.arange(2 * rows_here, dtype=jnp.int32) // 2
    expert_ids = jnp.arange(experts, dtype=jnp.int32)

    def block_mask(start, count):
        key_pos = lax.dynamic_slice_in_dim(everywhere, start, count, 0)
        key_seq = lax.dynamic_slice_in_dim(every_seq, start, count, 0)
        return (own_seq[:, None] == key_seq[None, :]) & (key_pos[None, :] <= own_pos[:, None])

    hidden_state = tokens[0].astype(jnp.float32)
    saved = []
    for layer in range(layers):
        shared = (
            lax.all_gather(attention_gain[layer], "wt", axis=0, tiled=True),
            lax.all_gather(query_weight[layer], "wt", axis=0, tiled=True),
            lax.all_gather(key_weight[layer], "wt", axis=0, tiled=True),
            lax.all_gather(value_weight[layer], "wt", axis=0, tiled=True),
            lax.all_gather(out_weight[layer], "wt", axis=0, tiled=True),
            lax.all_gather(mixture_gain[layer], "wt", axis=0, tiled=True),
            lax.all_gather(router_weight[layer], "wt", axis=0, tiled=True),
        )
        gain_one, full_query, full_key, full_value, full_out, gain_two, full_router = shared
        normed = rms_scale(hidden_state, gain_one.astype(jnp.float32)).astype(jnp.bfloat16)
        queries = jnp.dot(normed, full_query, preferred_element_type=jnp.float32).astype(
            jnp.bfloat16
        )
        keys = jnp.dot(normed, full_key, preferred_element_type=jnp.float32).astype(jnp.bfloat16)
        values = jnp.dot(normed, full_value, preferred_element_type=jnp.float32).astype(
            jnp.bfloat16
        )
        query_heads = queries.reshape(rows_here, kv_groups, per_group, head_size)
        start_state = (
            jnp.full((kv_groups, per_group, rows_here), NEG, jnp.float32),
            jnp.zeros((kv_groups, per_group, rows_here), jnp.float32),
            jnp.zeros((kv_groups, per_group, rows_here, head_size), jnp.float32),
        )
        gathered = None
        key_piece = lax.all_gather(keys, "ctx", axis=0, tiled=True)
        value_piece = lax.all_gather(values, "ctx", axis=0, tiled=True)
        absorb_count = key_piece.shape[0]
        absorb_span = 512

        def turn(index, state):
            first = index * absorb_span
            key_block = lax.dynamic_slice_in_dim(key_piece, first, absorb_span, 0).reshape(
                absorb_span, kv_groups, head_size
            )
            value_block = lax.dynamic_slice_in_dim(value_piece, first, absorb_span, 0).reshape(
                absorb_span, kv_groups, head_size
            )
            allowed = block_mask(first, absorb_span)

            def work(state):
                top, total, summed = state
                scores = (
                    jnp.einsum(
                        "tgrd,kgd->grtk", query_heads, key_block, preferred_element_type=jnp.float32
                    )
                    * scale
                )
                scores = jnp.where(allowed[None, None], scores, NEG)
                top_new = jnp.maximum(top, jnp.max(scores, axis=-1))
                fade = jnp.exp(top - top_new)
                weights = jnp.where(allowed[None, None], jnp.exp(scores - top_new[..., None]), 0.0)
                total = total * fade + jnp.sum(weights, axis=-1)
                summed = summed * fade[..., None] + jnp.einsum(
                    "grtk,kgd->grtd",
                    weights.astype(jnp.bfloat16),
                    value_block,
                    preferred_element_type=jnp.float32,
                )
                return (top_new, total, summed)

            return lax.cond(jnp.any(allowed), work, unchanged, state)

        top, total, summed = lax.fori_loop(0, absorb_count // absorb_span, turn, start_state)
        attended = (summed / total[..., None]).transpose(2, 0, 1, 3).reshape(rows_here, width)
        log_total = top + jnp.log(total)
        attended_low = attended.astype(jnp.bfloat16)
        middle = hidden_state + jnp.dot(attended_low, full_out, preferred_element_type=jnp.float32)
        mixed_low = rms_scale(middle, gain_two.astype(jnp.float32)).astype(jnp.bfloat16)
        probs = jax.nn.softmax(
            jnp.dot(mixed_low, full_router, preferred_element_type=jnp.float32), axis=-1
        )
        chosen = routes[layer, 0]
        picked = jnp.take_along_axis(probs, chosen, axis=1)
        gates = picked / jnp.sum(picked, axis=1, keepdims=True)
        flat_choice = chosen.reshape(-1)
        onehot = (flat_choice[:, None] == expert_ids[None, :]).astype(jnp.int32)
        rank = jnp.sum((jnp.cumsum(onehot, axis=0) - onehot) * onehot, axis=1)
        slots = flat_choice * capacity + rank
        outgoing = (
            jnp.zeros((experts * capacity, width), jnp.bfloat16)
            .at[slots]
            .set(mixed_low[choice_rows])
            .reshape(experts, capacity, width)
        )
        arrived = lax.all_to_all(outgoing, "ctx", split_axis=0, concat_axis=0, tiled=True)
        expert_full = (
            lax.all_gather(gate_weight[layer, 0], "wt", axis=1, tiled=True),
            lax.all_gather(up_weight[layer, 0], "wt", axis=1, tiled=True),
            lax.all_gather(down_weight[layer, 0], "wt", axis=0, tiled=True),
        )
        gate_full, up_full, down_full = expert_full
        expert_rows = arrived.reshape(-1, width)
        gate_value = jnp.dot(expert_rows, gate_full, preferred_element_type=jnp.float32)
        up_value = jnp.dot(expert_rows, up_full, preferred_element_type=jnp.float32)
        inner = (jax.nn.silu(gate_value) * up_value).astype(jnp.bfloat16)
        produced = (
            jnp.dot(inner, down_full, preferred_element_type=jnp.float32)
            .astype(jnp.bfloat16)
            .reshape(experts, capacity, width)
        )
        returned = lax.all_to_all(produced, "ctx", split_axis=0, concat_axis=0, tiled=True)
        expert_out = (
            returned.reshape(-1, width)[slots].reshape(rows_here, 2, width).astype(jnp.float32)
        )
        saved.append(
            (
                hidden_state,
                shared,
                normed,
                query_heads,
                keys,
                values,
                gathered,
                attended,
                attended_low,
                log_total,
                middle,
                mixed_low,
                probs,
                chosen,
                picked,
                gates,
                slots,
                expert_full,
                expert_rows,
                gate_value,
                up_value,
                inner,
                expert_out,
            )
        )
        hidden_state = middle + jnp.sum(gates[:, :, None] * expert_out, axis=1)
    block_output = hidden_state.astype(jnp.bfloat16)[None]
    upstream = cotangent[0].astype(jnp.float32)
    collected = []
    for layer in reversed(range(layers)):
        (
            layer_input,
            shared,
            normed,
            query_heads,
            keys,
            values,
            gathered,
            attended,
            attended_low,
            log_total,
            middle,
            mixed_low,
            probs,
            chosen,
            picked,
            gates,
            slots,
            expert_full,
            expert_rows,
            gate_value,
            up_value,
            inner,
            expert_out,
        ) = saved[layer]
        gain_one, full_query, full_key, full_value, full_out, gain_two, full_router = shared
        gate_full, up_full, down_full = expert_full
        gate_signal = jnp.sum(upstream[:, None, :] * expert_out, axis=-1)
        back_rows = (
            (gates[:, :, None] * upstream[:, None, :]).astype(jnp.bfloat16).reshape(-1, width)
        )
        outgoing_grad = (
            jnp.zeros((experts * capacity, width), jnp.bfloat16)
            .at[slots]
            .set(back_rows)
            .reshape(experts, capacity, width)
        )
        arrived_grad = lax.all_to_all(
            outgoing_grad, "ctx", split_axis=0, concat_axis=0, tiled=True
        ).reshape(-1, width)
        grad_down = outer_rows(inner, arrived_grad)
        grad_inner = times_transposed(arrived_grad, down_full)
        sigma = jax.nn.sigmoid(gate_value)
        grad_gate_value = (
            grad_inner * up_value * sigma * (1.0 + gate_value * (1.0 - sigma))
        ).astype(jnp.bfloat16)
        grad_up_value = (grad_inner * gate_value * sigma).astype(jnp.bfloat16)
        grad_gate = outer_rows(expert_rows, grad_gate_value)
        grad_up = outer_rows(expert_rows, grad_up_value)
        grad_rows = (
            (
                times_transposed(grad_gate_value, gate_full)
                + times_transposed(grad_up_value, up_full)
            )
            .astype(jnp.bfloat16)
            .reshape(experts, capacity, width)
        )
        back_grad = lax.all_to_all(grad_rows, "ctx", split_axis=0, concat_axis=0, tiled=True)
        grad_mixed = jnp.sum(
            back_grad.reshape(-1, width)[slots].reshape(rows_here, 2, width).astype(jnp.float32),
            axis=1,
        )
        pair_total = jnp.sum(picked, axis=1, keepdims=True)
        grad_picked = (
            gate_signal - jnp.sum(gates * gate_signal, axis=1, keepdims=True)
        ) / pair_total
        grad_probs = jnp.sum(
            grad_picked[:, :, None]
            * (chosen[:, :, None] == expert_ids[None, None, :]).astype(jnp.float32),
            axis=1,
        )
        grad_logits = probs * (grad_probs - jnp.sum(probs * grad_probs, axis=1, keepdims=True))
        grad_router = lax.dot_general(
            mixed_low.astype(jnp.float32),
            grad_logits,
            (((0,), (0,)), ((), ())),
            precision=lax.Precision.HIGHEST,
            preferred_element_type=jnp.float32,
        )
        grad_mixed = grad_mixed + lax.dot_general(
            grad_logits,
            full_router.astype(jnp.float32),
            (((1,), (1,)), ((), ())),
            precision=lax.Precision.HIGHEST,
            preferred_element_type=jnp.float32,
        )
        norm_value, pull_two = jax.vjp(rms_scale, middle, gain_two.astype(jnp.float32))
        grad_middle_norm, grad_gain_two = pull_two(grad_mixed)
        grad_middle = upstream + grad_middle_norm
        middle_low = grad_middle.astype(jnp.bfloat16)
        grad_out = outer_rows(attended_low, middle_low)
        grad_attended = times_transposed(middle_low, full_out).astype(jnp.bfloat16)
        grad_heads = grad_attended.reshape(rows_here, kv_groups, per_group, head_size)
        attended_heads = attended.reshape(rows_here, kv_groups, per_group, head_size)
        delta = jnp.sum(grad_heads.astype(jnp.float32) * attended_heads, axis=-1).transpose(1, 2, 0)
        whole = (
            lax.all_gather(keys, "ctx", axis=0, tiled=True),
            lax.all_gather(values, "ctx", axis=0, tiled=True),
        )
        key_all, value_all = whole
        total_rows = key_all.shape[0]
        span = 512

        def score_block(first, count, allowed):
            key_block = lax.dynamic_slice_in_dim(key_all, first, count, 0).reshape(
                count, kv_groups, head_size
            )
            value_block = lax.dynamic_slice_in_dim(value_all, first, count, 0).reshape(
                count, kv_groups, head_size
            )
            scores = (
                jnp.einsum(
                    "tgrd,kgd->grtk", query_heads, key_block, preferred_element_type=jnp.float32
                )
                * scale
            )
            probs_block = jnp.where(
                allowed[None, None], jnp.exp(scores - log_total[..., None]), 0.0
            )
            grad_probs_block = jnp.einsum(
                "tgrd,kgd->grtk", grad_heads, value_block, preferred_element_type=jnp.float32
            )
            grad_scores = (probs_block * (grad_probs_block - delta[..., None])).astype(jnp.bfloat16)
            return (key_block, probs_block, grad_scores)

        def key_terms(probs_block, grad_scores, count):
            key_part = (
                jnp.einsum(
                    "grtk,tgrd->kgd", grad_scores, query_heads, preferred_element_type=jnp.float32
                )
                * scale
            ).reshape(count, kv_width)
            value_part = jnp.einsum(
                "grtk,tgrd->kgd",
                probs_block.astype(jnp.bfloat16),
                grad_heads,
                preferred_element_type=jnp.float32,
            ).reshape(count, kv_width)
            return (key_part, value_part)

        query_start = jnp.zeros((rows_here, kv_groups, per_group, head_size), jnp.float32)

        def turn_back(index, state):
            first = index * span
            allowed = block_mask(first, span)

            def work(state):
                grad_query, grad_keys, grad_values = state
                key_block, probs_block, grad_scores = score_block(first, span, allowed)
                grad_query = (
                    grad_query
                    + jnp.einsum(
                        "grtk,kgd->tgrd", grad_scores, key_block, preferred_element_type=jnp.float32
                    )
                    * scale
                )
                key_part, value_part = key_terms(probs_block, grad_scores, span)
                grad_keys = lax.dynamic_update_slice_in_dim(grad_keys, key_part, first, 0)
                grad_values = lax.dynamic_update_slice_in_dim(grad_values, value_part, first, 0)
                return (grad_query, grad_keys, grad_values)

            return lax.cond(jnp.any(allowed), work, unchanged, state)

        back_start = (
            query_start,
            jnp.zeros((total_rows, kv_width), jnp.float32),
            jnp.zeros((total_rows, kv_width), jnp.float32),
        )
        grad_query, grad_keys, grad_values = lax.fori_loop(
            0, total_rows // span, turn_back, back_start
        )
        grad_keys, grad_values = (
            lax.psum_scatter(
                grad_keys.astype(jnp.bfloat16), "ctx", scatter_dimension=0, tiled=True
            ).astype(jnp.float32),
            lax.psum_scatter(
                grad_values.astype(jnp.bfloat16), "ctx", scatter_dimension=0, tiled=True
            ).astype(jnp.float32),
        )
        query_low = grad_query.reshape(rows_here, width).astype(jnp.bfloat16)
        key_low = grad_keys.astype(jnp.bfloat16)
        value_low = grad_values.astype(jnp.bfloat16)
        grad_query_weight = outer_rows(normed, query_low)
        grad_key_weight = outer_rows(normed, key_low)
        grad_value_weight = outer_rows(normed, value_low)
        grad_normed = (
            times_transposed(query_low, full_query)
            + times_transposed(key_low, full_key)
            + times_transposed(value_low, full_value)
        )
        norm_value, pull_one = jax.vjp(rms_scale, layer_input, gain_one.astype(jnp.float32))
        grad_input_norm, grad_gain_one = pull_one(grad_normed)
        upstream = grad_middle + grad_input_norm
        part_one, part_query, part_key, part_value, part_out, part_two, part_router = (
            lax.psum_scatter(
                grad_gain_one.astype(jnp.bfloat16), "wt", scatter_dimension=0, tiled=True
            ).astype(jnp.float32),
            lax.psum_scatter(
                grad_query_weight.astype(jnp.bfloat16), "wt", scatter_dimension=0, tiled=True
            ).astype(jnp.float32),
            lax.psum_scatter(
                grad_key_weight.astype(jnp.bfloat16), "wt", scatter_dimension=0, tiled=True
            ).astype(jnp.float32),
            lax.psum_scatter(
                grad_value_weight.astype(jnp.bfloat16), "wt", scatter_dimension=0, tiled=True
            ).astype(jnp.float32),
            lax.psum_scatter(
                grad_out.astype(jnp.bfloat16), "wt", scatter_dimension=0, tiled=True
            ).astype(jnp.float32),
            lax.psum_scatter(
                grad_gain_two.astype(jnp.bfloat16), "wt", scatter_dimension=0, tiled=True
            ).astype(jnp.float32),
            lax.psum_scatter(
                grad_router.astype(jnp.bfloat16), "wt", scatter_dimension=0, tiled=True
            ).astype(jnp.float32),
        )
        summed_parts = (
            lax.psum(part_one.astype(jnp.bfloat16), "ctx").astype(jnp.float32),
            lax.psum(part_query.astype(jnp.bfloat16), "ctx").astype(jnp.float32),
            lax.psum(part_key.astype(jnp.bfloat16), "ctx").astype(jnp.float32),
            lax.psum(part_value.astype(jnp.bfloat16), "ctx").astype(jnp.float32),
            lax.psum(part_out.astype(jnp.bfloat16), "ctx").astype(jnp.float32),
            lax.psum(part_two.astype(jnp.bfloat16), "ctx").astype(jnp.float32),
            lax.psum(part_router.astype(jnp.bfloat16), "ctx").astype(jnp.float32),
        )
        expert_parts = (
            lax.psum_scatter(
                grad_gate.astype(jnp.bfloat16), "wt", scatter_dimension=1, tiled=True
            ).astype(jnp.float32),
            lax.psum_scatter(
                grad_up.astype(jnp.bfloat16), "wt", scatter_dimension=1, tiled=True
            ).astype(jnp.float32),
            lax.psum_scatter(
                grad_down.astype(jnp.bfloat16), "wt", scatter_dimension=0, tiled=True
            ).astype(jnp.float32),
        )
        collected.append((summed_parts, expert_parts))
    ordered = collected[::-1]
    attention_gain_grad = jnp.stack([item[0][0] for item in ordered])
    query_grad = jnp.stack([item[0][1] for item in ordered])
    key_grad = jnp.stack([item[0][2] for item in ordered])
    value_grad = jnp.stack([item[0][3] for item in ordered])
    out_grad = jnp.stack([item[0][4] for item in ordered])
    mixture_gain_grad = jnp.stack([item[0][5] for item in ordered])
    router_grad = jnp.stack([item[0][6] for item in ordered])
    gate_grad = jnp.stack([item[1][0] for item in ordered])[:, None]
    up_grad = jnp.stack([item[1][1] for item in ordered])[:, None]
    down_grad = jnp.stack([item[1][2] for item in ordered])[:, None]
    return (
        block_output,
        upstream[None],
        attention_gain_grad,
        query_grad,
        key_grad,
        value_grad,
        out_grad,
        mixture_gain_grad,
        router_grad,
        gate_grad,
        up_grad,
        down_grad,
    )


def solution(mesh):
    placed = (
        P("wt", "ctx", None),
        P("wt", "ctx", None),
        P("wt", None),
        P("wt", None, None),
        P(None, "wt", "ctx", None),
        P(None, "wt"),
        P(None, "wt", None),
        P(None, "wt", None),
        P(None, "wt", None),
        P(None, "wt", None),
        P(None, "wt"),
        P(None, "wt", None),
        P(None, "ctx", None, "wt"),
        P(None, "ctx", None, "wt"),
        P(None, "ctx", "wt", None),
    )
    return jax.shard_map(
        local,
        mesh=mesh,
        in_specs=placed,
        out_specs=(
            P("wt", "ctx", None),
            P("wt", "ctx", None),
            P(None, "wt"),
            P(None, "wt", None),
            P(None, "wt", None),
            P(None, "wt", None),
            P(None, "wt", None),
            P(None, "wt"),
            P(None, "wt", None),
            P(None, "ctx", None, "wt"),
            P(None, "ctx", None, "wt"),
            P(None, "ctx", "wt", None),
        ),
        check_vma=False,
    )
```

profile of v0, /device:TPU:0, one launch (start us, length us, event | category | flops | bytes accessed | tf_op | source)
XLA Modules:
  0.0 1955.3 jit_solution(4716241793147687085)
XLA Ops:
  11.0 6.1 all-gather
  17.4 15.2 all-gather.47.cloned.1.call-done
  35.1 19.3 all-gather.51.cloned.1.call-done
  70.4 5.3 all-gather.5
  76.9 20.5 %all-gather.39.cloned.1.call-done = bf16[1024,512]{1,0:T(8,128)(2,1)} async-done(((bf16[128,512]{1,0:T(8,128)(2,1)}), bf16[1024,512]{1,0:T(8,128)(2,1)}) %all-gather.39.cloned.1.call-update) | async-done | bytes 1048592 | tf_op jit(solution)/shard_map/all_gather | solution.py:114
  98.9 39.4 %all-gather.41.cloned.1.call-done = bf16[1024,512]{1,0:T(8,128)(2,1)} async-done(((bf16[128,512]{1,0:T(8,128)(2,1)}), bf16[1024,512]{1,0:T(8,128)(2,1)}) %all-gather.41.cloned.1.call-update) | async-done | bytes 1048592 | tf_op jit(solution)/shard_map/all_gather | solution.py:115
  139.8 36.7 %all-gather.49.cloned.1.call-done = bf16[1,1536,1536]{2,1,0:T(8,128)(2,1)} async-done(((bf16[1,384,1536]{2,1,0:T(8,128)(2,1)}), bf16[1,1536,1536]{2,1,0:T(8,128)(2,1)}) %all-gather.49.cloned.1.call-update) | async-done | bytes 4718608 | tf_op jit(solution)/shard_map/all_gather | solution.py:91
  180.9 8.8 while.68
  182.6 5.4 conditional.8
  191.8 24.2 %all-gather.53.cloned.1.call-done = bf16[1,1536,1536]{2,1,0:T(8,128)(2,1)} async-done(((bf16[1,384,1536]{2,1,0:T(8,128)(2,1)}), bf16[1,1536,1536]{2,1,0:T(8,128)(2,1)}) %all-gather.53.cloned.1.call-update) | async-done | bytes 4718608 | tf_op jit(solution)/shard_map/all_gather | solution.py:94
  220.3 5.7 scatter_custom_fusion
  226.0 5.5 all-to-all-start
  232.1 15.0 all-gather.55.cloned.1.call-done
  247.1 13.5 all-to-all-done
  264.3 13.9 all-gather.57.cloned.1.call-done
  283.0 25.9 %all-gather.59.cloned.1.call-done = bf16[1,1,1024,1536]{3,2,1,0:T(8,128)(2,1)} async-done(((bf16[1,1,256,1536]{3,2,1,0:T(8,128)(2,1)}), bf16[1,1,1024,1536]{3,2,1,0:T(8,128)(2,1)}) %all-gather.59.cloned.1.call-update) | async-done | bytes 3145744 | tf_op jit(solution)/shard_map/all_gather | solution.py:178
  313.4 5.6 all-to-all-start.1
  325.1 5.2 all-gather.6
  333.0 15.0 all-to-all-done.1
  363.5 5.6 all-gather.15
  370.2 21.1 %all-gather.63.cloned.1.call-done = bf16[1,1536,1536]{2,1,0:T(8,128)(2,1)} async-done(((bf16[1,384,1536]{2,1,0:T(8,128)(2,1)}), bf16[1,1536,1536]{2,1,0:T(8,128)(2,1)}) %all-gather.63.cloned.1.call-update) | async-done | bytes 4718608 | tf_op jit(solution)/shard_map/all_gather | solution.py:91
  394.7 39.5 %all-gather.45.cloned.1.call-done = bf16[1024,512]{1,0:T(8,128)(2,1)} async-done(((bf16[128,512]{1,0:T(8,128)(2,1)}), bf16[1024,512]{1,0:T(8,128)(2,1)}) %all-gather.45.cloned.1.call-update) | async-done | bytes 1048592 | tf_op jit(solution)/shard_map/all_gather | solution.py:115
  435.7 40.0 %all-gather.43.cloned.1.call-done = bf16[1024,512]{1,0:T(8,128)(2,1)} async-done(((bf16[128,512]{1,0:T(8,128)(2,1)}), bf16[1024,512]{1,0:T(8,128)(2,1)}) %all-gather.43.cloned.1.call-update) | async-done | bytes 1048592 | tf_op jit(solution)/shard_map/all_gather | solution.py:114
  478.2 8.7 while.69
  479.9 5.4 conditional.9
  489.6 24.4 %all-gather.67.cloned.1.call-done = bf16[1,1536,1536]{2,1,0:T(8,128)(2,1)} async-done(((bf16[1,384,1536]{2,1,0:T(8,128)(2,1)}), bf16[1,1536,1536]{2,1,0:T(8,128)(2,1)}) %all-gather.67.cloned.1.call-update) | async-done | bytes 4718608 | tf_op jit(solution)/shard_map/all_gather | solution.py:94
  518.4 5.8 scatter_custom_fusion.1
  524.2 5.5 all-to-all-start.2
  532.8 5.3 all-gather.16
  543.5 15.4 all-to-all-done.2
  567.3 7.1 all-gather.73.cloned.1.call-done
  574.4 16.8 all-to-all-done.4
  596.1 8.7 all-gather.69.cloned.1.call-done
  604.8 6.2 multiply_convert_fusion.4
  613.4 5.5 all-to-all-start.3
  625.1 22.8 %all-to-all-done.3 = bf16[8,48,1536]{2,1,0:T(8,128)(2,1)S(1)} async-done(((bf16[8,48,1536]{2,1,0:T(8,128)(2,1)}), bf16[8,48,1536]{2,1,0:T(8,128)(2,1)S(1)}, u32[]{:S(2)}, u32[]{:S(2)}) %all-to-all-start.3) | async-done | bytes 1179680 | tf_op jit(solution)/shard_map/all_to_all | solution.py:190
  666.8 13.6 all-to-all-done.5
  699.3 11.1 while.70
  701.4 7.4 conditional.10
  720.3 61.7 %reduce-scatter.61.cloned.1.call-done = bf16[128,512]{1,0:T(8,128)(2,1)} async-done(((bf16[1024,512]{1,0:T(8,128)(2,1)}), bf16[128,512]{1,0:T(8,128)(2,1)}) %reduce-scatter.61.cloned.1.call-update) | async-done | bytes 131088
  783.9 64.9 %reduce-scatter.63.cloned.1.call-done = bf16[128,512]{1,0:T(8,128)(2,1)} async-done(((bf16[1024,512]{1,0:T(8,128)(2,1)}), bf16[128,512]{1,0:T(8,128)(2,1)}) %reduce-scatter.63.cloned.1.call-update) | async-done | bytes 131088
  857.7 30.9 %all_to_all.40 = bf16[8,48,1536]{2,1,0:T(8,128)(2,1)S(1)} all-to-all(bf16[8,48,1536]{2,1,0:T(8,128)(2,1)S(1)} %bitcast.560), channel_id=1, replica_groups=mesh['ctx'=8,'wt'=4] {'ctx'}, dimensions={0} | all-to-all | bytes 2359296 | tf_op jit(solution)/shard_map/all_to_all | solution.py:263
  906.5 23.1 %all-to-all-done.7 = bf16[8,48,1536]{2,1,0:T(8,128)(2,1)S(1)} async-done(((bf16[8,48,1536]{2,1,0:T(8,128)(2,1)}), bf16[8,48,1536]{2,1,0:T(8,128)(2,1)S(1)}, u32[]{:S(2)}, u32[]{:S(2)}) %all-to-all-start.7) | async-done | bytes 1179680 | tf_op jit(solution)/shard_map/all_to_all | solution.py:283
  949.4 11.0 while.71
  951.3 7.4 conditional.11
  976.5 56.1 %reduce-scatter.65.cloned.1.call-done = bf16[128,512]{1,0:T(8,128)(2,1)} async-done(((bf16[1024,512]{1,0:T(8,128)(2,1)}), bf16[128,512]{1,0:T(8,128)(2,1)}) %reduce-scatter.65.cloned.1.call-update) | async-done | bytes 131088
  1035.4 64.1 %reduce-scatter.67.cloned.1.call-done = bf16[128,512]{1,0:T(8,128)(2,1)} async-done(((bf16[1024,512]{1,0:T(8,128)(2,1)}), bf16[128,512]{1,0:T(8,128)(2,1)}) %reduce-scatter.67.cloned.1.call-update) | async-done | bytes 131088
  1145.1 15.5 reduce-scatter.43.cloned.1.call-done
  1160.6 51.0 %reduce-scatter.35.cloned.1.call-done = bf16[384,1536]{1,0:T(8,128)(2,1)} async-done(((bf16[1536,1536]{1,0:T(8,128)(2,1)}), bf16[384,1536]{1,0:T(8,128)(2,1)}) %reduce-scatter.35.cloned.1.call-update) | async-done | bytes 1179664 | tf_op jit(solution)/shard_map/reduce_scatter | solution.py:423
  1211.6 50.4 %reduce-scatter.47.cloned.1.call-done = bf16[384,1536]{1,0:T(8,128)(2,1)} async-done(((bf16[1536,1536]{1,0:T(8,128)(2,1)}), bf16[384,1536]{1,0:T(8,128)(2,1)}) %reduce-scatter.47.cloned.1.call-update) | async-done | bytes 1179664 | tf_op jit(solution)/shard_map/reduce_scatter | solution.py:432
  1262.0 31.2 %reduce-scatter.37.cloned.1.call-done = bf16[384,512]{1,0:T(8,128)(2,1)} async-done(((bf16[1536,512]{1,0:T(8,128)(2,1)}), bf16[384,512]{1,0:T(8,128)(2,1)}) %reduce-scatter.37.cloned.1.call-update) | async-done | bytes 393232 | tf_op jit(solution)/shard_map/reduce_scatter | solution.py:426
  1293.2 30.9 %reduce-scatter.41.cloned.1.call-done = bf16[384,512]{1,0:T(8,128)(2,1)} async-done(((bf16[1536,512]{1,0:T(8,128)(2,1)}), bf16[384,512]{1,0:T(8,128)(2,1)}) %reduce-scatter.41.cloned.1.call-update) | async-done | bytes 393232 | tf_op jit(solution)/shard_map/reduce_scatter | solution.py:429
  1324.2 50.4 %reduce-scatter.45.cloned.1.call-done = bf16[384,1536]{1,0:T(8,128)(2,1)} async-done(((bf16[1536,1536]{1,0:T(8,128)(2,1)}), bf16[384,1536]{1,0:T(8,128)(2,1)}) %reduce-scatter.45.cloned.1.call-update) | async-done | bytes 1179664 | tf_op jit(solution)/shard_map/reduce_scatter | solution.py:432
  1374.6 51.0 %reduce-scatter.33.cloned.1.call-done = bf16[384,1536]{1,0:T(8,128)(2,1)} async-done(((bf16[1536,1536]{1,0:T(8,128)(2,1)}), bf16[384,1536]{1,0:T(8,128)(2,1)}) %reduce-scatter.33.cloned.1.call-update) | async-done | bytes 1179664 | tf_op jit(solution)/shard_map/reduce_scatter | solution.py:423
  1427.5 22.0 %reduce-scatter.71.cloned.1.call-done = bf16[384,8]{1,0:T(8,128)(2,1)} async-done(((bf16[1536,8]{1,0:T(8,128)(2,1)}), bf16[384,8]{1,0:T(8,128)(2,1)}) %reduce-scatter.71.cloned.1.call-update) | async-done | bytes 6160
  1450.5 22.4 %reduce-scatter.69.cloned.1.call-done = bf16[384,8]{1,0:T(8,128)(2,1)} async-done(((bf16[1536,8]{1,0:T(8,128)(2,1)}), bf16[384,8]{1,0:T(8,128)(2,1)}) %reduce-scatter.69.cloned.1.call-update) | async-done | bytes 6160
  1480.3 10.2 all-reduce.6
  1490.8 37.1 %all-reduce.4 = (bf16[1,384]{1,0:T(2,128)(2,1)S(1)}, bf16[1,384]{1,0:T(2,128)(2,1)S(1)}, bf16[1,384]{1,0:T(2,128)(2,1)S(1)}, bf16[1,384]{1,0:T(2,128)(2,1)S(1)},...) all-reduce(bf16[1,384]{1,0:T(2,128)(2,1)S(1)} %stack.135, ...), channel_id=1, replica_groups=mesh['ctx'=8,'wt'=4] {'ctx'}, use_global_device_ids=true, to_apply=%region_71.73 | all-reduce | flops 7680 | bytes 30720 | tf_op jit(solution)/shard_map/psum | solution.py:443
  1530.3 24.3 %reduce-scatter.57.cloned.1.call-done = bf16[256,1536]{1,0:T(8,128)(2,1)} async-done(((bf16[1024,1536]{1,0:T(8,128)(2,1)}), bf16[256,1536]{1,0:T(8,128)(2,1)}) %reduce-scatter.57.cloned.1.call-update) | async-done | bytes 786448 | tf_op jit(solution)/shard_map/reduce_scatter | solution.py:458
  1557.7 37.9 %reduce-scatter.55.cloned.1.call-done = bf16[1536,256]{1,0:T(8,128)(2,1)} async-done(((bf16[1536,1024]{1,0:T(8,128)(2,1)}), bf16[1536,256]{1,0:T(8,128)(2,1)}) %reduce-scatter.55.cloned.1.call-update) | async-done | bytes 786448 | tf_op jit(solution)/shard_map/reduce_scatter | solution.py:455
  1595.6 40.5 %reduce-scatter.53.cloned.1.call-done = bf16[1536,256]{1,0:T(8,128)(2,1)} async-done(((bf16[1536,1024]{1,0:T(8,128)(2,1)}), bf16[1536,256]{1,0:T(8,128)(2,1)}) %reduce-scatter.53.cloned.1.call-update) | async-done | bytes 786448 | tf_op jit(solution)/shard_map/reduce_scatter | solution.py:455
  1639.4 37.7 %reduce-scatter.51.cloned.1.call-done = bf16[1536,256]{1,0:T(8,128)(2,1)} async-done(((bf16[1536,1024]{1,0:T(8,128)(2,1)}), bf16[1536,256]{1,0:T(8,128)(2,1)}) %reduce-scatter.51.cloned.1.call-update) | async-done | bytes 786448 | tf_op jit(solution)/shard_map/reduce_scatter | solution.py:452
  1677.1 40.7 %reduce-scatter.49.cloned.1.call-done = bf16[1536,256]{1,0:T(8,128)(2,1)} async-done(((bf16[1536,1024]{1,0:T(8,128)(2,1)}), bf16[1536,256]{1,0:T(8,128)(2,1)}) %reduce-scatter.49.cloned.1.call-update) | async-done | bytes 786448 | tf_op jit(solution)/shard_map/reduce_scatter | solution.py:452
  1721.0 219.5 %all-reduce.9.cloned.1.call-done = (bf16[1,384,1536]{2,1,0:T(8,128)(2,1)}, bf16[1,384,1536]{2,1,0:T(8,128)(2,1)}, bf16[1,384,512]{2,1,0:T(8,128)(2,1)}, bf16[1,3...) async-done(((bf16[1,384,1536]{2,1,0:T(8,128)(2,1)}, ...) | async-done | bytes 6291472 | tf_op jit(solution)/shard_map/psum | solution.py:444
  (756 shorter events, 341.8 us)
Async XLA Ops:
  7.2 25.4 %all-gather.47.cloned.1.call-start = ((), (), s32[]{:S(2)}) async-start(), calls=%async_computation.46 | async-start | bytes 1966080 | tf_op jit(solution)/shard_map/all_gather | solution.py:92
  9.4 45.0 %all-gather.51.cloned.1.call-start = ((), (), s32[]{:S(2)}) async-start(), calls=%async_computation.48 | async-start | bytes 1966080 | tf_op jit(solution)/shard_map/all_gather | solution.py:93
  10.4 86.9 %all-gather.39.cloned.1.call-start = ((), (), s32[]{:S(2)}) async-start(), calls=%async_computation.28 | async-start | bytes 1179648 | tf_op jit(solution)/shard_map/all_gather | solution.py:114
  17.2 159.4 %copy-start.95 = (f32[1536]{0:T(1024)}, f32[1536]{0:T(1024)S(1)}, u32[]{:S(2)}) copy-start(f32[1536]{0:T(1024)S(1)} %convert_reduce_fusion.3) | copy-start | bytes 18436
  35.1 103.2 %all-gather.41.cloned.1.call-start = ((), (), s32[]{:S(2)}) async-start(), calls=%async_computation.29 | async-start | bytes 1179648 | tf_op jit(solution)/shard_map/all_gather | solution.py:115
  56.9 119.6 %all-gather.49.cloned.1.call-start = ((), (), s32[]{:S(2)}) async-start(), calls=%async_computation.47 | async-start | bytes 5898240 | tf_op jit(solution)/shard_map/all_gather | solution.py:91
  58.6 157.4 %all-gather.53.cloned.1.call-start = ((), (), s32[]{:S(2)}) async-start(), calls=%async_computation.49 | async-start | bytes 5898240 | tf_op jit(solution)/shard_map/all_gather | solution.py:94
  61.9 185.2 %all-gather.55.cloned.1.call-start = ((), (), s32[]{:S(2)}) async-start(), calls=%async_computation.50 | async-start | bytes 3932160 | tf_op jit(solution)/shard_map/all_gather | solution.py:176
  63.3 214.9 %all-gather.57.cloned.1.call-start = ((), (), s32[]{:S(2)}) async-start(), calls=%async_computation.51 | async-start | bytes 3932160 | tf_op jit(solution)/shard_map/all_gather | solution.py:177
  65.2 243.7 %all-gather.59.cloned.1.call-start = ((), (), s32[]{:S(2)}) async-start(), calls=%async_computation.52 | async-start | bytes 3932160 | tf_op jit(solution)/shard_map/all_gather | solution.py:178
  66.5 289.1 %all-gather.65.cloned.1.call-start = ((), (), s32[]{:S(2)}) async-start(), calls=%async_computation.55 | async-start | bytes 1966080 | tf_op jit(solution)/shard_map/all_gather | solution.py:93
  67.1 291.2 %all-gather.61.cloned.1.call-start = ((), (), s32[]{:S(2)}) async-start(), calls=%async_computation.53 | async-start | bytes 1966080 | tf_op jit(solution)/shard_map/all_gather | solution.py:92
  68.4 108.1 %copy-start.130 = (f32[128]{0:T(128)S(1)}, f32[128]{0:T(128)}, u32[]{:S(2)}) copy-start(f32[128]{0:T(128)} %copy-done.129) | copy-start | bytes 1540
  68.5 263.7 %copy-start.43 = (s32[1,1,128,2]{3,2,1,0:T(8,128)}, s32[1,1,128,2]{3,2,1,0:T(8,128)S(1)}, u32[]{:S(2)}) copy-start(s32[1,1,128,2]{3,2,1,0:T(8,128)S(1)} %copy.171) | copy-start | bytes 3076
  75.7 143.6 %copy-start.117 = (f32[1536]{0:T(1024)}, f32[1536]{0:T(1024)S(1)}, u32[]{:S(2)}) copy-start(f32[1536]{0:T(1024)S(1)} %convert_reduce_fusion.2) | copy-start | bytes 18436
  76.7 143.6 %copy-start.170 = (s32[1024]{0:T(1024)}, s32[1024]{0:T(1024)S(1)}, u32[]{:S(2)}) copy-start(s32[1024]{0:T(1024)S(1)} %pad_clamp_fusion.2) | copy-start | bytes 12292
  76.9 253.4 %copy-start.168 = (s32[256,1]{0,1:T(1,128)}, s32[256,1]{0,1:T(1,128)S(1)}, u32[]{:S(2)}) copy-start(s32[256,1]{0,1:T(1,128)S(1)} %compare_select_fusion.4) | copy-start | bytes 3076
  220.3 110.0 %copy-start.58 = (bf16[128,1536]{1,0:T(8,128)(2,1)}, bf16[128,1536]{1,0:T(8,128)(2,1)S(1)}, u32[]{:S(2)}) copy-start(bf16[128,1536]{1,0:T(8,128)(2,1)S(1)} %multiply_convert_fusion.12) | copy-start | bytes 1179652
  226.0 34.5 %all-to-all-start = ((bf16[8,48,1536]{2,1,0:T(8,128)(2,1)}), bf16[8,48,1536]{2,1,0:T(8,128)(2,1)S(1)}, u32[]{:S(2)}, u32[]{:S(2)}) async-start(bf16[8,48,1536]{2,1,0:T(8,128)(2,1)} %bitcast.73), calls=%async_computation | async-start | bytes 2359296 | tf_op jit(solution)/shard_map/all_to_all | solution.py:174
  231.5 159.8 %all-gather.63.cloned.1.call-start = ((), (), s32[]{:S(2)}) async-start(), calls=%async_computation.54 | async-start | bytes 5898240 | tf_op jit(solution)/shard_map/all_gather | solution.py:91
  313.4 34.6 %all-to-all-start.1 = ((bf16[8,48,1536]{2,1,0:T(8,128)(2,1)}), bf16[8,48,1536]{2,1,0:T(8,128)(2,1)S(1)}, u32[]{:S(2)}, u32[]{:S(2)}) async-start(bf16[8,48,1536]{2,1,0:T(8,128)(2,1)} %bitcast.78), calls=%async_computation.1 | async-start | bytes 2359296 | tf_op jit(solution)/shard_map/all_to_all | solution.py:190
  319.1 115.2 %all-gather.45.cloned.1.call-start = ((), (), s32[]{:S(2)}) async-start(), calls=%async_computation.31 | async-start | bytes 1179648 | tf_op jit(solution)/shard_map/all_gather | solution.py:115
  354.8 159.1 %copy-start.21 = (f32[128,1536]{1,0:T(8,128)}, f32[128,1536]{1,0:T(8,128)S(1)}, u32[]{:S(2)}) copy-start(f32[128,1536]{1,0:T(8,128)S(1)} %get-tuple-element.1508) | copy-start | bytes 2359300
  358.2 117.6 %all-gather.43.cloned.1.call-start = ((), (), s32[]{:S(2)}) async-start(), calls=%async_computation.30 | async-start | bytes 1179648 | tf_op jit(solution)/shard_map/all_gather | solution.py:114
  360.8 153.2 %all-gather.67.cloned.1.call-start = ((), (), s32[]{:S(2)}) async-start(), calls=%async_computation.56 | async-start | bytes 5898240 | tf_op jit(solution)/shard_map/all_gather | solution.py:94
  361.3 201.2 %all-gather.71.cloned.1.call-start = ((), (), s32[]{:S(2)}) async-start(), calls=%async_computation.58 | async-start | bytes 3932160 | tf_op jit(solution)/shard_map/all_gather | solution.py:177
  361.9 212.5 %all-gather.73.cloned.1.call-start = ((), (), s32[]{:S(2)}) async-start(), calls=%async_computation.59 | async-start | bytes 3932160 | tf_op jit(solution)/shard_map/all_gather | solution.py:178
  362.5 242.3 %all-gather.69.cloned.1.call-start = ((), (), s32[]{:S(2)}) async-start(), calls=%async_computation.57 | async-start | bytes 3932160 | tf_op jit(solution)/shard_map/all_gather | solution.py:176
  363.2 166.5 %copy-start.44 = (s32[1,1,128,2]{3,2,1,0:T(8,128)}, s32[1,1,128,2]{3,2,1,0:T(8,128)S(1)}, u32[]{:S(2)}) copy-start(s32[1,1,128,2]{3,2,1,0:T(8,128)S(1)} %copy.172) | copy-start | bytes 3076
  369.1 148.3 %copy-start.121 = (f32[1536]{0:T(1024)}, f32[1536]{0:T(1024)S(1)}, u32[]{:S(2)}) copy-start(f32[1536]{0:T(1024)S(1)} %convert_reduce_fusion) | copy-start | bytes 18436
  370.2 148.2 %copy-start.169 = (s32[256,1]{0,1:T(1,128)}, s32[256,1]{0,1:T(1,128)S(1)}, u32[]{:S(2)}) copy-start(s32[256,1]{0,1:T(1,128)S(1)} %compare_select_fusion.2) | copy-start | bytes 3076
  394.7 83.5 %copy-start.109 = (s32[128]{0:T(128)S(1)}, s32[128]{0:T(128)}, u32[]{:S(2)}) copy-start(s32[128]{0:T(128)} %copy-done.108) | copy-start | bytes 1540
  394.7 83.5 %copy-start.113 = (s32[128]{0:T(128)S(1)}, s32[128]{0:T(128)}, u32[]{:S(2)}) copy-start(s32[128]{0:T(128)} %copy-done.112) | copy-start | bytes 1540
  524.2 34.6 %all-to-all-start.2 = ((bf16[8,48,1536]{2,1,0:T(8,128)(2,1)}), bf16[8,48,1536]{2,1,0:T(8,128)(2,1)}, u32[]{:S(2)}, u32[]{:S(2)}) async-start(bf16[8,48,1536]{2,1,0:T(8,128)(2,1)} %bitcast.94), calls=%async_computation.2 | async-start | bytes 2359296 | tf_op jit(solution)/shard_map/all_to_all | solution.py:174
  538.4 146.3 %copy-start.2 = (f32[128,8]{0,1:T(8,128)}, f32[128,8]{0,1:T(8,128)S(1)}, u32[]{:S(2)}) copy-start(f32[128,8]{0,1:T(8,128)S(1)} %fusion.212) | copy-start | bytes 12292
  558.8 32.4 %all-to-all-start.4 = ((bf16[8,48,1536]{2,1,0:T(8,128)(2,1)}), bf16[8,48,1536]{2,1,0:T(8,128)(2,1)S(1)}, u32[]{:S(2)}, u32[]{:S(2)}) async-start(bf16[8,48,1536]{2,1,0:T(8,128)(2,1)} %bitcast.559), calls=%async_computation.4 | async-start | bytes 2359296 | tf_op jit(solution)/shard_map/all_to_all | solution.py:263
  613.4 34.5 %all-to-all-start.3 = ((bf16[8,48,1536]{2,1,0:T(8,128)(2,1)}), bf16[8,48,1536]{2,1,0:T(8,128)(2,1)S(1)}, u32[]{:S(2)}, u32[]{:S(2)}) async-start(bf16[8,48,1536]{2,1,0:T(8,128)(2,1)} %bitcast.99), calls=%async_computation.3 | async-start | bytes 2359296 | tf_op jit(solution)/shard_map/all_to_all | solution.py:190
  647.9 32.4 %all-to-all-start.5 = ((bf16[8,48,1536]{2,1,0:T(8,128)(2,1)}), bf16[8,48,1536]{2,1,0:T(8,128)(2,1)S(1)}, u32[]{:S(2)}, u32[]{:S(2)}) async-start(bf16[8,48,1536]{2,1,0:T(8,128)(2,1)} %bitcast.579), calls=%async_computation.5 | async-start | bytes 2359296 | tf_op jit(solution)/shard_map/all_to_all | solution.py:283
  651.7 130.3 %reduce-scatter.61.cloned.1.call-start = ((), (), s32[]{:S(2)}) async-start(), calls=%async_computation.60 | async-start | bytes 1179648
  712.9 135.8 %reduce-scatter.63.cloned.1.call-start = ((), (), s32[]{:S(2)}) async-start(), calls=%async_computation.61 | async-start | bytes 1179648
  720.3 128.4 %copy-start.22 = (f32[128,1536]{1,0:T(8,128)S(1)}, f32[128,1536]{1,0:T(8,128)}, u32[]{:S(2)}) copy-start(f32[128,1536]{1,0:T(8,128)} %copy-done.21) | copy-start | bytes 2359300
  720.3 128.4 %copy-start.120 = (f32[1536]{0:T(1024)S(1)}, f32[1536]{0:T(1024)}, u32[]{:S(2)}) copy-start(f32[1536]{0:T(1024)} %copy-done.119) | copy-start | bytes 18436
  720.3 128.4 %copy-start.164 = (f32[128]{0:T(128)S(1)}, f32[128]{0:T(128)}, u32[]{:S(2)}) copy-start(f32[128]{0:T(128)} %copy-done.163) | copy-start | bytes 1540
  783.9 67.7 %copy-start.28 = (f32[128,1536]{1,0:T(8,128)S(1)}, f32[128,1536]{1,0:T(8,128)}, u32[]{:S(2)}) copy-start(f32[128,1536]{1,0:T(8,128)} %copy-done.27) | copy-start | bytes 2359300
  898.2 31.4 %all-to-all-start.7 = ((bf16[8,48,1536]{2,1,0:T(8,128)(2,1)}), bf16[8,48,1536]{2,1,0:T(8,128)(2,1)S(1)}, u32[]{:S(2)}, u32[]{:S(2)}) async-start(bf16[8,48,1536]{2,1,0:T(8,128)(2,1)} %bitcast.580), calls=%async_computation.7 | async-start | bytes 2359296 | tf_op jit(solution)/shard_map/all_to_all | solution.py:283
  901.9 130.7 %reduce-scatter.65.cloned.1.call-start = ((), (), s32[]{:S(2)}) async-start(), calls=%async_computation.62 | async-start | bytes 1179648
  962.8 136.7 %reduce-scatter.67.cloned.1.call-start = ((), (), s32[]{:S(2)}) async-start(), calls=%async_computation.63 | async-start | bytes 1179648
  964.2 180.8 %reduce-scatter.39.cloned.1.call-start = ((), (), s32[]{:S(2)}) async-start(), calls=%async_computation.35 | async-start | bytes 1966080 | tf_op jit(solution)/shard_map/reduce_scatter | solution.py:426
  966.1 194.5 %reduce-scatter.43.cloned.1.call-start = ((), (), s32[]{:S(2)}) async-start(), calls=%async_computation.37 | async-start | bytes 1966080 | tf_op jit(solution)/shard_map/reduce_scatter | solution.py:429
  967.9 243.7 %reduce-scatter.35.cloned.1.call-start = ((), (), s32[]{:S(2)}) async-start(), calls=%async_computation.33 | async-start | bytes 5898240 | tf_op jit(solution)/shard_map/reduce_scatter | solution.py:423
  971.6 290.4 %reduce-scatter.47.cloned.1.call-start = ((), (), s32[]{:S(2)}) async-start(), calls=%async_computation.39 | async-start | bytes 5898240 | tf_op jit(solution)/shard_map/reduce_scatter | solution.py:432
  976.5 316.8 %reduce-scatter.37.cloned.1.call-start = ((), (), s32[]{:S(2)}) async-start(), calls=%async_computation.34 | async-start | bytes 1966080 | tf_op jit(solution)/shard_map/reduce_scatter | solution.py:426
  1035.4 288.8 %reduce-scatter.41.cloned.1.call-start = ((), (), s32[]{:S(2)}) async-start(), calls=%async_computation.36 | async-start | bytes 1966080 | tf_op jit(solution)/shard_map/reduce_scatter | solution.py:429
  1102.2 272.4 %reduce-scatter.45.cloned.1.call-start = ((), (), s32[]{:S(2)}) async-start(), calls=%async_computation.38 | async-start | bytes 5898240 | tf_op jit(solution)/shard_map/reduce_scatter | solution.py:432
  1106.2 319.4 %reduce-scatter.33.cloned.1.call-start = ((), (), s32[]{:S(2)}) async-start(), calls=%async_computation.32 | async-start | bytes 5898240 | tf_op jit(solution)/shard_map/reduce_scatter | solution.py:423
  1110.1 339.4 %reduce-scatter.71.cloned.1.call-start = ((), (), s32[]{:S(2)}) async-start(), calls=%async_computation.65 | async-start | bytes 491520
  1112.3 360.6 %reduce-scatter.69.cloned.1.call-start = ((), (), s32[]{:S(2)}) async-start(), calls=%async_computation.64 | async-start | bytes 491520
  1113.6 416.7 %reduce-scatter.59.cloned.1.call-start = ((), (), s32[]{:S(2)}) async-start(), calls=%async_computation.45 | async-start | bytes 3932160 | tf_op jit(solution)/shard_map/reduce_scatter | solution.py:458
  1118.5 436.1 %reduce-scatter.57.cloned.1.call-start = ((), (), s32[]{:S(2)}) async-start(), calls=%async_computation.44 | async-start | bytes 3932160 | tf_op jit(solution)/shard_map/reduce_scatter | solution.py:458
  1123.5 472.1 %reduce-scatter.55.cloned.1.call-start = ((), (), s32[]{:S(2)}) async-start(), calls=%async_computation.43 | async-start | bytes 3932160 | tf_op jit(solution)/shard_map/reduce_scatter | solution.py:455
  1129.4 506.8 %reduce-scatter.53.cloned.1.call-start = ((), (), s32[]{:S(2)}) async-start(), calls=%async_computation.42 | async-start | bytes 3932160 | tf_op jit(solution)/shard_map/reduce_scatter | solution.py:455
  1134.4 542.7 %reduce-scatter.51.cloned.1.call-start = ((), (), s32[]{:S(2)}) async-start(), calls=%async_computation.41 | async-start | bytes 3932160 | tf_op jit(solution)/shard_map/reduce_scatter | solution.py:452
  1140.3 577.4 %reduce-scatter.49.cloned.1.call-start = ((), (), s32[]{:S(2)}) async-start(), calls=%async_computation.40 | async-start | bytes 3932160 | tf_op jit(solution)/shard_map/reduce_scatter | solution.py:452
  1145.0 795.5 %all-reduce.9.cloned.1.call-start = ((), (), s32[]{:S(2)}) async-start(), calls=%async_computation.66 | async-start | bytes 12582912 | tf_op jit(solution)/shard_map/psum | solution.py:444
  (180 other events, 1666.6 us)
Sparse Core Ops, SparseCore 0:
  10.2 22.3 all-gather.46
  34.7 19.6 all-gather.50
  57.1 40.2 all-gather.38
  99.3 38.8 all-gather.40
  140.3 36.1 all-gather.48
  178.5 37.4 all-gather.52
  218.1 28.9 all-gather.54
  249.2 28.9 all-gather.56
  280.3 28.5 all-gather.58
  310.3 19.6 all-gather.64
  332.2 19.6 all-gather.60
  353.8 37.4 all-gather.62
  394.1 40.1 all-gather.44
  436.8 38.8 all-gather.42
  477.7 36.1 all-gather.66
  515.4 29.0 all-gather.70
  545.9 28.5 all-gather.72
  575.9 28.9 all-gather.68
  713.0 68.9 reduce-scatter.60
  786.2 62.4 reduce-scatter.62
  963.0 69.6 reduce-scatter.64
  1037.0 62.4 reduce-scatter.66
  1102.6 27.1 reduce-scatter.38
  1132.4 28.1 reduce-scatter.42
  1163.7 47.8 reduce-scatter.34
  1214.2 47.8 reduce-scatter.46
  1265.0 28.1 reduce-scatter.36
  1295.9 28.1 reduce-scatter.40
  1326.7 47.8 reduce-scatter.44
  1377.7 47.8 reduce-scatter.32
  1428.7 20.7 reduce-scatter.70
  1452.0 20.7 reduce-scatter.68
  1475.8 37.9 reduce-scatter.58
  1516.5 37.9 reduce-scatter.56
  1557.6 37.9 reduce-scatter.54
  1598.2 37.9 reduce-scatter.52
  1639.1 37.9 reduce-scatter.50
  1679.8 37.9 reduce-scatter.48
  1722.9 217.5 all-reduce.8
where the time goes:
time: 1960 us
  waiting for transfers between devices  1450 us (74%)
  matrix products  165 us (8%)
  blocking collectives  111 us (6%)
  local copies, waits for them, and re-layouts  106 us (5%)
  other arithmetic  66.1 us (3%)
  starting transfers between devices  35.5 us (2%)
    unnamed x45, waiting for transfers between devices  295 us
    psum x1, waiting for transfers between devices, local(): lax.psum(part_query.astype(jnp.bfloat16), 'ctx').astype(jnp.float32)  219 us
    reduce_scatter x2, waiting for transfers between devices, local(): lax.psum_scatter(grad_query_weight.astype(jnp.bfloat16), 'wt', scatter_di...  102 us
    reduce_scatter x2, waiting for transfers between devices, local(): lax.psum_scatter(grad_out.astype(jnp.bfloat16), 'wt', scatter_dimension=0...  101 us
    all_gather x2, waiting for transfers between devices, local(): value_piece = lax.all_gather(values, 'ctx', axis=0, tiled=True)  78.9 us
    reduce_scatter x2, waiting for transfers between devices, local(): lax.psum_scatter(grad_gate.astype(jnp.bfloat16), 'wt', scatter_dimension=...  78.4 us
    reduce_scatter x2, waiting for transfers between devices, local(): lax.psum_scatter(grad_up.astype(jnp.bfloat16), 'wt', scatter_dimension=1,...  78.4 us
    all_gather x2, waiting for transfers between devices, local(): key_piece = lax.all_gather(keys, 'ctx', axis=0, tiled=True)  60.5 us
  transfers between devices with their start and end apart: 46, of which 41 were waited for; matrix products, arithmetic and copies ran while one was open for 11% of the time, Pallas kernels for 0%

commit v1 on v0

--- a/solution.py
+++ b/solution.py
@@ -1,6 +1,10 @@
+import functools
+
 import jax
 import jax.numpy as jnp
 from jax import lax
+from jax.experimental import pallas as pl
+from jax.experimental.pallas import tpu as pltpu
 from jax.sharding import PartitionSpec as P
 
 HEADS = 24
@@ -43,7 +47,473 @@
     return state
 
 
-def local(
+def times(left, right, a, b):
+    return lax.dot_general(left, right, (((a,), (b,)), ((), ())), preferred_element_type=jnp.float32)
+
+
+def causal_mask(keys_count, span):
+    key_at = lax.broadcasted_iota(jnp.int32, (span, span), 0)
+    query_at = lax.broadcasted_iota(jnp.int32, (span, span), 1)
+    return key_at <= query_at
+
+
+def attend_kernel(rep, head, span, owner_ref, qkv_ref, sent_ref, exact_ref, log_ref):
+    tokens = qkv_ref.shape[1]
+    width = rep * head
+    blocks = span // BLK
+    scale = head ** (-0.5)
+    mask = causal_mask(span, span)
+    for part in range(tokens // span):
+        lanes = pl.ds(part * span, span)
+        seen = (part + 1) * span
+        keys = qkv_ref[width : width + head, :seen]
+        values = qkv_ref[width + head :, :seen]
+        for h in range(rep):
+            rows = slice(h * head, (h + 1) * head)
+            scores = times(keys, qkv_ref[rows, lanes], 0, 0) * scale
+            last = jnp.where(mask, scores[seen - span :], NEG)
+            top = jnp.max(last, axis=0, keepdims=True)
+            if part:
+                top = jnp.maximum(top, jnp.max(scores[: seen - span], axis=0, keepdims=True))
+            last = jnp.exp(last - top)
+            weights = last if part == 0 else jnp.concatenate([jnp.exp(scores[: seen - span] - top), last], axis=0)
+            total = jnp.sum(weights, axis=0, keepdims=True)
+            result = times(values, weights.astype(jnp.bfloat16), 1, 0) / total
+            exact_ref[rows, lanes] = result
+            log_ref[h : h + 1, lanes] = top + jnp.log(total)
+            for b in range(blocks):
+                sent_ref[owner_ref[part * blocks + b], rows, :] = result[:, b * BLK : (b + 1) * BLK].astype(jnp.bfloat16)
+
+
+def attend_back_kernel(rep, head, span, owner_ref, qkv_ref, exact_ref, log_ref, grad_ref, whole_ref, sent_ref, grad_all, keys_sum, values_sum):
+    tokens = qkv_ref.shape[1]
+    width = rep * head
+    blocks = span // BLK
+    scale = head ** (-0.5)
+    mask = causal_mask(span, span)
+    for block in range(tokens // BLK):
+        grad_all[:, block * BLK : (block + 1) * BLK] = grad_ref[owner_ref[block]]
+    keys_sum[...] = jnp.zeros_like(keys_sum)
+    values_sum[...] = jnp.zeros_like(values_sum)
+    for part in range(tokens // span):
+        lanes = pl.ds(part * span, span)
+        seen = (part + 1) * span
+        keys = qkv_ref[width : width + head, :seen]
+        values = qkv_ref[width + head :, :seen]
+        for h in range(rep):
+            rows = slice(h * head, (h + 1) * head)
+            queries = qkv_ref[rows, lanes]
+            grads = grad_all[rows, lanes]
+            delta = jnp.sum(grads.astype(jnp.float32) * exact_ref[rows, lanes], axis=0, keepdims=True)
+            scores = times(keys, queries, 0, 0) * scale
+            probs = jnp.exp(scores - log_ref[h : h + 1, lanes])
+            last = jnp.where(mask, probs[seen - span :], 0.0)
+            probs = last if part == 0 else jnp.concatenate([probs[: seen - span], last], axis=0)
+            pulled = times(values, grads, 0, 0)
+            slopes = (probs * (pulled - delta)).astype(jnp.bfloat16)
+            back = (times(keys, slopes, 1, 0) * scale).astype(jnp.bfloat16)
+            whole_ref[rows, lanes] = back
+            for b in range(blocks):
+                sent_ref[owner_ref[part * blocks + b], rows, :] = back[:, b * BLK : (b + 1) * BLK]
+            keys_sum[:, :seen] += times(queries, slopes, 1, 1)
+            values_sum[:, :seen] += times(grads, probs.astype(jnp.bfloat16), 1, 1)
+    keys_low = (keys_sum[...] * scale).astype(jnp.bfloat16)
+    values_low = values_sum[...].astype(jnp.bfloat16)
+    whole_ref[width : width + head, :] = keys_low
+    whole_ref[width + head :, :] = values_low
+    for block in range(tokens // BLK):
+        cut = slice(block * BLK, (block + 1) * BLK)
+        sent_ref[owner_ref[block], width : width + head, :] = keys_low[:, cut]
+        sent_ref[owner_ref[block], width + head :, :] = values_low[:, cut]
+
+
+def attend(owner_of, qkv, rep, head, count):
+    tokens = qkv.shape[1]
+    span = min(256, tokens)
+    pairs = rep * tokens * (tokens + span) // 2
+    return pl.pallas_call(
+        functools.partial(attend_kernel, rep, head, span),
+        out_shape=(
+            jax.ShapeDtypeStruct((count, rep * head, BLK), jnp.bfloat16),
+            jax.ShapeDtypeStruct((rep * head, tokens), jnp.float32),
+            jax.ShapeDtypeStruct((rep, tokens), jnp.float32),
+        ),
+        in_specs=[pl.BlockSpec(memory_space=pltpu.SMEM), pl.BlockSpec(memory_space=pltpu.VMEM)],
+        out_specs=(pl.BlockSpec(memory_space=pltpu.VMEM),) * 3,
+        compiler_params=pltpu.CompilerParams(vmem_limit_bytes=40 * 2**20),
+        cost_estimate=pl.CostEstimate(flops=4 * head * pairs, bytes_accessed=4 * 2**20, transcendentals=pairs),
+        name="attend",
+    )(owner_of, qkv)
+
+
+def attend_back(owner_of, qkv, exact, log_total, grads, rep, head, count):
+    tokens = qkv.shape[1]
+    span = min(256, tokens)
+    pairs = rep * tokens * (tokens + span) // 2
+    rows = qkv.shape[0]
+    return pl.pallas_call(
+        functools.partial(attend_back_kernel, rep, head, span),
+        out_shape=(
+            jax.ShapeDtypeStruct((rows, tokens), jnp.bfloat16),
+            jax.ShapeDtypeStruct((count, rows, BLK), jnp.bfloat16),
+        ),
+        in_specs=[pl.BlockSpec(memory_space=pltpu.SMEM)] + [pl.BlockSpec(memory_space=pltpu.VMEM)] * 4,
+        out_specs=(pl.BlockSpec(memory_space=pltpu.VMEM),) * 2,
+        scratch_shapes=[
+            pltpu.VMEM((rep * head, tokens), jnp.bfloat16),
+            pltpu.VMEM((head, tokens), jnp.float32),
+            pltpu.VMEM((head, tokens), jnp.float32),
+        ],
+        compiler_params=pltpu.CompilerParams(vmem_limit_bytes=40 * 2**20),
+        cost_estimate=pl.CostEstimate(flops=10 * head * pairs, bytes_accessed=6 * 2**20, transcendentals=pairs),
+        name="attend_back",
+    )(owner_of, qkv, exact, log_total, grads)
+
+
+def swap(x, axis, count, mask):
+    return lax.ppermute(x, axis, [(i, i ^ mask) for i in range(count)])
+
+
+def wt_gather(own):
+    far = swap(own, "wt", 4, 2)
+    near = swap(own, "wt", 4, 1)
+    return (own, near, far, swap(far, "wt", 4, 1))
+
+
+def wt_scatter_sum(pieces):
+    got = swap(jnp.stack([pieces[1], pieces[3]]).astype(jnp.bfloat16), "wt", 4, 1).astype(jnp.float32)
+    kept = pieces[0] + got[0]
+    far = swap((pieces[2] + got[1]).astype(jnp.bfloat16), "wt", 4, 2)
+    return kept + far.astype(jnp.float32)
+
+
+def wt_exchange(slices, me):
+    def cut(m):
+        return lax.dynamic_index_in_dim(slices, me ^ m, 0, keepdims=False)
+
+    far = swap(jnp.stack([cut(2), cut(3)]), "wt", 4, 2)
+    near = swap(jnp.stack([cut(1), far[1]]), "wt", 4, 1)
+    return (cut(0), near[0], far[0], near[1])
+
+
+def in_order(pieces, me, axis):
+    own, near, far, last = pieces
+    odd, high = me % 2 == 1, me >= 2
+    low = (jnp.where(odd, near, own), jnp.where(odd, own, near))
+    up = (jnp.where(odd, last, far), jnp.where(odd, far, last))
+    first = [jnp.where(high, b, a) for a, b in zip(low, up)]
+    second = [jnp.where(high, a, b) for a, b in zip(low, up)]
+    return jnp.concatenate(first + second, axis=axis)
+
+
+def tie(*arrays):
+    return lax.optimization_barrier(arrays)
+
+
+def ring_gather(x, me, count, place):
+    ring = list(range(0, count, 2)) + list(range(count - 1, 0, -2))
+    around = jnp.asarray([[ring[(ring.index(i) + k) % count] for k in range(count)] for i in range(count)], jnp.int32)
+    spots = place[lax.dynamic_index_in_dim(around, me, 0, keepdims=False)].astype(jnp.uint32)
+    right = [(ring[i], ring[(i + 1) % count]) for i in range(count)]
+    left = [(b, a) for a, b in right]
+    full = jnp.zeros((count,) + x.shape, x.dtype)
+
+    def put(full, block, offset):
+        return lax.dynamic_update_index_in_dim(full, block, spots[offset % count], 0)
+
+    full = put(full, x, 0)
+    ahead = behind = x
+    for step in range(1, count // 2):
+        ahead, behind = lax.ppermute(ahead, "ctx", right), lax.ppermute(behind, "ctx", left)
+        full = put(put(full, ahead, -step), behind, step)
+    half = x.shape[0] // 2
+    last = jnp.concatenate([lax.ppermute(ahead[:half], "ctx", right), lax.ppermute(behind[half:], "ctx", left)])
+    return put(full, last, count // 2)
+
+
+def all_to_all(x):
+    return lax.all_to_all(x, "ctx", split_axis=0, concat_axis=0, tiled=True)
+
+
+def rms_back(rows, gain, grad):
+    scale = lax.rsqrt(jnp.mean(rows * rows, axis=-1, keepdims=True) + EPS)
+    unit = rows * scale
+    pulled = grad * gain
+    return scale * (pulled - unit * jnp.mean(pulled * unit, axis=-1, keepdims=True)), grad * unit
+
+
+def by_heads(mesh, tokens, cotangent, seq_lengths, block_deal, *rest):
+    return (
+        mesh.shape["ctx"] == KV_HEADS
+        and mesh.shape["wt"] == 4
+        and seq_lengths.shape[1] == 1
+        and block_deal.shape[2] == 1
+        and tokens.shape[1] == BLK
+    )
+
+
+def local_heads(
+    mesh,
+    tokens,
+    cotangent,
+    seq_lengths,
+    block_deal,
+    routes,
+    attention_gain,
+    query_weight,
+    key_weight,
+    value_weight,
+    out_weight,
+    mixture_gain,
+    router_weight,
+    gate_weight,
+    up_weight,
+    down_weight,
+):
+    n_ctx = mesh.shape["ctx"]
+    rows = tokens.shape[1]
+    width = tokens.shape[2]
+    layers = query_weight.shape[0]
+    experts = router_weight.shape[2]
+    capacity = 3 * rows // experts
+    rep = HEADS // KV_HEADS
+    wide = rep * HEAD
+    part = width // 4
+    hidden = gate_weight.shape[3]
+    ctx = lax.axis_index("ctx")
+    wt = lax.axis_index("wt").astype(jnp.uint32)
+    table = block_deal[0, :, 0]
+    devices = jnp.arange(n_ctx, dtype=jnp.int32)
+    owner_of = jnp.sum(jnp.where(table[None, :] == devices[:, None], devices[None, :], 0), axis=1)
+
+    expert_ids = jnp.arange(experts, dtype=jnp.int32)
+    chosen = routes[:, 0]
+    flat = chosen.reshape(layers, 2 * rows)
+    onehot = flat[:, :, None] == expert_ids
+    earlier = jnp.tril(jnp.ones((2 * rows, 2 * rows), jnp.bfloat16), -1)
+    rank = jnp.einsum("ij,lje->lie", earlier, onehot.astype(jnp.bfloat16), preferred_element_type=jnp.float32)
+    rank = jnp.sum(jnp.where(onehot, rank, 0.0), axis=2).astype(jnp.int32)
+    slots = (flat * capacity + rank).reshape(layers, rows, 2).transpose(0, 2, 1)
+    place = (slots[..., None] == jnp.arange(experts * capacity, dtype=jnp.int32)).astype(jnp.bfloat16)
+    named = (chosen.transpose(0, 2, 1)[..., None] == expert_ids).astype(jnp.float32)
+
+    def head_rows(layer):
+        return [
+            lax.dynamic_slice_in_dim(query_weight[layer], ctx * wide, wide, 1).T,
+            lax.dynamic_slice_in_dim(key_weight[layer], ctx * HEAD, HEAD, 1).T,
+            lax.dynamic_slice_in_dim(value_weight[layer], ctx * HEAD, HEAD, 1).T,
+            router_weight[layer].T,
+            attention_gain[layer][None],
+            mixture_gain[layer][None],
+            jnp.zeros((14 - experts, part), jnp.bfloat16),
+        ]
+
+    lanes = wide + 2 * HEAD
+    deep = lanes + 16
+    head_own = jnp.concatenate(sum([head_rows(layer) for layer in range(layers)], []), axis=0)
+    head_all = in_order(wt_gather(head_own), wt, 1).reshape(layers, deep, width)
+    token_all = ring_gather(tokens[0], ctx, n_ctx, table).reshape(n_ctx * rows, width)
+
+    def far_start(own):
+        return swap(own, "wt", 4, 2), own
+
+    def near_finish(far, own):
+        return (own, swap(own, "wt", 4, 1), far, swap(far, "wt", 4, 1))
+
+    far_pair = [
+        far_start(jnp.concatenate([gate_weight[layer, 0], up_weight[layer, 0]], axis=1)) for layer in range(layers)
+    ]
+    far_down = [far_start(down_weight[layer, 0]) for layer in range(layers)]
+    far_project = [
+        far_start(jnp.concatenate([query_weight[layer], key_weight[layer], value_weight[layer]], axis=1))
+        for layer in range(layers)
+    ]
+
+    state = tokens[0].astype(jnp.float32)
+    saved = []
+    for layer in range(layers):
+        head_weight = head_all[layer, :lanes]
+        router = head_all[layer, lanes : lanes + experts]
+        gain_one = head_all[layer, lanes + experts : lanes + experts + 1].astype(jnp.float32)
+        gain_two = head_all[layer, lanes + experts + 1 : lanes + experts + 2].astype(jnp.float32)
+        out_pieces = wt_gather(out_weight[layer])
+        pair_far, pair_own = far_pair[layer]
+        down_far, down_own = far_down[layer]
+        if layer == 0:
+            normed = rms_scale(token_all.astype(jnp.float32), gain_one).astype(jnp.bfloat16)
+        else:
+            normed = rms_scale(state, gain_one).astype(jnp.bfloat16)
+            normed = ring_gather(normed, ctx, n_ctx, table).reshape(n_ctx * rows, width)
+        qkv = times(head_weight, normed, 1, 1).astype(jnp.bfloat16)
+        sent, exact, log_total = attend(owner_of, qkv, rep, HEAD, n_ctx)
+        sent, pair_far = tie(sent, pair_far)
+        pair_pieces = near_finish(pair_far, pair_own)
+        attended = all_to_all(sent).reshape(4, part, rows)
+        middle = state
+        for m in range(4):
+            middle = middle + times(lax.dynamic_index_in_dim(attended, wt ^ m, 0, keepdims=False), out_pieces[m], 0, 0)
+        mixed = rms_scale(middle, gain_two).astype(jnp.bfloat16)
+        probs = jax.nn.softmax(times(mixed, router, 1, 1), axis=-1)
+        picked = jnp.sum(named[layer] * probs[None], axis=-1, keepdims=True)
+        pair_total = picked[0] + picked[1]
+        gates = picked / pair_total
+        both = place[layer, 0] + place[layer, 1]
+        outgoing = times(both, mixed, 0, 0).astype(jnp.bfloat16).reshape(experts, capacity, width)
+        if layer == 0:
+            outgoing, down_far = tie(outgoing, down_far)
+        else:
+            outgoing, down_far = tie(outgoing, down_far)
+        down_pieces = near_finish(down_far, down_own)
+        arrived = all_to_all(outgoing).reshape(experts * capacity, width)
+        pairs = [times(arrived, piece, 1, 0) for piece in pair_pieces]
+        inner = [(jax.nn.silu(p[:, :hidden]) * p[:, hidden:]).astype(jnp.bfloat16) for p in pairs]
+        produced = sum(times(z, piece, 1, 0) for z, piece in zip(inner, down_pieces)).astype(jnp.bfloat16)
+        returned = all_to_all(produced.reshape(experts, capacity, width)).reshape(experts * capacity, width)
+        results = [times(place[layer, choice], returned, 1, 0) for choice in range(2)]
+        saved.append(
+            dict(
+                state=state,
+                normed=normed,
+                qkv=qkv,
+                exact=exact,
+                log_total=log_total,
+                attended=attended,
+                middle=middle,
+                mixed=mixed,
+                probs=probs,
+                pair_total=pair_total,
+                gates=gates,
+                both=both,
+                arrived=arrived,
+                pairs=pairs,
+                inner=inner,
+                results=results,
+                gain_one=gain_one,
+                gain_two=gain_two,
+                router=router,
+                out_pieces=out_pieces,
+                pair_pieces=pair_pieces,
+                down_pieces=down_pieces,
+            )
+        )
+        state = middle + gates[0] * results[0] + gates[1] * results[1]
+    block_output = state.astype(jnp.bfloat16)[None]
+
+    upstream = cotangent[0].astype(jnp.float32)
+    grads = [None] * layers
+    for layer in reversed(range(layers)):
+        k = saved[layer]
+        gates = k["gates"]
+        back_rows = (gates * upstream[None]).astype(jnp.bfloat16).reshape(2 * rows, width)
+        outgoing = times(place[layer].reshape(2 * rows, -1), back_rows, 0, 0).astype(jnp.bfloat16)
+        arrived_grad = all_to_all(outgoing.reshape(experts, capacity, width)).reshape(experts * capacity, width)
+        grad_rows = 0.0
+        pair_grads, down_grads = [], []
+        for m in range(4):
+            gate_value, up_value = k["pairs"][m][:, :hidden], k["pairs"][m][:, hidden:]
+            grad_inner = times(arrived_grad, k["down_pieces"][m], 1, 1)
+            sigma = jax.nn.sigmoid(gate_value)
+            grad_pair = jnp.concatenate(
+                [
+                    (grad_inner * up_value * sigma * (1.0 + gate_value * (1.0 - sigma))).astype(jnp.bfloat16),
+                    (grad_inner * gate_value * sigma).astype(jnp.bfloat16),
+                ],
+                axis=1,
+            )
+            grad_rows = grad_rows + times(grad_pair, k["pair_pieces"][m], 1, 1)
+            pair_grads.append(times(k["arrived"], grad_pair, 0, 0))
+            down_grads.append(times(k["inner"][m], arrived_grad, 0, 0))
+        pair_sum = wt_scatter_sum(pair_grads)
+        down_sum = wt_scatter_sum(down_grads)
+        back = all_to_all(grad_rows.astype(jnp.bfloat16).reshape(experts, capacity, width))
+        grad_mixed = times(k["both"], back.reshape(experts * capacity, width), 1, 0)
+        signal = jnp.stack([jnp.sum(upstream * r, axis=-1, keepdims=True) for r in k["results"]])
+        grad_picked = (signal - jnp.sum(gates * signal, axis=0, keepdims=True)) / k["pair_total"][None]
+        grad_probs = jnp.sum(grad_picked * named[layer], axis=0)
+        grad_logits = k["probs"] * (grad_probs - jnp.sum(k["probs"] * grad_probs, axis=1, keepdims=True))
+        router_part = lax.dot_general(
+            k["mixed"].astype(jnp.float32),
+            grad_logits,
+            (((0,), (0,)), ((), ())),
+            precision=lax.Precision.HIGHEST,
+            preferred_element_type=jnp.float32,
+        )
+        grad_mixed = grad_mixed + lax.dot_general(
+            grad_logits,
+            k["router"].astype(jnp.float32),
+            (((1,), (0,)), ((), ())),
+            precision=lax.Precision.HIGHEST,
+            preferred_element_type=jnp.float32,
+        )
+        pulled, gain_two_rows = rms_back(k["middle"], k["gain_two"], grad_mixed)
+        grad_middle = upstream + pulled
+        middle_low = grad_middle.astype(jnp.bfloat16)
+        grad_attended = jnp.zeros((4, part, rows), jnp.bfloat16)
+        for m in range(4):
+            grad_attended = lax.dynamic_update_index_in_dim(
+                grad_attended, times(k["out_pieces"][m], middle_low, 1, 1).astype(jnp.bfloat16), wt ^ m, 0
+            )
+        grad_heads = all_to_all(grad_attended.reshape(n_ctx, wide, rows))
+        grad_whole, grad_sent = attend_back(
+            owner_of, k["qkv"], k["exact"], k["log_total"], grad_heads, rep, HEAD, n_ctx
+        )
+        grad_own = all_to_all(grad_sent)
+        small = jnp.concatenate([jnp.sum(gain_two_rows, axis=0)[:, None], router_part], axis=1)
+        head_part = jnp.concatenate([times(k["normed"], grad_whole, 0, 1), small], axis=1)
+        head_part = head_part.reshape(4, part, lanes + 1 + experts)
+        head_sum = wt_scatter_sum(
+            [lax.dynamic_index_in_dim(head_part, wt ^ m, 0, keepdims=False) for m in range(4)]
+        ).astype(jnp.bfloat16)
+        if layer == 0:
+            head_grads = ring_gather(head_sum, ctx, n_ctx, devices)
+        else:
+            head_grads = lax.all_gather(head_sum, "ctx", axis=0)
+        middle_pieces = wt_gather(middle_low)
+        attended_pieces = wt_exchange(k["attended"], wt)
+        out_part = times(jnp.concatenate(attended_pieces, axis=1), jnp.concatenate(middle_pieces, axis=0), 1, 0)
+        out_sum = lax.psum(out_part.astype(jnp.bfloat16), "ctx").astype(jnp.float32)
+        own = jnp.concatenate(
+            [
+                grad_own[:, :wide].reshape(width, rows),
+                grad_own[:, wide : wide + HEAD].reshape(n_ctx * HEAD, rows),
+                grad_own[:, wide + HEAD :].reshape(n_ctx * HEAD, rows),
+            ],
+            axis=0,
+        )
+        project = near_finish(*far_project[layer])
+        grad_normed = jnp.zeros((rows, width), jnp.float32)
+        for m in range(4):
+            grad_normed = lax.dynamic_update_slice_in_dim(
+                grad_normed, times(own, project[m], 0, 1), (wt ^ m) * part, 1
+            )
+        pulled, _ = rms_back(k["state"], k["gain_one"], grad_normed)
+        upstream = grad_middle + pulled
+        head_grads = head_grads.astype(jnp.float32)
+        small_sum = jnp.sum(head_grads[:, :, lanes:], axis=0)
+        columns = head_grads.transpose(1, 0, 2)
+        projected = [
+            columns[:, :, :wide].reshape(part, width),
+            columns[:, :, wide : wide + HEAD].reshape(part, n_ctx * HEAD),
+            columns[:, :, wide + HEAD : lanes].reshape(part, n_ctx * HEAD),
+        ]
+        gain_one_sum = sum(
+            jnp.sum(weight[layer].astype(jnp.float32) * grad, axis=1)
+            for weight, grad in zip((query_weight, key_weight, value_weight), projected)
+        ) / attention_gain[layer].astype(jnp.float32)
+        grads[layer] = (
+            gain_one_sum,
+            *projected,
+            out_sum,
+            small_sum[:, 0],
+            small_sum[:, 1:],
+            pair_sum[None, :, :hidden],
+            pair_sum[None, :, hidden:],
+            down_sum[None],
+        )
+    return (block_output, upstream[None], *[jnp.stack(items) for items in zip(*grads)])
+
+
+def local_rows(
     tokens,
     cotangent,
     seq_lengths,
@@ -505,6 +975,11 @@
         P(None, "ctx", None, "wt"),
         P(None, "ctx", "wt", None),
     )
+    def local(*arrays):
+        if by_heads(mesh, *arrays):
+            return local_heads(mesh, *arrays)
+        return local_rows(*arrays)
+
     return jax.shard_map(
         local,
         mesh=mesh,

time: 1960 us -> 909 us (0.46)
  waiting for transfers between devices: 1450 us -> 335 us
  blocking collectives: 111 us -> 0 us
  starting transfers between devices: 35.5 us -> 135 us
  Pallas kernels: 0 us -> 28.8 us
  other arithmetic: 66.1 us -> 94.1 us
    reduce_scatter x14 -> x0, waiting for transfers between devices: 462 us -> none  [the longest x2 102 us: local(): lax.psum_scatter(grad_query_weight.astype(jnp.bfloat16), 'wt', scatter_di...]
    all_gather x18 -> x1, waiting for transfers between devices: 351 us -> 0.01 us  [local_heads(): head_grads = lax.all_gather(head_sum, 'ctx', axis=0)]
    unnamed x45 -> x2, waiting for transfers between devices: 295 us -> 0.03 us
    psum x1, waiting for transfers between devices: 219 us -> 19.4 us  [local_heads(): out_sum = lax.psum(out_part.astype(jnp.bfloat16), 'ctx').astype(jnp.float32)]
    ppermute x0 -> x73, waiting for transfers between devices: none -> 157 us  [the longest x49 96.8 us: swap(): return lax.ppermute(x, axis, [(i, i ^ mask) for i in range(count)])]
    ppermute x0 -> x73, starting transfers between devices: none -> 65.6 us  [the longest x9 27.3 us: ring_gather(): lax.ppermute(ahead, 'ctx', right)]
    all_to_all x7 -> x14, waiting for transfers between devices: 120 us -> 159 us  [all_to_all(): return lax.all_to_all(x, 'ctx', split_axis=0, concat_axis=0, tiled=True)]
    psum x1 -> x0, blocking collectives: 37.1 us -> none  [local(): lax.psum(part_one.astype(jnp.bfloat16), 'ctx').astype(jnp.float32)]
  transfers between devices with their start and end apart: 46 -> 89, of which waited for: 41 -> 36; matrix products, arithmetic and copies ran while one was open for 11% -> 36% of each run, Pallas kernels for 0% -> 3%
where the time goes in v1:
time: 909 us; the launch traced here: 900 us
  waiting for transfers between devices  335 us (37%)
  matrix products  165 us (18%)
  starting transfers between devices  135 us (15%)
  local copies, waits for them, and re-layouts  124 us (14%)
  other arithmetic  94.1 us (10%)
  Pallas kernels  28.8 us (3%)
  between operations  18.3 us (2%)
    dot_general x90, matrix products, times(): lax.dot_general(left, right, (((a,), (b,)), ((), ())), preferred_element_...  160 us
    all_to_all x14, waiting for transfers between devices, all_to_all(): return lax.all_to_all(x, 'ctx', split_axis=0, concat_axis=0, tiled=True)  159 us
    ppermute x49, waiting for transfers between devices, swap(): return lax.ppermute(x, axis, [(i, i ^ mask) for i in range(count)])  96.8 us
    all_to_all x14, starting transfers between devices, all_to_all(): return lax.all_to_all(x, 'ctx', split_axis=0, concat_axis=0, tiled=True)  69.1 us
    unnamed x479, local copies, waits for them, and re-layouts  41.4 us
    ppermute x9, waiting for transfers between devices, ring_gather(): lax.ppermute(ahead, 'ctx', right)  29.2 us
    ppermute x9, starting transfers between devices, ring_gather(): lax.ppermute(ahead, 'ctx', right)  27.3 us
    ppermute x49, starting transfers between devices, swap(): return lax.ppermute(x, axis, [(i, i ^ mask) for i in range(count)])  26.2 us
  transfers between devices with their start and end apart: 89, of which 36 were waited for; matrix products, arithmetic and copies ran while one was open for 36% of the time, Pallas kernels for 3%

profile of v1, /device:TPU:0, one launch (start us, length us, event | category | flops | bytes accessed | tf_op | source)
XLA Modules:
  0.0 899.9 jit_solution(8088026811368617299)
XLA Ops:
  20.1 7.1 concatenate.101
  27.3 2.9 collective-permute-start
  32.3 3.2 slice_bitcast_fusion.14
  51.4 8.5 collective-permute-done.5
  69.5 7.6 collective-permute-done.8
  92.0 6.8 attend.2
  98.8 3.2 collective-permute-done.11
  103.1 6.4 all-to-all-start
  110.4 8.8 all-to-all-done
  126.3 3.9 all-to-all-start.1
  134.1 23.9 %all-to-all-done.1 = bf16[8,48,1536]{2,1,0:T(8,128)(2,1)S(1)} async-done(((bf16[8,48,1536]{2,1,0:T(8,128)(2,1)}), bf16[8,48,1536]{2,1,0:T(8,128)(2,1)S(1)}, u32[]{:S(2)}, u32[]{:S(2)}) %all-to-all-start.1) | async-done | bytes 1179680 | tf_op jit(solution)/shard_map/all_to_all | solution.py:235
  173.7 3.6 all-to-all-start.2
  179.0 26.9 %all-to-all-done.2 = bf16[8,48,1536]{2,1,0:T(8,128)(2,1)S(1)} async-done(((bf16[8,48,1536]{2,1,0:T(8,128)(2,1)}), bf16[8,48,1536]{2,1,0:T(8,128)(2,1)S(1)}, u32[]{:S(2)}, u32[]{:S(2)}) %all-to-all-start.2) | async-done | bytes 1179680 | tf_op jit(solution)/shard_map/all_to_all | solution.py:235
  215.3 5.5 collective-permute-done.20
  225.2 4.9 collective-permute-done.22
  233.6 7.6 collective-permute-done.25
  251.5 6.8 attend.3
  258.3 13.4 %collective-permute-done.28 = bf16[1536,512]{1,0:T(8,128)(2,1)S(1)} collective-permute-done((bf16[1536,512]{1,0:T(8,128)(2,1)S(1)}, bf16[1536,512]{1,0:T(8,128)(2,1)S(1)}, u32[]{:S(2)}, u32[]{:S(2)}) %collective-permute-start.28) | collective-permute-done | bytes 1572896 | tf_op jit(solution)/shard_map/ppermute | solution.py:174
  272.9 5.1 all-to-all-start.3
  280.0 8.8 all-to-all-done.3
  298.3 6.0 all-to-all-start.4
  304.9 3.0 pad_maximum_fusion.9
  311.8 3.0 pad_maximum_fusion.10
  315.5 17.0 %all-to-all-done.4 = bf16[8,48,1536]{2,1,0:T(8,128)(2,1)} async-done(((bf16[8,48,1536]{2,1,0:T(8,128)(2,1)}), bf16[8,48,1536]{2,1,0:T(8,128)(2,1)}, u32[]{:S(2)}, u32[]{:S(2)}) %all-to-all-start.4) | async-done | bytes 1179680 | tf_op jit(solution)/shard_map/all_to_all | solution.py:235
  351.0 4.4 all-to-all-start.5
  361.0 22.6 %all-to-all-done.5 = bf16[8,48,1536]{2,1,0:T(8,128)(2,1)} async-done(((bf16[8,48,1536]{2,1,0:T(8,128)(2,1)}), bf16[8,48,1536]{2,1,0:T(8,128)(2,1)}, u32[]{:S(2)}, u32[]{:S(2)}) %all-to-all-start.5) | async-done | bytes 1179680 | tf_op jit(solution)/shard_map/all_to_all | solution.py:235
  390.3 3.9 all-to-all-start.6
  399.0 4.4 fusion.1
  403.3 4.7 copy.153
  412.1 3.0 collective-permute-done.60
  417.1 4.6 copy.167
  439.3 5.7 all-to-all-start.7
  456.1 18.3 %all-to-all-done.7 = bf16[8,48,1536]{2,1,0:T(8,128)(2,1)} async-done(((bf16[8,48,1536]{2,1,0:T(8,128)(2,1)}), bf16[8,48,1536]{2,1,0:T(8,128)(2,1)}, u32[]{:S(2)}, u32[]{:S(2)}) %all-to-all-start.7) | async-done | bytes 1179680 | tf_op jit(solution)/shard_map/all_to_all | solution.py:235
  491.0 3.9 all-to-all-start.8
  494.9 3.1 fusion.217
  498.0 3.9 fusion.117
  507.8 7.6 attend_back.2
  515.4 6.0 all-to-all-start.9
  521.7 3.1 fusion.78
  525.2 8.5 collective-permute-done.63
  545.5 4.0 fusion.3
  549.6 41.4 %collective-permute-done.54 = bf16[384,329]{0,1:T(8,128)(2,1)S(1)} collective-permute-done((bf16[384,329]{0,1:T(8,128)(2,1)S(1)}, bf16[384,329]{0,1:T(8,128)(2,1)S(1)}, u32[]{:S(2)}, u32[]{:S(2)}) %collective-permute-start.54) | collective-permute-done | bytes 252704 | tf_op jit(solution)/shard_map/ppermute | solution.py:174
  605.4 6.4 all-to-all-start.10
  612.1 14.7 %collective-permute-done.68 = bf16[1536,512]{1,0:T(8,128)(2,1)} collective-permute-done((bf16[1536,512]{1,0:T(8,128)(2,1)}, bf16[1536,512]{1,0:T(8,128)(2,1)}, u32[]{:S(2)}, u32[]{:S(2)}) %collective-permute-start.68) | collective-permute-done | bytes 1572896 | tf_op jit(solution)/shard_map/ppermute | solution.py:174
  626.8 4.3 fusion.5
  633.0 24.2 %all-to-all-done.10 = bf16[8,48,1536]{2,1,0:T(8,128)(2,1)S(1)} async-done(((bf16[8,48,1536]{2,1,0:T(8,128)(2,1)}), bf16[8,48,1536]{2,1,0:T(8,128)(2,1)S(1)}, u32[]{:S(2)}, u32[]{:S(2)}) %all-to-all-start.10) | async-done | bytes 1179680 | tf_op jit(solution)/shard_map/all_to_all | solution.py:235
  672.3 4.6 all-to-all-start.11
  697.2 4.7 all-to-all-done.11
  717.1 3.7 all-to-all-start.12
  727.3 3.6 all-to-all-done.12.grad_ref
  730.8 7.6 attend_back.3
  740.0 6.1 collective-permute-done.70
  747.6 3.8 collective-permute-done.58
  755.5 5.7 all-to-all-start.13
  761.4 3.1 fusion.22
  776.1 10.2 %collective-permute-done.45 = bf16[384,329]{0,1:T(8,128)(2,1)S(1)} collective-permute-done((bf16[384,329]{0,1:T(8,128)(2,1)S(1)}, bf16[384,329]{0,1:T(8,128)(2,1)S(1)}, u32[]{:S(2)}, u32[]{:S(2)}) %collective-permute-start.45) | collective-permute-done | bytes 252704 | tf_op jit(solution)/shard_map/ppermute | solution.py:227
  786.4 15.8 %collective-permute-start.47 = (bf16[384,329]{0,1:T(8,128)(2,1)S(1)}, bf16[384,329]{0,1:T(8,128)(2,1)S(1)}, u32[]{:S(2)}, u32[]{:S(2)}) collective-permute-start(bf16[384,329]{0,1:T(8,128)(2,1)S(1)} %collective-permute-done.45), channel_id=1, source_target_pairs={{0,8},{8,16},{16,24},{24,28},{28,20},{20,12},{12,4},{4,0},{1,9},{9... | collective-permute-start | bytes 758024 | tf_op jit(solution)/shard_map/ppermute | solution.py:227
  816.0 3.6 collective-permute-start.49
  822.4 7.3 collective-permute-done.50
  847.4 6.1 copy.156
  855.1 3.0 copy.158
  859.3 4.6 fusion.9
  869.2 19.4 %all-reduce.3.cloned.1.call-done = (bf16[1,384,1536]{2,1,0:T(8,128)(2,1)}, bf16[1,384,1536]{2,1,0:T(8,128)(2,1)}) async-done(((bf16[1,384,1536]{2,1,0:T(8,128)(2,1)}, bf16[1,384,1536]{2,1,0:T(8,128)(2,1)}), (bf16[1,384,1536]{2,1,0:T(8,128)(2,1)}, bf16[1,384,1536]{2,1,0:T(8,128)(2,1)})) %all-reduce.3.cloned.1.call-update) | async-done | bytes 2359312 | tf_op jit(solution)/shard_map/psum | solution.py:474
  888.7 4.1 maximum_convert_fusion
  (910 shorter events, 368.2 us)
Async XLA Ops:
  27.3 24.1 %collective-permute-start = (bf16[672,384]{1,0:T(8,128)(2,1)}, bf16[672,384]{1,0:T(8,128)(2,1)}, u32[]{:S(2)}, u32[]{:S(2)}) collective-permute-start(bf16[672,384]{1,0:T(8,128)(2,1)} %concatenate.101), channel_id=1, source_target_pairs={{0,2},{1,3},{2,0},{3,1},{4,6},{5,7},{6,4},{7,5},{8,10},{9,11},{10,... | collective-permute-start | bytes 1548296 | tf_op jit(solution)/shard_map/ppermute | solution.py:174
  30.2 35.3 %collective-permute-start.2 = (bf16[672,384]{1,0:T(8,128)(2,1)}, bf16[672,384]{1,0:T(8,128)(2,1)}, u32[]{:S(2)}, u32[]{:S(2)}) collective-permute-start(bf16[672,384]{1,0:T(8,128)(2,1)} %concatenate.101), channel_id=1, source_target_pairs={{0,1},{1,0},{2,3},{3,2},{4,5},{5,4},{6,7},{7,6},{8,9},{9,8},{10,11... | collective-permute-start | bytes 1548296 | tf_op jit(solution)/shard_map/ppermute | solution.py:174
  30.3 15.2 %collective-permute-start.3 = (bf16[128,1536]{1,0:T(8,128)(2,1)S(1)}, bf16[128,1536]{1,0:T(8,128)(2,1)}, u32[]{:S(2)}, u32[]{:S(2)}) collective-permute-start(bf16[128,1536]{1,0:T(8,128)(2,1)S(1)} %bitcast.687), channel_id=1, source_target_pairs={{0,8},{8,16},{16,24},{24,28},{28,20},{20,12},{12,4},{4,0},{1,9},{9... | collective-permute-start | bytes 1179656 | tf_op jit(solution)/shard_map/ppermute | solution.py:227
  31.9 16.1 %collective-permute-start.4 = (bf16[128,1536]{1,0:T(8,128)(2,1)S(1)}, bf16[128,1536]{1,0:T(8,128)(2,1)S(1)}, u32[]{:S(2)}, u32[]{:S(2)}) collective-permute-start(bf16[128,1536]{1,0:T(8,128)(2,1)S(1)} %bitcast.688), channel_id=1, source_target_pairs={{8,0},{16,8},{24,16},{28,24},{20,28},{12,20},{4,12},{0,4},{9,1},{1... | collective-permute-start | bytes 1179656 | tf_op jit(solution)/shard_map/ppermute | solution.py:227
  35.5 74.6 %collective-permute-start.13 = (bf16[384,1536]{1,0:T(8,128)(2,1)}, bf16[384,1536]{1,0:T(8,128)(2,1)}, u32[]{:S(2)}, u32[]{:S(2)}) collective-permute-start(bf16[384,1536]{1,0:T(8,128)(2,1)} %get-tuple-element.115), channel_id=1, source_target_pairs={{0,2},{1,3},{2,0},{3,1},{4,6},{5,7},{6,4},{7,5},{8,10},{9,11},{10,... | collective-permute-start | bytes 3538952 | tf_op jit(solution)/shard_map/ppermute | solution.py:174
  45.5 76.3 %collective-permute-start.12 = (bf16[384,1536]{1,0:T(8,128)(2,1)}, bf16[384,1536]{1,0:T(8,128)(2,1)S(1)}, u32[]{:S(2)}, u32[]{:S(2)}) collective-permute-start(bf16[384,1536]{1,0:T(8,128)(2,1)} %get-tuple-element.115), channel_id=1, source_target_pairs={{0,1},{1,0},{2,3},{3,2},{4,5},{5,4},{6,7},{7,6},{8,9},{9,8},{10,11... | collective-permute-start | bytes 3538952 | tf_op jit(solution)/shard_map/ppermute | solution.py:174
  48.0 11.9 %collective-permute-start.5 = (bf16[128,1536]{1,0:T(8,128)(2,1)}, bf16[128,1536]{1,0:T(8,128)(2,1)S(1)}, u32[]{:S(2)}, u32[]{:S(2)}) collective-permute-start(bf16[128,1536]{1,0:T(8,128)(2,1)} %collective-permute-done.3), channel_id=1, source_target_pairs={{0,8},{8,16},{16,24},{24,28},{28,20},{20,12},{12,4},{4,0},{1,9},{9... | collective-permute-start | bytes 1179656 | tf_op jit(solution)/shard_map/ppermute | solution.py:227
  62.6 39.4 %collective-permute-start.11 = (bf16[1536,512]{1,0:T(8,128)(2,1)S(1)}, bf16[1536,512]{1,0:T(8,128)(2,1)S(1)}, u32[]{:S(2)}, u32[]{:S(2)}) collective-permute-start(bf16[1536,512]{1,0:T(8,128)(2,1)S(1)} %pad_maximum_fusion.11), channel_id=1, source_target_pairs={{0,2},{1,3},{2,0},{3,1},{4,6},{5,7},{6,4},{7,5},{8,10},{9,11},{10,... | collective-permute-start | bytes 4718600 | tf_op jit(solution)/shard_map/ppermute | solution.py:174
  65.5 12.0 %collective-permute-start.7 = (bf16[128,1536]{1,0:T(8,128)(2,1)S(1)}, bf16[128,1536]{1,0:T(8,128)(2,1)S(1)}, u32[]{:S(2)}, u32[]{:S(2)}) collective-permute-start(bf16[128,1536]{1,0:T(8,128)(2,1)S(1)} %collective-permute-done.5), channel_id=1, source_target_pairs={{0,8},{8,16},{16,24},{24,28},{28,20},{20,12},{12,4},{4,0},{1,9},{9... | collective-permute-start | bytes 1179656 | tf_op jit(solution)/shard_map/ppermute | solution.py:227
  82.8 43.5 %collective-permute-start.15 = (bf16[256,1536]{1,0:T(8,128)(2,1)}, bf16[256,1536]{1,0:T(8,128)(2,1)}, u32[]{:S(2)}, u32[]{:S(2)}) collective-permute-start(bf16[256,1536]{1,0:T(8,128)(2,1)} %get-tuple-element.131), channel_id=1, source_target_pairs={{0,2},{1,3},{2,0},{3,1},{4,6},{5,7},{6,4},{7,5},{8,10},{9,11},{10,... | collective-permute-start | bytes 2359304 | tf_op jit(solution)/shard_map/ppermute | solution.py:174
  103.1 16.1 %all-to-all-start = ((bf16[8,192,128]{2,1,0:T(8,128)(2,1)}), bf16[8,192,128]{2,1,0:T(8,128)(2,1)S(1)}, u32[]{:S(2)}, u32[]{:S(2)}) async-start(bf16[8,192,128]{2,1,0:T(8,128)(2,1)} %get-tuple-element.31), calls=%async_computation | async-start | bytes 786432 | tf_op jit(solution)/shard_map/all_to_all | solution.py:235
  110.1 12.8 %collective-permute-start.14 = (bf16[384,1536]{1,0:T(8,128)(2,1)}, bf16[384,1536]{1,0:T(8,128)(2,1)}, u32[]{:S(2)}, u32[]{:S(2)}) collective-permute-start(bf16[384,1536]{1,0:T(8,128)(2,1)} %collective-permute-done.13), channel_id=1, source_target_pairs={{0,1},{1,0},{2,3},{3,2},{4,5},{5,4},{6,7},{7,6},{8,9},{9,8},{10,11... | collective-permute-start | bytes 3538952 | tf_op jit(solution)/shard_map/ppermute | solution.py:174
  126.3 31.6 %all-to-all-start.1 = ((bf16[8,48,1536]{2,1,0:T(8,128)(2,1)}), bf16[8,48,1536]{2,1,0:T(8,128)(2,1)S(1)}, u32[]{:S(2)}, u32[]{:S(2)}) async-start(bf16[8,48,1536]{2,1,0:T(8,128)(2,1)} %bitcast.692), calls=%async_computation.1 | async-start | bytes 2359296 | tf_op jit(solution)/shard_map/all_to_all | solution.py:235
  130.3 32.8 %collective-permute-start.16 = (bf16[1536,512]{1,0:T(8,128)(2,1)}, bf16[1536,512]{1,0:T(8,128)(2,1)}, u32[]{:S(2)}, u32[]{:S(2)}) collective-permute-start(bf16[1536,512]{1,0:T(8,128)(2,1)} %copy-done.108), channel_id=1, source_target_pairs={{0,1},{1,0},{2,3},{3,2},{4,5},{5,4},{6,7},{7,6},{8,9},{9,8},{10,11... | collective-permute-start | bytes 4718600 | tf_op jit(solution)/shard_map/ppermute | solution.py:174
  130.8 38.6 %collective-permute-start.17 = (bf16[256,1536]{1,0:T(8,128)(2,1)}, bf16[256,1536]{1,0:T(8,128)(2,1)}, u32[]{:S(2)}, u32[]{:S(2)}) collective-permute-start(bf16[256,1536]{1,0:T(8,128)(2,1)} %get-tuple-element.131), channel_id=1, source_target_pairs={{0,1},{1,0},{2,3},{3,2},{4,5},{5,4},{6,7},{7,6},{8,9},{9,8},{10,11... | collective-permute-start | bytes 2359304 | tf_op jit(solution)/shard_map/ppermute | solution.py:174
  130.9 36.9 %collective-permute-start.19 = (bf16[256,1536]{1,0:T(8,128)(2,1)}, bf16[256,1536]{1,0:T(8,128)(2,1)}, u32[]{:S(2)}, u32[]{:S(2)}) collective-permute-start(bf16[256,1536]{1,0:T(8,128)(2,1)} %collective-permute-done.15), channel_id=1, source_target_pairs={{0,1},{1,0},{2,3},{3,2},{4,5},{5,4},{6,7},{7,6},{8,9},{9,8},{10,11... | collective-permute-start | bytes 2359304 | tf_op jit(solution)/shard_map/ppermute | solution.py:174
  173.7 32.1 %all-to-all-start.2 = ((bf16[8,48,1536]{2,1,0:T(8,128)(2,1)}), bf16[8,48,1536]{2,1,0:T(8,128)(2,1)S(1)}, u32[]{:S(2)}, u32[]{:S(2)}) async-start(bf16[8,48,1536]{2,1,0:T(8,128)(2,1)} %bitcast.697), calls=%async_computation.2 | async-start | bytes 2359296 | tf_op jit(solution)/shard_map/all_to_all | solution.py:235
  211.1 66.9 %collective-permute-start.30 = (bf16[384,1536]{1,0:T(8,128)(2,1)}, bf16[384,1536]{1,0:T(8,128)(2,1)}, u32[]{:S(2)}, u32[]{:S(2)}) collective-permute-start(bf16[384,1536]{1,0:T(8,128)(2,1)} %get-tuple-element.116), channel_id=1, source_target_pairs={{0,2},{1,3},{2,0},{3,1},{4,6},{5,7},{6,4},{7,5},{8,10},{9,11},{10,... | collective-permute-start | bytes 3538952 | tf_op jit(solution)/shard_map/ppermute | solution.py:174
  212.8 58.9 %collective-permute-start.28 = (bf16[1536,512]{1,0:T(8,128)(2,1)S(1)}, bf16[1536,512]{1,0:T(8,128)(2,1)S(1)}, u32[]{:S(2)}, u32[]{:S(2)}) collective-permute-start(bf16[1536,512]{1,0:T(8,128)(2,1)S(1)} %pad_maximum_fusion.12), channel_id=1, source_target_pairs={{0,2},{1,3},{2,0},{3,1},{4,6},{5,7},{6,4},{7,5},{8,10},{9,11},{10,... | collective-permute-start | bytes 4718600 | tf_op jit(solution)/shard_map/ppermute | solution.py:174
  230.1 11.7 %collective-permute-start.24 = (bf16[128,1536]{1,0:T(8,128)(2,1)S(1)}, bf16[128,1536]{1,0:T(8,128)(2,1)S(1)}, u32[]{:S(2)}, u32[]{:S(2)}) collective-permute-start(bf16[128,1536]{1,0:T(8,128)(2,1)S(1)} %collective-permute-done.22), channel_id=1, source_target_pairs={{0,8},{8,16},{16,24},{24,28},{28,20},{20,12},{12,4},{4,0},{1,9},{9... | collective-permute-start | bytes 1179656 | tf_op jit(solution)/shard_map/ppermute | solution.py:227
  272.9 15.9 %all-to-all-start.3 = ((bf16[8,192,128]{2,1,0:T(8,128)(2,1)}), bf16[8,192,128]{2,1,0:T(8,128)(2,1)S(1)}, u32[]{:S(2)}, u32[]{:S(2)}) async-start(bf16[8,192,128]{2,1,0:T(8,128)(2,1)} %get-tuple-element.36), calls=%async_computation.3 | async-start | bytes 786432 | tf_op jit(solution)/shard_map/all_to_all | solution.py:235
  277.9 13.4 %collective-permute-start.29 = (bf16[384,1536]{1,0:T(8,128)(2,1)}, bf16[384,1536]{1,0:T(8,128)(2,1)}, u32[]{:S(2)}, u32[]{:S(2)}) collective-permute-start(bf16[384,1536]{1,0:T(8,128)(2,1)} %get-tuple-element.116), channel_id=1, source_target_pairs={{0,1},{1,0},{2,3},{3,2},{4,5},{5,4},{6,7},{7,6},{8,9},{9,8},{10,11... | collective-permute-start | bytes 3538952 | tf_op jit(solution)/shard_map/ppermute | solution.py:174
  278.0 15.1 %collective-permute-start.31 = (bf16[384,1536]{1,0:T(8,128)(2,1)}, bf16[384,1536]{1,0:T(8,128)(2,1)}, u32[]{:S(2)}, u32[]{:S(2)}) collective-permute-start(bf16[384,1536]{1,0:T(8,128)(2,1)} %collective-permute-done.30), channel_id=1, source_target_pairs={{0,1},{1,0},{2,3},{3,2},{4,5},{5,4},{6,7},{7,6},{8,9},{9,8},{10,11... | collective-permute-start | bytes 3538952 | tf_op jit(solution)/shard_map/ppermute | solution.py:174
  278.5 19.8 %collective-permute-start.32 = (bf16[256,1536]{1,0:T(8,128)(2,1)}, bf16[256,1536]{1,0:T(8,128)(2,1)}, u32[]{:S(2)}, u32[]{:S(2)}) collective-permute-start(bf16[256,1536]{1,0:T(8,128)(2,1)} %get-tuple-element.130), channel_id=1, source_target_pairs={{0,2},{1,3},{2,0},{3,1},{4,6},{5,7},{6,4},{7,5},{8,10},{9,11},{10,... | collective-permute-start | bytes 2359304 | tf_op jit(solution)/shard_map/ppermute | solution.py:174
  298.3 34.3 %all-to-all-start.4 = ((bf16[8,48,1536]{2,1,0:T(8,128)(2,1)}), bf16[8,48,1536]{2,1,0:T(8,128)(2,1)}, u32[]{:S(2)}, u32[]{:S(2)}) async-start(bf16[8,48,1536]{2,1,0:T(8,128)(2,1)} %bitcast.691), calls=%async_computation.4 | async-start | bytes 2359296 | tf_op jit(solution)/shard_map/all_to_all | solution.py:235
  304.3 35.8 %collective-permute-start.33 = (bf16[1536,512]{1,0:T(8,128)(2,1)}, bf16[1536,512]{1,0:T(8,128)(2,1)}, u32[]{:S(2)}, u32[]{:S(2)}) collective-permute-start(bf16[1536,512]{1,0:T(8,128)(2,1)} %copy-done.109), channel_id=1, source_target_pairs={{0,1},{1,0},{2,3},{3,2},{4,5},{5,4},{6,7},{7,6},{8,9},{9,8},{10,11... | collective-permute-start | bytes 4718600 | tf_op jit(solution)/shard_map/ppermute | solution.py:174
  304.8 42.0 %collective-permute-start.34 = (bf16[256,1536]{1,0:T(8,128)(2,1)}, bf16[256,1536]{1,0:T(8,128)(2,1)}, u32[]{:S(2)}, u32[]{:S(2)}) collective-permute-start(bf16[256,1536]{1,0:T(8,128)(2,1)} %get-tuple-element.130), channel_id=1, source_target_pairs={{0,1},{1,0},{2,3},{3,2},{4,5},{5,4},{6,7},{7,6},{8,9},{9,8},{10,11... | collective-permute-start | bytes 2359304 | tf_op jit(solution)/shard_map/ppermute | solution.py:174
  307.9 287.1 %collective-permute-start.37 = (bf16[384,2560]{0,1:T(8,128)(2,1)}, bf16[384,2560]{0,1:T(8,128)(2,1)}, u32[]{:S(2)}, u32[]{:S(2)}) collective-permute-start(bf16[384,2560]{0,1:T(8,128)(2,1)} %pad_maximum_fusion.9), channel_id=1, source_target_pairs={{0,1},{1,0},{2,3},{3,2},{4,5},{5,4},{6,7},{7,6},{8,9},{9,8},{10,11... | collective-permute-start | bytes 5898248 | tf_op jit(solution)/shard_map/ppermute | solution.py:174
  308.4 216.8 %collective-permute-start.38 = (bf16[384,2560]{0,1:T(8,128)(2,1)}, bf16[384,2560]{0,1:T(8,128)(2,1)}, u32[]{:S(2)}, u32[]{:S(2)}) collective-permute-start(bf16[384,2560]{0,1:T(8,128)(2,1)} %pad_maximum_fusion.9), channel_id=1, source_target_pairs={{0,2},{1,3},{2,0},{3,1},{4,6},{5,7},{6,4},{7,5},{8,10},{9,11},{10,... | collective-permute-start | bytes 5898248 | tf_op jit(solution)/shard_map/ppermute | solution.py:174
  315.5 29.6 %collective-permute-start.36 = (bf16[256,1536]{1,0:T(8,128)(2,1)}, bf16[256,1536]{1,0:T(8,128)(2,1)}, u32[]{:S(2)}, u32[]{:S(2)}) collective-permute-start(bf16[256,1536]{1,0:T(8,128)(2,1)} %collective-permute-done.32), channel_id=1, source_target_pairs={{0,1},{1,0},{2,3},{3,2},{4,5},{5,4},{6,7},{7,6},{8,9},{9,8},{10,11... | collective-permute-start | bytes 2359304 | tf_op jit(solution)/shard_map/ppermute | solution.py:174
  351.0 32.6 %all-to-all-start.5 = ((bf16[8,48,1536]{2,1,0:T(8,128)(2,1)}), bf16[8,48,1536]{2,1,0:T(8,128)(2,1)}, u32[]{:S(2)}, u32[]{:S(2)}) async-start(bf16[8,48,1536]{2,1,0:T(8,128)(2,1)} %bitcast.698), calls=%async_computation.5 | async-start | bytes 2359296 | tf_op jit(solution)/shard_map/all_to_all | solution.py:235
  390.3 33.1 %all-to-all-start.6 = ((bf16[8,48,1536]{2,1,0:T(8,128)(2,1)}), bf16[8,48,1536]{2,1,0:T(8,128)(2,1)S(1)}, u32[]{:S(2)}, u32[]{:S(2)}) async-start(bf16[8,48,1536]{2,1,0:T(8,128)(2,1)} %bitcast.693), calls=%async_computation.6 | async-start | bytes 2359296 | tf_op jit(solution)/shard_map/all_to_all | solution.py:235
  397.4 12.1 %collective-permute-start.55 = (bf16[2,384,128]{2,1,0:T(8,128)(2,1)}, bf16[2,384,128]{2,1,0:T(8,128)(2,1)}, u32[]{:S(2)}, u32[]{:S(2)}) collective-permute-start(bf16[2,384,128]{2,1,0:T(8,128)(2,1)} %pad_maximum_fusion.49), channel_id=1, source_target_pairs={{0,2},{1,3},{2,0},{3,1},{4,6},{5,7},{6,4},{7,5},{8,10},{9,11},{10,... | collective-permute-start | bytes 589832 | tf_op jit(solution)/shard_map/ppermute | solution.py:174
  439.3 35.1 %all-to-all-start.7 = ((bf16[8,48,1536]{2,1,0:T(8,128)(2,1)}), bf16[8,48,1536]{2,1,0:T(8,128)(2,1)}, u32[]{:S(2)}, u32[]{:S(2)}) async-start(bf16[8,48,1536]{2,1,0:T(8,128)(2,1)} %bitcast.696), calls=%async_computation.7 | async-start | bytes 2359296 | tf_op jit(solution)/shard_map/all_to_all | solution.py:235
  453.1 87.4 %collective-permute-start.67 = (bf16[2,1536,512]{2,1,0:T(8,128)(2,1)}, bf16[2,1536,512]{2,1,0:T(8,128)(2,1)}, u32[]{:S(2)}, u32[]{:S(2)}) collective-permute-start(bf16[2,1536,512]{2,1,0:T(8,128)(2,1)} %pad_maximum_fusion.2), channel_id=1, source_target_pairs={{0,1},{1,0},{2,3},{3,2},{4,5},{5,4},{6,7},{7,6},{8,9},{9,8},{10,11... | collective-permute-start | bytes 9437192 | tf_op jit(solution)/shard_map/ppermute | solution.py:174
  455.9 46.0 %collective-permute-start.71 = (bf16[2,256,1536]{2,1,0:T(8,128)(2,1)}, bf16[2,256,1536]{2,1,0:T(8,128)(2,1)}, u32[]{:S(2)}, u32[]{:S(2)}) collective-permute-start(bf16[2,256,1536]{2,1,0:T(8,128)(2,1)} %pad_maximum_fusion.16), channel_id=1, source_target_pairs={{0,1},{1,0},{2,3},{3,2},{4,5},{5,4},{6,7},{7,6},{8,9},{9,8},{10,11... | collective-permute-start | bytes 4718600 | tf_op jit(solution)/shard_map/ppermute | solution.py:174
  491.0 16.8 %all-to-all-start.8 = ((bf16[8,192,128]{2,1,0:T(8,128)(2,1)}), bf16[8,192,128]{2,1,0:T(8,128)(2,1)S(1)}, u32[]{:S(2)}, u32[]{:S(2)}) async-start(bf16[8,192,128]{2,1,0:T(8,128)(2,1)} %bitcast.116), calls=%async_computation.8 | async-start | bytes 786432 | tf_op jit(solution)/shard_map/all_to_all | solution.py:235
  505.8 28.0 %collective-permute-start.72 = (bf16[256,1536]{1,0:T(8,128)(2,1)}, bf16[256,1536]{1,0:T(8,128)(2,1)}, u32[]{:S(2)}, u32[]{:S(2)}) collective-permute-start(bf16[256,1536]{1,0:T(8,128)(2,1)} %fusion.33), channel_id=1, source_target_pairs={{0,2},{1,3},{2,0},{3,1},{4,6},{5,7},{6,4},{7,5},{8,10},{9,11},{10,... | collective-permute-start | bytes 2359304 | tf_op jit(solution)/shard_map/ppermute | solution.py:174
  506.3 27.4 %collective-permute-start.63 = (bf16[128,1536]{1,0:T(8,128)(2,1)}, bf16[128,1536]{1,0:T(8,128)(2,1)}, u32[]{:S(2)}, u32[]{:S(2)}) collective-permute-start(bf16[128,1536]{1,0:T(8,128)(2,1)} %fusion.188), channel_id=1, source_target_pairs={{0,2},{1,3},{2,0},{3,1},{4,6},{5,7},{6,4},{7,5},{8,10},{9,11},{10,... | collective-permute-start | bytes 1179656 | tf_op jit(solution)/shard_map/ppermute | solution.py:174
  515.4 76.9 %all-to-all-start.9 = ((bf16[8,320,128]{2,1,0:T(8,128)(2,1)}), bf16[8,320,128]{2,1,0:T(8,128)(2,1)}, u32[]{:S(2)}, u32[]{:S(2)}) async-start(bf16[8,320,128]{2,1,0:T(8,128)(2,1)} %get-tuple-element.42), calls=%async_computation.9 | async-start | bytes 1310720 | tf_op jit(solution)/shard_map/all_to_all | solution.py:235
  521.4 167.9 %all-gather.3.cloned.1.call-start = ((), (), s32[]{:S(2)}) async-start(), calls=%async_computation.14 | async-start | bytes 2322432 | tf_op jit(solution)/shard_map/all_gather | solution.py:470
  525.2 11.8 %collective-permute-start.62 = (bf16[128,1536]{1,0:T(8,128)(2,1)}, bf16[128,1536]{1,0:T(8,128)(2,1)S(1)}, u32[]{:S(2)}, u32[]{:S(2)}) collective-permute-start(bf16[128,1536]{1,0:T(8,128)(2,1)} %fusion.188), channel_id=1, source_target_pairs={{0,1},{1,0},{2,3},{3,2},{4,5},{5,4},{6,7},{7,6},{8,9},{9,8},{10,11... | collective-permute-start | bytes 1179656 | tf_op jit(solution)/shard_map/ppermute | solution.py:174
  537.0 271.1 %collective-permute-start.40 = (bf16[384,2560]{0,1:T(8,128)(2,1)}, bf16[384,2560]{0,1:T(8,128)(2,1)}, u32[]{:S(2)}, u32[]{:S(2)}) collective-permute-start(bf16[384,2560]{0,1:T(8,128)(2,1)} %pad_maximum_fusion.10), channel_id=1, source_target_pairs={{0,1},{1,0},{2,3},{3,2},{4,5},{5,4},{6,7},{7,6},{8,9},{9,8},{10,11... | collective-permute-start | bytes 5898248 | tf_op jit(solution)/shard_map/ppermute | solution.py:174
  537.0 62.3 %collective-permute-start.39 = (bf16[384,2560]{0,1:T(8,128)(2,1)}, bf16[384,2560]{0,1:T(8,128)(2,1)}, u32[]{:S(2)}, u32[]{:S(2)}) collective-permute-start(bf16[384,2560]{0,1:T(8,128)(2,1)} %collective-permute-done.38), channel_id=1, source_target_pairs={{0,1},{1,0},{2,3},{3,2},{4,5},{5,4},{6,7},{7,6},{8,9},{9,8},{10,11... | collective-permute-start | bytes 5898248 | tf_op jit(solution)/shard_map/ppermute | solution.py:174
  540.4 211.7 %collective-permute-start.41 = (bf16[384,2560]{0,1:T(8,128)(2,1)}, bf16[384,2560]{0,1:T(8,128)(2,1)}, u32[]{:S(2)}, u32[]{:S(2)}) collective-permute-start(bf16[384,2560]{0,1:T(8,128)(2,1)} %pad_maximum_fusion.10), channel_id=1, source_target_pairs={{0,2},{1,3},{2,0},{3,1},{4,6},{5,7},{6,4},{7,5},{8,10},{9,11},{10,... | collective-permute-start | bytes 5898248 | tf_op jit(solution)/shard_map/ppermute | solution.py:174
  543.9 47.0 %collective-permute-start.54 = (bf16[384,329]{0,1:T(8,128)(2,1)S(1)}, bf16[384,329]{0,1:T(8,128)(2,1)S(1)}, u32[]{:S(2)}, u32[]{:S(2)}) collective-permute-start(bf16[384,329]{0,1:T(8,128)(2,1)S(1)} %fusion.109), channel_id=1, source_target_pairs={{0,2},{1,3},{2,0},{3,1},{4,6},{5,7},{6,4},{7,5},{8,10},{9,11},{10,... | collective-permute-start | bytes 758024 | tf_op jit(solution)/shard_map/ppermute | solution.py:174
  590.9 35.8 %collective-permute-start.68 = (bf16[1536,512]{1,0:T(8,128)(2,1)}, bf16[1536,512]{1,0:T(8,128)(2,1)}, u32[]{:S(2)}, u32[]{:S(2)}) collective-permute-start(bf16[1536,512]{1,0:T(8,128)(2,1)} %fusion.3), channel_id=1, source_target_pairs={{0,2},{1,3},{2,0},{3,1},{4,6},{5,7},{6,4},{7,5},{8,10},{9,11},{10,... | collective-permute-start | bytes 4718600 | tf_op jit(solution)/shard_map/ppermute | solution.py:174
  605.4 51.8 %all-to-all-start.10 = ((bf16[8,48,1536]{2,1,0:T(8,128)(2,1)}), bf16[8,48,1536]{2,1,0:T(8,128)(2,1)S(1)}, u32[]{:S(2)}, u32[]{:S(2)}) async-start(bf16[8,48,1536]{2,1,0:T(8,128)(2,1)} %bitcast.694), calls=%async_computation.10 | async-start | bytes 2359296 | tf_op jit(solution)/shard_map/all_to_all | solution.py:235
  672.3 29.7 %all-to-all-start.11 = ((bf16[8,48,1536]{2,1,0:T(8,128)(2,1)}), bf16[8,48,1536]{2,1,0:T(8,128)(2,1)}, u32[]{:S(2)}, u32[]{:S(2)}) async-start(bf16[8,48,1536]{2,1,0:T(8,128)(2,1)} %bitcast.695), calls=%async_computation.11 | async-start | bytes 2359296 | tf_op jit(solution)/shard_map/all_to_all | solution.py:235
  681.9 82.6 %collective-permute-start.65 = (bf16[2,1536,512]{2,1,0:T(8,128)(2,1)}, bf16[2,1536,512]{2,1,0:T(8,128)(2,1)}, u32[]{:S(2)}, u32[]{:S(2)}) collective-permute-start(bf16[2,1536,512]{2,1,0:T(8,128)(2,1)} %pad_maximum_fusion.1), channel_id=1, source_target_pairs={{0,1},{1,0},{2,3},{3,2},{4,5},{5,4},{6,7},{7,6},{8,9},{9,8},{10,11... | collective-permute-start | bytes 9437192 | tf_op jit(solution)/shard_map/ppermute | solution.py:174
  684.7 36.8 %collective-permute-start.69 = (bf16[2,256,1536]{2,1,0:T(8,128)(2,1)}, bf16[2,256,1536]{2,1,0:T(8,128)(2,1)}, u32[]{:S(2)}, u32[]{:S(2)}) collective-permute-start(bf16[2,256,1536]{2,1,0:T(8,128)(2,1)} %pad_maximum_fusion.15), channel_id=1, source_target_pairs={{0,1},{1,0},{2,3},{3,2},{4,5},{5,4},{6,7},{7,6},{8,9},{9,8},{10,11... | collective-permute-start | bytes 4718600 | tf_op jit(solution)/shard_map/ppermute | solution.py:174
  717.1 13.7 %all-to-all-start.12 = ((bf16[8,192,128]{2,1,0:T(8,128)(2,1)}), bf16[8,192,128]{2,1,0:T(8,128)(2,1)S(1)}, u32[]{:S(2)}, u32[]{:S(2)}) async-start(bf16[8,192,128]{2,1,0:T(8,128)(2,1)} %bitcast.139), calls=%async_computation.12 | async-start | bytes 786432 | tf_op jit(solution)/shard_map/all_to_all | solution.py:235
  725.2 20.8 %collective-permute-start.70 = (bf16[256,1536]{1,0:T(8,128)(2,1)}, bf16[256,1536]{1,0:T(8,128)(2,1)}, u32[]{:S(2)}, u32[]{:S(2)}) collective-permute-start(bf16[256,1536]{1,0:T(8,128)(2,1)} %fusion.38), channel_id=1, source_target_pairs={{0,2},{1,3},{2,0},{3,1},{4,6},{5,7},{6,4},{7,5},{8,10},{9,11},{10,... | collective-permute-start | bytes 2359304 | tf_op jit(solution)/shard_map/ppermute | solution.py:174
  726.5 24.8 %collective-permute-start.58 = (bf16[128,1536]{1,0:T(8,128)(2,1)S(1)}, bf16[128,1536]{1,0:T(8,128)(2,1)}, u32[]{:S(2)}, u32[]{:S(2)}) collective-permute-start(bf16[128,1536]{1,0:T(8,128)(2,1)S(1)} %get-tuple-element.92), channel_id=1, source_target_pairs={{0,2},{1,3},{2,0},{3,1},{4,6},{5,7},{6,4},{7,5},{8,10},{9,11},{10,... | collective-permute-start | bytes 1179656 | tf_op jit(solution)/shard_map/ppermute | solution.py:174
  752.1 15.2 %collective-permute-start.44 = (bf16[384,329]{0,1:T(8,128)(2,1)S(1)}, bf16[384,329]{0,1:T(8,128)(2,1)S(1)}, u32[]{:S(2)}, u32[]{:S(2)}) collective-permute-start(bf16[384,329]{0,1:T(8,128)(2,1)S(1)} %fusion.108), channel_id=1, source_target_pairs={{0,2},{1,3},{2,0},{3,1},{4,6},{5,7},{6,4},{7,5},{8,10},{9,11},{10,... | collective-permute-start | bytes 758024 | tf_op jit(solution)/shard_map/ppermute | solution.py:174
  755.5 49.9 %all-to-all-start.13 = ((bf16[8,320,128]{2,1,0:T(8,128)(2,1)}), bf16[8,320,128]{2,1,0:T(8,128)(2,1)}, u32[]{:S(2)}, u32[]{:S(2)}) async-start(bf16[8,320,128]{2,1,0:T(8,128)(2,1)} %get-tuple-element.45), calls=%async_computation.13 | async-start | bytes 1310720 | tf_op jit(solution)/shard_map/all_to_all | solution.py:235
  761.2 127.5 %all-reduce.3.cloned.1.call-start = ((), (), s32[]{:S(2)}) async-start(), calls=%async_computation.15 | async-start | bytes 4718592 | tf_op jit(solution)/shard_map/psum | solution.py:474
  761.2 51.1 %collective-permute-start.42 = (bf16[384,2560]{0,1:T(8,128)(2,1)}, bf16[384,2560]{0,1:T(8,128)(2,1)}, u32[]{:S(2)}, u32[]{:S(2)}) collective-permute-start(bf16[384,2560]{0,1:T(8,128)(2,1)} %collective-permute-done.41), channel_id=1, source_target_pairs={{0,1},{1,0},{2,3},{3,2},{4,5},{5,4},{6,7},{7,6},{8,9},{9,8},{10,11... | collective-permute-start | bytes 5898248 | tf_op jit(solution)/shard_map/ppermute | solution.py:174
  771.3 15.1 %collective-permute-start.45 = (bf16[384,329]{0,1:T(8,128)(2,1)S(1)}, bf16[384,329]{0,1:T(8,128)(2,1)S(1)}, u32[]{:S(2)}, u32[]{:S(2)}) collective-permute-start(bf16[384,329]{0,1:T(8,128)(2,1)S(1)} %get-tuple-element.91), channel_id=1, source_target_pairs={{0,8},{8,16},{16,24},{24,28},{28,20},{20,12},{12,4},{4,0},{1,9},{9... | collective-permute-start | bytes 758024 | tf_op jit(solution)/shard_map/ppermute | solution.py:227
  773.3 28.9 %collective-permute-start.46 = (bf16[384,329]{0,1:T(8,128)(2,1)S(1)}, bf16[384,329]{0,1:T(8,128)(2,1)S(1)}, u32[]{:S(2)}, u32[]{:S(2)}) collective-permute-start(bf16[384,329]{0,1:T(8,128)(2,1)S(1)} %get-tuple-element.91), channel_id=1, source_target_pairs={{8,0},{16,8},{24,16},{28,24},{20,28},{12,20},{4,12},{0,4},{9,1},{1... | collective-permute-start | bytes 758024 | tf_op jit(solution)/shard_map/ppermute | solution.py:227
  775.5 83.8 %collective-permute-start.66 = (bf16[1536,512]{1,0:T(8,128)(2,1)}, bf16[1536,512]{1,0:T(8,128)(2,1)}, u32[]{:S(2)}, u32[]{:S(2)}) collective-permute-start(bf16[1536,512]{1,0:T(8,128)(2,1)} %fusion.7), channel_id=1, source_target_pairs={{0,2},{1,3},{2,0},{3,1},{4,6},{5,7},{6,4},{7,5},{8,10},{9,11},{10,... | collective-permute-start | bytes 4718600 | tf_op jit(solution)/shard_map/ppermute | solution.py:174
  786.4 29.7 %collective-permute-start.47 = (bf16[384,329]{0,1:T(8,128)(2,1)S(1)}, bf16[384,329]{0,1:T(8,128)(2,1)S(1)}, u32[]{:S(2)}, u32[]{:S(2)}) collective-permute-start(bf16[384,329]{0,1:T(8,128)(2,1)S(1)} %collective-permute-done.45), channel_id=1, source_target_pairs={{0,8},{8,16},{16,24},{24,28},{28,20},{20,12},{12,4},{4,0},{1,9},{9... | collective-permute-start | bytes 758024 | tf_op jit(solution)/shard_map/ppermute | solution.py:227
  802.2 17.4 %collective-permute-start.48 = (bf16[384,329]{0,1:T(8,128)(2,1)S(1)}, bf16[384,329]{0,1:T(8,128)(2,1)S(1)}, u32[]{:S(2)}, u32[]{:S(2)}) collective-permute-start(bf16[384,329]{0,1:T(8,128)(2,1)S(1)} %collective-permute-done.46), channel_id=1, source_target_pairs={{8,0},{16,8},{24,16},{28,24},{20,28},{12,20},{4,12},{0,4},{9,1},{1... | collective-permute-start | bytes 758024 | tf_op jit(solution)/shard_map/ppermute | solution.py:227
  816.0 13.8 %collective-permute-start.49 = (bf16[384,329]{0,1:T(8,128)(2,1)S(1)}, bf16[384,329]{0,1:T(8,128)(2,1)S(1)}, u32[]{:S(2)}, u32[]{:S(2)}) collective-permute-start(bf16[384,329]{0,1:T(8,128)(2,1)S(1)} %collective-permute-done.47), channel_id=1, source_target_pairs={{0,8},{8,16},{16,24},{24,28},{28,20},{20,12},{12,4},{4,0},{1,9},{9... | collective-permute-start | bytes 758024 | tf_op jit(solution)/shard_map/ppermute | solution.py:227
  (259 other events, 2302.9 us)
Sparse Core Ops, SparseCore 0:
  592.4 66.4 all-gather.2
  765.6 122.9 all-reduce.2

commit v2 on v1

--- a/solution.py
+++ b/solution.py
@@ -51,48 +51,103 @@
     return lax.dot_general(left, right, (((a,), (b,)), ((), ())), preferred_element_type=jnp.float32)
 
 
-def causal_mask(keys_count, span):
+def vmem(count):
+    return [pl.BlockSpec(memory_space=pltpu.VMEM)] * count
+
+
+def kernel_params():
+    return pltpu.CompilerParams(vmem_limit_bytes=56 * 2**20)
+
+
+def cost(flops, nbytes, transcendentals=0):
+    return pl.CostEstimate(flops=int(flops), bytes_accessed=int(nbytes), transcendentals=int(transcendentals))
+
+
+def causal_mask(span):
     key_at = lax.broadcasted_iota(jnp.int32, (span, span), 0)
     query_at = lax.broadcasted_iota(jnp.int32, (span, span), 1)
     return key_at <= query_at
 
 
-def attend_kernel(rep, head, span, owner_ref, qkv_ref, sent_ref, exact_ref, log_ref):
-    tokens = qkv_ref.shape[1]
+def front_kernel(raw, rep, head, span, spot_ref, owner_ref, *refs):
+    *blocks, weight_ref, gain_ref, normed_ref, qkv_ref, sent_ref, exact_ref, log_ref = refs
+    rows = blocks[0].shape[0]
+    count = len(blocks) - 1
+    tokens = count * rows
     width = rep * head
-    blocks = span // BLK
     scale = head ** (-0.5)
-    mask = causal_mask(span, span)
+    gain = gain_ref[...]
+    for k in range(count):
+        low, high = (blocks[k],) * 2 if k < count - 1 else blocks[k:]
+        half = low.shape[0] if k == count - 1 else rows
+        for start, ref in ((0, low), (half, high)) if k == count - 1 else ((0, low),):
+            block = ref[...]
+            if raw:
+                block = rms_scale(block.astype(jnp.float32), gain).astype(jnp.bfloat16)
+            normed_ref[spot_ref[k], start : start + ref.shape[0], :] = block
+    lanes_all = weight_ref.shape[0]
+    for part in range(tokens // span):
+        take = span // rows
+        piece = normed_ref[part * take : (part + 1) * take].reshape(span, normed_ref.shape[2])
+        qkv_ref[:, part * span : (part + 1) * span] = times(weight_ref[...], piece, 1, 1).astype(jnp.bfloat16)
+    mask = causal_mask(span)
+    per = span // rows
     for part in range(tokens // span):
         lanes = pl.ds(part * span, span)
         seen = (part + 1) * span
         keys = qkv_ref[width : width + head, :seen]
-        values = qkv_ref[width + head :, :seen]
+        values = qkv_ref[width + head : lanes_all, :seen]
         for h in range(rep):
-            rows = slice(h * head, (h + 1) * head)
-            scores = times(keys, qkv_ref[rows, lanes], 0, 0) * scale
+            at = slice(h * head, (h + 1) * head)
+            scores = times(keys, qkv_ref[at, lanes], 0, 0) * scale
             last = jnp.where(mask, scores[seen - span :], NEG)
             top = jnp.max(last, axis=0, keepdims=True)
             if part:
                 top = jnp.maximum(top, jnp.max(scores[: seen - span], axis=0, keepdims=True))
-            last = jnp.exp(last - top)
-            weights = last if part == 0 else jnp.concatenate([jnp.exp(scores[: seen - span] - top), last], axis=0)
+            weights = jnp.exp(last - top)
+            if part:
+                weights = jnp.concatenate([jnp.exp(scores[: seen - span] - top), weights], axis=0)
             total = jnp.sum(weights, axis=0, keepdims=True)
             result = times(values, weights.astype(jnp.bfloat16), 1, 0) / total
-            exact_ref[rows, lanes] = result
+            exact_ref[at, lanes] = result
             log_ref[h : h + 1, lanes] = top + jnp.log(total)
-            for b in range(blocks):
-                sent_ref[owner_ref[part * blocks + b], rows, :] = result[:, b * BLK : (b + 1) * BLK].astype(jnp.bfloat16)
+            for b in range(per):
+                sent_ref[owner_ref[part * per + b], at, :] = result[:, b * rows : (b + 1) * rows].astype(jnp.bfloat16)
+
+
+def front(raw, spots, owner_of, blocks, weight, gain, rep, head):
+    rows, width = blocks[0].shape
+    count = len(blocks) - 1
+    tokens = count * rows
+    span = min(256, tokens)
+    deep = weight.shape[0]
+    pairs = rep * tokens * (tokens + span) // 2
+    return pl.pallas_call(
+        functools.partial(front_kernel, raw, rep, head, span),
+        out_shape=(
+            jax.ShapeDtypeStruct((count, rows, width), jnp.bfloat16),
+            jax.ShapeDtypeStruct((deep, tokens), jnp.bfloat16),
+            jax.ShapeDtypeStruct((count, rep * head, rows), jnp.bfloat16),
+            jax.ShapeDtypeStruct((rep * head, tokens), jnp.float32),
+            jax.ShapeDtypeStruct((rep, tokens), jnp.float32),
+        ),
+        in_specs=[pl.BlockSpec(memory_space=pltpu.SMEM)] * 2 + vmem(len(blocks) + 2),
+        out_specs=tuple(vmem(5)),
+        compiler_params=kernel_params(),
+        cost_estimate=cost(4 * head * pairs + 2 * deep * width * tokens, 9 * 2**20, pairs),
+        name="front",
+    )(spots, owner_of, *blocks, weight, gain)
 
 
 def attend_back_kernel(rep, head, span, owner_ref, qkv_ref, exact_ref, log_ref, grad_ref, whole_ref, sent_ref, grad_all, keys_sum, values_sum):
     tokens = qkv_ref.shape[1]
+    rows = grad_ref.shape[2]
     width = rep * head
-    blocks = span // BLK
+    per = span // rows
     scale = head ** (-0.5)
-    mask = causal_mask(span, span)
-    for block in range(tokens // BLK):
-        grad_all[:, block * BLK : (block + 1) * BLK] = grad_ref[owner_ref[block]]
+    mask = causal_mask(span)
+    for block in range(tokens // rows):
+        grad_all[:, block * rows : (block + 1) * rows] = grad_ref[owner_ref[block]]
     keys_sum[...] = jnp.zeros_like(keys_sum)
     values_sum[...] = jnp.zeros_like(values_sum)
     for part in range(tokens // span):
@@ -101,10 +156,10 @@
         keys = qkv_ref[width : width + head, :seen]
         values = qkv_ref[width + head :, :seen]
         for h in range(rep):
-            rows = slice(h * head, (h + 1) * head)
-            queries = qkv_ref[rows, lanes]
-            grads = grad_all[rows, lanes]
-            delta = jnp.sum(grads.astype(jnp.float32) * exact_ref[rows, lanes], axis=0, keepdims=True)
+            at = slice(h * head, (h + 1) * head)
+            queries = qkv_ref[at, lanes]
+            grads = grad_all[at, lanes]
+            delta = jnp.sum(grads.astype(jnp.float32) * exact_ref[at, lanes], axis=0, keepdims=True)
             scores = times(keys, queries, 0, 0) * scale
             probs = jnp.exp(scores - log_ref[h : h + 1, lanes])
             last = jnp.where(mask, probs[seen - span :], 0.0)
@@ -112,87 +167,365 @@
             pulled = times(values, grads, 0, 0)
             slopes = (probs * (pulled - delta)).astype(jnp.bfloat16)
             back = (times(keys, slopes, 1, 0) * scale).astype(jnp.bfloat16)
-            whole_ref[rows, lanes] = back
-            for b in range(blocks):
-                sent_ref[owner_ref[part * blocks + b], rows, :] = back[:, b * BLK : (b + 1) * BLK]
+            whole_ref[at, lanes] = back
+            for b in range(per):
+                sent_ref[owner_ref[part * per + b], at, :] = back[:, b * rows : (b + 1) * rows]
             keys_sum[:, :seen] += times(queries, slopes, 1, 1)
             values_sum[:, :seen] += times(grads, probs.astype(jnp.bfloat16), 1, 1)
     keys_low = (keys_sum[...] * scale).astype(jnp.bfloat16)
     values_low = values_sum[...].astype(jnp.bfloat16)
     whole_ref[width : width + head, :] = keys_low
     whole_ref[width + head :, :] = values_low
-    for block in range(tokens // BLK):
-        cut = slice(block * BLK, (block + 1) * BLK)
+    for block in range(tokens // rows):
+        cut = slice(block * rows, (block + 1) * rows)
         sent_ref[owner_ref[block], width : width + head, :] = keys_low[:, cut]
         sent_ref[owner_ref[block], width + head :, :] = values_low[:, cut]
 
 
-def attend(owner_of, qkv, rep, head, count):
-    tokens = qkv.shape[1]
+def attend_back(owner_of, qkv, exact, log_total, grads, rep, head):
+    deep, tokens = qkv.shape
+    count, _, rows = grads.shape
     span = min(256, tokens)
     pairs = rep * tokens * (tokens + span) // 2
     return pl.pallas_call(
-        functools.partial(attend_kernel, rep, head, span),
-        out_shape=(
-            jax.ShapeDtypeStruct((count, rep * head, BLK), jnp.bfloat16),
-            jax.ShapeDtypeStruct((rep * head, tokens), jnp.float32),
-            jax.ShapeDtypeStruct((rep, tokens), jnp.float32),
-        ),
-        in_specs=[pl.BlockSpec(memory_space=pltpu.SMEM), pl.BlockSpec(memory_space=pltpu.VMEM)],
-        out_specs=(pl.BlockSpec(memory_space=pltpu.VMEM),) * 3,
-        compiler_params=pltpu.CompilerParams(vmem_limit_bytes=40 * 2**20),
-        cost_estimate=pl.CostEstimate(flops=4 * head * pairs, bytes_accessed=4 * 2**20, transcendentals=pairs),
-        name="attend",
-    )(owner_of, qkv)
-
-
-def attend_back(owner_of, qkv, exact, log_total, grads, rep, head, count):
-    tokens = qkv.shape[1]
-    span = min(256, tokens)
-    pairs = rep * tokens * (tokens + span) // 2
-    rows = qkv.shape[0]
-    return pl.pallas_call(
         functools.partial(attend_back_kernel, rep, head, span),
         out_shape=(
-            jax.ShapeDtypeStruct((rows, tokens), jnp.bfloat16),
-            jax.ShapeDtypeStruct((count, rows, BLK), jnp.bfloat16),
+            jax.ShapeDtypeStruct((deep, tokens), jnp.bfloat16),
+            jax.ShapeDtypeStruct((count, deep, rows), jnp.bfloat16),
         ),
-        in_specs=[pl.BlockSpec(memory_space=pltpu.SMEM)] + [pl.BlockSpec(memory_space=pltpu.VMEM)] * 4,
-        out_specs=(pl.BlockSpec(memory_space=pltpu.VMEM),) * 2,
+        in_specs=[pl.BlockSpec(memory_space=pltpu.SMEM)] + vmem(4),
+        out_specs=tuple(vmem(2)),
         scratch_shapes=[
             pltpu.VMEM((rep * head, tokens), jnp.bfloat16),
             pltpu.VMEM((head, tokens), jnp.float32),
             pltpu.VMEM((head, tokens), jnp.float32),
         ],
-        compiler_params=pltpu.CompilerParams(vmem_limit_bytes=40 * 2**20),
-        cost_estimate=pl.CostEstimate(flops=10 * head * pairs, bytes_accessed=6 * 2**20, transcendentals=pairs),
+        compiler_params=kernel_params(),
+        cost_estimate=cost(10 * head * pairs, 6 * 2**20, pairs),
         name="attend_back",
     )(owner_of, qkv, exact, log_total, grads)
 
 
-def swap(x, axis, count, mask):
-    return lax.ppermute(x, axis, [(i, i ^ mask) for i in range(count)])
+def silu_pair(gate_value, up_value):
+    return (gate_value * jax.nn.sigmoid(gate_value) * up_value).astype(jnp.bfloat16)
+
+
+def pair_back(grad_inner, gate_value, up_value):
+    sigma = jax.nn.sigmoid(gate_value)
+    grad_gate = grad_inner * up_value * sigma * (1.0 + gate_value * (1.0 - sigma))
+    return grad_gate.astype(jnp.bfloat16), (grad_inner * gate_value * sigma).astype(jnp.bfloat16)
+
+
+def expert_forward_kernel(rows_ref, *refs):
+    gate, up, down = refs[:4], refs[4:8], refs[8:12]
+    made_ref, gates_ref, ups_ref, inner_ref, total = refs[12:]
+    rows = rows_ref[...]
+    for m in range(4):
+        gate_value = times(rows, gate[m][...], 1, 0)
+        up_value = times(rows, up[m][...], 1, 0)
+        gates_ref[m] = gate_value
+        ups_ref[m] = up_value
+        inner = silu_pair(gate_value, up_value)
+        inner_ref[m] = inner
+        part = times(inner, down[m][...], 1, 0)
+        if m == 0:
+            total[...] = part
+        elif m < 3:
+            total[...] += part
+        else:
+            made_ref[...] = (total[...] + part).astype(jnp.bfloat16)
+
+
+def expert_forward(rows, gate, up, down):
+    count, width = rows.shape
+    hidden = gate[0].shape[1]
+    return pl.pallas_call(
+        expert_forward_kernel,
+        out_shape=(
+            jax.ShapeDtypeStruct((count, width), jnp.bfloat16),
+            jax.ShapeDtypeStruct((4, count, hidden), jnp.float32),
+            jax.ShapeDtypeStruct((4, count, hidden), jnp.float32),
+            jax.ShapeDtypeStruct((4, count, hidden), jnp.bfloat16),
+        ),
+        in_specs=vmem(13),
+        out_specs=tuple(vmem(4)),
+        scratch_shapes=[pltpu.VMEM((count, width), jnp.float32)],
+        compiler_params=kernel_params(),
+        cost_estimate=cost(24 * count * width * hidden, 16 * 2**20, 4 * count * hidden),
+        name="expert_forward",
+    )(rows, *gate, *up, *down)
+
+
+def expert_backward_kernel(grad_ref, *refs):
+    gate, up, down = refs[:4], refs[4:8], refs[8:12]
+    gates_ref, ups_ref, back_ref, grad_gate_ref, grad_up_ref, total = refs[12:]
+    grads = grad_ref[...]
+    for m in range(4):
+        grad_gate, grad_up = pair_back(times(grads, down[m][...], 1, 1), gates_ref[m], ups_ref[m])
+        grad_gate_ref[m] = grad_gate
+        grad_up_ref[m] = grad_up
+        part = times(grad_gate, gate[m][...], 1, 1) + times(grad_up, up[m][...], 1, 1)
+        if m == 0:
+            total[...] = part
+        elif m < 3:
+            total[...] += part
+        else:
+            back_ref[...] = (total[...] + part).astype(jnp.bfloat16)
+
+
+def expert_backward(grads, gate, up, down, gates, ups):
+    count, width = grads.shape
+    hidden = gate[0].shape[1]
+    return pl.pallas_call(
+        expert_backward_kernel,
+        out_shape=(
+            jax.ShapeDtypeStruct((count, width), jnp.bfloat16),
+            jax.ShapeDtypeStruct((4, count, hidden), jnp.bfloat16),
+            jax.ShapeDtypeStruct((4, count, hidden), jnp.bfloat16),
+        ),
+        in_specs=vmem(15),
+        out_specs=tuple(vmem(3)),
+        scratch_shapes=[pltpu.VMEM((count, width), jnp.float32)],
+        compiler_params=kernel_params(),
+        cost_estimate=cost(24 * count * width * hidden, 16 * 2**20, 4 * count * hidden),
+        name="expert_backward",
+    )(grads, *gate, *up, *down, gates, ups)
+
+
+def expert_both_kernel(experts, mine_ref, rows_ref, cot_ref, router_ref, *refs):
+    gate, up, down = refs[:4], refs[4:8], refs[8:12]
+    made_ref, back_ref, grad_ref, inner_ref, grad_gate_ref, grad_up_ref, total, total_back = refs[12:]
+    rows = rows_ref[...]
+    count, width = rows.shape
+    cot = cot_ref[:, :width].astype(jnp.float32)
+    logits = times(rows, router_ref[...], 1, 1)
+    ids = lax.broadcasted_iota(jnp.int32, logits.shape, 1)
+    logits = jnp.where(ids < experts, logits, NEG)
+    odds = jnp.exp(logits - jnp.max(logits, axis=1, keepdims=True))
+    other = cot_ref[:, width : width + 1].astype(jnp.float32).astype(jnp.int32)
+    own_odds = jnp.sum(jnp.where(ids == mine_ref[0], odds, 0.0), axis=1, keepdims=True)
+    other_odds = jnp.sum(jnp.where(ids == other, odds, 0.0), axis=1, keepdims=True)
+    grad_ref[...] = (own_odds / (own_odds + other_odds) * cot).astype(jnp.bfloat16)
+    grads = grad_ref[...]
+    for m in range(4):
+        gate_value = times(rows, gate[m][...], 1, 0)
+        up_value = times(rows, up[m][...], 1, 0)
+        inner = silu_pair(gate_value, up_value)
+        inner_ref[m] = inner
+        grad_gate, grad_up = pair_back(times(grads, down[m][...], 1, 1), gate_value, up_value)
+        grad_gate_ref[m] = grad_gate
+        grad_up_ref[m] = grad_up
+        part = times(inner, down[m][...], 1, 0)
+        part_back = times(grad_gate, gate[m][...], 1, 1) + times(grad_up, up[m][...], 1, 1)
+        total[...] = part if m == 0 else total[...] + part
+        total_back[...] = part_back if m == 0 else total_back[...] + part_back
+    made = total[...].astype(jnp.bfloat16)
+    made_ref[...] = made
+    back_ref[:, :width] = total_back[...].astype(jnp.bfloat16)
+    signal = jnp.sum(cot * made.astype(jnp.float32), axis=1, keepdims=True)
+    high = signal.astype(jnp.bfloat16)
+    low = (signal - high.astype(jnp.float32)).astype(jnp.bfloat16)
+    at = lax.broadcasted_iota(jnp.int32, (count, back_ref.shape[1] - width), 1)
+    back_ref[:, width:] = jnp.where(
+        at == 0, high.astype(jnp.float32), jnp.where(at == 1, low.astype(jnp.float32), 0.0)
+    ).astype(jnp.bfloat16)
+
+
+def expert_both(experts, mine, rows, cot, router, gate, up, down):
+    count, width = rows.shape
+    hidden = gate[0].shape[1]
+    return pl.pallas_call(
+        functools.partial(expert_both_kernel, experts),
+        out_shape=(
+            jax.ShapeDtypeStruct((count, width), jnp.bfloat16),
+            jax.ShapeDtypeStruct(cot.shape, jnp.bfloat16),
+            jax.ShapeDtypeStruct((count, width), jnp.bfloat16),
+            jax.ShapeDtypeStruct((4, count, hidden), jnp.bfloat16),
+            jax.ShapeDtypeStruct((4, count, hidden), jnp.bfloat16),
+            jax.ShapeDtypeStruct((4, count, hidden), jnp.bfloat16),
+        ),
+        in_specs=[pl.BlockSpec(memory_space=pltpu.SMEM)] + vmem(15),
+        out_specs=tuple(vmem(6)),
+        scratch_shapes=[pltpu.VMEM((count, width), jnp.float32)] * 2,
+        compiler_params=kernel_params(),
+        cost_estimate=cost(48 * count * width * hidden, 18 * 2**20, 8 * count * hidden),
+        name="expert_both",
+    )(mine, rows, cot, router, *gate, *up, *down)
+
+
+def expert_grads_kernel(rows_ref, grad_ref, inner_ref, grad_gate_ref, grad_up_ref, pair_give, pair_own, pair_far, down_give, down_own, down_far):
+    for m, (pairs, at, downs, down_at) in enumerate(
+        (
+            (pair_own, 0, down_own, 0),
+            (pair_give, 0, down_give, 0),
+            (pair_far, 0, down_far, 0),
+            (pair_give, 2, down_give, 1),
+        )
+    ):
+        pairs[at] = times(rows_ref[...], grad_gate_ref[m], 0, 0).astype(jnp.bfloat16)
+        pairs[at + 1] = times(rows_ref[...], grad_up_ref[m], 0, 0).astype(jnp.bfloat16)
+        downs[down_at] = times(inner_ref[m], grad_ref[...], 0, 0).astype(jnp.bfloat16)
+
+
+def expert_grads(rows, grads, inner, grad_gate, grad_up):
+    count, width = rows.shape
+    hidden = inner.shape[2]
+    shapes = [(4, width, hidden), (2, width, hidden), (2, width, hidden)]
+    shapes += [(2, hidden, width), (1, hidden, width), (1, hidden, width)]
+    return pl.pallas_call(
+        expert_grads_kernel,
+        out_shape=tuple(jax.ShapeDtypeStruct(shape, jnp.bfloat16) for shape in shapes),
+        in_specs=vmem(5),
+        out_specs=tuple(vmem(6)),
+        compiler_params=kernel_params(),
+        cost_estimate=cost(24 * count * width * hidden, 14 * 2**20),
+        name="expert_grads",
+    )(rows, grads, inner, grad_gate, grad_up)
+
+
+def head_grads_kernel(part, at_ref, normed_ref, whole_ref, small_ref, give_ref, own_ref, far_ref):
+    tokens = whole_ref.shape[1]
+    deep = whole_ref.shape[0]
+    for m, (ref, slot) in enumerate(((own_ref, 0), (give_ref, 0), (far_ref, 0), (give_ref, 1))):
+        lanes = pl.ds(pl.multiple_of(at_ref[m] * part, 128), part)
+        rows = normed_ref[:, :, lanes].reshape(tokens, part)
+        ref[slot, :deep, :] = times(whole_ref[...], rows, 1, 0).astype(jnp.bfloat16)
+        ref[slot, deep:, :] = small_ref[:, lanes].astype(jnp.bfloat16)
+
+
+def head_grads(at, normed, whole, small):
+    deep, tokens = whole.shape
+    width = normed.shape[2]
+    part = width // 4
+    full = deep + small.shape[0]
+    return pl.pallas_call(
+        functools.partial(head_grads_kernel, part),
+        out_shape=tuple(jax.ShapeDtypeStruct((n, full, part), jnp.bfloat16) for n in (2, 1, 1)),
+        in_specs=[pl.BlockSpec(memory_space=pltpu.SMEM)] + vmem(3),
+        out_specs=tuple(vmem(3)),
+        compiler_params=kernel_params(),
+        cost_estimate=cost(2 * deep * width * tokens, 6 * 2**20),
+        name="head_grads",
+    )(at, normed, whole, small)
+
+
+def spread_kernel(wide, head, ringed, *refs):
+    if ringed:
+        spot_ref, *blocks, query_ref, key_ref, value_ref = refs[: ringed + 4]
+        gathered_ref = refs[-1]
+        outs = refs[-7:-1]
+        for k, block in enumerate(blocks[:-2]):
+            gathered_ref[spot_ref[k]] = block[...]
+        half = blocks[-2].shape[0]
+        gathered_ref[spot_ref[ringed - 2], :half, :] = blocks[-2][...]
+        gathered_ref[spot_ref[ringed - 2], half:, :] = blocks[-1][...]
+    else:
+        gathered_ref, out_ref, query_ref, key_ref, value_ref = refs[:5]
+        outs = refs[-6:]
+    query_out, key_out, value_out, out_out, small_out, sum_ref = outs
+    count, _, part = gathered_ref.shape
+    deep = wide + 2 * head
+    small = small_out.shape[0]
+    sums = jnp.zeros((part, 1), jnp.float32)
+    for i in range(count // 2):
+        block = gathered_ref[2 * i : 2 * i + 2, :wide, :].astype(jnp.float32).reshape(2 * wide, part).T
+        lanes = slice(2 * i * wide, 2 * (i + 1) * wide)
+        query_out[0, :, lanes] = block
+        sums += jnp.sum(block * query_ref[:, lanes].astype(jnp.float32), axis=1, keepdims=True)
+    for start, weight_ref, out in ((wide, key_ref, key_out), (wide + head, value_ref, value_out)):
+        block = gathered_ref[:, start : start + head, :].astype(jnp.float32).reshape(count * head, part).T
+        out[0] = block
+        sums += jnp.sum(block * weight_ref[...].astype(jnp.float32), axis=1, keepdims=True)
+    sum_ref[...] = sums
+    total = gathered_ref[0, deep : deep + small, :].astype(jnp.float32)
+    for c in range(1, count):
+        total += gathered_ref[c, deep : deep + small, :].astype(jnp.float32)
+    small_out[...] = total
+    if ringed:
+        rows = part // count
+        for c in range(count):
+            for j in range(out_out.shape[2] // part):
+                piece = gathered_ref[c, deep + small + j * rows : deep + small + (j + 1) * rows, :]
+                out_out[0, c * rows : (c + 1) * rows, j * part : (j + 1) * part] = piece.astype(jnp.float32)
+    else:
+        out_out[0] = out_ref[...].astype(jnp.float32)
+
+
+def spread(layer, layers, spots, sources, weights, wide, head, small, before):
+    ringed = len(sources) if spots is not None else 0
+    part = weights[0].shape[0]
+    width = weights[0].shape[1]
+    count = width // wide
+    shapes = [(layers,) + weight.shape for weight in weights] + [(layers, part, width)]
+    aliased = [] if before is None else list(before)
+    one = lambda shape: pl.BlockSpec((1,) + shape[1:], lambda i: (layer, 0, 0))
+    whole = lambda shape: pl.BlockSpec(shape, lambda i: (0,) * len(shape))
+    deep = sources[0].shape[-2]
+    lead = [spots] if ringed else []
+    return pl.pallas_call(
+        functools.partial(spread_kernel, wide, head, ringed),
+        grid=(1,),
+        out_shape=tuple(jax.ShapeDtypeStruct(shape, jnp.float32) for shape in shapes)
+        + (jax.ShapeDtypeStruct((small, part), jnp.float32), jax.ShapeDtypeStruct((part, 1), jnp.float32)),
+        in_specs=[pl.BlockSpec(memory_space=pltpu.SMEM)] * len(lead)
+        + [whole(source.shape) for source in sources]
+        + [whole(weight.shape) for weight in weights]
+        + [pl.BlockSpec(memory_space=pl.ANY)] * len(aliased),
+        out_specs=tuple(one(shape) for shape in shapes) + (whole((small, part)), whole((part, 1))),
+        scratch_shapes=[pltpu.VMEM((count, deep, part), jnp.bfloat16)] if ringed else [],
+        input_output_aliases={len(lead) + len(sources) + 3 + i: i for i in range(len(aliased))},
+        compiler_params=kernel_params(),
+        cost_estimate=cost(4 * count * part * wide, 12 * 2**20),
+        name="spread",
+    )(*lead, *sources, *weights, *aliased)
+
+
+def finish_kernel(*refs):
+    own_ref, near_ref, far_ref = refs[:3]
+    outs = refs[-own_ref.shape[0] :]
+    for i, out in enumerate(outs):
+        total = own_ref[i].astype(jnp.float32) + near_ref[i].astype(jnp.float32) + far_ref[i].astype(jnp.float32)
+        out[0, 0] = total
+
+
+def finish(layer, layers, own, near, far, before):
+    count, rows, columns = own.shape
+    steps = 2
+    block = rows // steps
+    aliased = [] if before is None else list(before)
+    taken = pl.BlockSpec((count, block, columns), lambda i: (0, i, 0))
+    made = pl.BlockSpec((1, 1, block, columns), lambda i: (layer, 0, i, 0))
+    return pl.pallas_call(
+        finish_kernel,
+        grid=(steps,),
+        out_shape=tuple(jax.ShapeDtypeStruct((layers, 1, rows, columns), jnp.float32) for _ in range(count)),
+        in_specs=[taken] * 3 + [pl.BlockSpec(memory_space=pl.ANY)] * len(aliased),
+        out_specs=(made,) * count,
+        input_output_aliases={3 + i: i for i in range(len(aliased))},
+        compiler_params=kernel_params(),
+        cost_estimate=cost(2 * count * rows * columns, 10 * count * rows * columns),
+        name="finish",
+    )(own, near, far, *aliased)
+
+
+def swap(x, mask):
+    return lax.ppermute(x, "wt", [(i, i ^ mask) for i in range(4)])
+
+
+def near_finish(far, own):
+    return (own, swap(own, 1), far, swap(far, 1))
 
 
 def wt_gather(own):
-    far = swap(own, "wt", 4, 2)
-    near = swap(own, "wt", 4, 1)
-    return (own, near, far, swap(far, "wt", 4, 1))
-
-
-def wt_scatter_sum(pieces):
-    got = swap(jnp.stack([pieces[1], pieces[3]]).astype(jnp.bfloat16), "wt", 4, 1).astype(jnp.float32)
-    kept = pieces[0] + got[0]
-    far = swap((pieces[2] + got[1]).astype(jnp.bfloat16), "wt", 4, 2)
-    return kept + far.astype(jnp.float32)
+    return near_finish(swap(own, 2), own)
 
 
 def wt_exchange(slices, me):
     def cut(m):
         return lax.dynamic_index_in_dim(slices, me ^ m, 0, keepdims=False)
 
-    far = swap(jnp.stack([cut(2), cut(3)]), "wt", 4, 2)
-    near = swap(jnp.stack([cut(1), far[1]]), "wt", 4, 1)
+    far = swap(jnp.stack([cut(2), cut(3)]), 2)
+    near = swap(jnp.stack([cut(1), far[1]]), 1)
     return (cut(0), near[0], far[0], near[1])
 
 
@@ -210,25 +543,30 @@
     return lax.optimization_barrier(arrays)
 
 
-def ring_gather(x, me, count, place):
+def ring_of(count):
     ring = list(range(0, count, 2)) + list(range(count - 1, 0, -2))
-    around = jnp.asarray([[ring[(ring.index(i) + k) % count] for k in range(count)] for i in range(count)], jnp.int32)
-    spots = place[lax.dynamic_index_in_dim(around, me, 0, keepdims=False)].astype(jnp.uint32)
-    right = [(ring[i], ring[(i + 1) % count]) for i in range(count)]
+    offsets = [0] + [sign * step for step in range(1, count // 2) for sign in (-1, 1)] + [count // 2]
+    table = [[ring[(ring.index(i) + k) % count] for k in offsets] for i in range(count)]
+    return ring, jnp.asarray(table, jnp.int32)
+
+
+def ring_start(x, ring):
+    right = [(a, b) for a, b in zip(ring, ring[1:] + ring[:1])]
     left = [(b, a) for a, b in right]
-    full = jnp.zeros((count,) + x.shape, x.dtype)
-
-    def put(full, block, offset):
-        return lax.dynamic_update_index_in_dim(full, block, spots[offset % count], 0)
-
-    full = put(full, x, 0)
-    ahead = behind = x
-    for step in range(1, count // 2):
+    return lax.ppermute(x, "ctx", right), lax.ppermute(x, "ctx", left)
+
+
+def ring_blocks(x, first, ring):
+    count = len(ring)
+    right = [(a, b) for a, b in zip(ring, ring[1:] + ring[:1])]
+    left = [(b, a) for a, b in right]
+    ahead, behind = first
+    blocks = [x, ahead, behind]
+    for _ in range(2, count // 2):
         ahead, behind = lax.ppermute(ahead, "ctx", right), lax.ppermute(behind, "ctx", left)
-        full = put(put(full, ahead, -step), behind, step)
+        blocks += [ahead, behind]
     half = x.shape[0] // 2
-    last = jnp.concatenate([lax.ppermute(ahead[:half], "ctx", right), lax.ppermute(behind[half:], "ctx", left)])
-    return put(full, last, count // 2)
+    return blocks + [lax.ppermute(ahead[:half], "ctx", right), lax.ppermute(behind[half:], "ctx", left)]
 
 
 def all_to_all(x):
@@ -276,15 +614,23 @@
     layers = query_weight.shape[0]
     experts = router_weight.shape[2]
     capacity = 3 * rows // experts
+    slot_count = experts * capacity
     rep = HEADS // KV_HEADS
     wide = rep * HEAD
+    lanes = wide + 2 * HEAD
     part = width // 4
-    hidden = gate_weight.shape[3]
     ctx = lax.axis_index("ctx")
+    mine = ctx.astype(jnp.int32).reshape(1)
     wt = lax.axis_index("wt").astype(jnp.uint32)
+    others = (wt ^ jnp.arange(4, dtype=jnp.uint32)).astype(jnp.int32)
     table = block_deal[0, :, 0]
     devices = jnp.arange(n_ctx, dtype=jnp.int32)
     owner_of = jnp.sum(jnp.where(table[None, :] == devices[:, None], devices[None, :], 0), axis=1)
+    ring, ring_table = ring_of(n_ctx)
+    ring_owners = lax.dynamic_index_in_dim(ring_table, ctx.astype(jnp.uint32), 0, keepdims=False)
+    spots = jnp.sum(jnp.where(ring_owners[:, None] == devices[None, :], table[None, :], 0), axis=1)
+
+    first = ring_start(tokens[0], ring)
 
     expert_ids = jnp.arange(experts, dtype=jnp.int32)
     chosen = routes[:, 0]
@@ -294,10 +640,10 @@
     rank = jnp.einsum("ij,lje->lie", earlier, onehot.astype(jnp.bfloat16), preferred_element_type=jnp.float32)
     rank = jnp.sum(jnp.where(onehot, rank, 0.0), axis=2).astype(jnp.int32)
     slots = (flat * capacity + rank).reshape(layers, rows, 2).transpose(0, 2, 1)
-    place = (slots[..., None] == jnp.arange(experts * capacity, dtype=jnp.int32)).astype(jnp.bfloat16)
+    place = (slots[..., None] == jnp.arange(slot_count, dtype=jnp.int32)).astype(jnp.bfloat16)
     named = (chosen.transpose(0, 2, 1)[..., None] == expert_ids).astype(jnp.float32)
 
-    def head_rows(layer):
+    def head_rows(layer, query_weight, key_weight, value_weight):
         return [
             lax.dynamic_slice_in_dim(query_weight[layer], ctx * wide, wide, 1).T,
             lax.dynamic_slice_in_dim(key_weight[layer], ctx * HEAD, HEAD, 1).T,
@@ -308,132 +654,136 @@
             jnp.zeros((14 - experts, part), jnp.bfloat16),
         ]
 
-    lanes = wide + 2 * HEAD
     deep = lanes + 16
-    head_own = jnp.concatenate(sum([head_rows(layer) for layer in range(layers)], []), axis=0)
+    first, *projections = tie(first, query_weight, key_weight, value_weight)
+    head_own = jnp.concatenate(sum([head_rows(layer, *projections) for layer in range(layers)], []), axis=0)
     head_all = in_order(wt_gather(head_own), wt, 1).reshape(layers, deep, width)
-    token_all = ring_gather(tokens[0], ctx, n_ctx, table).reshape(n_ctx * rows, width)
-
-    def far_start(own):
-        return swap(own, "wt", 4, 2), own
-
-    def near_finish(far, own):
-        return (own, swap(own, "wt", 4, 1), far, swap(far, "wt", 4, 1))
-
-    far_pair = [
-        far_start(jnp.concatenate([gate_weight[layer, 0], up_weight[layer, 0]], axis=1)) for layer in range(layers)
+
+    out_own = list(out_weight)
+    gate_own = [gate_weight[layer, 0] for layer in range(layers)]
+    up_own = [up_weight[layer, 0] for layer in range(layers)]
+    down_own = [down_weight[layer, 0] for layer in range(layers)]
+    project_own = [
+        jnp.concatenate([query_weight[layer], key_weight[layer], value_weight[layer]], axis=1) for layer in range(layers)
     ]
-    far_down = [far_start(down_weight[layer, 0]) for layer in range(layers)]
-    far_project = [
-        far_start(jnp.concatenate([query_weight[layer], key_weight[layer], value_weight[layer]], axis=1))
-        for layer in range(layers)
+    out_far, gate_far, up_far, down_far, project_far = [
+        [swap(own, 2) for own in group] for group in (out_own, gate_own, up_own, down_own, project_own)
     ]
 
     state = tokens[0].astype(jnp.float32)
     saved = []
+    last = layers - 1
+    cot_slots = None
     for layer in range(layers):
         head_weight = head_all[layer, :lanes]
         router = head_all[layer, lanes : lanes + experts]
         gain_one = head_all[layer, lanes + experts : lanes + experts + 1].astype(jnp.float32)
         gain_two = head_all[layer, lanes + experts + 1 : lanes + experts + 2].astype(jnp.float32)
-        out_pieces = wt_gather(out_weight[layer])
-        pair_far, pair_own = far_pair[layer]
-        down_far, down_own = far_down[layer]
         if layer == 0:
-            normed = rms_scale(token_all.astype(jnp.float32), gain_one).astype(jnp.bfloat16)
+            blocks = ring_blocks(tokens[0], first, ring)
         else:
             normed = rms_scale(state, gain_one).astype(jnp.bfloat16)
-            normed = ring_gather(normed, ctx, n_ctx, table).reshape(n_ctx * rows, width)
-        qkv = times(head_weight, normed, 1, 1).astype(jnp.bfloat16)
-        sent, exact, log_total = attend(owner_of, qkv, rep, HEAD, n_ctx)
-        sent, pair_far = tie(sent, pair_far)
-        pair_pieces = near_finish(pair_far, pair_own)
+            normed, out_far[layer] = tie(normed, out_far[layer])
+            blocks = ring_blocks(normed, ring_start(normed, ring), ring)
+        normed_all, qkv, sent, exact, log_total = front(
+            layer == 0, spots, owner_of, blocks, head_weight, gain_one, rep, HEAD
+        )
+        if layer == 0:
+            other = chosen[last].transpose(1, 0)[::-1, :, None].astype(jnp.bfloat16)
+            cot_rows = jnp.concatenate(
+                [jnp.broadcast_to(cotangent[0][None], (2, rows, width)), jnp.broadcast_to(other, (2, rows, 128))], axis=2
+            ).reshape(2 * rows, width + 128)
+            cot_out = times(place[last].reshape(2 * rows, slot_count), cot_rows, 0, 0).astype(jnp.bfloat16)
+            cot_out, blocks[1] = tie(cot_out, blocks[1])
+            cot_slots = all_to_all(cot_out.reshape(experts, capacity, width + 128)).reshape(slot_count, width + 128)
+            sent, out_far[layer] = tie(sent, out_far[layer])
+        else:
+            sent, gate_far[layer], up_far[layer] = tie(sent, gate_far[layer], up_far[layer])
+        out_pieces = near_finish(out_far[layer], out_own[layer])
         attended = all_to_all(sent).reshape(4, part, rows)
         middle = state
         for m in range(4):
             middle = middle + times(lax.dynamic_index_in_dim(attended, wt ^ m, 0, keepdims=False), out_pieces[m], 0, 0)
         mixed = rms_scale(middle, gain_two).astype(jnp.bfloat16)
+        both = place[layer, 0] + place[layer, 1]
+        outgoing = times(both, mixed, 0, 0).astype(jnp.bfloat16).reshape(experts, capacity, width)
+        if layer == 0:
+            outgoing, gate_far[layer] = tie(outgoing, gate_far[layer])
+        else:
+            outgoing, down_far[layer] = tie(outgoing, down_far[layer])
+        arrived = all_to_all(outgoing).reshape(slot_count, width)
         probs = jax.nn.softmax(times(mixed, router, 1, 1), axis=-1)
         picked = jnp.sum(named[layer] * probs[None], axis=-1, keepdims=True)
         pair_total = picked[0] + picked[1]
         gates = picked / pair_total
-        both = place[layer, 0] + place[layer, 1]
-        outgoing = times(both, mixed, 0, 0).astype(jnp.bfloat16).reshape(experts, capacity, width)
-        if layer == 0:
-            outgoing, down_far = tie(outgoing, down_far)
-        else:
-            outgoing, down_far = tie(outgoing, down_far)
-        down_pieces = near_finish(down_far, down_own)
-        arrived = all_to_all(outgoing).reshape(experts * capacity, width)
-        pairs = [times(arrived, piece, 1, 0) for piece in pair_pieces]
-        inner = [(jax.nn.silu(p[:, :hidden]) * p[:, hidden:]).astype(jnp.bfloat16) for p in pairs]
-        produced = sum(times(z, piece, 1, 0) for z, piece in zip(inner, down_pieces)).astype(jnp.bfloat16)
-        returned = all_to_all(produced.reshape(experts, capacity, width)).reshape(experts * capacity, width)
-        results = [times(place[layer, choice], returned, 1, 0) for choice in range(2)]
-        saved.append(
-            dict(
-                state=state,
-                normed=normed,
-                qkv=qkv,
-                exact=exact,
-                log_total=log_total,
-                attended=attended,
-                middle=middle,
-                mixed=mixed,
-                probs=probs,
-                pair_total=pair_total,
-                gates=gates,
-                both=both,
-                arrived=arrived,
-                pairs=pairs,
-                inner=inner,
-                results=results,
-                gain_one=gain_one,
-                gain_two=gain_two,
-                router=router,
-                out_pieces=out_pieces,
-                pair_pieces=pair_pieces,
-                down_pieces=down_pieces,
-            )
-        )
-        state = middle + gates[0] * results[0] + gates[1] * results[1]
-    block_output = state.astype(jnp.bfloat16)[None]
+        kept = dict(
+            state=state,
+            normed_all=normed_all,
+            qkv=qkv,
+            exact=exact,
+            log_total=log_total,
+            attended=attended,
+            middle=middle,
+            mixed=mixed,
+            probs=probs,
+            pair_total=pair_total,
+            gates=gates,
+            both=both,
+            arrived=arrived,
+            gain_one=gain_one,
+            gain_two=gain_two,
+            router=router,
+            out_pieces=out_pieces,
+        )
+        pieces = [near_finish(far[layer], own[layer]) for far, own in ((gate_far, gate_own), (up_far, up_own), (down_far, down_own))]
+        kept["pieces"] = pieces
+        saved.append(kept)
+        if layer == last:
+            break
+        made, kept["gate_values"], kept["up_values"], kept["inner"] = expert_forward(arrived, *pieces)
+        returned = all_to_all(made.reshape(experts, capacity, width)).reshape(slot_count, width)
+        kept["results"] = [times(place[layer, choice], returned, 1, 0) for choice in range(2)]
+        state = middle + gates[0] * kept["results"][0] + gates[1] * kept["results"][1]
 
     upstream = cotangent[0].astype(jnp.float32)
-    grads = [None] * layers
+    expert_done = [None, None]
+    head_done = None
+    smalls, gain_sums = [None] * layers, [None] * layers
+    block_output = None
     for layer in reversed(range(layers)):
         k = saved[layer]
-        gates = k["gates"]
-        back_rows = (gates * upstream[None]).astype(jnp.bfloat16).reshape(2 * rows, width)
-        outgoing = times(place[layer].reshape(2 * rows, -1), back_rows, 0, 0).astype(jnp.bfloat16)
-        arrived_grad = all_to_all(outgoing.reshape(experts, capacity, width)).reshape(experts * capacity, width)
-        grad_rows = 0.0
-        pair_grads, down_grads = [], []
-        for m in range(4):
-            gate_value, up_value = k["pairs"][m][:, :hidden], k["pairs"][m][:, hidden:]
-            grad_inner = times(arrived_grad, k["down_pieces"][m], 1, 1)
-            sigma = jax.nn.sigmoid(gate_value)
-            grad_pair = jnp.concatenate(
-                [
-                    (grad_inner * up_value * sigma * (1.0 + gate_value * (1.0 - sigma))).astype(jnp.bfloat16),
-                    (grad_inner * gate_value * sigma).astype(jnp.bfloat16),
-                ],
-                axis=1,
+        gates, both, pieces = k["gates"], k["both"], k["pieces"]
+        if layer == last:
+            router_rows = jnp.concatenate([k["router"], jnp.zeros((128 - experts, width), jnp.bfloat16)])
+            arrived, project_far[layer] = tie(k["arrived"], project_far[layer])
+            made, back, arrived_grad, inner, grad_gate, grad_up = expert_both(
+                experts, mine, arrived, cot_slots, router_rows, *pieces
             )
-            grad_rows = grad_rows + times(grad_pair, k["pair_pieces"][m], 1, 1)
-            pair_grads.append(times(k["arrived"], grad_pair, 0, 0))
-            down_grads.append(times(k["inner"][m], arrived_grad, 0, 0))
-        pair_sum = wt_scatter_sum(pair_grads)
-        down_sum = wt_scatter_sum(down_grads)
-        back = all_to_all(grad_rows.astype(jnp.bfloat16).reshape(experts, capacity, width))
-        grad_mixed = times(k["both"], back.reshape(experts * capacity, width), 1, 0)
-        signal = jnp.stack([jnp.sum(upstream * r, axis=-1, keepdims=True) for r in k["results"]])
+            back = all_to_all(back.reshape(experts, capacity, width + 128)).reshape(slot_count, width + 128)
+            signal = jnp.stack([jnp.sum(times(p, back[:, width:], 1, 0), axis=1, keepdims=True) for p in place[layer]])
+            back = back[:, :width]
+        else:
+            arrived, inner = k["arrived"], k["inner"]
+            back_rows = (gates * upstream[None]).astype(jnp.bfloat16).reshape(2 * rows, width)
+            outgoing = times(place[layer].reshape(2 * rows, slot_count), back_rows, 0, 0).astype(jnp.bfloat16)
+            arrived_grad = all_to_all(outgoing.reshape(experts, capacity, width)).reshape(slot_count, width)
+            back, grad_gate, grad_up = expert_backward(arrived_grad, *pieces, k["gate_values"], k["up_values"])
+            back = all_to_all(back.reshape(experts, capacity, width)).reshape(slot_count, width)
+            signal = jnp.stack([jnp.sum(upstream * r, axis=-1, keepdims=True) for r in k["results"]])
+        pair_give, pair_own, pair_far, down_give, down_kept, down_far_part = expert_grads(
+            arrived, arrived_grad, inner, grad_gate, grad_up
+        )
+        pair_near, down_near = swap(pair_give, 1), swap(down_give, 1)
+        add = lambda a, b: (a.astype(jnp.float32) + b.astype(jnp.float32)).astype(jnp.bfloat16)
+        pair_last = swap(add(pair_far, pair_near[2:]), 2)
+        down_last = swap(add(down_far_part, down_near[1:]), 2)
+        grad_mixed = times(both, back, 1, 0)
         grad_picked = (signal - jnp.sum(gates * signal, axis=0, keepdims=True)) / k["pair_total"][None]
         grad_probs = jnp.sum(grad_picked * named[layer], axis=0)
         grad_logits = k["probs"] * (grad_probs - jnp.sum(k["probs"] * grad_probs, axis=1, keepdims=True))
         router_part = lax.dot_general(
+            grad_logits,
             k["mixed"].astype(jnp.float32),
-            grad_logits,
             (((0,), (0,)), ((), ())),
             precision=lax.Precision.HIGHEST,
             preferred_element_type=jnp.float32,
@@ -447,31 +797,52 @@
         )
         pulled, gain_two_rows = rms_back(k["middle"], k["gain_two"], grad_mixed)
         grad_middle = upstream + pulled
+        if layer == last:
+            grad_middle, project_far[0] = tie(grad_middle, project_far[0])
         middle_low = grad_middle.astype(jnp.bfloat16)
         grad_attended = jnp.zeros((4, part, rows), jnp.bfloat16)
         for m in range(4):
             grad_attended = lax.dynamic_update_index_in_dim(
                 grad_attended, times(k["out_pieces"][m], middle_low, 1, 1).astype(jnp.bfloat16), wt ^ m, 0
             )
+        if layer == last:
+            made, back = tie(made, grad_attended)[0], back
+            returned = all_to_all(made.reshape(experts, capacity, width)).reshape(slot_count, width)
+            state = k["middle"] + sum(gates[i] * times(place[layer, i], returned, 1, 0) for i in range(2))
+            block_output = state.astype(jnp.bfloat16)[None]
         grad_heads = all_to_all(grad_attended.reshape(n_ctx, wide, rows))
-        grad_whole, grad_sent = attend_back(
-            owner_of, k["qkv"], k["exact"], k["log_total"], grad_heads, rep, HEAD, n_ctx
-        )
+        grad_whole, grad_sent = attend_back(owner_of, k["qkv"], k["exact"], k["log_total"], grad_heads, rep, HEAD)
+        grad_sent, grad_whole, pair_last, down_last = tie(grad_sent, grad_whole, pair_last, down_last)
+        pair_done = finish(layer, layers, pair_own, pair_near, pair_last, expert_done[0])
+        down_done = finish(layer, layers, down_kept, down_near, down_last, expert_done[1])
+        expert_done = [pair_done, down_done]
         grad_own = all_to_all(grad_sent)
-        small = jnp.concatenate([jnp.sum(gain_two_rows, axis=0)[:, None], router_part], axis=1)
-        head_part = jnp.concatenate([times(k["normed"], grad_whole, 0, 1), small], axis=1)
-        head_part = head_part.reshape(4, part, lanes + 1 + experts)
-        head_sum = wt_scatter_sum(
-            [lax.dynamic_index_in_dim(head_part, wt ^ m, 0, keepdims=False) for m in range(4)]
+        small = jnp.concatenate(
+            [router_part, jnp.sum(gain_two_rows, axis=0)[None], jnp.zeros((15 - experts, width), jnp.float32)]
+        )
+        head_give, head_kept, head_far = head_grads(others, k["normed_all"], grad_whole, small)
+        head_near = swap(head_give, 1)
+        head_last = swap(add(head_far[0], head_near[1]), 2)
+        head_sum = (
+            head_kept[0].astype(jnp.float32) + head_near[0].astype(jnp.float32) + head_last.astype(jnp.float32)
         ).astype(jnp.bfloat16)
-        if layer == 0:
-            head_grads = ring_gather(head_sum, ctx, n_ctx, devices)
-        else:
-            head_grads = lax.all_gather(head_sum, "ctx", axis=0)
         middle_pieces = wt_gather(middle_low)
         attended_pieces = wt_exchange(k["attended"], wt)
         out_part = times(jnp.concatenate(attended_pieces, axis=1), jnp.concatenate(middle_pieces, axis=0), 1, 0)
-        out_sum = lax.psum(out_part.astype(jnp.bfloat16), "ctx").astype(jnp.float32)
+        out_part = out_part.astype(jnp.bfloat16)
+        weights = (query_weight[layer], key_weight[layer], value_weight[layer])
+        if layer == last:
+            out_sum = lax.psum(out_part, "ctx")
+            gathered = lax.all_gather(head_sum, "ctx", axis=0)
+            sources, ring_spots = (gathered, out_sum), None
+        else:
+            out_rows = all_to_all(out_part.reshape(n_ctx, part // n_ctx, width))
+            out_rows = jnp.sum(out_rows.astype(jnp.float32), axis=0).astype(jnp.bfloat16)
+            merged = jnp.concatenate([head_sum] + [out_rows[:, i * part : (i + 1) * part] for i in range(4)], axis=0)
+            sources, ring_spots = ring_blocks(merged, ring_start(merged, ring), ring), ring_owners
+        *head_done, smalls[layer], gain_sums[layer] = spread(
+            layer, layers, ring_spots, sources, weights, wide, HEAD, 16, head_done
+        )
         own = jnp.concatenate(
             [
                 grad_own[:, :wide].reshape(width, rows),
@@ -480,7 +851,7 @@
             ],
             axis=0,
         )
-        project = near_finish(*far_project[layer])
+        project = near_finish(project_far[layer], project_own[layer])
         grad_normed = jnp.zeros((rows, width), jnp.float32)
         for m in range(4):
             grad_normed = lax.dynamic_update_slice_in_dim(
@@ -488,29 +859,22 @@
             )
         pulled, _ = rms_back(k["state"], k["gain_one"], grad_normed)
         upstream = grad_middle + pulled
-        head_grads = head_grads.astype(jnp.float32)
-        small_sum = jnp.sum(head_grads[:, :, lanes:], axis=0)
-        columns = head_grads.transpose(1, 0, 2)
-        projected = [
-            columns[:, :, :wide].reshape(part, width),
-            columns[:, :, wide : wide + HEAD].reshape(part, n_ctx * HEAD),
-            columns[:, :, wide + HEAD : lanes].reshape(part, n_ctx * HEAD),
-        ]
-        gain_one_sum = sum(
-            jnp.sum(weight[layer].astype(jnp.float32) * grad, axis=1)
-            for weight, grad in zip((query_weight, key_weight, value_weight), projected)
-        ) / attention_gain[layer].astype(jnp.float32)
-        grads[layer] = (
-            gain_one_sum,
-            *projected,
-            out_sum,
-            small_sum[:, 0],
-            small_sum[:, 1:],
-            pair_sum[None, :, :hidden],
-            pair_sum[None, :, hidden:],
-            down_sum[None],
-        )
-    return (block_output, upstream[None], *[jnp.stack(items) for items in zip(*grads)])
+    gain_one_grad = jnp.stack([s[:, 0] for s in gain_sums]) / attention_gain.astype(jnp.float32)
+    small_all = jnp.stack(smalls)
+    query_grad, key_grad, value_grad, out_grad = head_done
+    return (
+        block_output,
+        upstream[None],
+        gain_one_grad,
+        query_grad,
+        key_grad,
+        value_grad,
+        out_grad,
+        small_all[:, experts],
+        small_all[:, :experts].transpose(0, 2, 1),
+        *expert_done[0],
+        *expert_done[1],
+    )
 
 
 def local_rows(

time: 909 us -> 794 us (0.87)
  Pallas kernels: 28.8 us -> 129 us
  matrix products: 165 us -> 74.7 us
  local copies, waits for them, and re-layouts: 124 us -> 58 us
  other arithmetic: 94.1 us -> 46.1 us
  waiting for transfers between devices: 335 us -> 317 us
    pallas_call x2 -> x15, Pallas kernels: 13.6 us -> 112 us  [the longest x2 21.3 us: front(): pl.pallas_call(functools.partial(front_kernel, raw, rep, head, span), out...]
    dot_general x90 -> x40, matrix products: 160 us -> 68.9 us  [times(): lax.dot_general(left, right, (((a,), (b,)), ((), ())), preferred_element_...]
    unnamed x479 -> x349, local copies, waits for them, and re-layouts: 41.4 us -> 13.2 us
    another operation x22 -> x4, other arithmetic: 30.3 us -> 4.17 us  [the longest x2 2.51 us: wt_exchange(): near = swap(jnp.stack([cut(1), far[1]]), 1)]
    dynamic_update_slice x19 -> x0, local copies, waits for them, and re-layouts: 23.1 us -> none  [put(): lax.dynamic_update_index_in_dim(full, block, spots[offset % count], 0)]
    psum x1, waiting for transfers between devices: 19.4 us -> 0.01 us  [local_heads(): out_sum = lax.psum(out_part, 'ctx')]
    all_to_all x14 -> x15, waiting for transfers between devices: 159 us -> 178 us  [all_to_all(): return lax.all_to_all(x, 'ctx', split_axis=0, concat_axis=0, tiled=True)]
    ppermute x73 -> x79, waiting for transfers between devices: 157 us -> 139 us  [the longest x55 93.7 us: swap(): return lax.ppermute(x, 'wt', [(i, i ^ mask) for i in range(4)])]
  transfers between devices with their start and end apart: 89 -> 96, of which waited for: 36 -> 41; matrix products, arithmetic and copies ran while one was open for 36% -> 20% of each run, Pallas kernels for 3% -> 13%
where the time goes in v2:
time: 794 us; the launch traced here: 782 us
  waiting for transfers between devices  317 us (40%)
  starting transfers between devices  140 us (18%)
  Pallas kernels  129 us (16%)
  matrix products  74.7 us (9%)
  local copies, waits for them, and re-layouts  58 us (7%)
  other arithmetic  46.1 us (6%)
  between operations  17 us (2%)
    all_to_all x15, waiting for transfers between devices, all_to_all(): return lax.all_to_all(x, 'ctx', split_axis=0, concat_axis=0, tiled=True)  178 us
    ppermute x55, waiting for transfers between devices, swap(): return lax.ppermute(x, 'wt', [(i, i ^ mask) for i in range(4)])  93.7 us
    all_to_all x15, starting transfers between devices, all_to_all(): return lax.all_to_all(x, 'ctx', split_axis=0, concat_axis=0, tiled=True)  73 us
    dot_general x40, matrix products, times(): lax.dot_general(left, right, (((a,), (b,)), ((), ())), preferred_element_...  68.9 us
    ppermute x55, starting transfers between devices, swap(): return lax.ppermute(x, 'wt', [(i, i ^ mask) for i in range(4)])  32.9 us
    ppermute x6, waiting for transfers between devices, ring_blocks(): lax.ppermute(ahead, 'ctx', right)  26.9 us
    pallas_call x2, Pallas kernels, front(): pl.pallas_call(functools.partial(front_kernel, raw, rep, head, span), out...  21.3 us
    pallas_call x2, Pallas kernels, expert_grads(): pl.pallas_call(expert_grads_kernel, out_shape=tuple((jax.ShapeDtypeStruct...  18.9 us
  transfers between devices with their start and end apart: 96, of which 41 were waited for; matrix products, arithmetic and copies ran while one was open for 20% of the time, Pallas kernels for 13%

profile of v2, /device:TPU:0, one launch (start us, length us, event | category | flops | bytes accessed | tf_op | source)
XLA Modules:
  0.0 782.1 jit_solution(18008560650962287290)
XLA Ops:
  7.2 3.1 collective-permute-start
  10.3 3.2 slice_bitcast_fusion.2
  36.9 6.2 collective-permute-done.2.refs_3_
  45.1 7.1 collective-permute-done.8
  64.4 11.3 %front.2 = (bf16[8,128,1536]{2,1,0:T(8,128)(2,1)}, bf16[320,1024]{1,0:T(8,128)(2,1)}, bf16[8,192,128]{2,1,0:T(8,128)(2,1)}, f32[192,1024]{1,0:T(8,128)}, f32[3,1024]{1,0:T(4,128)}) custom-call(s32[8]{0:T(128)} %get-tuple-element.205.spot_ref, s32[8]{0:T(128)} %get-tuple-element.204.owner_ref, bf16[128,1536]{1,0:T(8,128)(2,1)} %bitcast.365, ...), custom_call_target="tpu_custom_call" | custom-call | flops 1509949440 | bytes 9437184 | tf_op jit(solution)/shard_map/front/pallas_call | solution.py:125
  75.7 5.3 all-to-all-start
  84.4 7.2 all-to-all-done
  100.1 4.4 all-to-all-start.1
  108.1 15.2 %collective-permute-done.21.refs_10_ = bf16[256,1536]{1,0:T(8,128)(2,1)S(1)} collective-permute-done((bf16[256,1536]{1,0:T(8,128)(2,1)S(1)}, bf16[256,1536]{1,0:T(8,128)(2,1)S(1)}, u32[]{:S(2)}, u32[]{:S(2)}) %collective-permute-start.21) | collective-permute-done | bytes 786464 | tf_op jit(solution)/shard_map/ppermute | solution.py:512
  127.0 5.1 all-to-all-done.1
  132.1 10.1 %expert_forward.1 = (bf16[384,1536]{1,0:T(8,128)(2,1)}, f32[4,384,256]{2,1,0:T(8,128)}, f32[4,384,256]{2,1,0:T(8,128)}, bf16[4,384,256]{2,1,0:T(8,128)(2,1)}) custom-call(bf16[384,1536]{1,0:T(8,128)(2,1)} %bitcast.42.rows_ref, bf16[1536,256]{1,0:T(8,128)(2,1)} %get-tuple-element.232.refs_0_, bf16[1536,256]{1,0:T(8,128)(2,1)} %copy-done.66, ...), custom_call_target="tpu_custom_call" | custom-call | flops 3623878656 | bytes 16777216 | tf_op jit(solution)/shard_map/expert_forward/pallas_call | solution.py:242
  142.2 3.7 all-to-all-start.2
  149.2 25.3 %all-to-all-done.2 = bf16[8,48,1536]{2,1,0:T(8,128)(2,1)S(1)} async-done(((bf16[8,48,1536]{2,1,0:T(8,128)(2,1)}), bf16[8,48,1536]{2,1,0:T(8,128)(2,1)S(1)}, u32[]{:S(2)}, u32[]{:S(2)}) %all-to-all-start.2) | async-done | bytes 1179680 | tf_op jit(solution)/shard_map/all_to_all | solution.py:573
  178.6 7.8 %collective-permute-done.24.refs_1_ = bf16[128,1536]{1,0:T(8,128)(2,1)S(1)} collective-permute-done((bf16[128,1536]{1,0:T(8,128)(2,1)S(1)}, bf16[128,1536]{1,0:T(8,128)(2,1)S(1)}, u32[]{:S(2)}, u32[]{:S(2)}) %collective-permute-start.24) | collective-permute-done | bytes 393248 | tf_op jit(solution)/shard_map/ppermute | solution.py:556
  190.5 5.1 collective-permute-done.26.refs_3_
  197.6 6.3 collective-permute-done.28.refs_5_
  207.4 3.1 collective-permute-done.30.refs_7_
  212.9 10.0 %front.3 = (bf16[8,128,1536]{2,1,0:T(8,128)(2,1)}, bf16[320,1024]{1,0:T(8,128)(2,1)}, bf16[8,192,128]{2,1,0:T(8,128)(2,1)}, f32[192,1024]{1,0:T(8,128)}, f32[3,1024]{1,0:T(4,128)}) custom-call(s32[8]{0:T(128)} %get-tuple-element.205.spot_ref, s32[8]{0:T(128)} %get-tuple-element.204.owner_ref, bf16[128,1536]{1,0:T(8,128)(2,1)} %copy-done.79, ...), custom_call_target="tpu_custom_call" | custom-call | flops 1509949440 | bytes 9437184 | tf_op jit(solution)/shard_map/front/pallas_call | solution.py:125
  224.7 5.7 all-to-all-start.3
  231.9 7.6 all-to-all-done.3
  250.7 6.0 all-to-all-start.4
  269.0 16.3 %all-to-all-done.4 = bf16[8,48,1536]{2,1,0:T(8,128)(2,1)} async-done(((bf16[8,48,1536]{2,1,0:T(8,128)(2,1)}), bf16[8,48,1536]{2,1,0:T(8,128)(2,1)}, u32[]{:S(2)}, u32[]{:S(2)}) %all-to-all-start.4) | async-done | bytes 1179680 | tf_op jit(solution)/shard_map/all_to_all | solution.py:573
  285.2 4.4 all-to-all-start.5
  292.7 13.1 %collective-permute-done.37 = bf16[384,2560]{1,0:T(8,128)(2,1)} collective-permute-done((bf16[384,2560]{1,0:T(8,128)(2,1)}, bf16[384,2560]{1,0:T(8,128)(2,1)}, u32[]{:S(2)}, u32[]{:S(2)}) %collective-permute-start.37) | collective-permute-done | bytes 1966112 | tf_op jit(solution)/shard_map/ppermute | solution.py:512
  307.3 12.7 %all-to-all-done.5 = bf16[8,48,1664]{2,1,0:T(8,128)(2,1)} async-done(((bf16[8,48,1664]{2,1,0:T(8,128)(2,1)}), bf16[8,48,1664]{2,1,0:T(8,128)(2,1)}, u32[]{:S(2)}, u32[]{:S(2)}) %all-to-all-start.5) | async-done | bytes 1277984 | tf_op jit(solution)/shard_map/all_to_all | solution.py:573
  320.1 14.7 %expert_both.1 = (bf16[384,1536]{1,0:T(8,128)(2,1)}, bf16[384,1664]{1,0:T(8,128)(2,1)}, bf16[384,1536]{1,0:T(8,128)(2,1)}, bf16[4,384,256]{2,1,0:T(8,128)(2,1)},...) custom-call(s32[1]{0:T(128)} %bitcast.65.mine_ref, bf16[384,1536]{1,0:T(8,128)(2,1)} %bitcast.69.rows_ref, ...), custom_call_target="tpu_custom_call" | custom-call | flops 7247757312 | bytes 18874368 | tf_op jit(solution)/shard_map/expert_both/pallas_call | solution.py:337
  334.7 4.5 all-to-all-start.6
  344.9 9.4 %expert_grads.2 = (bf16[4,1536,256]{2,1,0:T(8,128)(2,1)}, bf16[2,1536,256]{2,1,0:T(8,128)(2,1)}, bf16[2,1536,256]{2,1,0:T(8,128)(2,1)}, bf16[2,256,1536]{2,1,0:T...) custom-call(bf16[384,1536]{1,0:T(8,128)(2,1)} %bitcast.69.rows_ref, ...), custom_call_target="tpu_custom_call" | custom-call | flops 3623878656 | bytes 14680064 | tf_op jit(solution)/shard_map/expert_grads/pallas_call | solution.py:375
  355.4 14.1 %all-to-all-done.6 = bf16[8,48,1664]{2,1,0:T(8,128)(2,1)} async-done(((bf16[8,48,1664]{2,1,0:T(8,128)(2,1)}), bf16[8,48,1664]{2,1,0:T(8,128)(2,1)}, u32[]{:S(2)}, u32[]{:S(2)}) %all-to-all-start.6) | async-done | bytes 1277984 | tf_op jit(solution)/shard_map/all_to_all | solution.py:573
  378.3 7.6 collective-permute-done.44
  397.5 3.0 add_convert_fusion.1
  404.6 6.2 all-to-all-start.8
  413.8 6.5 all-to-all-done.8.grad_ref
  420.3 8.7 %attend_back.2 = (bf16[320,1024]{1,0:T(8,128)(2,1)}, bf16[8,320,128]{2,1,0:T(8,128)(2,1)}) custom-call(s32[8]{0:T(128)} %get-tuple-element.204.owner_ref, bf16[320,1024]{1,0:T(8,128)(2,1)} %get-tuple-element.128.qkv_ref, f32[192,1024]{1,0:T(8,128)} %get-tuple-element.129.exact_ref, f32[3,1024]{1,0:T(4,128)} %get-tuple-element.130.log_ref, ...), custom_call_target="tpu_custom_call" | custom-call | flops 1258291200 | bytes 6291456 | tf_op jit(solution)/shard_map/attend_back/pallas_call | solution.py:190
  429.0 23.2 %collective-permute-done.48.refs_2_ = bf16[1,256,1536]{2,1,0:T(8,128)(2,1)} collective-permute-done((bf16[1,256,1536]{2,1,0:T(8,128)(2,1)}, bf16[1,256,1536]{2,1,0:T(8,128)(2,1)}, u32[]{:S(2)}, u32[]{:S(2)}) %collective-permute-start.48) | collective-permute-done | bytes 786464 | tf_op jit(solution)/shard_map/ppermute | solution.py:512
  452.2 5.5 all-to-all-start.9
  457.7 14.5 %all-to-all-done.9 = bf16[8,320,128]{2,1,0:T(8,128)(2,1)} async-done(((bf16[8,320,128]{2,1,0:T(8,128)(2,1)}), bf16[8,320,128]{2,1,0:T(8,128)(2,1)}, u32[]{:S(2)}, u32[]{:S(2)}) %all-to-all-start.9) | async-done | bytes 655392 | tf_op jit(solution)/shard_map/all_to_all | solution.py:573
  486.6 4.4 all-to-all-start.10
  495.5 4.5 collective-permute-done.59
  505.0 13.0 %all-to-all-done.10 = bf16[8,48,1536]{2,1,0:T(8,128)(2,1)} async-done(((bf16[8,48,1536]{2,1,0:T(8,128)(2,1)}), bf16[8,48,1536]{2,1,0:T(8,128)(2,1)}, u32[]{:S(2)}, u32[]{:S(2)}) %all-to-all-start.10) | async-done | bytes 1179680 | tf_op jit(solution)/shard_map/all_to_all | solution.py:573
  517.9 12.4 %expert_backward.1 = (bf16[384,1536]{1,0:T(8,128)(2,1)}, bf16[4,384,256]{2,1,0:T(8,128)(2,1)}, bf16[4,384,256]{2,1,0:T(8,128)(2,1)}) custom-call(bf16[384,1536]{1,0:T(8,128)(2,1)} %bitcast.105.grad_ref, bf16[1536,256]{1,0:T(8,128)(2,1)} %get-tuple-element.232.refs_0_, bf16[1536,256]{1,0:T(8,128)(2,1)} %copy-done.66, ...), custom_call_target="tpu_custom_call" | custom-call | flops 3623878656 | bytes 16777216 | tf_op jit(solution)/shard_map/expert_backward/pallas_call | solution.py:279
  530.3 4.4 all-to-all-start.11
  544.3 9.5 %expert_grads.3 = (bf16[4,1536,256]{2,1,0:T(8,128)(2,1)}, bf16[2,1536,256]{2,1,0:T(8,128)(2,1)}, bf16[2,1536,256]{2,1,0:T(8,128)(2,1)}, bf16[2,256,1536]{2,1,0:T...) custom-call(bf16[384,1536]{1,0:T(8,128)(2,1)} %bitcast.42.rows_ref, ...), custom_call_target="tpu_custom_call" | custom-call | flops 3623878656 | bytes 14680064 | tf_op jit(solution)/shard_map/expert_grads/pallas_call | solution.py:375
  555.2 20.5 %all-to-all-done.11 = bf16[8,48,1536]{2,1,0:T(8,128)(2,1)} async-done(((bf16[8,48,1536]{2,1,0:T(8,128)(2,1)}), bf16[8,48,1536]{2,1,0:T(8,128)(2,1)}, u32[]{:S(2)}, u32[]{:S(2)}) %all-to-all-start.11) | async-done | bytes 1179680 | tf_op jit(solution)/shard_map/all_to_all | solution.py:573
  575.7 4.2 all-to-all-start.7
  591.2 4.6 head_grads.3
  600.3 3.0 add_convert_fusion
  606.3 4.0 all-to-all-done.7
  610.3 4.1 all-to-all-start.12
  617.9 3.0 convolution_convert_fusion.1
  621.0 5.1 all-to-all-done.12.grad_ref
  626.1 4.3 all-to-all-start.14
  633.4 8.7 %attend_back.3 = (bf16[320,1024]{1,0:T(8,128)(2,1)}, bf16[8,320,128]{2,1,0:T(8,128)(2,1)}) custom-call(s32[8]{0:T(128)} %get-tuple-element.204.owner_ref, bf16[320,1024]{1,0:T(8,128)(2,1)} %get-tuple-element.146.qkv_ref, f32[192,1024]{1,0:T(8,128)} %get-tuple-element.147.exact_ref, f32[3,1024]{1,0:T(4,128)} %get-tuple-element.148.log_ref, ...), custom_call_target="tpu_custom_call" | custom-call | flops 1258291200 | bytes 6291456 | tf_op jit(solution)/shard_map/attend_back/pallas_call | solution.py:190
  642.1 15.4 %collective-permute-done.54.refs_2_ = bf16[1,256,1536]{2,1,0:T(8,128)(2,1)S(1)} collective-permute-done((bf16[1,256,1536]{2,1,0:T(8,128)(2,1)S(1)}, bf16[1,256,1536]{2,1,0:T(8,128)(2,1)S(1)}, u32[]{:S(2)}, u32[]{:S(2)}) %collective-permute-start.54) | collective-permute-done | bytes 786464 | tf_op jit(solution)/shard_map/ppermute | solution.py:512
  657.5 4.8 head_grads.2
  674.1 3.7 finish.4
  680.4 3.7 finish.5
  684.0 5.9 all-to-all-start.13
  695.1 25.8 %all-to-all-done.13 = bf16[8,320,128]{2,1,0:T(8,128)(2,1)S(1)} async-done(((bf16[8,320,128]{2,1,0:T(8,128)(2,1)}), bf16[8,320,128]{2,1,0:T(8,128)(2,1)S(1)}, u32[]{:S(2)}, u32[]{:S(2)}) %all-to-all-start.13) | async-done | bytes 655392 | tf_op jit(solution)/shard_map/all_to_all | solution.py:573
  721.8 9.0 %collective-permute-start.66 = (bf16[528,384]{1,0:T(8,128)(2,1)}, bf16[528,384]{1,0:T(8,128)(2,1)S(1)}, u32[]{:S(2)}, u32[]{:S(2)}) collective-permute-start(bf16[528,384]{1,0:T(8,128)(2,1)} %collective-permute-done.64.refs_2_), channel_id=1, source_target_pairs={{0,8},{8,16},{16,24},{24,28},{28,20},{20,12},{12,4},{4,0},{1,9},{9... | collective-permute-start | bytes 1216520 | tf_op jit(solution)/shard_map/ppermute | solution.py:566
  735.3 3.9 collective-permute-done.66.refs_4_
  746.0 5.3 collective-permute-done.68.refs_6_
  756.3 6.0 spread.2
  764.1 6.4 spread.3
  (682 shorter events, 242.5 us)
Async XLA Ops:
  13.5 62.2 %collective-permute-start.11 = (bf16[384,1536]{1,0:T(8,128)(2,1)}, bf16[384,1536]{1,0:T(8,128)(2,1)}, u32[]{:S(2)}, u32[]{:S(2)}) collective-permute-start(bf16[384,1536]{1,0:T(8,128)(2,1)} %get-tuple-element.216), channel_id=1, source_target_pairs={{0,2},{1,3},{2,0},{3,1},{4,6},{5,7},{6,4},{7,5},{8,10},{9,11},{10,... | collective-permute-start | bytes 3538952 | tf_op jit(solution)/shard_map/ppermute | solution.py:512
  32.0 20.2 %collective-permute-start.8 = (bf16[672,384]{1,0:T(8,128)(2,1)S(1)}, bf16[672,384]{1,0:T(8,128)(2,1)S(1)}, u32[]{:S(2)}, u32[]{:S(2)}) collective-permute-start(bf16[672,384]{1,0:T(8,128)(2,1)S(1)} %concatenate.61), channel_id=1, source_target_pairs={{0,2},{1,3},{2,0},{3,1},{4,6},{5,7},{6,4},{7,5},{8,10},{9,11},{10,... | collective-permute-start | bytes 1548296 | tf_op jit(solution)/shard_map/ppermute | solution.py:512
  36.9 18.9 %collective-permute-start.10 = (bf16[672,384]{1,0:T(8,128)(2,1)S(1)}, bf16[672,384]{1,0:T(8,128)(2,1)S(1)}, u32[]{:S(2)}, u32[]{:S(2)}) collective-permute-start(bf16[672,384]{1,0:T(8,128)(2,1)S(1)} %concatenate.61), channel_id=1, source_target_pairs={{0,1},{1,0},{2,3},{3,2},{4,5},{5,4},{6,7},{7,6},{8,9},{9,8},{10,11... | collective-permute-start | bytes 1548296 | tf_op jit(solution)/shard_map/ppermute | solution.py:512
  53.5 42.1 %collective-permute-start.12 = (bf16[384,1536]{1,0:T(8,128)(2,1)}, bf16[384,1536]{1,0:T(8,128)(2,1)}, u32[]{:S(2)}, u32[]{:S(2)}) collective-permute-start(bf16[384,1536]{1,0:T(8,128)(2,1)} %get-tuple-element.216), channel_id=1, source_target_pairs={{0,1},{1,0},{2,3},{3,2},{4,5},{5,4},{6,7},{7,6},{8,9},{9,8},{10,11... | collective-permute-start | bytes 3538952 | tf_op jit(solution)/shard_map/ppermute | solution.py:512
  54.1 46.0 %collective-permute-start.14 = (bf16[1536,256]{1,0:T(8,128)(2,1)}, bf16[1536,256]{1,0:T(8,128)(2,1)}, u32[]{:S(2)}, u32[]{:S(2)}) collective-permute-start(bf16[1536,256]{1,0:T(8,128)(2,1)} %get-tuple-element.232.refs_0_), channel_id=1, source_target_pairs={{0,2},{1,3},{2,0},{3,1},{4,6},{5,7},{6,4},{7,5},{8,10},{9,11},{10,... | collective-permute-start | bytes 2359304 | tf_op jit(solution)/shard_map/ppermute | solution.py:512
  62.4 45.1 %collective-permute-start.18 = (bf16[1536,256]{1,0:T(8,128)(2,1)}, bf16[1536,256]{1,0:T(8,128)(2,1)}, u32[]{:S(2)}, u32[]{:S(2)}) collective-permute-start(bf16[1536,256]{1,0:T(8,128)(2,1)} %get-tuple-element.230.refs_4_), channel_id=1, source_target_pairs={{0,2},{1,3},{2,0},{3,1},{4,6},{5,7},{6,4},{7,5},{8,10},{9,11},{10,... | collective-permute-start | bytes 2359304 | tf_op jit(solution)/shard_map/ppermute | solution.py:512
  75.7 15.8 %all-to-all-start = ((bf16[8,192,128]{2,1,0:T(8,128)(2,1)}), bf16[8,192,128]{2,1,0:T(8,128)(2,1)S(1)}, u32[]{:S(2)}, u32[]{:S(2)}) async-start(bf16[8,192,128]{2,1,0:T(8,128)(2,1)} %get-tuple-element.109), calls=%async_computation | async-start | bytes 786432 | tf_op jit(solution)/shard_map/all_to_all | solution.py:573
  100.1 32.0 %all-to-all-start.1 = ((bf16[8,48,1536]{2,1,0:T(8,128)(2,1)}), bf16[8,48,1536]{2,1,0:T(8,128)(2,1)}, u32[]{:S(2)}, u32[]{:S(2)}) async-start(bf16[8,48,1536]{2,1,0:T(8,128)(2,1)} %bitcast.40), calls=%async_computation.1 | async-start | bytes 2359296 | tf_op jit(solution)/shard_map/all_to_all | solution.py:573
  105.6 17.7 %collective-permute-start.21 = (bf16[256,1536]{1,0:T(8,128)(2,1)S(1)}, bf16[256,1536]{1,0:T(8,128)(2,1)S(1)}, u32[]{:S(2)}, u32[]{:S(2)}) collective-permute-start(bf16[256,1536]{1,0:T(8,128)(2,1)S(1)} %get-tuple-element.228.refs_8_), channel_id=1, source_target_pairs={{0,2},{1,3},{2,0},{3,1},{4,6},{5,7},{6,4},{7,5},{8,10},{9,11},{10,... | collective-permute-start | bytes 2359304 | tf_op jit(solution)/shard_map/ppermute | solution.py:512
  107.0 16.2 %collective-permute-start.15 = (bf16[1536,256]{1,0:T(8,128)(2,1)}, bf16[1536,256]{1,0:T(8,128)(2,1)S(1)}, u32[]{:S(2)}, u32[]{:S(2)}) collective-permute-start(bf16[1536,256]{1,0:T(8,128)(2,1)} %get-tuple-element.232.refs_0_), channel_id=1, source_target_pairs={{0,1},{1,0},{2,3},{3,2},{4,5},{5,4},{6,7},{7,6},{8,9},{9,8},{10,11... | collective-permute-start | bytes 2359304 | tf_op jit(solution)/shard_map/ppermute | solution.py:512
  107.0 16.7 %collective-permute-start.17 = (bf16[1536,256]{1,0:T(8,128)(2,1)}, bf16[1536,256]{1,0:T(8,128)(2,1)S(1)}, u32[]{:S(2)}, u32[]{:S(2)}) collective-permute-start(bf16[1536,256]{1,0:T(8,128)(2,1)} %get-tuple-element.230.refs_4_), channel_id=1, source_target_pairs={{0,1},{1,0},{2,3},{3,2},{4,5},{5,4},{6,7},{7,6},{8,9},{9,8},{10,11... | collective-permute-start | bytes 2359304 | tf_op jit(solution)/shard_map/ppermute | solution.py:512
  107.6 16.2 %collective-permute-start.20 = (bf16[256,1536]{1,0:T(8,128)(2,1)S(1)}, bf16[256,1536]{1,0:T(8,128)(2,1)S(1)}, u32[]{:S(2)}, u32[]{:S(2)}) collective-permute-start(bf16[256,1536]{1,0:T(8,128)(2,1)S(1)} %get-tuple-element.228.refs_8_), channel_id=1, source_target_pairs={{0,1},{1,0},{2,3},{3,2},{4,5},{5,4},{6,7},{7,6},{8,9},{9,8},{10,11... | collective-permute-start | bytes 2359304 | tf_op jit(solution)/shard_map/ppermute | solution.py:512
  107.6 16.2 %collective-permute-start.19 = (bf16[1536,256]{1,0:T(8,128)(2,1)}, bf16[1536,256]{1,0:T(8,128)(2,1)S(1)}, u32[]{:S(2)}, u32[]{:S(2)}) collective-permute-start(bf16[1536,256]{1,0:T(8,128)(2,1)} %collective-permute-done.18.refs_6_), channel_id=1, source_target_pairs={{0,1},{1,0},{2,3},{3,2},{4,5},{5,4},{6,7},{7,6},{8,9},{9,8},{10,11... | collective-permute-start | bytes 2359304 | tf_op jit(solution)/shard_map/ppermute | solution.py:512
  142.2 32.3 %all-to-all-start.2 = ((bf16[8,48,1536]{2,1,0:T(8,128)(2,1)}), bf16[8,48,1536]{2,1,0:T(8,128)(2,1)S(1)}, u32[]{:S(2)}, u32[]{:S(2)}) async-start(bf16[8,48,1536]{2,1,0:T(8,128)(2,1)} %bitcast.381), calls=%async_computation.2 | async-start | bytes 2359296 | tf_op jit(solution)/shard_map/all_to_all | solution.py:573
  145.9 30.6 %collective-permute-start.23 = (bf16[384,1536]{1,0:T(8,128)(2,1)}, bf16[384,1536]{1,0:T(8,128)(2,1)}, u32[]{:S(2)}, u32[]{:S(2)}) collective-permute-start(bf16[384,1536]{1,0:T(8,128)(2,1)} %get-tuple-element.215), channel_id=1, source_target_pairs={{0,2},{1,3},{2,0},{3,1},{4,6},{5,7},{6,4},{7,5},{8,10},{9,11},{10,... | collective-permute-start | bytes 3538952 | tf_op jit(solution)/shard_map/ppermute | solution.py:512
  188.4 34.5 %collective-permute-start.32 = (bf16[1536,256]{1,0:T(8,128)(2,1)S(1)}, bf16[1536,256]{1,0:T(8,128)(2,1)S(1)}, u32[]{:S(2)}, u32[]{:S(2)}) collective-permute-start(bf16[1536,256]{1,0:T(8,128)(2,1)S(1)} %copy-done.62), channel_id=1, source_target_pairs={{0,2},{1,3},{2,0},{3,1},{4,6},{5,7},{6,4},{7,5},{8,10},{9,11},{10,... | collective-permute-start | bytes 2359304 | tf_op jit(solution)/shard_map/ppermute | solution.py:512
  189.9 33.0 %collective-permute-start.33 = (bf16[1536,256]{1,0:T(8,128)(2,1)S(1)}, bf16[1536,256]{1,0:T(8,128)(2,1)S(1)}, u32[]{:S(2)}, u32[]{:S(2)}) collective-permute-start(bf16[1536,256]{1,0:T(8,128)(2,1)S(1)} %copy-done.63), channel_id=1, source_target_pairs={{0,2},{1,3},{2,0},{3,1},{4,6},{5,7},{6,4},{7,5},{8,10},{9,11},{10,... | collective-permute-start | bytes 2359304 | tf_op jit(solution)/shard_map/ppermute | solution.py:512
  207.4 34.0 %collective-permute-start.35 = (bf16[384,1536]{1,0:T(8,128)(2,1)}, bf16[384,1536]{1,0:T(8,128)(2,1)}, u32[]{:S(2)}, u32[]{:S(2)}) collective-permute-start(bf16[384,1536]{1,0:T(8,128)(2,1)} %collective-permute-done.23), channel_id=1, source_target_pairs={{0,1},{1,0},{2,3},{3,2},{4,5},{5,4},{6,7},{7,6},{8,9},{9,8},{10,11... | collective-permute-start | bytes 3538952 | tf_op jit(solution)/shard_map/ppermute | solution.py:512
  224.7 14.9 %all-to-all-start.3 = ((bf16[8,192,128]{2,1,0:T(8,128)(2,1)}), bf16[8,192,128]{2,1,0:T(8,128)(2,1)S(1)}, u32[]{:S(2)}, u32[]{:S(2)}) async-start(bf16[8,192,128]{2,1,0:T(8,128)(2,1)} %get-tuple-element.116), calls=%async_computation.3 | async-start | bytes 786432 | tf_op jit(solution)/shard_map/all_to_all | solution.py:573
  230.4 13.2 %collective-permute-start.34 = (bf16[384,1536]{1,0:T(8,128)(2,1)}, bf16[384,1536]{1,0:T(8,128)(2,1)S(1)}, u32[]{:S(2)}, u32[]{:S(2)}) collective-permute-start(bf16[384,1536]{1,0:T(8,128)(2,1)} %get-tuple-element.215), channel_id=1, source_target_pairs={{0,1},{1,0},{2,3},{3,2},{4,5},{5,4},{6,7},{7,6},{8,9},{9,8},{10,11... | collective-permute-start | bytes 3538952 | tf_op jit(solution)/shard_map/ppermute | solution.py:512
  230.4 20.3 %collective-permute-start.36 = (bf16[256,1536]{1,0:T(8,128)(2,1)}, bf16[256,1536]{1,0:T(8,128)(2,1)}, u32[]{:S(2)}, u32[]{:S(2)}) collective-permute-start(bf16[256,1536]{1,0:T(8,128)(2,1)} %get-tuple-element.227.refs_8_), channel_id=1, source_target_pairs={{0,2},{1,3},{2,0},{3,1},{4,6},{5,7},{6,4},{7,5},{8,10},{9,11},{10,... | collective-permute-start | bytes 2359304 | tf_op jit(solution)/shard_map/ppermute | solution.py:512
  250.7 34.6 %all-to-all-start.4 = ((bf16[8,48,1536]{2,1,0:T(8,128)(2,1)}), bf16[8,48,1536]{2,1,0:T(8,128)(2,1)}, u32[]{:S(2)}, u32[]{:S(2)}) async-start(bf16[8,48,1536]{2,1,0:T(8,128)(2,1)} %bitcast.367), calls=%async_computation.4 | async-start | bytes 2359296 | tf_op jit(solution)/shard_map/all_to_all | solution.py:573
  261.3 44.5 %collective-permute-start.37 = (bf16[384,2560]{1,0:T(8,128)(2,1)}, bf16[384,2560]{1,0:T(8,128)(2,1)}, u32[]{:S(2)}, u32[]{:S(2)}) collective-permute-start(bf16[384,2560]{1,0:T(8,128)(2,1)} %pad_maximum_fusion.1), channel_id=1, source_target_pairs={{0,2},{1,3},{2,0},{3,1},{4,6},{5,7},{6,4},{7,5},{8,10},{9,11},{10,... | collective-permute-start | bytes 5898248 | tf_op jit(solution)/shard_map/ppermute | solution.py:512
  285.2 34.8 %all-to-all-start.5 = ((bf16[8,48,1664]{2,1,0:T(8,128)(2,1)}), bf16[8,48,1664]{2,1,0:T(8,128)(2,1)}, u32[]{:S(2)}, u32[]{:S(2)}) async-start(bf16[8,48,1664]{2,1,0:T(8,128)(2,1)} %bitcast.366), calls=%async_computation.5 | async-start | bytes 2555904 | tf_op jit(solution)/shard_map/all_to_all | solution.py:573
  289.7 17.5 %collective-permute-start.40 = (bf16[1536,256]{1,0:T(8,128)(2,1)}, bf16[1536,256]{1,0:T(8,128)(2,1)}, u32[]{:S(2)}, u32[]{:S(2)}) collective-permute-start(bf16[1536,256]{1,0:T(8,128)(2,1)} %get-tuple-element.229.refs_4_), channel_id=1, source_target_pairs={{0,1},{1,0},{2,3},{3,2},{4,5},{5,4},{6,7},{7,6},{8,9},{9,8},{10,11... | collective-permute-start | bytes 2359304 | tf_op jit(solution)/shard_map/ppermute | solution.py:512
  290.2 17.1 %collective-permute-start.42 = (bf16[256,1536]{1,0:T(8,128)(2,1)}, bf16[256,1536]{1,0:T(8,128)(2,1)}, u32[]{:S(2)}, u32[]{:S(2)}) collective-permute-start(bf16[256,1536]{1,0:T(8,128)(2,1)} %get-tuple-element.227.refs_8_), channel_id=1, source_target_pairs={{0,1},{1,0},{2,3},{3,2},{4,5},{5,4},{6,7},{7,6},{8,9},{9,8},{10,11... | collective-permute-start | bytes 2359304 | tf_op jit(solution)/shard_map/ppermute | solution.py:512
  290.3 29.7 %collective-permute-start.39 = (bf16[1536,256]{1,0:T(8,128)(2,1)}, bf16[1536,256]{1,0:T(8,128)(2,1)}, u32[]{:S(2)}, u32[]{:S(2)}) collective-permute-start(bf16[1536,256]{1,0:T(8,128)(2,1)} %copy-done.154), channel_id=1, source_target_pairs={{0,1},{1,0},{2,3},{3,2},{4,5},{5,4},{6,7},{7,6},{8,9},{9,8},{10,11... | collective-permute-start | bytes 2359304 | tf_op jit(solution)/shard_map/ppermute | solution.py:512
  292.6 27.5 %collective-permute-start.41 = (bf16[1536,256]{1,0:T(8,128)(2,1)}, bf16[1536,256]{1,0:T(8,128)(2,1)}, u32[]{:S(2)}, u32[]{:S(2)}) collective-permute-start(bf16[1536,256]{1,0:T(8,128)(2,1)} %copy-done.155), channel_id=1, source_target_pairs={{0,1},{1,0},{2,3},{3,2},{4,5},{5,4},{6,7},{7,6},{8,9},{9,8},{10,11... | collective-permute-start | bytes 2359304 | tf_op jit(solution)/shard_map/ppermute | solution.py:512
  305.8 14.3 %collective-permute-start.43 = (bf16[256,1536]{1,0:T(8,128)(2,1)}, bf16[256,1536]{1,0:T(8,128)(2,1)}, u32[]{:S(2)}, u32[]{:S(2)}) collective-permute-start(bf16[256,1536]{1,0:T(8,128)(2,1)} %collective-permute-done.36.refs_10_), channel_id=1, source_target_pairs={{0,1},{1,0},{2,3},{3,2},{4,5},{5,4},{6,7},{7,6},{8,9},{9,8},{10,11... | collective-permute-start | bytes 2359304 | tf_op jit(solution)/shard_map/ppermute | solution.py:512
  334.7 34.8 %all-to-all-start.6 = ((bf16[8,48,1664]{2,1,0:T(8,128)(2,1)}), bf16[8,48,1664]{2,1,0:T(8,128)(2,1)}, u32[]{:S(2)}, u32[]{:S(2)}) async-start(bf16[8,48,1664]{2,1,0:T(8,128)(2,1)} %bitcast.377), calls=%async_computation.6 | async-start | bytes 2555904 | tf_op jit(solution)/shard_map/all_to_all | solution.py:573
  341.8 44.1 %collective-permute-start.44 = (bf16[384,2560]{1,0:T(8,128)(2,1)}, bf16[384,2560]{1,0:T(8,128)(2,1)}, u32[]{:S(2)}, u32[]{:S(2)}) collective-permute-start(bf16[384,2560]{1,0:T(8,128)(2,1)} %pad_maximum_fusion.2), channel_id=1, source_target_pairs={{0,2},{1,3},{2,0},{3,1},{4,6},{5,7},{6,4},{7,5},{8,10},{9,11},{10,... | collective-permute-start | bytes 5898248 | tf_op jit(solution)/shard_map/ppermute | solution.py:512
  354.4 43.2 %collective-permute-start.45 = (bf16[4,1536,256]{2,1,0:T(8,128)(2,1)}, bf16[4,1536,256]{2,1,0:T(8,128)(2,1)}, u32[]{:S(2)}, u32[]{:S(2)}) collective-permute-start(bf16[4,1536,256]{2,1,0:T(8,128)(2,1)} %get-tuple-element.138), channel_id=1, source_target_pairs={{0,1},{1,0},{2,3},{3,2},{4,5},{5,4},{6,7},{7,6},{8,9},{9,8},{10,11... | collective-permute-start | bytes 9437192 | tf_op jit(solution)/shard_map/ppermute | solution.py:512
  354.9 55.9 %collective-permute-start.47 = (bf16[2,256,1536]{2,1,0:T(8,128)(2,1)}, bf16[2,256,1536]{2,1,0:T(8,128)(2,1)}, u32[]{:S(2)}, u32[]{:S(2)}) collective-permute-start(bf16[2,256,1536]{2,1,0:T(8,128)(2,1)} %get-tuple-element.140), channel_id=1, source_target_pairs={{0,1},{1,0},{2,3},{3,2},{4,5},{5,4},{6,7},{7,6},{8,9},{9,8},{10,11... | collective-permute-start | bytes 4718600 | tf_op jit(solution)/shard_map/ppermute | solution.py:512
  400.6 51.6 %collective-permute-start.46 = (bf16[2,1536,256]{2,1,0:T(8,128)(2,1)}, bf16[2,1536,256]{2,1,0:T(8,128)(2,1)}, u32[]{:S(2)}, u32[]{:S(2)}) collective-permute-start(bf16[2,1536,256]{2,1,0:T(8,128)(2,1)} %add_convert_fusion.1), channel_id=1, source_target_pairs={{0,2},{1,3},{2,0},{3,1},{4,6},{5,7},{6,4},{7,5},{8,10},{9,11},{10,... | collective-permute-start | bytes 4718600 | tf_op jit(solution)/shard_map/ppermute | solution.py:512
  404.6 15.7 %all-to-all-start.8 = ((bf16[8,192,128]{2,1,0:T(8,128)(2,1)}), bf16[8,192,128]{2,1,0:T(8,128)(2,1)}, u32[]{:S(2)}, u32[]{:S(2)}) async-start(bf16[8,192,128]{2,1,0:T(8,128)(2,1)} %bitcast.376), calls=%async_computation.8 | async-start | bytes 786432 | tf_op jit(solution)/shard_map/all_to_all | solution.py:573
  413.2 39.0 %collective-permute-start.48 = (bf16[1,256,1536]{2,1,0:T(8,128)(2,1)}, bf16[1,256,1536]{2,1,0:T(8,128)(2,1)}, u32[]{:S(2)}, u32[]{:S(2)}) collective-permute-start(bf16[1,256,1536]{2,1,0:T(8,128)(2,1)} %add_convert_fusion.3), channel_id=1, source_target_pairs={{0,2},{1,3},{2,0},{3,1},{4,6},{5,7},{6,4},{7,5},{8,10},{9,11},{10,... | collective-permute-start | bytes 2359304 | tf_op jit(solution)/shard_map/ppermute | solution.py:512
  413.8 61.5 %collective-permute-start.49 = (bf16[384,2560]{1,0:T(8,128)(2,1)}, bf16[384,2560]{1,0:T(8,128)(2,1)}, u32[]{:S(2)}, u32[]{:S(2)}) collective-permute-start(bf16[384,2560]{1,0:T(8,128)(2,1)} %pad_maximum_fusion.1), channel_id=1, source_target_pairs={{0,1},{1,0},{2,3},{3,2},{4,5},{5,4},{6,7},{7,6},{8,9},{9,8},{10,11... | collective-permute-start | bytes 5898248 | tf_op jit(solution)/shard_map/ppermute | solution.py:512
  452.2 20.0 %all-to-all-start.9 = ((bf16[8,320,128]{2,1,0:T(8,128)(2,1)}), bf16[8,320,128]{2,1,0:T(8,128)(2,1)}, u32[]{:S(2)}, u32[]{:S(2)}) async-start(bf16[8,320,128]{2,1,0:T(8,128)(2,1)} %get-tuple-element.141), calls=%async_computation.9 | async-start | bytes 1310720 | tf_op jit(solution)/shard_map/all_to_all | solution.py:573
  457.7 22.1 %collective-permute-start.50 = (bf16[384,2560]{1,0:T(8,128)(2,1)}, bf16[384,2560]{1,0:T(8,128)(2,1)}, u32[]{:S(2)}, u32[]{:S(2)}) collective-permute-start(bf16[384,2560]{1,0:T(8,128)(2,1)} %collective-permute-done.37), channel_id=1, source_target_pairs={{0,1},{1,0},{2,3},{3,2},{4,5},{5,4},{6,7},{7,6},{8,9},{9,8},{10,11... | collective-permute-start | bytes 5898248 | tf_op jit(solution)/shard_map/ppermute | solution.py:512
  486.6 31.4 %all-to-all-start.10 = ((bf16[8,48,1536]{2,1,0:T(8,128)(2,1)}), bf16[8,48,1536]{2,1,0:T(8,128)(2,1)}, u32[]{:S(2)}, u32[]{:S(2)}) async-start(bf16[8,48,1536]{2,1,0:T(8,128)(2,1)} %bitcast.368), calls=%async_computation.10 | async-start | bytes 2359296 | tf_op jit(solution)/shard_map/all_to_all | solution.py:573
  491.0 239.8 %collective-permute-start.55 = (bf16[384,2560]{1,0:T(8,128)(2,1)}, bf16[384,2560]{1,0:T(8,128)(2,1)}, u32[]{:S(2)}, u32[]{:S(2)}) collective-permute-start(bf16[384,2560]{1,0:T(8,128)(2,1)} %pad_maximum_fusion.2), channel_id=1, source_target_pairs={{0,1},{1,0},{2,3},{3,2},{4,5},{5,4},{6,7},{7,6},{8,9},{9,8},{10,11... | collective-permute-start | bytes 5898248 | tf_op jit(solution)/shard_map/ppermute | solution.py:512
  502.2 34.8 %collective-permute-start.60 = (bf16[2,384,128]{2,1,0:T(8,128)(2,1)}, bf16[2,384,128]{2,1,0:T(8,128)(2,1)}, u32[]{:S(2)}, u32[]{:S(2)}) collective-permute-start(bf16[2,384,128]{2,1,0:T(8,128)(2,1)} %pad_maximum_fusion.7), channel_id=1, source_target_pairs={{0,1},{1,0},{2,3},{3,2},{4,5},{5,4},{6,7},{7,6},{8,9},{9,8},{10,11... | collective-permute-start | bytes 589832 | tf_op jit(solution)/shard_map/ppermute | solution.py:512
  502.9 32.1 %collective-permute-start.74 = (bf16[2,384,128]{2,1,0:T(8,128)(2,1)}, bf16[2,384,128]{2,1,0:T(8,128)(2,1)}, u32[]{:S(2)}, u32[]{:S(2)}) collective-permute-start(bf16[2,384,128]{2,1,0:T(8,128)(2,1)} %pad_maximum_fusion.8), channel_id=1, source_target_pairs={{0,2},{1,3},{2,0},{3,1},{4,6},{5,7},{6,4},{7,5},{8,10},{9,11},{10,... | collective-permute-start | bytes 589832 | tf_op jit(solution)/shard_map/ppermute | solution.py:512
  504.4 34.7 %collective-permute-start.77 = (bf16[128,1536]{1,0:T(8,128)(2,1)S(1)}, bf16[128,1536]{1,0:T(8,128)(2,1)}, u32[]{:S(2)}, u32[]{:S(2)}) collective-permute-start(bf16[128,1536]{1,0:T(8,128)(2,1)S(1)} %copy-done.24), channel_id=1, source_target_pairs={{0,2},{1,3},{2,0},{3,1},{4,6},{5,7},{6,4},{7,5},{8,10},{9,11},{10,... | collective-permute-start | bytes 1179656 | tf_op jit(solution)/shard_map/ppermute | solution.py:512
  530.3 45.3 %all-to-all-start.11 = ((bf16[8,48,1536]{2,1,0:T(8,128)(2,1)}), bf16[8,48,1536]{2,1,0:T(8,128)(2,1)}, u32[]{:S(2)}, u32[]{:S(2)}) async-start(bf16[8,48,1536]{2,1,0:T(8,128)(2,1)} %bitcast.380), calls=%async_computation.11 | async-start | bytes 2359296 | tf_op jit(solution)/shard_map/all_to_all | solution.py:573
  534.7 221.5 %all-reduce.3.cloned.1.call-start = ((), (), s32[]{:S(2)}) async-start(), calls=%async_computation.15 | async-start | bytes 2359296 | tf_op jit(solution)/shard_map/psum | solution.py:835
  553.8 46.5 %collective-permute-start.51 = (bf16[4,1536,256]{2,1,0:T(8,128)(2,1)}, bf16[4,1536,256]{2,1,0:T(8,128)(2,1)}, u32[]{:S(2)}, u32[]{:S(2)}) collective-permute-start(bf16[4,1536,256]{2,1,0:T(8,128)(2,1)} %get-tuple-element.155), channel_id=1, source_target_pairs={{0,1},{1,0},{2,3},{3,2},{4,5},{5,4},{6,7},{7,6},{8,9},{9,8},{10,11... | collective-permute-start | bytes 9437192 | tf_op jit(solution)/shard_map/ppermute | solution.py:512
  555.1 59.3 %collective-permute-start.53 = (bf16[2,256,1536]{2,1,0:T(8,128)(2,1)}, bf16[2,256,1536]{2,1,0:T(8,128)(2,1)}, u32[]{:S(2)}, u32[]{:S(2)}) collective-permute-start(bf16[2,256,1536]{2,1,0:T(8,128)(2,1)} %get-tuple-element.157), channel_id=1, source_target_pairs={{0,1},{1,0},{2,3},{3,2},{4,5},{5,4},{6,7},{7,6},{8,9},{9,8},{10,11... | collective-permute-start | bytes 4718600 | tf_op jit(solution)/shard_map/ppermute | solution.py:512
  575.7 34.6 %all-to-all-start.7 = ((bf16[8,48,1536]{2,1,0:T(8,128)(2,1)}), bf16[8,48,1536]{2,1,0:T(8,128)(2,1)}, u32[]{:S(2)}, u32[]{:S(2)}) async-start(bf16[8,48,1536]{2,1,0:T(8,128)(2,1)} %bitcast.378), calls=%async_computation.7 | async-start | bytes 2359296 | tf_op jit(solution)/shard_map/all_to_all | solution.py:573
  584.8 29.8 %collective-permute-start.62 = (bf16[128,1536]{1,0:T(8,128)(2,1)}, bf16[128,1536]{1,0:T(8,128)(2,1)}, u32[]{:S(2)}, u32[]{:S(2)}) collective-permute-start(bf16[128,1536]{1,0:T(8,128)(2,1)} %get-tuple-element.206), channel_id=1, source_target_pairs={{0,2},{1,3},{2,0},{3,1},{4,6},{5,7},{6,4},{7,5},{8,10},{9,11},{10,... | collective-permute-start | bytes 1179656 | tf_op jit(solution)/shard_map/ppermute | solution.py:512
  586.3 30.1 %collective-permute-start.61 = (bf16[128,1536]{1,0:T(8,128)(2,1)}, bf16[128,1536]{1,0:T(8,128)(2,1)}, u32[]{:S(2)}, u32[]{:S(2)}) collective-permute-start(bf16[128,1536]{1,0:T(8,128)(2,1)} %get-tuple-element.206), channel_id=1, source_target_pairs={{0,1},{1,0},{2,3},{3,2},{4,5},{5,4},{6,7},{7,6},{8,9},{9,8},{10,11... | collective-permute-start | bytes 1179656 | tf_op jit(solution)/shard_map/ppermute | solution.py:512
  603.3 54.3 %collective-permute-start.52 = (bf16[2,1536,256]{2,1,0:T(8,128)(2,1)}, bf16[2,1536,256]{2,1,0:T(8,128)(2,1)}, u32[]{:S(2)}, u32[]{:S(2)}) collective-permute-start(bf16[2,1536,256]{2,1,0:T(8,128)(2,1)} %add_convert_fusion), channel_id=1, source_target_pairs={{0,2},{1,3},{2,0},{3,1},{4,6},{5,7},{6,4},{7,5},{8,10},{9,11},{10,... | collective-permute-start | bytes 4718600 | tf_op jit(solution)/shard_map/ppermute | solution.py:512
  610.3 15.8 %all-to-all-start.12 = ((bf16[8,192,128]{2,1,0:T(8,128)(2,1)}), bf16[8,192,128]{2,1,0:T(8,128)(2,1)}, u32[]{:S(2)}, u32[]{:S(2)}) async-start(bf16[8,192,128]{2,1,0:T(8,128)(2,1)} %bitcast.116), calls=%async_computation.12 | async-start | bytes 786432 | tf_op jit(solution)/shard_map/all_to_all | solution.py:573
  614.4 16.2 %collective-permute-start.72 = (bf16[2,336,384]{2,1,0:T(8,128)(2,1)}, bf16[2,336,384]{2,1,0:T(8,128)(2,1)}, u32[]{:S(2)}, u32[]{:S(2)}) collective-permute-start(bf16[2,336,384]{2,1,0:T(8,128)(2,1)} %get-tuple-element.168), channel_id=1, source_target_pairs={{0,1},{1,0},{2,3},{3,2},{4,5},{5,4},{6,7},{7,6},{8,9},{9,8},{10,11... | collective-permute-start | bytes 1548296 | tf_op jit(solution)/shard_map/ppermute | solution.py:512
  616.4 41.2 %collective-permute-start.54 = (bf16[1,256,1536]{2,1,0:T(8,128)(2,1)S(1)}, bf16[1,256,1536]{2,1,0:T(8,128)(2,1)S(1)}, u32[]{:S(2)}, u32[]{:S(2)}) collective-permute-start(bf16[1,256,1536]{2,1,0:T(8,128)(2,1)S(1)} %add_convert_fusion.2), channel_id=1, source_target_pairs={{0,2},{1,3},{2,0},{3,1},{4,6},{5,7},{6,4},{7,5},{8,10},{9,11},{10,... | collective-permute-start | bytes 2359304 | tf_op jit(solution)/shard_map/ppermute | solution.py:512
  626.1 57.9 %all-to-all-start.14 = ((bf16[8,48,1536]{2,1,0:T(8,128)(2,1)}), bf16[8,48,1536]{2,1,0:T(8,128)(2,1)}, u32[]{:S(2)}, u32[]{:S(2)}) async-start(bf16[8,48,1536]{2,1,0:T(8,128)(2,1)} %bitcast.379), calls=%async_computation.14 | async-start | bytes 2359296 | tf_op jit(solution)/shard_map/all_to_all | solution.py:573
  630.4 125.9 %all-gather.3.cloned.1.call-start = ((), (), s32[]{:S(2)}) async-start(), calls=%async_computation.16 | async-start | bytes 2322432 | tf_op jit(solution)/shard_map/all_gather | solution.py:836
  631.8 31.2 %collective-permute-start.73 = (bf16[336,384]{1,0:T(8,128)(2,1)S(1)}, bf16[336,384]{1,0:T(8,128)(2,1)S(1)}, u32[]{:S(2)}, u32[]{:S(2)}) collective-permute-start(bf16[336,384]{1,0:T(8,128)(2,1)S(1)} %fusion.64), channel_id=1, source_target_pairs={{0,2},{1,3},{2,0},{3,1},{4,6},{5,7},{6,4},{7,5},{8,10},{9,11},{10,... | collective-permute-start | bytes 774152 | tf_op jit(solution)/shard_map/ppermute | solution.py:512
  662.5 80.9 %collective-permute-start.56 = (bf16[384,2560]{1,0:T(8,128)(2,1)}, bf16[384,2560]{1,0:T(8,128)(2,1)}, u32[]{:S(2)}, u32[]{:S(2)}) collective-permute-start(bf16[384,2560]{1,0:T(8,128)(2,1)} %collective-permute-done.44), channel_id=1, source_target_pairs={{0,1},{1,0},{2,3},{3,2},{4,5},{5,4},{6,7},{7,6},{8,9},{9,8},{10,11... | collective-permute-start | bytes 5898248 | tf_op jit(solution)/shard_map/ppermute | solution.py:512
  666.7 24.6 %collective-permute-start.58 = (bf16[336,384]{1,0:T(8,128)(2,1)}, bf16[336,384]{1,0:T(8,128)(2,1)}, u32[]{:S(2)}, u32[]{:S(2)}) collective-permute-start(bf16[336,384]{1,0:T(8,128)(2,1)} %fusion.63), channel_id=1, source_target_pairs={{0,2},{1,3},{2,0},{3,1},{4,6},{5,7},{6,4},{7,5},{8,10},{9,11},{10,... | collective-permute-start | bytes 774152 | tf_op jit(solution)/shard_map/ppermute | solution.py:512
  684.0 36.8 %all-to-all-start.13 = ((bf16[8,320,128]{2,1,0:T(8,128)(2,1)}), bf16[8,320,128]{2,1,0:T(8,128)(2,1)S(1)}, u32[]{:S(2)}, u32[]{:S(2)}) async-start(bf16[8,320,128]{2,1,0:T(8,128)(2,1)} %get-tuple-element.158), calls=%async_computation.13 | async-start | bytes 1310720 | tf_op jit(solution)/shard_map/all_to_all | solution.py:573
  693.0 28.7 %collective-permute-start.64 = (bf16[528,384]{1,0:T(8,128)(2,1)S(1)}, bf16[528,384]{1,0:T(8,128)(2,1)}, u32[]{:S(2)}, u32[]{:S(2)}) collective-permute-start(bf16[528,384]{1,0:T(8,128)(2,1)S(1)} %slice_dynamic-update-slice_fusion.refs_1_), channel_id=1, source_target_pairs={{0,8},{8,16},{16,24},{24,28},{28,20},{20,12},{12,4},{4,0},{1,9},{9... | collective-permute-start | bytes 1216520 | tf_op jit(solution)/shard_map/ppermute | solution.py:556
  695.0 35.7 %collective-permute-start.65 = (bf16[528,384]{1,0:T(8,128)(2,1)S(1)}, bf16[528,384]{1,0:T(8,128)(2,1)}, u32[]{:S(2)}, u32[]{:S(2)}) collective-permute-start(bf16[528,384]{1,0:T(8,128)(2,1)S(1)} %slice_dynamic-update-slice_fusion.refs_1_), channel_id=1, source_target_pairs={{8,0},{16,8},{24,16},{28,24},{20,28},{12,20},{4,12},{0,4},{9,1},{1... | collective-permute-start | bytes 1216520 | tf_op jit(solution)/shard_map/ppermute | solution.py:556
  721.8 17.5 %collective-permute-start.66 = (bf16[528,384]{1,0:T(8,128)(2,1)}, bf16[528,384]{1,0:T(8,128)(2,1)S(1)}, u32[]{:S(2)}, u32[]{:S(2)}) collective-permute-start(bf16[528,384]{1,0:T(8,128)(2,1)} %collective-permute-done.64.refs_2_), channel_id=1, source_target_pairs={{0,8},{8,16},{16,24},{24,28},{28,20},{20,12},{12,4},{4,0},{1,9},{9... | collective-permute-start | bytes 1216520 | tf_op jit(solution)/shard_map/ppermute | solution.py:566
  (204 other events, 2072.1 us)
Sparse Core Ops, SparseCore 0:
  544.3 107.0 all-reduce.2
  664.9 62.6 all-gather.2

commit v3 on v2

--- a/solution.py
+++ b/solution.py
@@ -69,8 +69,8 @@
     return key_at <= query_at
 
 
-def front_kernel(raw, rep, head, span, spot_ref, owner_ref, *refs):
-    *blocks, weight_ref, gain_ref, normed_ref, qkv_ref, sent_ref, exact_ref, log_ref = refs
+def front_kernel(raw, rep, head, span, base, spot_ref, owner_ref, at_ref, *refs):
+    *blocks, gain_ref, w0, w1, w2, w3, normed_ref, qkv_ref, sent_ref, exact_ref, log_ref = refs
     rows = blocks[0].shape[0]
     count = len(blocks) - 1
     tokens = count * rows
@@ -85,11 +85,16 @@
             if raw:
                 block = rms_scale(block.astype(jnp.float32), gain).astype(jnp.bfloat16)
             normed_ref[spot_ref[k], start : start + ref.shape[0], :] = block
-    lanes_all = weight_ref.shape[0]
+    lanes_all = qkv_ref.shape[0]
+    slice_width = w0.shape[1]
     for part in range(tokens // span):
         take = span // rows
-        piece = normed_ref[part * take : (part + 1) * take].reshape(span, normed_ref.shape[2])
-        qkv_ref[:, part * span : (part + 1) * span] = times(weight_ref[...], piece, 1, 1).astype(jnp.bfloat16)
+        total = 0.0
+        for m, weight_ref in enumerate((w0, w1, w2, w3)):
+            lanes = pl.ds(pl.multiple_of(at_ref[m] * slice_width, 128), slice_width)
+            piece = normed_ref[part * take : (part + 1) * take, :, lanes].reshape(span, slice_width)
+            total = total + times(weight_ref[base : base + lanes_all, :], piece, 1, 1)
+        qkv_ref[:, part * span : (part + 1) * span] = total.astype(jnp.bfloat16)
     mask = causal_mask(span)
     per = span // rows
     for part in range(tokens // span):
@@ -115,15 +120,15 @@
                 sent_ref[owner_ref[part * per + b], at, :] = result[:, b * rows : (b + 1) * rows].astype(jnp.bfloat16)
 
 
-def front(raw, spots, owner_of, blocks, weight, gain, rep, head):
+def front(raw, spots, owner_of, at, blocks, gain, pieces, base, rep, head):
     rows, width = blocks[0].shape
     count = len(blocks) - 1
     tokens = count * rows
     span = min(256, tokens)
-    deep = weight.shape[0]
+    deep = (rep + 2) * head
     pairs = rep * tokens * (tokens + span) // 2
     return pl.pallas_call(
-        functools.partial(front_kernel, raw, rep, head, span),
+        functools.partial(front_kernel, raw, rep, head, span, base),
         out_shape=(
             jax.ShapeDtypeStruct((count, rows, width), jnp.bfloat16),
             jax.ShapeDtypeStruct((deep, tokens), jnp.bfloat16),
@@ -131,12 +136,12 @@
             jax.ShapeDtypeStruct((rep * head, tokens), jnp.float32),
             jax.ShapeDtypeStruct((rep, tokens), jnp.float32),
         ),
-        in_specs=[pl.BlockSpec(memory_space=pltpu.SMEM)] * 2 + vmem(len(blocks) + 2),
+        in_specs=[pl.BlockSpec(memory_space=pltpu.SMEM)] * 3 + vmem(len(blocks) + 5),
         out_specs=tuple(vmem(5)),
         compiler_params=kernel_params(),
         cost_estimate=cost(4 * head * pairs + 2 * deep * width * tokens, 9 * 2**20, pairs),
         name="front",
-    )(spots, owner_of, *blocks, weight, gain)
+    )(spots, owner_of, at, *blocks, gain, *pieces)
 
 
 def attend_back_kernel(rep, head, span, owner_ref, qkv_ref, exact_ref, log_ref, grad_ref, whole_ref, sent_ref, grad_all, keys_sum, values_sum):
@@ -216,18 +221,21 @@
     return grad_gate.astype(jnp.bfloat16), (grad_inner * gate_value * sigma).astype(jnp.bfloat16)
 
 
+def by_piece(gate, up, down):
+    return [piece for pieces in zip(gate, up, down) for piece in pieces]
+
+
 def expert_forward_kernel(rows_ref, *refs):
-    gate, up, down = refs[:4], refs[4:8], refs[8:12]
-    made_ref, gates_ref, ups_ref, inner_ref, total = refs[12:]
+    weights, (made_ref, gates_ref, ups_ref, inner_ref, total) = refs[:12], refs[12:]
     rows = rows_ref[...]
     for m in range(4):
-        gate_value = times(rows, gate[m][...], 1, 0)
-        up_value = times(rows, up[m][...], 1, 0)
+        gate_value = times(rows, weights[3 * m][...], 1, 0)
+        up_value = times(rows, weights[3 * m + 1][...], 1, 0)
         gates_ref[m] = gate_value
         ups_ref[m] = up_value
         inner = silu_pair(gate_value, up_value)
         inner_ref[m] = inner
-        part = times(inner, down[m][...], 1, 0)
+        part = times(inner, weights[3 * m + 2][...], 1, 0)
         if m == 0:
             total[...] = part
         elif m < 3:
@@ -239,6 +247,7 @@
 def expert_forward(rows, gate, up, down):
     count, width = rows.shape
     hidden = gate[0].shape[1]
+    weights = by_piece(gate, up, down)
     return pl.pallas_call(
         expert_forward_kernel,
         out_shape=(
@@ -247,24 +256,24 @@
             jax.ShapeDtypeStruct((4, count, hidden), jnp.float32),
             jax.ShapeDtypeStruct((4, count, hidden), jnp.bfloat16),
         ),
-        in_specs=vmem(13),
+        in_specs=vmem(1) + vmem(12),
         out_specs=tuple(vmem(4)),
         scratch_shapes=[pltpu.VMEM((count, width), jnp.float32)],
         compiler_params=kernel_params(),
         cost_estimate=cost(24 * count * width * hidden, 16 * 2**20, 4 * count * hidden),
         name="expert_forward",
-    )(rows, *gate, *up, *down)
+    )(rows, *weights)
 
 
 def expert_backward_kernel(grad_ref, *refs):
-    gate, up, down = refs[:4], refs[4:8], refs[8:12]
-    gates_ref, ups_ref, back_ref, grad_gate_ref, grad_up_ref, total = refs[12:]
+    weights, (gates, ups, back_ref, grad_gate_ref, grad_up_ref, total) = refs[2:14], refs[:2] + refs[14:]
     grads = grad_ref[...]
     for m in range(4):
-        grad_gate, grad_up = pair_back(times(grads, down[m][...], 1, 1), gates_ref[m], ups_ref[m])
+        grad_inner = times(grads, weights[3 * m + 2][...], 1, 1)
+        grad_gate, grad_up = pair_back(grad_inner, gates[m], ups[m])
         grad_gate_ref[m] = grad_gate
         grad_up_ref[m] = grad_up
-        part = times(grad_gate, gate[m][...], 1, 1) + times(grad_up, up[m][...], 1, 1)
+        part = times(grad_gate, weights[3 * m][...], 1, 1) + times(grad_up, weights[3 * m + 1][...], 1, 1)
         if m == 0:
             total[...] = part
         elif m < 3:
@@ -276,6 +285,7 @@
 def expert_backward(grads, gate, up, down, gates, ups):
     count, width = grads.shape
     hidden = gate[0].shape[1]
+    weights = [gates, ups] + by_piece(gate, up, down)
     return pl.pallas_call(
         expert_backward_kernel,
         out_shape=(
@@ -283,18 +293,18 @@
             jax.ShapeDtypeStruct((4, count, hidden), jnp.bfloat16),
             jax.ShapeDtypeStruct((4, count, hidden), jnp.bfloat16),
         ),
-        in_specs=vmem(15),
+        in_specs=vmem(1) + vmem(14),
         out_specs=tuple(vmem(3)),
         scratch_shapes=[pltpu.VMEM((count, width), jnp.float32)],
         compiler_params=kernel_params(),
         cost_estimate=cost(24 * count * width * hidden, 16 * 2**20, 4 * count * hidden),
         name="expert_backward",
-    )(grads, *gate, *up, *down, gates, ups)
+    )(grads, *weights)
 
 
 def expert_both_kernel(experts, mine_ref, rows_ref, cot_ref, router_ref, *refs):
-    gate, up, down = refs[:4], refs[4:8], refs[8:12]
-    made_ref, back_ref, grad_ref, inner_ref, grad_gate_ref, grad_up_ref, total, total_back = refs[12:]
+    weights, outs = refs[:12], refs[12:]
+    made_ref, back_ref, grad_ref, inner_ref, grad_gate_ref, grad_up_ref, total, total_back = outs
     rows = rows_ref[...]
     count, width = rows.shape
     cot = cot_ref[:, :width].astype(jnp.float32)
@@ -308,15 +318,17 @@
     grad_ref[...] = (own_odds / (own_odds + other_odds) * cot).astype(jnp.bfloat16)
     grads = grad_ref[...]
     for m in range(4):
-        gate_value = times(rows, gate[m][...], 1, 0)
-        up_value = times(rows, up[m][...], 1, 0)
+        gate, up = weights[3 * m], weights[3 * m + 1]
+        gate_value = times(rows, gate[...], 1, 0)
+        up_value = times(rows, up[...], 1, 0)
         inner = silu_pair(gate_value, up_value)
         inner_ref[m] = inner
-        grad_gate, grad_up = pair_back(times(grads, down[m][...], 1, 1), gate_value, up_value)
+        down = weights[3 * m + 2]
+        grad_gate, grad_up = pair_back(times(grads, down[...], 1, 1), gate_value, up_value)
         grad_gate_ref[m] = grad_gate
         grad_up_ref[m] = grad_up
-        part = times(inner, down[m][...], 1, 0)
-        part_back = times(grad_gate, gate[m][...], 1, 1) + times(grad_up, up[m][...], 1, 1)
+        part = times(inner, down[...], 1, 0)
+        part_back = times(grad_gate, gate[...], 1, 1) + times(grad_up, up[...], 1, 1)
         total[...] = part if m == 0 else total[...] + part
         total_back[...] = part_back if m == 0 else total_back[...] + part_back
     made = total[...].astype(jnp.bfloat16)
@@ -334,6 +346,7 @@
 def expert_both(experts, mine, rows, cot, router, gate, up, down):
     count, width = rows.shape
     hidden = gate[0].shape[1]
+    weights = by_piece(gate, up, down)
     return pl.pallas_call(
         functools.partial(expert_both_kernel, experts),
         out_shape=(
@@ -344,22 +357,22 @@
             jax.ShapeDtypeStruct((4, count, hidden), jnp.bfloat16),
             jax.ShapeDtypeStruct((4, count, hidden), jnp.bfloat16),
         ),
-        in_specs=[pl.BlockSpec(memory_space=pltpu.SMEM)] + vmem(15),
+        in_specs=[pl.BlockSpec(memory_space=pltpu.SMEM)] + vmem(3) + vmem(12),
         out_specs=tuple(vmem(6)),
         scratch_shapes=[pltpu.VMEM((count, width), jnp.float32)] * 2,
         compiler_params=kernel_params(),
         cost_estimate=cost(48 * count * width * hidden, 18 * 2**20, 8 * count * hidden),
         name="expert_both",
-    )(mine, rows, cot, router, *gate, *up, *down)
-
-
-def expert_grads_kernel(rows_ref, grad_ref, inner_ref, grad_gate_ref, grad_up_ref, pair_give, pair_own, pair_far, down_give, down_own, down_far):
+    )(mine, rows, cot, router, *weights)
+
+
+def expert_grads_kernel(rows_ref, grad_ref, inner_ref, grad_gate_ref, grad_up_ref, pair_give, far_give, pair_own, pair_far, down_give, down_own, down_far):
     for m, (pairs, at, downs, down_at) in enumerate(
         (
             (pair_own, 0, down_own, 0),
             (pair_give, 0, down_give, 0),
             (pair_far, 0, down_far, 0),
-            (pair_give, 2, down_give, 1),
+            (far_give, 0, down_give, 1),
         )
     ):
         pairs[at] = times(rows_ref[...], grad_gate_ref[m], 0, 0).astype(jnp.bfloat16)
@@ -370,13 +383,13 @@
 def expert_grads(rows, grads, inner, grad_gate, grad_up):
     count, width = rows.shape
     hidden = inner.shape[2]
-    shapes = [(4, width, hidden), (2, width, hidden), (2, width, hidden)]
+    shapes = [(2, width, hidden)] * 4
     shapes += [(2, hidden, width), (1, hidden, width), (1, hidden, width)]
     return pl.pallas_call(
         expert_grads_kernel,
         out_shape=tuple(jax.ShapeDtypeStruct(shape, jnp.bfloat16) for shape in shapes),
         in_specs=vmem(5),
-        out_specs=tuple(vmem(6)),
+        out_specs=tuple(vmem(7)),
         compiler_params=kernel_params(),
         cost_estimate=cost(24 * count * width * hidden, 14 * 2**20),
         name="expert_grads",
@@ -404,7 +417,7 @@
         in_specs=[pl.BlockSpec(memory_space=pltpu.SMEM)] + vmem(3),
         out_specs=tuple(vmem(3)),
         compiler_params=kernel_params(),
-        cost_estimate=cost(2 * deep * width * tokens, 6 * 2**20),
+        cost_estimate=cost(2**20, 2**16),
         name="head_grads",
     )(at, normed, whole, small)
 
@@ -420,7 +433,7 @@
         gathered_ref[spot_ref[ringed - 2], :half, :] = blocks[-2][...]
         gathered_ref[spot_ref[ringed - 2], half:, :] = blocks[-1][...]
     else:
-        gathered_ref, out_ref, query_ref, key_ref, value_ref = refs[:5]
+        gathered_ref, query_ref, key_ref, value_ref = refs[:4]
         outs = refs[-6:]
     query_out, key_out, value_out, out_out, small_out, sum_ref = outs
     count, _, part = gathered_ref.shape
@@ -441,14 +454,11 @@
     for c in range(1, count):
         total += gathered_ref[c, deep : deep + small, :].astype(jnp.float32)
     small_out[...] = total
-    if ringed:
-        rows = part // count
-        for c in range(count):
-            for j in range(out_out.shape[2] // part):
-                piece = gathered_ref[c, deep + small + j * rows : deep + small + (j + 1) * rows, :]
-                out_out[0, c * rows : (c + 1) * rows, j * part : (j + 1) * part] = piece.astype(jnp.float32)
-    else:
-        out_out[0] = out_ref[...].astype(jnp.float32)
+    rows = part // count
+    for c in range(count):
+        for j in range(out_out.shape[2] // part):
+            piece = gathered_ref[c, deep + small + j * rows : deep + small + (j + 1) * rows, :]
+            out_out[0, c * rows : (c + 1) * rows, j * part : (j + 1) * part] = piece.astype(jnp.float32)
 
 
 def spread(layer, layers, spots, sources, weights, wide, head, small, before):
@@ -475,16 +485,16 @@
         scratch_shapes=[pltpu.VMEM((count, deep, part), jnp.bfloat16)] if ringed else [],
         input_output_aliases={len(lead) + len(sources) + 3 + i: i for i in range(len(aliased))},
         compiler_params=kernel_params(),
-        cost_estimate=cost(4 * count * part * wide, 12 * 2**20),
+        cost_estimate=cost(2**20, 2**16),
         name="spread",
     )(*lead, *sources, *weights, *aliased)
 
 
 def finish_kernel(*refs):
-    own_ref, near_ref, far_ref = refs[:3]
-    outs = refs[-own_ref.shape[0] :]
-    for i, out in enumerate(outs):
-        total = own_ref[i].astype(jnp.float32) + near_ref[i].astype(jnp.float32) + far_ref[i].astype(jnp.float32)
+    own_ref, near_ref = refs[:2]
+    count = own_ref.shape[0]
+    for i, (far_ref, out) in enumerate(zip(refs[2 : 2 + count], refs[-count:])):
+        total = own_ref[i].astype(jnp.float32) + near_ref[i].astype(jnp.float32) + far_ref[...].astype(jnp.float32)
         out[0, 0] = total
 
 
@@ -499,13 +509,134 @@
         finish_kernel,
         grid=(steps,),
         out_shape=tuple(jax.ShapeDtypeStruct((layers, 1, rows, columns), jnp.float32) for _ in range(count)),
-        in_specs=[taken] * 3 + [pl.BlockSpec(memory_space=pl.ANY)] * len(aliased),
+        in_specs=[taken] * 2
+        + [pl.BlockSpec((block, columns), lambda i: (i, 0))] * count
+        + [pl.BlockSpec(memory_space=pl.ANY)] * len(aliased),
         out_specs=(made,) * count,
-        input_output_aliases={3 + i: i for i in range(len(aliased))},
+        input_output_aliases={2 + count + i: i for i in range(len(aliased))},
         compiler_params=kernel_params(),
-        cost_estimate=cost(2 * count * rows * columns, 10 * count * rows * columns),
+        cost_estimate=cost(2**20, 2**16),
         name="finish",
-    )(own, near, far, *aliased)
+    )(own, near, *far, *aliased)
+
+
+def head_rows_kernel(wide, head, at_ref, query_ref, key_ref, value_ref, small_ref, out_ref):
+    odd = at_ref[0] % 2
+    top = 0
+    for ref, size in ((query_ref, wide), (key_ref, head), (value_ref, head)):
+        turned = ref[0].astype(jnp.float32).T
+        out_ref[0, top : top + size, :] = jnp.where(odd == 1, turned[size:], turned[:size]).astype(jnp.bfloat16)
+        top += size
+    out_ref[0, top:, :] = small_ref[0]
+
+
+def head_rows(mine, query_weight, key_weight, value_weight, small, wide, head):
+    layers, part, _ = query_weight.shape
+    rows = wide + 2 * head + small.shape[1]
+    taken = lambda size: pl.BlockSpec((1, part, 2 * size), lambda i, at: (i, 0, at[0] // 2))
+    return pl.pallas_call(
+        functools.partial(head_rows_kernel, wide, head),
+        grid_spec=pltpu.PrefetchScalarGridSpec(
+            num_scalar_prefetch=1,
+            grid=(layers,),
+            in_specs=[taken(wide), taken(head), taken(head), pl.BlockSpec((1,) + small.shape[1:], lambda i, at: (i, 0, 0))],
+            out_specs=pl.BlockSpec((1, rows, part), lambda i, at: (i, 0, 0)),
+        ),
+        out_shape=jax.ShapeDtypeStruct((layers, rows, part), jnp.bfloat16),
+        compiler_params=kernel_params(),
+        cost_estimate=cost(2**20, 2**16),
+        name="head_rows",
+    )(mine, query_weight, key_weight, value_weight, small)
+
+
+def middle_forward_kernel(at_ref, attended_ref, state_ref, gain_ref, place_ref, *refs):
+    weights, (middle_ref, mixed_ref, out_ref) = refs[:4], refs[4:]
+    part = weights[0].shape[0]
+    total = state_ref[...]
+    for m in range(4):
+        rows = attended_ref[pl.ds(pl.multiple_of(at_ref[m] * part, 128), part), :]
+        total = total + times(rows, weights[m][...], 0, 0)
+    middle_ref[...] = total
+    mixed = rms_scale(total, gain_ref[...]).astype(jnp.bfloat16)
+    mixed_ref[...] = mixed
+    out_ref[...] = times(place_ref[0] + place_ref[1], mixed, 0, 0).astype(jnp.bfloat16)
+
+
+def middle_forward(at, attended, pieces, state, gain, place):
+    rows, width = state.shape
+    slots = place.shape[2]
+    return pl.pallas_call(
+        middle_forward_kernel,
+        out_shape=(
+            jax.ShapeDtypeStruct((rows, width), jnp.float32),
+            jax.ShapeDtypeStruct((rows, width), jnp.bfloat16),
+            jax.ShapeDtypeStruct((slots, width), jnp.bfloat16),
+        ),
+        in_specs=[pl.BlockSpec(memory_space=pltpu.SMEM)] + vmem(4) + vmem(4),
+        out_specs=tuple(vmem(3)),
+        compiler_params=kernel_params(),
+        cost_estimate=cost(2 * rows * width * (width + slots), 9 * 2**20),
+        name="middle_forward",
+    )(at, attended, state, gain, place, *pieces)
+
+
+def middle_back_kernel(experts, at_ref, place_ref, back_ref, upstream_ref, middle_ref, mixed_ref, gain_ref, router_ref, chosen_ref, *refs):
+    *results, w0, w1, w2, w3, grad_ref, low_ref, heads_ref, small_ref = refs
+    weights = (w0, w1, w2, w3)
+    rows, width = upstream_ref.shape
+    part = w0.shape[0]
+    upstream, mixed, router = upstream_ref[...], mixed_ref[...], router_ref[...]
+    logits = times(mixed, router, 1, 1)
+    ids = lax.broadcasted_iota(jnp.int32, logits.shape, 1)
+    logits = jnp.where(ids < experts, logits, NEG)
+    odds = jnp.exp(logits - jnp.max(logits, axis=1, keepdims=True))
+    probs = odds / jnp.sum(odds, axis=1, keepdims=True)
+    hits = [ids == chosen_ref[:, c : c + 1] for c in range(2)]
+    picked = [jnp.sum(jnp.where(hit, probs, 0.0), axis=1, keepdims=True) for hit in hits]
+    pair_total = picked[0] + picked[1]
+    if results:
+        signal = [jnp.sum(upstream * r[...].astype(jnp.float32), axis=1, keepdims=True) for r in results]
+    else:
+        signal = [jnp.sum(times(place_ref[c], back_ref[:, width:], 1, 0), axis=1, keepdims=True) for c in range(2)]
+    mean = (picked[0] * signal[0] + picked[1] * signal[1]) / pair_total
+    slopes = [(s - mean) / pair_total for s in signal]
+    grad_probs = jnp.where(hits[0], slopes[0], 0.0) + jnp.where(hits[1], slopes[1], 0.0)
+    grad_logits = probs * (grad_probs - jnp.sum(probs * grad_probs, axis=1, keepdims=True))
+    high = grad_logits.astype(jnp.bfloat16)
+    rest = (grad_logits - high.astype(jnp.float32)).astype(jnp.bfloat16)
+    small_ref[...] = jnp.zeros_like(small_ref)
+    router_part = times(high, mixed, 0, 0) + times(rest, mixed, 0, 0)
+    small_ref[:experts, :] = router_part[:experts]
+    grad_mixed = times(place_ref[0] + place_ref[1], back_ref[:, :width], 1, 0)
+    grad_mixed = grad_mixed + times(high, router, 1, 0) + times(rest, router, 1, 0)
+    pulled, gain_rows = rms_back(middle_ref[...], gain_ref[...], grad_mixed)
+    small_ref[experts : experts + 1, :] = jnp.sum(gain_rows, axis=0, keepdims=True)
+    grad = upstream + pulled
+    grad_ref[...] = grad
+    low = grad.astype(jnp.bfloat16)
+    low_ref[...] = low
+    for m in range(4):
+        lanes = pl.ds(pl.multiple_of(at_ref[m] * part, 128), part)
+        heads_ref[lanes, :] = times(weights[m][...], low, 1, 1).astype(jnp.bfloat16)
+
+
+def middle_back(experts, at, place, back, upstream, middle, mixed, gain, router, chosen, results, pieces):
+    rows, width = upstream.shape
+    slots = place.shape[2]
+    return pl.pallas_call(
+        functools.partial(middle_back_kernel, experts),
+        out_shape=(
+            jax.ShapeDtypeStruct((rows, width), jnp.float32),
+            jax.ShapeDtypeStruct((rows, width), jnp.bfloat16),
+            jax.ShapeDtypeStruct((width, rows), jnp.bfloat16),
+            jax.ShapeDtypeStruct((experts + 8, width), jnp.float32),
+        ),
+        in_specs=[pl.BlockSpec(memory_space=pltpu.SMEM)] + vmem(8 + len(results)) + vmem(4),
+        out_specs=tuple(vmem(4)),
+        compiler_params=kernel_params(),
+        cost_estimate=cost(2 * rows * width * (width + slots), 10 * 2**20),
+        name="middle_back",
+    )(at, place, back, upstream, middle, mixed, gain, router, chosen, *results, *pieces)
 
 
 def swap(x, mask):
@@ -556,7 +687,7 @@
     return lax.ppermute(x, "ctx", right), lax.ppermute(x, "ctx", left)
 
 
-def ring_blocks(x, first, ring):
+def ring_blocks(x, first, ring, early=None):
     count = len(ring)
     right = [(a, b) for a, b in zip(ring, ring[1:] + ring[:1])]
     left = [(b, a) for a, b in right]
@@ -565,8 +696,11 @@
     for _ in range(2, count // 2):
         ahead, behind = lax.ppermute(ahead, "ctx", right), lax.ppermute(behind, "ctx", left)
         blocks += [ahead, behind]
+    if early is not None:
+        ahead, behind, *early = tie(ahead, behind, *early)
     half = x.shape[0] // 2
-    return blocks + [lax.ppermute(ahead[:half], "ctx", right), lax.ppermute(behind[half:], "ctx", left)]
+    blocks += [lax.ppermute(ahead[:half], "ctx", right), lax.ppermute(behind[half:], "ctx", left)]
+    return blocks if early is None else (blocks, early)
 
 
 def all_to_all(x):
@@ -643,76 +777,79 @@
     place = (slots[..., None] == jnp.arange(slot_count, dtype=jnp.int32)).astype(jnp.bfloat16)
     named = (chosen.transpose(0, 2, 1)[..., None] == expert_ids).astype(jnp.float32)
 
-    def head_rows(layer, query_weight, key_weight, value_weight):
-        return [
-            lax.dynamic_slice_in_dim(query_weight[layer], ctx * wide, wide, 1).T,
-            lax.dynamic_slice_in_dim(key_weight[layer], ctx * HEAD, HEAD, 1).T,
-            lax.dynamic_slice_in_dim(value_weight[layer], ctx * HEAD, HEAD, 1).T,
-            router_weight[layer].T,
-            attention_gain[layer][None],
-            mixture_gain[layer][None],
-            jnp.zeros((14 - experts, part), jnp.bfloat16),
-        ]
-
+    small_rows = jnp.concatenate(
+        [
+            router_weight.transpose(0, 2, 1),
+            attention_gain[:, None],
+            mixture_gain[:, None],
+            jnp.zeros((layers, 14 - experts, part), jnp.bfloat16),
+        ],
+        axis=1,
+    )
     deep = lanes + 16
-    first, *projections = tie(first, query_weight, key_weight, value_weight)
-    head_own = jnp.concatenate(sum([head_rows(layer, *projections) for layer in range(layers)], []), axis=0)
-    head_all = in_order(wt_gather(head_own), wt, 1).reshape(layers, deep, width)
+    head_own = head_rows(mine, query_weight, key_weight, value_weight, small_rows, wide, HEAD)
+    head_own = head_own.reshape(layers * deep, part)
+    head_far = swap(head_own, 2)
 
     out_own = list(out_weight)
     gate_own = [gate_weight[layer, 0] for layer in range(layers)]
     up_own = [up_weight[layer, 0] for layer in range(layers)]
     down_own = [down_weight[layer, 0] for layer in range(layers)]
-    project_own = [
-        jnp.concatenate([query_weight[layer], key_weight[layer], value_weight[layer]], axis=1) for layer in range(layers)
+    query_own = list(query_weight)
+    pair_own_weights = [jnp.concatenate([key_weight[layer], value_weight[layer]], axis=1) for layer in range(layers)]
+    out_far, gate_far, up_far, down_far, query_far, key_far = [
+        [swap(own, 2) for own in group]
+        for group in (out_own, gate_own, up_own, down_own, query_own, pair_own_weights)
     ]
-    out_far, gate_far, up_far, down_far, project_far = [
-        [swap(own, 2) for own in group] for group in (out_own, gate_own, up_own, down_own, project_own)
-    ]
+
+    last = layers - 1
+    other = chosen[last].transpose(1, 0)[::-1, :, None].astype(jnp.bfloat16)
+    cot_rows = jnp.concatenate(
+        [jnp.broadcast_to(cotangent[0][None], (2, rows, width)), jnp.broadcast_to(other, (2, rows, 128))], axis=2
+    ).reshape(2 * rows, width + 128)
+    cot_out = times(place[last].reshape(2 * rows, slot_count), cot_rows, 0, 0).astype(jnp.bfloat16)
 
     state = tokens[0].astype(jnp.float32)
     saved = []
-    last = layers - 1
-    cot_slots = None
     for layer in range(layers):
-        head_weight = head_all[layer, :lanes]
-        router = head_all[layer, lanes : lanes + experts]
-        gain_one = head_all[layer, lanes + experts : lanes + experts + 1].astype(jnp.float32)
-        gain_two = head_all[layer, lanes + experts + 1 : lanes + experts + 2].astype(jnp.float32)
         if layer == 0:
-            blocks = ring_blocks(tokens[0], first, ring)
-        else:
+            blocks, head_pieces = ring_blocks(tokens[0], first, ring, near_finish(head_far, head_own))
+            small_all = [
+                in_order([piece[i * deep + lanes : (i + 1) * deep] for piece in head_pieces], wt, 1)
+                for i in range(layers)
+            ]
+            cot_out = tie(cot_out, *blocks[-2:])[0]
+            cot_slots = all_to_all(cot_out.reshape(experts, capacity, width + 128)).reshape(slot_count, width + 128)
+        router = jnp.concatenate([small_all[layer][:experts], jnp.zeros((128 - experts, width), jnp.bfloat16)])
+        gain_one = small_all[layer][experts : experts + 1].astype(jnp.float32)
+        gain_two = small_all[layer][experts + 1 : experts + 2].astype(jnp.float32)
+        if layer > 0:
             normed = rms_scale(state, gain_one).astype(jnp.bfloat16)
-            normed, out_far[layer] = tie(normed, out_far[layer])
             blocks = ring_blocks(normed, ring_start(normed, ring), ring)
         normed_all, qkv, sent, exact, log_total = front(
-            layer == 0, spots, owner_of, blocks, head_weight, gain_one, rep, HEAD
+            layer == 0, spots, owner_of, others, blocks, gain_one, head_pieces, layer * deep, rep, HEAD
         )
         if layer == 0:
-            other = chosen[last].transpose(1, 0)[::-1, :, None].astype(jnp.bfloat16)
-            cot_rows = jnp.concatenate(
-                [jnp.broadcast_to(cotangent[0][None], (2, rows, width)), jnp.broadcast_to(other, (2, rows, 128))], axis=2
-            ).reshape(2 * rows, width + 128)
-            cot_out = times(place[last].reshape(2 * rows, slot_count), cot_rows, 0, 0).astype(jnp.bfloat16)
-            cot_out, blocks[1] = tie(cot_out, blocks[1])
-            cot_slots = all_to_all(cot_out.reshape(experts, capacity, width + 128)).reshape(slot_count, width + 128)
-            sent, out_far[layer] = tie(sent, out_far[layer])
+            sent, cot_slots = tie(sent, cot_slots)
         else:
-            sent, gate_far[layer], up_far[layer] = tie(sent, gate_far[layer], up_far[layer])
+            sent, out_far[layer], up_far[layer] = tie(sent, out_far[layer], up_far[layer])
+        attended = all_to_all(sent).reshape(width, rows)
+        if layer == 0:
+            attended, out_far[layer] = tie(attended, out_far[layer])
         out_pieces = near_finish(out_far[layer], out_own[layer])
-        attended = all_to_all(sent).reshape(4, part, rows)
-        middle = state
-        for m in range(4):
-            middle = middle + times(lax.dynamic_index_in_dim(attended, wt ^ m, 0, keepdims=False), out_pieces[m], 0, 0)
-        mixed = rms_scale(middle, gain_two).astype(jnp.bfloat16)
-        both = place[layer, 0] + place[layer, 1]
-        outgoing = times(both, mixed, 0, 0).astype(jnp.bfloat16).reshape(experts, capacity, width)
+        middle, mixed, outgoing = middle_forward(others, attended, out_pieces, state, gain_two, place[layer])
+        outgoing = outgoing.reshape(experts, capacity, width)
         if layer == 0:
             outgoing, gate_far[layer] = tie(outgoing, gate_far[layer])
         else:
-            outgoing, down_far[layer] = tie(outgoing, down_far[layer])
+            outgoing, down_far[layer], *saved[0]["attended"] = tie(outgoing, down_far[layer], *saved[0]["attended"])
+            kept_exchange = wt_exchange(attended.reshape(4, part, rows), wt)
         arrived = all_to_all(outgoing).reshape(slot_count, width)
-        probs = jax.nn.softmax(times(mixed, router, 1, 1), axis=-1)
+        if layer == 0:
+            kept_exchange = wt_exchange(attended.reshape(4, part, rows), wt)
+        else:
+            arrived, query_far[layer] = tie(arrived, query_far[layer])
+        probs = jax.nn.softmax(times(mixed, router[:experts], 1, 1), axis=-1)
         picked = jnp.sum(named[layer] * probs[None], axis=-1, keepdims=True)
         pair_total = picked[0] + picked[1]
         gates = picked / pair_total
@@ -722,13 +859,10 @@
             qkv=qkv,
             exact=exact,
             log_total=log_total,
-            attended=attended,
+            attended=kept_exchange,
             middle=middle,
             mixed=mixed,
-            probs=probs,
-            pair_total=pair_total,
             gates=gates,
-            both=both,
             arrived=arrived,
             gain_one=gain_one,
             gain_two=gain_two,
@@ -742,125 +876,136 @@
             break
         made, kept["gate_values"], kept["up_values"], kept["inner"] = expert_forward(arrived, *pieces)
         returned = all_to_all(made.reshape(experts, capacity, width)).reshape(slot_count, width)
-        kept["results"] = [times(place[layer, choice], returned, 1, 0) for choice in range(2)]
-        state = middle + gates[0] * kept["results"][0] + gates[1] * kept["results"][1]
+        returned, gate_far[last] = tie(returned, gate_far[last])
+        results = [times(place[layer, choice], returned, 1, 0) for choice in range(2)]
+        kept["results"] = [result.astype(jnp.bfloat16) for result in results]
+        state = middle + gates[0] * results[0] + gates[1] * results[1]
 
     upstream = cotangent[0].astype(jnp.float32)
-    expert_done = [None, None]
-    head_done = None
+    expert_done, head_done, returned, sources = None, None, None, None
+    merge = lambda head, out: jnp.concatenate([head] + [out[:, i * part : (i + 1) * part] for i in range(4)], axis=0)
     smalls, gain_sums = [None] * layers, [None] * layers
     block_output = None
     for layer in reversed(range(layers)):
         k = saved[layer]
-        gates, both, pieces = k["gates"], k["both"], k["pieces"]
+        gates, pieces = k["gates"], k["pieces"]
         if layer == last:
-            router_rows = jnp.concatenate([k["router"], jnp.zeros((128 - experts, width), jnp.bfloat16)])
-            arrived, project_far[layer] = tie(k["arrived"], project_far[layer])
+            arrived = k["arrived"]
             made, back, arrived_grad, inner, grad_gate, grad_up = expert_both(
-                experts, mine, arrived, cot_slots, router_rows, *pieces
+                experts, mine, arrived, cot_slots, k["router"], *pieces
             )
-            back = all_to_all(back.reshape(experts, capacity, width + 128)).reshape(slot_count, width + 128)
-            signal = jnp.stack([jnp.sum(times(p, back[:, width:], 1, 0), axis=1, keepdims=True) for p in place[layer]])
-            back = back[:, :width]
+            back = all_to_all(back.reshape(experts, capacity, width + 128))
+            back = back.reshape(slot_count, width + 128)
+            results = []
         else:
             arrived, inner = k["arrived"], k["inner"]
             back_rows = (gates * upstream[None]).astype(jnp.bfloat16).reshape(2 * rows, width)
             outgoing = times(place[layer].reshape(2 * rows, slot_count), back_rows, 0, 0).astype(jnp.bfloat16)
+            outgoing, returned, head_sum, key_far[layer] = tie(outgoing, returned, sources[0], key_far[layer])
+            sources = [lax.all_gather(merge(head_sum, sources[1]), "ctx", axis=0)]
             arrived_grad = all_to_all(outgoing.reshape(experts, capacity, width)).reshape(slot_count, width)
+            state = saved[last]["middle"] + sum(
+                saved[last]["gates"][i] * times(place[last, i], returned, 1, 0) for i in range(2)
+            )
+            block_output = state.astype(jnp.bfloat16)[None]
             back, grad_gate, grad_up = expert_backward(arrived_grad, *pieces, k["gate_values"], k["up_values"])
+            back, *last_parts[2:4] = tie(back, *last_parts[2:4])
             back = all_to_all(back.reshape(experts, capacity, width)).reshape(slot_count, width)
-            signal = jnp.stack([jnp.sum(upstream * r, axis=-1, keepdims=True) for r in k["results"]])
-        pair_give, pair_own, pair_far, down_give, down_kept, down_far_part = expert_grads(
+            results = k["results"]
+        pair_give, far_give, pair_own, pair_far, down_give, down_kept, down_far_part = expert_grads(
             arrived, arrived_grad, inner, grad_gate, grad_up
         )
-        pair_near, down_near = swap(pair_give, 1), swap(down_give, 1)
+        pair_near, far_near, down_near = swap(pair_give, 1), swap(far_give, 1), swap(down_give, 1)
         add = lambda a, b: (a.astype(jnp.float32) + b.astype(jnp.float32)).astype(jnp.bfloat16)
-        pair_last = swap(add(pair_far, pair_near[2:]), 2)
-        down_last = swap(add(down_far_part, down_near[1:]), 2)
-        grad_mixed = times(both, back, 1, 0)
-        grad_picked = (signal - jnp.sum(gates * signal, axis=0, keepdims=True)) / k["pair_total"][None]
-        grad_probs = jnp.sum(grad_picked * named[layer], axis=0)
-        grad_logits = k["probs"] * (grad_probs - jnp.sum(k["probs"] * grad_probs, axis=1, keepdims=True))
-        router_part = lax.dot_general(
-            grad_logits,
-            k["mixed"].astype(jnp.float32),
-            (((0,), (0,)), ((), ())),
-            precision=lax.Precision.HIGHEST,
-            preferred_element_type=jnp.float32,
-        )
-        grad_mixed = grad_mixed + lax.dot_general(
-            grad_logits,
-            k["router"].astype(jnp.float32),
-            (((1,), (0,)), ((), ())),
-            precision=lax.Precision.HIGHEST,
-            preferred_element_type=jnp.float32,
-        )
-        pulled, gain_two_rows = rms_back(k["middle"], k["gain_two"], grad_mixed)
-        grad_middle = upstream + pulled
+        pair_sums = [add(pair_far[i], far_near[i]) for i in range(2)]
+        down_sum = add(down_far_part, down_near[1:])
         if layer == last:
-            grad_middle, project_far[0] = tie(grad_middle, project_far[0])
-        middle_low = grad_middle.astype(jnp.bfloat16)
-        grad_attended = jnp.zeros((4, part, rows), jnp.bfloat16)
-        for m in range(4):
-            grad_attended = lax.dynamic_update_index_in_dim(
-                grad_attended, times(k["out_pieces"][m], middle_low, 1, 1).astype(jnp.bfloat16), wt ^ m, 0
-            )
+            back, key_far[layer] = tie(back, key_far[layer])
+        else:
+            back, last_parts[6] = tie(back, last_parts[6])
+            pair_done, down_done = last_finish(*last_parts)
+            expert_done = [*pair_done, *down_done]
+        pair_last = [swap(pair_sum, 2) for pair_sum in pair_sums]
         if layer == last:
-            made, back = tie(made, grad_attended)[0], back
-            returned = all_to_all(made.reshape(experts, capacity, width)).reshape(slot_count, width)
-            state = k["middle"] + sum(gates[i] * times(place[layer, i], returned, 1, 0) for i in range(2))
-            block_output = state.astype(jnp.bfloat16)[None]
+            down_last = [swap(down_sum[0], 2)]
+        grad_middle, middle_low, grad_attended, small = middle_back(
+            experts,
+            others,
+            place[layer],
+            back,
+            upstream,
+            k["middle"],
+            k["mixed"],
+            k["gain_two"],
+            k["router"],
+            chosen[layer],
+            results,
+            k["out_pieces"],
+        )
         grad_heads = all_to_all(grad_attended.reshape(n_ctx, wide, rows))
+        if layer == last:
+            grad_heads, *k["attended"] = tie(grad_heads, *k["attended"])
         grad_whole, grad_sent = attend_back(owner_of, k["qkv"], k["exact"], k["log_total"], grad_heads, rep, HEAD)
-        grad_sent, grad_whole, pair_last, down_last = tie(grad_sent, grad_whole, pair_last, down_last)
-        pair_done = finish(layer, layers, pair_own, pair_near, pair_last, expert_done[0])
-        down_done = finish(layer, layers, down_kept, down_near, down_last, expert_done[1])
-        expert_done = [pair_done, down_done]
+        middle_pieces = wt_gather(middle_low)
+        out_part = times(jnp.concatenate(k["attended"], axis=1), jnp.concatenate(middle_pieces, axis=0), 1, 0)
+        out_part = out_part.astype(jnp.bfloat16)
+        if layer == 0:
+            out_rows = all_to_all(out_part.reshape(n_ctx, part // n_ctx, width))
+            grad_sent, out_rows, *expert_done = tie(grad_sent, out_rows, *expert_done)
+        else:
+            grad_sent, query_far[0], out_part = tie(grad_sent, query_far[0], out_part)
+            out_rows = lax.psum_scatter(out_part, "ctx", scatter_dimension=0, tiled=True)
         grad_own = all_to_all(grad_sent)
-        small = jnp.concatenate(
-            [router_part, jnp.sum(gain_two_rows, axis=0)[None], jnp.zeros((15 - experts, width), jnp.float32)]
-        )
+        if layer == 0:
+            grad_whole, *pair_last = tie(grad_whole, *pair_last)
         head_give, head_kept, head_far = head_grads(others, k["normed_all"], grad_whole, small)
         head_near = swap(head_give, 1)
         head_last = swap(add(head_far[0], head_near[1]), 2)
         head_sum = (
             head_kept[0].astype(jnp.float32) + head_near[0].astype(jnp.float32) + head_last.astype(jnp.float32)
         ).astype(jnp.bfloat16)
-        middle_pieces = wt_gather(middle_low)
-        attended_pieces = wt_exchange(k["attended"], wt)
-        out_part = times(jnp.concatenate(attended_pieces, axis=1), jnp.concatenate(middle_pieces, axis=0), 1, 0)
-        out_part = out_part.astype(jnp.bfloat16)
-        weights = (query_weight[layer], key_weight[layer], value_weight[layer])
+        weights = [(query_weight[i], key_weight[i], value_weight[i]) for i in range(layers)]
+        columns = lambda at, *rest: spread(at, layers, *rest[:2], weights[at], wide, HEAD, 16, rest[2])
         if layer == last:
-            out_sum = lax.psum(out_part, "ctx")
-            gathered = lax.all_gather(head_sum, "ctx", axis=0)
-            sources, ring_spots = (gathered, out_sum), None
+            sources = [head_sum, out_rows]
+            last_parts = [pair_own, pair_near, *pair_last, down_kept, down_near, *down_last]
+            last_finish = lambda *p: (finish(last, layers, *p[:2], p[2:4], None), finish(last, layers, *p[4:6], p[6:], None))
+            made = tie(made, grad_own)[0]
+            returned = all_to_all(made.reshape(experts, capacity, width)).reshape(slot_count, width)
         else:
-            out_rows = all_to_all(out_part.reshape(n_ctx, part // n_ctx, width))
+            *head_done, smalls[last], gain_sums[last] = columns(last, None, sources, None)
             out_rows = jnp.sum(out_rows.astype(jnp.float32), axis=0).astype(jnp.bfloat16)
-            merged = jnp.concatenate([head_sum] + [out_rows[:, i * part : (i + 1) * part] for i in range(4)], axis=0)
-            sources, ring_spots = ring_blocks(merged, ring_start(merged, ring), ring), ring_owners
-        *head_done, smalls[layer], gain_sums[layer] = spread(
-            layer, layers, ring_spots, sources, weights, wide, HEAD, 16, head_done
-        )
-        own = jnp.concatenate(
+            merged = merge(head_sum, out_rows)
+            merged, *head_done = tie(merged, *head_done)
+            down_last = [swap(tie(down_sum, head_last)[0][0], 2)]
+            sources, down_last = ring_blocks(merged, ring_start(merged, ring), ring, down_last)
+            pair_done = finish(layer, layers, pair_own, pair_near, pair_last, expert_done[:2])
+            down_done = finish(layer, layers, down_kept, down_near, down_last, expert_done[2:])
+            expert_done = [*pair_done, *down_done]
+            sources[-1], *expert_done = tie(sources[-1], *expert_done)
+            *head_done, smalls[layer], gain_sums[layer] = columns(layer, ring_owners, sources, head_done)
+        own_query = grad_own[:, :wide].reshape(width, rows)
+        own_pair = jnp.concatenate(
             [
-                grad_own[:, :wide].reshape(width, rows),
                 grad_own[:, wide : wide + HEAD].reshape(n_ctx * HEAD, rows),
                 grad_own[:, wide + HEAD :].reshape(n_ctx * HEAD, rows),
             ],
             axis=0,
         )
-        project = near_finish(project_far[layer], project_own[layer])
+        query_pieces = near_finish(query_far[layer], query_own[layer])
+        key_pieces = near_finish(key_far[layer], pair_own_weights[layer])
         grad_normed = jnp.zeros((rows, width), jnp.float32)
         for m in range(4):
             grad_normed = lax.dynamic_update_slice_in_dim(
-                grad_normed, times(own, project[m], 0, 1), (wt ^ m) * part, 1
+                grad_normed,
+                times(own_query, query_pieces[m], 0, 1) + times(own_pair, key_pieces[m], 0, 1),
+                (wt ^ m) * part,
+                1,
             )
         pulled, _ = rms_back(k["state"], k["gain_one"], grad_normed)
         upstream = grad_middle + pulled
     gain_one_grad = jnp.stack([s[:, 0] for s in gain_sums]) / attention_gain.astype(jnp.float32)
-    small_all = jnp.stack(smalls)
+    small_grads = jnp.stack(smalls)
     query_grad, key_grad, value_grad, out_grad = head_done
     return (
         block_output,
@@ -870,10 +1015,9 @@
         key_grad,
         value_grad,
         out_grad,
-        small_all[:, experts],
-        small_all[:, :experts].transpose(0, 2, 1),
-        *expert_done[0],
-        *expert_done[1],
+        small_grads[:, experts],
+        small_grads[:, :experts].transpose(0, 2, 1),
+        *expert_done,
     )
 
 

time: 794 us -> 754 us (0.950)
  matrix products: 74.7 us -> 34.7 us
  Pallas kernels: 129 us -> 158 us
  waiting for transfers between devices: 317 us -> 294 us
    all_to_all x15, waiting for transfers between devices: 178 us -> 78.1 us  [all_to_all(): return lax.all_to_all(x, 'ctx', split_axis=0, concat_axis=0, tiled=True)]
    ppermute x55 -> x65, waiting for transfers between devices: 93.7 us -> 145 us  [swap(): return lax.ppermute(x, 'wt', [(i, i ^ mask) for i in range(4)])]
    dot_general x40 -> x26, matrix products: 68.9 us -> 34.5 us  [times(): lax.dot_general(left, right, (((a,), (b,)), ((), ())), preferred_element_...]
    pallas_call x2 -> x7, Pallas kernels: 21.3 us -> 51.2 us  [the longest x2 22.8 us: front(): pl.pallas_call(functools.partial(front_kernel, raw, rep, head, span, base...]
    reduce_scatter x0 -> x1, waiting for transfers between devices: none -> 23 us  [local_heads(): lax.psum_scatter(out_part, 'ctx', scatter_dimension=0, tiled=True)]
    unnamed x349 -> x273, local copies, waits for them, and re-layouts: 13.2 us -> 19.6 us
    ppermute x55 -> x65, starting transfers between devices: 32.9 us -> 38.5 us  [swap(): return lax.ppermute(x, 'wt', [(i, i ^ mask) for i in range(4)])]
  transfers between devices with their start and end apart: 96 -> 106, of which waited for: 41 -> 45; matrix products, arithmetic and copies ran while one was open for 20% -> 15% of each run, Pallas kernels for 13% -> 17%
where the time goes in v3:
time: 754 us; the launch traced here: 743 us
  waiting for transfers between devices  294 us (39%)
  Pallas kernels  158 us (21%)
  starting transfers between devices  146 us (19%)
  local copies, waits for them, and re-layouts  52.3 us (7%)
  other arithmetic  40.7 us (5%)
  matrix products  34.7 us (5%)
  between operations  16.4 us (2%)
    ppermute x65, waiting for transfers between devices, swap(): return lax.ppermute(x, 'wt', [(i, i ^ mask) for i in range(4)])  145 us
    all_to_all x15, waiting for transfers between devices, all_to_all(): return lax.all_to_all(x, 'ctx', split_axis=0, concat_axis=0, tiled=True)  78.1 us
    all_to_all x15, starting transfers between devices, all_to_all(): return lax.all_to_all(x, 'ctx', split_axis=0, concat_axis=0, tiled=True)  74.7 us
    ppermute x65, starting transfers between devices, swap(): return lax.ppermute(x, 'wt', [(i, i ^ mask) for i in range(4)])  38.5 us
    dot_general x26, matrix products, times(): lax.dot_general(left, right, (((a,), (b,)), ((), ())), preferred_element_...  34.5 us
    reduce_scatter x1, waiting for transfers between devices, local_heads(): lax.psum_scatter(out_part, 'ctx', scatter_dimension=0, tiled=True)  23 us
    pallas_call x2, Pallas kernels, front(): pl.pallas_call(functools.partial(front_kernel, raw, rep, head, span, base...  22.8 us
    ppermute x6, waiting for transfers between devices, ring_blocks(): lax.ppermute(ahead, 'ctx', right)  21.8 us
  transfers between devices with their start and end apart: 106, of which 45 were waited for; matrix products, arithmetic and copies ran while one was open for 15% of the time, Pallas kernels for 17%

profile of v3, /device:TPU:0, one launch (start us, length us, event | category | flops | bytes accessed | tf_op | source)
XLA Modules:
  0.0 742.6 jit_solution(13861214944759319776)
XLA Ops:
  7.2 3.1 collective-permute-start
  22.5 7.5 %collective-permute-done.7.refs_12_ = bf16[672,384]{1,0:T(8,128)(2,1)} collective-permute-done((bf16[672,384]{1,0:T(8,128)(2,1)}, bf16[672,384]{1,0:T(8,128)(2,1)}, u32[]{:S(2)}, u32[]{:S(2)}) %collective-permute-start.7) | collective-permute-done | bytes 516128 | tf_op jit(solution)/shard_map/ppermute | solution.py:643
  34.0 8.7 %collective-permute-done.4.refs_5_ = bf16[128,1536]{1,0:T(8,128)(2,1)S(1)} collective-permute-done((bf16[128,1536]{1,0:T(8,128)(2,1)}, bf16[128,1536]{1,0:T(8,128)(2,1)S(1)}, u32[]{:S(2)}, u32[]{:S(2)}) %collective-permute-start.4) | collective-permute-done | bytes 393248 | tf_op jit(solution)/shard_map/ppermute | solution.py:697
  51.8 4.3 all-to-all-start
  65.5 12.0 %front.2 = (bf16[8,128,1536]{2,1,0:T(8,128)(2,1)}, bf16[320,1024]{1,0:T(8,128)(2,1)}, bf16[8,192,128]{2,1,0:T(8,128)(2,1)}, f32[192,1024]{1,0:T(8,128)}, f32[3,1024]{1,0:T(4,128)}) custom-call(s32[8]{0:T(128)} %get-tuple-element.301.spot_ref, s32[8]{0:T(128)} %get-tuple-element.300.owner_ref, s32[4]{0:T(128)} %xor_convert_fusion.at_ref, ...), custom_call_target="tpu_custom_call" | custom-call | flops 1509949440 | bytes 9437184 | tf_op jit(solution)/shard_map/front/pallas_call | solution.py:130
  77.5 8.1 %all-to-all-done = bf16[8,48,1664]{2,1,0:T(8,128)(2,1)} async-done(((bf16[8,48,1664]{2,1,0:T(8,128)(2,1)}), bf16[8,48,1664]{2,1,0:T(8,128)(2,1)}, u32[]{:S(2)}, u32[]{:S(2)}) %all-to-all-start) | async-done | bytes 1277984 | tf_op jit(solution)/shard_map/all_to_all | solution.py:707
  85.6 3.7 all-to-all-start.1
  93.3 7.8 %all-to-all-done.1 = bf16[8,192,128]{2,1,0:T(8,128)(2,1)S(1)} async-done(((bf16[8,192,128]{2,1,0:T(8,128)(2,1)}), bf16[8,192,128]{2,1,0:T(8,128)(2,1)S(1)}, u32[]{:S(2)}, u32[]{:S(2)}) %all-to-all-start.1) | async-done | bytes 393248 | tf_op jit(solution)/shard_map/all_to_all | solution.py:707
  108.9 5.4 middle_forward.2
  114.3 4.3 all-to-all-start.2
  122.6 6.5 collective-permute-done.18.refs_7_.refs_9_
  129.1 16.3 %collective-permute-done.19.refs_8_.refs_10_ = bf16[256,1536]{1,0:T(8,128)(2,1)S(1)} collective-permute-done((bf16[256,1536]{1,0:T(8,128)(2,1)S(1)}, bf16[256,1536]{1,0:T(8,128)(2,1)S(1)}, u32[]{:S(2)}, u32[]{:S(2)}) %collective-permute-start.19) | collective-permute-done | bytes 786464 | tf_op jit(solution)/shard_map/ppermute | solution.py:643
  149.9 10.1 %expert_forward.1 = (bf16[384,1536]{1,0:T(8,128)(2,1)}, f32[4,384,256]{2,1,0:T(8,128)}, f32[4,384,256]{2,1,0:T(8,128)}, bf16[4,384,256]{2,1,0:T(8,128)(2,1)}) custom-call(bf16[384,1536]{1,0:T(8,128)(2,1)} %bitcast.30.rows_ref, bf16[1536,256]{1,0:T(8,128)(2,1)} %copy-done.22, bf16[1536,256]{1,0:T(8,128)(2,1)} %get-tuple-element.327.refs_1_.refs_3_, ...), custom_call_target="tpu_custom_call" | custom-call | flops 3623878656 | bytes 16777216 | tf_op jit(solution)/shard_map/expert_forward/pallas_call | solution.py:251
  160.1 6.1 all-to-all-start.3
  170.0 15.9 %collective-permute-done.23.refs_6_ = bf16[1536,256]{1,0:T(8,128)(2,1)} collective-permute-done((bf16[1536,256]{1,0:T(8,128)(2,1)}, bf16[1536,256]{1,0:T(8,128)(2,1)}, u32[]{:S(2)}, u32[]{:S(2)}) %collective-permute-start.23) | collective-permute-done | bytes 786464 | tf_op jit(solution)/shard_map/ppermute | solution.py:643
  185.9 9.3 %all-to-all-done.3 = bf16[8,48,1536]{2,1,0:T(8,128)(2,1)S(1)} async-done(((bf16[8,48,1536]{2,1,0:T(8,128)(2,1)}), bf16[8,48,1536]{2,1,0:T(8,128)(2,1)S(1)}, u32[]{:S(2)}, u32[]{:S(2)}) %all-to-all-start.3) | async-done | bytes 1179680 | tf_op jit(solution)/shard_map/all_to_all | solution.py:707
  201.7 6.5 collective-permute-done.24.refs_1_
  211.8 5.8 collective-permute-done.26.refs_3_
  219.7 6.2 collective-permute-done.28.refs_5_
  235.0 10.8 %front.3 = (bf16[8,128,1536]{2,1,0:T(8,128)(2,1)}, bf16[320,1024]{1,0:T(8,128)(2,1)}, bf16[8,192,128]{2,1,0:T(8,128)(2,1)}, f32[192,1024]{1,0:T(8,128)}, f32[3,1024]{1,0:T(4,128)}) custom-call(s32[8]{0:T(128)} %get-tuple-element.301.spot_ref, s32[8]{0:T(128)} %get-tuple-element.300.owner_ref, s32[4]{0:T(128)} %xor_convert_fusion.at_ref, ...), custom_call_target="tpu_custom_call" | custom-call | flops 1509949440 | bytes 9437184 | tf_op jit(solution)/shard_map/front/pallas_call | solution.py:130
  248.9 6.1 all-to-all-start.4
  257.9 8.8 %all-to-all-done.4 = bf16[8,192,128]{2,1,0:T(8,128)(2,1)S(1)} async-done(((bf16[8,192,128]{2,1,0:T(8,128)(2,1)}), bf16[8,192,128]{2,1,0:T(8,128)(2,1)S(1)}, u32[]{:S(2)}, u32[]{:S(2)}) %all-to-all-start.4) | async-done | bytes 393248 | tf_op jit(solution)/shard_map/all_to_all | solution.py:707
  267.4 5.4 middle_forward.3
  272.8 4.6 all-to-all-start.5
  284.1 22.4 %collective-permute-done.39 = bf16[384,1536]{1,0:T(8,128)(2,1)} collective-permute-done((bf16[384,1536]{1,0:T(8,128)(2,1)}, bf16[384,1536]{1,0:T(8,128)(2,1)}, u32[]{:S(2)}, u32[]{:S(2)}) %collective-permute-start.39) | collective-permute-done | bytes 1179680 | tf_op jit(solution)/shard_map/ppermute | solution.py:643
  309.1 14.5 %expert_both.1 = (bf16[384,1536]{1,0:T(8,128)(2,1)}, bf16[384,1664]{1,0:T(8,128)(2,1)}, bf16[384,1536]{1,0:T(8,128)(2,1)}, bf16[4,384,256]{2,1,0:T(8,128)(2,1)},...) custom-call(s32[1]{0:T(128)} %bitcast.3.at_ref.mine_ref, bf16[384,1536]{1,0:T(8,128)(2,1)} %bitcast.279, ...), custom_call_target="tpu_custom_call" | custom-call | flops 7247757312 | bytes 18874368 | tf_op jit(solution)/shard_map/expert_both/pallas_call | solution.py:350
  323.7 5.7 all-to-all-start.6
  337.0 14.6 %collective-permute-done.46 = bf16[384,1024]{1,0:T(8,128)(2,1)} collective-permute-done((bf16[384,1024]{1,0:T(8,128)(2,1)S(1)}, bf16[384,1024]{1,0:T(8,128)(2,1)}, u32[]{:S(2)}, u32[]{:S(2)}) %collective-permute-start.46) | collective-permute-done | bytes 786464 | tf_op jit(solution)/shard_map/ppermute | solution.py:643
  351.6 9.1 %all-to-all-done.6 = bf16[8,48,1664]{2,1,0:T(8,128)(2,1)} async-done(((bf16[8,48,1664]{2,1,0:T(8,128)(2,1)}), bf16[8,48,1664]{2,1,0:T(8,128)(2,1)}, u32[]{:S(2)}, u32[]{:S(2)}) %all-to-all-start.6) | async-done | bytes 1277984 | tf_op jit(solution)/shard_map/all_to_all | solution.py:707
  360.7 7.6 %middle_back.2 = (f32[128,1536]{1,0:T(8,128)}, bf16[128,1536]{1,0:T(8,128)(2,1)}, bf16[1536,128]{1,0:T(8,128)(2,1)}, f32[16,1536]{1,0:T(8,128)}) custom-call(s32[4]{0:T(128)} %xor_convert_fusion.at_ref, bf16[2,128,384]{2,1,0:T(8,128)(2,1)} %get-tuple-element.348.place_ref, bf16[384,1664]{1,0:T(8,128)(2,1)} %bitcast.58.back_ref, ...), custom_call_target="tpu_custom_call" | custom-call | flops 754974720 | bytes 10485760 | tf_op jit(solution)/shard_map/middle_back/pallas_call | solution.py:626
  368.2 3.9 all-to-all-start.7
  373.7 7.4 collective-permute-done.47
  384.2 4.4 collective-permute-done.51
  390.6 8.7 %attend_back.2 = (bf16[320,1024]{1,0:T(8,128)(2,1)}, bf16[8,320,128]{2,1,0:T(8,128)(2,1)}) custom-call(s32[8]{0:T(128)} %get-tuple-element.300.owner_ref, bf16[320,1024]{1,0:T(8,128)(2,1)} %get-tuple-element.189.qkv_ref, f32[192,1024]{1,0:T(8,128)} %get-tuple-element.190.exact_ref, f32[3,1024]{1,0:T(4,128)} %get-tuple-element.191.log_ref, ...), custom_call_target="tpu_custom_call" | custom-call | flops 1258291200 | bytes 6291456 | tf_op jit(solution)/shard_map/attend_back/pallas_call | solution.py:195
  399.3 4.5 head_grads.2
  407.5 5.9 all-to-all-start.8
  417.8 9.3 %expert_grads.2 = (bf16[2,1536,256]{2,1,0:T(8,128)(2,1)}, bf16[2,1536,256]{2,1,0:T(8,128)(2,1)}, bf16[2,1536,256]{2,1,0:T(8,128)(2,1)}, bf16[2,1536,256]{2,1,0:T...) custom-call(bf16[384,1536]{1,0:T(8,128)(2,1)} %bitcast.280, ...), custom_call_target="tpu_custom_call" | custom-call | flops 3623878656 | bytes 14680064 | tf_op jit(solution)/shard_map/expert_grads/pallas_call | solution.py:388
  427.1 12.5 %collective-permute-done.58 = bf16[336,384]{1,0:T(8,128)(2,1)S(1)} collective-permute-done((bf16[336,384]{1,0:T(8,128)(2,1)S(1)}, bf16[336,384]{1,0:T(8,128)(2,1)S(1)}, u32[]{:S(2)}, u32[]{:S(2)}) %collective-permute-start.58) | collective-permute-done | bytes 258080 | tf_op jit(solution)/shard_map/ppermute | solution.py:643
  441.3 5.7 all-to-all-start.9
  463.5 16.2 %all-to-all-done.9 = bf16[8,48,1536]{2,1,0:T(8,128)(2,1)S(1)} async-done(((bf16[8,48,1536]{2,1,0:T(8,128)(2,1)}), bf16[8,48,1536]{2,1,0:T(8,128)(2,1)S(1)}, u32[]{:S(2)}, u32[]{:S(2)}) %all-to-all-start.9) | async-done | bytes 1179680 | tf_op jit(solution)/shard_map/all_to_all | solution.py:707
  479.7 4.7 all-to-all-start.10
  484.5 3.4 fusion.29
  490.7 23.0 %reduce-scatter.2.cloned.1.call-done = bf16[48,1536]{1,0:T(8,128)(2,1)} async-done(((bf16[384,1536]{1,0:T(8,128)(2,1)}), bf16[48,1536]{1,0:T(8,128)(2,1)}) %reduce-scatter.2.cloned.1.call-update) | async-done | bytes 147472 | tf_op jit(solution)/shard_map/reduce_scatter | solution.py:957
  518.0 12.4 %expert_backward.1 = (bf16[384,1536]{1,0:T(8,128)(2,1)}, bf16[4,384,256]{2,1,0:T(8,128)(2,1)}, bf16[4,384,256]{2,1,0:T(8,128)(2,1)}) custom-call(bf16[384,1536]{1,0:T(8,128)(2,1)} %bitcast.82.grad_ref, f32[4,384,256]{2,1,0:T(8,128)} %get-tuple-element.213.refs_0_, f32[4,384,256]{2,1,0:T(8,128)} %get-tuple-element.214.refs_1_, bf16[1536,256]{1,0:T(8,128)(2,1)} %copy-done.22, ...), custom_call_target="tpu_custom_call" | custom-call | flops 3623878656 | bytes 16777216 | tf_op jit(solution)/shard_map/expert_backward/pallas_call | solution.py:289
  530.3 4.3 all-to-all-start.11
  536.3 9.3 %expert_grads.3 = (bf16[2,1536,256]{2,1,0:T(8,128)(2,1)}, bf16[2,1536,256]{2,1,0:T(8,128)(2,1)}, bf16[2,1536,256]{2,1,0:T(8,128)(2,1)}, bf16[2,1536,256]{2,1,0:T...) custom-call(bf16[384,1536]{1,0:T(8,128)(2,1)} %bitcast.30.rows_ref, ...), custom_call_target="tpu_custom_call" | custom-call | flops 3623878656 | bytes 14680064 | tf_op jit(solution)/shard_map/expert_grads/pallas_call | solution.py:388
  551.6 16.5 %collective-permute-done.64.refs_2_ = bf16[256,1536]{1,0:T(8,128)(2,1)} collective-permute-done((bf16[256,1536]{1,0:T(8,128)(2,1)}, bf16[256,1536]{1,0:T(8,128)(2,1)}, u32[]{:S(2)}, u32[]{:S(2)}) %collective-permute-start.64) | collective-permute-done | bytes 786464 | tf_op jit(solution)/shard_map/ppermute | solution.py:643
  568.1 7.9 %all-to-all-done.11 = bf16[8,48,1536]{2,1,0:T(8,128)(2,1)} async-done(((bf16[8,48,1536]{2,1,0:T(8,128)(2,1)}), bf16[8,48,1536]{2,1,0:T(8,128)(2,1)}, u32[]{:S(2)}, u32[]{:S(2)}) %all-to-all-start.11) | async-done | bytes 1179680 | tf_op jit(solution)/shard_map/all_to_all | solution.py:707
  576.0 7.9 %middle_back.3 = (f32[128,1536]{1,0:T(8,128)}, bf16[128,1536]{1,0:T(8,128)(2,1)}, bf16[1536,128]{1,0:T(8,128)(2,1)}, f32[16,1536]{1,0:T(8,128)}) custom-call(s32[4]{0:T(128)} %xor_convert_fusion.at_ref, bf16[2,128,384]{2,1,0:T(8,128)(2,1)} %get-tuple-element.349.place_ref, bf16[384,1536]{1,0:T(8,128)(2,1)} %bitcast.86.back_ref, f32[128,1536]{1,0:T(8,128)} %copy-done.5, ...), custom_call_target="tpu_custom_call" | custom-call | flops 754974720 | bytes 10485760 | tf_op jit(solution)/shard_map/middle_back/pallas_call | solution.py:626
  586.7 4.1 all-to-all-start.12
  592.1 3.4 fusion.32
  601.9 10.8 %all-to-all-done.12.grad_ref = bf16[8,192,128]{2,1,0:T(8,128)(2,1)} async-done(((bf16[8,192,128]{2,1,0:T(8,128)(2,1)}), bf16[8,192,128]{2,1,0:T(8,128)(2,1)}, u32[]{:S(2)}, u32[]{:S(2)}) %all-to-all-start.12) | async-done | bytes 393248 | tf_op jit(solution)/shard_map/all_to_all | solution.py:707
  612.7 5.2 all-to-all-start.13
  618.6 8.7 %attend_back.3 = (bf16[320,1024]{1,0:T(8,128)(2,1)}, bf16[8,320,128]{2,1,0:T(8,128)(2,1)}) custom-call(s32[8]{0:T(128)} %get-tuple-element.300.owner_ref, bf16[320,1024]{1,0:T(8,128)(2,1)} %get-tuple-element.227.qkv_ref, f32[192,1024]{1,0:T(8,128)} %get-tuple-element.228.exact_ref, f32[3,1024]{1,0:T(4,128)} %get-tuple-element.229.log_ref, ...), custom_call_target="tpu_custom_call" | custom-call | flops 1258291200 | bytes 6291456 | tf_op jit(solution)/shard_map/attend_back/pallas_call | solution.py:195
  627.3 5.3 collective-permute-done.75.refs_3_
  632.6 4.5 head_grads.3
  644.6 3.6 finish.4
  651.0 6.0 spread.2
  657.0 6.2 all-to-all-start.14
  674.0 3.7 finish.6
  677.7 4.9 collective-permute-done.78.refs_2_
  682.6 5.0 collective-permute-start.80
  706.8 7.1 collective-permute-done.85.refs_2_
  724.7 6.4 spread.3
  (582 shorter events, 216.5 us)
Async XLA Ops:
  15.3 18.6 %collective-permute-start.6 = (bf16[672,384]{1,0:T(8,128)(2,1)}, bf16[672,384]{1,0:T(8,128)(2,1)S(1)}, u32[]{:S(2)}, u32[]{:S(2)}) collective-permute-start(bf16[672,384]{1,0:T(8,128)(2,1)} %bitcast.287), channel_id=1, source_target_pairs={{0,1},{1,0},{2,3},{3,2},{4,5},{5,4},{6,7},{7,6},{8,9},{9,8},{10,11... | collective-permute-start | bytes 1548296 | tf_op jit(solution)/shard_map/ppermute | solution.py:643
  51.8 33.8 %all-to-all-start = ((bf16[8,48,1664]{2,1,0:T(8,128)(2,1)}), bf16[8,48,1664]{2,1,0:T(8,128)(2,1)}, u32[]{:S(2)}, u32[]{:S(2)}) async-start(bf16[8,48,1664]{2,1,0:T(8,128)(2,1)} %bitcast.17), calls=%async_computation | async-start | bytes 2555904 | tf_op jit(solution)/shard_map/all_to_all | solution.py:707
  58.0 35.3 %collective-permute-start.11 = (bf16[384,1536]{1,0:T(8,128)(2,1)S(1)}, bf16[384,1536]{1,0:T(8,128)(2,1)}, u32[]{:S(2)}, u32[]{:S(2)}) collective-permute-start(bf16[384,1536]{1,0:T(8,128)(2,1)S(1)} %get-tuple-element.315.refs_0_.refs_2_), channel_id=1, source_target_pairs={{0,2},{1,3},{2,0},{3,1},{4,6},{5,7},{6,4},{7,5},{8,10},{9,11},{10,... | collective-permute-start | bytes 3538952 | tf_op jit(solution)/shard_map/ppermute | solution.py:643
  89.3 18.6 %collective-permute-start.12 = (bf16[384,1536]{1,0:T(8,128)(2,1)S(1)}, bf16[384,1536]{1,0:T(8,128)(2,1)}, u32[]{:S(2)}, u32[]{:S(2)}) collective-permute-start(bf16[384,1536]{1,0:T(8,128)(2,1)S(1)} %get-tuple-element.315.refs_0_.refs_2_), channel_id=1, source_target_pairs={{0,1},{1,0},{2,3},{3,2},{4,5},{5,4},{6,7},{7,6},{8,9},{9,8},{10,11... | collective-permute-start | bytes 3538952 | tf_op jit(solution)/shard_map/ppermute | solution.py:643
  91.8 22.5 %collective-permute-start.14 = (bf16[1536,256]{1,0:T(8,128)(2,1)S(1)}, bf16[1536,256]{1,0:T(8,128)(2,1)}, u32[]{:S(2)}, u32[]{:S(2)}) collective-permute-start(bf16[1536,256]{1,0:T(8,128)(2,1)S(1)} %get-tuple-element.329.refs_0_.refs_2_), channel_id=1, source_target_pairs={{0,2},{1,3},{2,0},{3,1},{4,6},{5,7},{6,4},{7,5},{8,10},{9,11},{10,... | collective-permute-start | bytes 2359304 | tf_op jit(solution)/shard_map/ppermute | solution.py:643
  104.0 25.1 %collective-permute-start.18 = (bf16[1536,256]{1,0:T(8,128)(2,1)}, bf16[1536,256]{1,0:T(8,128)(2,1)}, u32[]{:S(2)}, u32[]{:S(2)}) collective-permute-start(bf16[1536,256]{1,0:T(8,128)(2,1)} %get-tuple-element.327.refs_1_.refs_3_), channel_id=1, source_target_pairs={{0,2},{1,3},{2,0},{3,1},{4,6},{5,7},{6,4},{7,5},{8,10},{9,11},{10,... | collective-permute-start | bytes 2359304 | tf_op jit(solution)/shard_map/ppermute | solution.py:643
  114.3 34.8 %all-to-all-start.2 = ((bf16[8,48,1536]{2,1,0:T(8,128)(2,1)}), bf16[8,48,1536]{2,1,0:T(8,128)(2,1)}, u32[]{:S(2)}, u32[]{:S(2)}) async-start(bf16[8,48,1536]{2,1,0:T(8,128)(2,1)} %bitcast.283), calls=%async_computation.2 | async-start | bytes 2359296 | tf_op jit(solution)/shard_map/all_to_all | solution.py:707
  120.9 24.5 %collective-permute-start.19 = (bf16[256,1536]{1,0:T(8,128)(2,1)S(1)}, bf16[256,1536]{1,0:T(8,128)(2,1)S(1)}, u32[]{:S(2)}, u32[]{:S(2)}) collective-permute-start(bf16[256,1536]{1,0:T(8,128)(2,1)S(1)} %get-tuple-element.325.refs_2_.refs_4_), channel_id=1, source_target_pairs={{0,2},{1,3},{2,0},{3,1},{4,6},{5,7},{6,4},{7,5},{8,10},{9,11},{10,... | collective-permute-start | bytes 2359304 | tf_op jit(solution)/shard_map/ppermute | solution.py:643
  122.1 23.4 %collective-permute-start.15 = (bf16[1536,256]{1,0:T(8,128)(2,1)S(1)}, bf16[1536,256]{1,0:T(8,128)(2,1)S(1)}, u32[]{:S(2)}, u32[]{:S(2)}) collective-permute-start(bf16[1536,256]{1,0:T(8,128)(2,1)S(1)} %get-tuple-element.329.refs_0_.refs_2_), channel_id=1, source_target_pairs={{0,1},{1,0},{2,3},{3,2},{4,5},{5,4},{6,7},{7,6},{8,9},{9,8},{10,11... | collective-permute-start | bytes 2359304 | tf_op jit(solution)/shard_map/ppermute | solution.py:643
  122.1 23.9 %collective-permute-start.16 = (bf16[1536,256]{1,0:T(8,128)(2,1)}, bf16[1536,256]{1,0:T(8,128)(2,1)S(1)}, u32[]{:S(2)}, u32[]{:S(2)}) collective-permute-start(bf16[1536,256]{1,0:T(8,128)(2,1)} %get-tuple-element.327.refs_1_.refs_3_), channel_id=1, source_target_pairs={{0,1},{1,0},{2,3},{3,2},{4,5},{5,4},{6,7},{7,6},{8,9},{9,8},{10,11... | collective-permute-start | bytes 2359304 | tf_op jit(solution)/shard_map/ppermute | solution.py:643
  122.6 23.4 %collective-permute-start.17 = (bf16[256,1536]{1,0:T(8,128)(2,1)S(1)}, bf16[256,1536]{1,0:T(8,128)(2,1)S(1)}, u32[]{:S(2)}, u32[]{:S(2)}) collective-permute-start(bf16[256,1536]{1,0:T(8,128)(2,1)S(1)} %get-tuple-element.325.refs_2_.refs_4_), channel_id=1, source_target_pairs={{0,1},{1,0},{2,3},{3,2},{4,5},{5,4},{6,7},{7,6},{8,9},{9,8},{10,11... | collective-permute-start | bytes 2359304 | tf_op jit(solution)/shard_map/ppermute | solution.py:643
  129.1 17.3 %collective-permute-start.21 = (bf16[1536,256]{1,0:T(8,128)(2,1)}, bf16[1536,256]{1,0:T(8,128)(2,1)S(1)}, u32[]{:S(2)}, u32[]{:S(2)}) collective-permute-start(bf16[1536,256]{1,0:T(8,128)(2,1)} %collective-permute-done.18.refs_7_.refs_9_), channel_id=1, source_target_pairs={{0,1},{1,0},{2,3},{3,2},{4,5},{5,4},{6,7},{7,6},{8,9},{9,8},{10,11... | collective-permute-start | bytes 2359304 | tf_op jit(solution)/shard_map/ppermute | solution.py:643
  160.1 35.0 %all-to-all-start.3 = ((bf16[8,48,1536]{2,1,0:T(8,128)(2,1)}), bf16[8,48,1536]{2,1,0:T(8,128)(2,1)S(1)}, u32[]{:S(2)}, u32[]{:S(2)}) async-start(bf16[8,48,1536]{2,1,0:T(8,128)(2,1)} %bitcast.285), calls=%async_computation.3 | async-start | bytes 2359296 | tf_op jit(solution)/shard_map/all_to_all | solution.py:707
  166.2 19.6 %collective-permute-start.23 = (bf16[1536,256]{1,0:T(8,128)(2,1)}, bf16[1536,256]{1,0:T(8,128)(2,1)}, u32[]{:S(2)}, u32[]{:S(2)}) collective-permute-start(bf16[1536,256]{1,0:T(8,128)(2,1)} %get-tuple-element.328.refs_0_), channel_id=1, source_target_pairs={{0,2},{1,3},{2,0},{3,1},{4,6},{5,7},{6,4},{7,5},{8,10},{9,11},{10,... | collective-permute-start | bytes 2359304 | tf_op jit(solution)/shard_map/ppermute | solution.py:643
  200.3 45.6 %collective-permute-start.32 = (bf16[384,1536]{1,0:T(8,128)(2,1)S(1)}, bf16[384,1536]{1,0:T(8,128)(2,1)S(1)}, u32[]{:S(2)}, u32[]{:S(2)}) collective-permute-start(bf16[384,1536]{1,0:T(8,128)(2,1)S(1)} %get-tuple-element.314.refs_0_), channel_id=1, source_target_pairs={{0,2},{1,3},{2,0},{3,1},{4,6},{5,7},{6,4},{7,5},{8,10},{9,11},{10,... | collective-permute-start | bytes 3538952 | tf_op jit(solution)/shard_map/ppermute | solution.py:643
  210.3 35.5 %collective-permute-start.33 = (bf16[1536,256]{1,0:T(8,128)(2,1)}, bf16[1536,256]{1,0:T(8,128)(2,1)}, u32[]{:S(2)}, u32[]{:S(2)}) collective-permute-start(bf16[1536,256]{1,0:T(8,128)(2,1)} %get-tuple-element.326.refs_1_), channel_id=1, source_target_pairs={{0,2},{1,3},{2,0},{3,1},{4,6},{5,7},{6,4},{7,5},{8,10},{9,11},{10,... | collective-permute-start | bytes 2359304 | tf_op jit(solution)/shard_map/ppermute | solution.py:643
  230.4 27.5 %collective-permute-start.34 = (bf16[384,1536]{1,0:T(8,128)(2,1)S(1)}, bf16[384,1536]{1,0:T(8,128)(2,1)}, u32[]{:S(2)}, u32[]{:S(2)}) collective-permute-start(bf16[384,1536]{1,0:T(8,128)(2,1)S(1)} %get-tuple-element.314.refs_0_), channel_id=1, source_target_pairs={{0,1},{1,0},{2,3},{3,2},{4,5},{5,4},{6,7},{7,6},{8,9},{9,8},{10,11... | collective-permute-start | bytes 3538952 | tf_op jit(solution)/shard_map/ppermute | solution.py:643
  245.9 20.8 %collective-permute-start.35 = (bf16[384,1536]{1,0:T(8,128)(2,1)S(1)}, bf16[384,1536]{1,0:T(8,128)(2,1)}, u32[]{:S(2)}, u32[]{:S(2)}) collective-permute-start(bf16[384,1536]{1,0:T(8,128)(2,1)S(1)} %collective-permute-done.32.refs_2_), channel_id=1, source_target_pairs={{0,1},{1,0},{2,3},{3,2},{4,5},{5,4},{6,7},{7,6},{8,9},{9,8},{10,11... | collective-permute-start | bytes 3538952 | tf_op jit(solution)/shard_map/ppermute | solution.py:643
  248.4 24.4 %collective-permute-start.36 = (bf16[256,1536]{1,0:T(8,128)(2,1)}, bf16[256,1536]{1,0:T(8,128)(2,1)}, u32[]{:S(2)}, u32[]{:S(2)}) collective-permute-start(bf16[256,1536]{1,0:T(8,128)(2,1)} %get-tuple-element.324.refs_2_), channel_id=1, source_target_pairs={{0,2},{1,3},{2,0},{3,1},{4,6},{5,7},{6,4},{7,5},{8,10},{9,11},{10,... | collective-permute-start | bytes 2359304 | tf_op jit(solution)/shard_map/ppermute | solution.py:643
  248.9 17.7 %all-to-all-start.4 = ((bf16[8,192,128]{2,1,0:T(8,128)(2,1)}), bf16[8,192,128]{2,1,0:T(8,128)(2,1)S(1)}, u32[]{:S(2)}, u32[]{:S(2)}) async-start(bf16[8,192,128]{2,1,0:T(8,128)(2,1)} %get-tuple-element.175), calls=%async_computation.4 | async-start | bytes 786432 | tf_op jit(solution)/shard_map/all_to_all | solution.py:707
  272.8 35.2 %all-to-all-start.5 = ((bf16[8,48,1536]{2,1,0:T(8,128)(2,1)}), bf16[8,48,1536]{2,1,0:T(8,128)(2,1)S(1)}, u32[]{:S(2)}, u32[]{:S(2)}) async-start(bf16[8,48,1536]{2,1,0:T(8,128)(2,1)} %bitcast.284), calls=%async_computation.5 | async-start | bytes 2359296 | tf_op jit(solution)/shard_map/all_to_all | solution.py:707
  279.1 27.4 %collective-permute-start.39 = (bf16[384,1536]{1,0:T(8,128)(2,1)}, bf16[384,1536]{1,0:T(8,128)(2,1)}, u32[]{:S(2)}, u32[]{:S(2)}) collective-permute-start(bf16[384,1536]{1,0:T(8,128)(2,1)} %get-tuple-element.313.refs_1_), channel_id=1, source_target_pairs={{0,2},{1,3},{2,0},{3,1},{4,6},{5,7},{6,4},{7,5},{8,10},{9,11},{10,... | collective-permute-start | bytes 3538952 | tf_op jit(solution)/shard_map/ppermute | solution.py:643
  280.6 27.4 %collective-permute-start.41 = (bf16[1536,256]{1,0:T(8,128)(2,1)}, bf16[1536,256]{1,0:T(8,128)(2,1)}, u32[]{:S(2)}, u32[]{:S(2)}) collective-permute-start(bf16[1536,256]{1,0:T(8,128)(2,1)} %get-tuple-element.326.refs_1_), channel_id=1, source_target_pairs={{0,1},{1,0},{2,3},{3,2},{4,5},{5,4},{6,7},{7,6},{8,9},{9,8},{10,11... | collective-permute-start | bytes 2359304 | tf_op jit(solution)/shard_map/ppermute | solution.py:643
  281.1 26.9 %collective-permute-start.42 = (bf16[256,1536]{1,0:T(8,128)(2,1)}, bf16[256,1536]{1,0:T(8,128)(2,1)}, u32[]{:S(2)}, u32[]{:S(2)}) collective-permute-start(bf16[256,1536]{1,0:T(8,128)(2,1)} %get-tuple-element.324.refs_2_), channel_id=1, source_target_pairs={{0,1},{1,0},{2,3},{3,2},{4,5},{5,4},{6,7},{7,6},{8,9},{9,8},{10,11... | collective-permute-start | bytes 2359304 | tf_op jit(solution)/shard_map/ppermute | solution.py:643
  281.1 26.9 %collective-permute-start.43 = (bf16[1536,256]{1,0:T(8,128)(2,1)}, bf16[1536,256]{1,0:T(8,128)(2,1)}, u32[]{:S(2)}, u32[]{:S(2)}) collective-permute-start(bf16[1536,256]{1,0:T(8,128)(2,1)} %collective-permute-done.23.refs_6_), channel_id=1, source_target_pairs={{0,1},{1,0},{2,3},{3,2},{4,5},{5,4},{6,7},{7,6},{8,9},{9,8},{10,11... | collective-permute-start | bytes 2359304 | tf_op jit(solution)/shard_map/ppermute | solution.py:643
  283.9 24.0 %collective-permute-start.44 = (bf16[1536,256]{1,0:T(8,128)(2,1)}, bf16[1536,256]{1,0:T(8,128)(2,1)}, u32[]{:S(2)}, u32[]{:S(2)}) collective-permute-start(bf16[1536,256]{1,0:T(8,128)(2,1)} %collective-permute-done.33.refs_7_), channel_id=1, source_target_pairs={{0,1},{1,0},{2,3},{3,2},{4,5},{5,4},{6,7},{7,6},{8,9},{9,8},{10,11... | collective-permute-start | bytes 2359304 | tf_op jit(solution)/shard_map/ppermute | solution.py:643
  323.7 37.0 %all-to-all-start.6 = ((bf16[8,48,1664]{2,1,0:T(8,128)(2,1)}), bf16[8,48,1664]{2,1,0:T(8,128)(2,1)}, u32[]{:S(2)}, u32[]{:S(2)}) async-start(bf16[8,48,1664]{2,1,0:T(8,128)(2,1)} %bitcast.277), calls=%async_computation.6 | async-start | bytes 2555904 | tf_op jit(solution)/shard_map/all_to_all | solution.py:707
  331.0 20.6 %collective-permute-start.46 = (bf16[384,1024]{1,0:T(8,128)(2,1)S(1)}, bf16[384,1024]{1,0:T(8,128)(2,1)}, u32[]{:S(2)}, u32[]{:S(2)}) collective-permute-start(bf16[384,1024]{1,0:T(8,128)(2,1)S(1)} %pad_maximum_fusion.1), channel_id=1, source_target_pairs={{0,2},{1,3},{2,0},{3,1},{4,6},{5,7},{6,4},{7,5},{8,10},{9,11},{10,... | collective-permute-start | bytes 2359304 | tf_op jit(solution)/shard_map/ppermute | solution.py:643
  332.6 74.9 %collective-permute-start.49 = (bf16[384,1536]{1,0:T(8,128)(2,1)}, bf16[384,1536]{1,0:T(8,128)(2,1)}, u32[]{:S(2)}, u32[]{:S(2)}) collective-permute-start(bf16[384,1536]{1,0:T(8,128)(2,1)} %get-tuple-element.312.refs_10_), channel_id=1, source_target_pairs={{0,2},{1,3},{2,0},{3,1},{4,6},{5,7},{6,4},{7,5},{8,10},{9,11},{10,... | collective-permute-start | bytes 3538952 | tf_op jit(solution)/shard_map/ppermute | solution.py:643
  334.5 46.6 %collective-permute-start.47 = (bf16[2,384,128]{2,1,0:T(8,128)(2,1)}, bf16[2,384,128]{2,1,0:T(8,128)(2,1)}, u32[]{:S(2)}, u32[]{:S(2)}) collective-permute-start(bf16[2,384,128]{2,1,0:T(8,128)(2,1)} %pad_maximum_fusion.7), channel_id=1, source_target_pairs={{0,2},{1,3},{2,0},{3,1},{4,6},{5,7},{6,4},{7,5},{8,10},{9,11},{10,... | collective-permute-start | bytes 589832 | tf_op jit(solution)/shard_map/ppermute | solution.py:643
  368.2 21.6 %all-to-all-start.7 = ((bf16[8,192,128]{2,1,0:T(8,128)(2,1)}), bf16[8,192,128]{2,1,0:T(8,128)(2,1)S(1)}, u32[]{:S(2)}, u32[]{:S(2)}) async-start(bf16[8,192,128]{2,1,0:T(8,128)(2,1)} %bitcast.298), calls=%async_computation.7 | async-start | bytes 786432 | tf_op jit(solution)/shard_map/all_to_all | solution.py:707
  372.1 16.5 %collective-permute-start.51 = (bf16[128,1536]{1,0:T(8,128)(2,1)}, bf16[128,1536]{1,0:T(8,128)(2,1)}, u32[]{:S(2)}, u32[]{:S(2)}) collective-permute-start(bf16[128,1536]{1,0:T(8,128)(2,1)} %get-tuple-element.199), channel_id=1, source_target_pairs={{0,2},{1,3},{2,0},{3,1},{4,6},{5,7},{6,4},{7,5},{8,10},{9,11},{10,... | collective-permute-start | bytes 1179656 | tf_op jit(solution)/shard_map/ppermute | solution.py:643
  383.7 20.2 %collective-permute-start.50 = (bf16[128,1536]{1,0:T(8,128)(2,1)}, bf16[128,1536]{1,0:T(8,128)(2,1)}, u32[]{:S(2)}, u32[]{:S(2)}) collective-permute-start(bf16[128,1536]{1,0:T(8,128)(2,1)} %get-tuple-element.199), channel_id=1, source_target_pairs={{0,1},{1,0},{2,3},{3,2},{4,5},{5,4},{6,7},{7,6},{8,9},{9,8},{10,11... | collective-permute-start | bytes 1179656 | tf_op jit(solution)/shard_map/ppermute | solution.py:643
  388.6 64.1 %collective-permute-start.54 = (bf16[384,1024]{1,0:T(8,128)(2,1)}, bf16[384,1024]{1,0:T(8,128)(2,1)}, u32[]{:S(2)}, u32[]{:S(2)}) collective-permute-start(bf16[384,1024]{1,0:T(8,128)(2,1)} %copy-done.41), channel_id=1, source_target_pairs={{0,1},{1,0},{2,3},{3,2},{4,5},{5,4},{6,7},{7,6},{8,9},{9,8},{10,11... | collective-permute-start | bytes 2359304 | tf_op jit(solution)/shard_map/ppermute | solution.py:643
  389.1 65.4 %collective-permute-start.53 = (bf16[384,1536]{1,0:T(8,128)(2,1)}, bf16[384,1536]{1,0:T(8,128)(2,1)}, u32[]{:S(2)}, u32[]{:S(2)}) collective-permute-start(bf16[384,1536]{1,0:T(8,128)(2,1)} %get-tuple-element.313.refs_1_), channel_id=1, source_target_pairs={{0,1},{1,0},{2,3},{3,2},{4,5},{5,4},{6,7},{7,6},{8,9},{9,8},{10,11... | collective-permute-start | bytes 3538952 | tf_op jit(solution)/shard_map/ppermute | solution.py:643
  407.5 33.9 %all-to-all-start.8 = ((bf16[8,320,128]{2,1,0:T(8,128)(2,1)}), bf16[8,320,128]{2,1,0:T(8,128)(2,1)}, u32[]{:S(2)}, u32[]{:S(2)}) async-start(bf16[8,320,128]{2,1,0:T(8,128)(2,1)} %get-tuple-element.200), calls=%async_computation.8 | async-start | bytes 1310720 | tf_op jit(solution)/shard_map/all_to_all | solution.py:707
  413.3 100.3 %reduce-scatter.2.cloned.1.call-start = ((), (), s32[]{:S(2)}) async-start(), calls=%async_computation.16 | async-start | bytes 1327104 | tf_op jit(solution)/shard_map/reduce_scatter | solution.py:957
  414.6 48.9 %collective-permute-start.59 = (bf16[384,1024]{1,0:T(8,128)(2,1)}, bf16[384,1024]{1,0:T(8,128)(2,1)}, u32[]{:S(2)}, u32[]{:S(2)}) collective-permute-start(bf16[384,1024]{1,0:T(8,128)(2,1)} %pad_maximum_fusion.2), channel_id=1, source_target_pairs={{0,2},{1,3},{2,0},{3,1},{4,6},{5,7},{6,4},{7,5},{8,10},{9,11},{10,... | collective-permute-start | bytes 2359304 | tf_op jit(solution)/shard_map/ppermute | solution.py:643
  416.1 42.4 %collective-permute-start.55 = (bf16[384,1536]{1,0:T(8,128)(2,1)}, bf16[384,1536]{1,0:T(8,128)(2,1)}, u32[]{:S(2)}, u32[]{:S(2)}) collective-permute-start(bf16[384,1536]{1,0:T(8,128)(2,1)} %collective-permute-done.39), channel_id=1, source_target_pairs={{0,1},{1,0},{2,3},{3,2},{4,5},{5,4},{6,7},{7,6},{8,9},{9,8},{10,11... | collective-permute-start | bytes 3538952 | tf_op jit(solution)/shard_map/ppermute | solution.py:643
  417.2 22.4 %collective-permute-start.58 = (bf16[336,384]{1,0:T(8,128)(2,1)S(1)}, bf16[336,384]{1,0:T(8,128)(2,1)S(1)}, u32[]{:S(2)}, u32[]{:S(2)}) collective-permute-start(bf16[336,384]{1,0:T(8,128)(2,1)S(1)} %fusion.50), channel_id=1, source_target_pairs={{0,2},{1,3},{2,0},{3,1},{4,6},{5,7},{6,4},{7,5},{8,10},{9,11},{10,... | collective-permute-start | bytes 774152 | tf_op jit(solution)/shard_map/ppermute | solution.py:643
  439.6 44.9 %collective-permute-start.60 = (bf16[2,1536,256]{2,1,0:T(8,128)(2,1)}, bf16[2,1536,256]{2,1,0:T(8,128)(2,1)}, u32[]{:S(2)}, u32[]{:S(2)}) collective-permute-start(bf16[2,1536,256]{2,1,0:T(8,128)(2,1)} %get-tuple-element.221), channel_id=1, source_target_pairs={{0,1},{1,0},{2,3},{3,2},{4,5},{5,4},{6,7},{7,6},{8,9},{9,8},{10,11... | collective-permute-start | bytes 4718600 | tf_op jit(solution)/shard_map/ppermute | solution.py:643
  441.3 38.4 %all-to-all-start.9 = ((bf16[8,48,1536]{2,1,0:T(8,128)(2,1)}), bf16[8,48,1536]{2,1,0:T(8,128)(2,1)S(1)}, u32[]{:S(2)}, u32[]{:S(2)}) async-start(bf16[8,48,1536]{2,1,0:T(8,128)(2,1)} %bitcast.278), calls=%async_computation.9 | async-start | bytes 2359296 | tf_op jit(solution)/shard_map/all_to_all | solution.py:707
  479.7 38.3 %all-to-all-start.10 = ((bf16[8,48,1536]{2,1,0:T(8,128)(2,1)}), bf16[8,48,1536]{2,1,0:T(8,128)(2,1)}, u32[]{:S(2)}, u32[]{:S(2)}) async-start(bf16[8,48,1536]{2,1,0:T(8,128)(2,1)} %bitcast.251), calls=%async_computation.10 | async-start | bytes 2359296 | tf_op jit(solution)/shard_map/all_to_all | solution.py:707
  484.4 61.1 %collective-permute-start.63 = (bf16[2,256,1536]{2,1,0:T(8,128)(2,1)}, bf16[2,256,1536]{2,1,0:T(8,128)(2,1)}, u32[]{:S(2)}, u32[]{:S(2)}) collective-permute-start(bf16[2,256,1536]{2,1,0:T(8,128)(2,1)} %get-tuple-element.224), channel_id=1, source_target_pairs={{0,1},{1,0},{2,3},{3,2},{4,5},{5,4},{6,7},{7,6},{8,9},{9,8},{10,11... | collective-permute-start | bytes 4718600 | tf_op jit(solution)/shard_map/ppermute | solution.py:643
  487.9 42.4 %collective-permute-start.61 = (bf16[1536,256]{1,0:T(8,128)(2,1)}, bf16[1536,256]{1,0:T(8,128)(2,1)}, u32[]{:S(2)}, u32[]{:S(2)}) collective-permute-start(bf16[1536,256]{1,0:T(8,128)(2,1)} %get-tuple-element.311), channel_id=1, source_target_pairs={{0,2},{1,3},{2,0},{3,1},{4,6},{5,7},{6,4},{7,5},{8,10},{9,11},{10,... | collective-permute-start | bytes 2359304 | tf_op jit(solution)/shard_map/ppermute | solution.py:643
  489.4 41.0 %collective-permute-start.62 = (bf16[1536,256]{1,0:T(8,128)(2,1)}, bf16[1536,256]{1,0:T(8,128)(2,1)}, u32[]{:S(2)}, u32[]{:S(2)}) collective-permute-start(bf16[1536,256]{1,0:T(8,128)(2,1)} %get-tuple-element.310), channel_id=1, source_target_pairs={{0,2},{1,3},{2,0},{3,1},{4,6},{5,7},{6,4},{7,5},{8,10},{9,11},{10,... | collective-permute-start | bytes 2359304 | tf_op jit(solution)/shard_map/ppermute | solution.py:643
  530.3 45.6 %all-to-all-start.11 = ((bf16[8,48,1536]{2,1,0:T(8,128)(2,1)}), bf16[8,48,1536]{2,1,0:T(8,128)(2,1)}, u32[]{:S(2)}, u32[]{:S(2)}) async-start(bf16[8,48,1536]{2,1,0:T(8,128)(2,1)} %bitcast.282), calls=%async_computation.11 | async-start | bytes 2359296 | tf_op jit(solution)/shard_map/all_to_all | solution.py:707
  534.6 116.3 %all-gather.3.cloned.1.call-start = ((), (), s32[]{:S(2)}) async-start(), calls=%async_computation.17 | async-start | bytes 3649536 | tf_op jit(solution)/shard_map/all_gather | solution.py:905
  545.5 46.5 %collective-permute-start.73 = (bf16[2,1536,256]{2,1,0:T(8,128)(2,1)}, bf16[2,1536,256]{2,1,0:T(8,128)(2,1)}, u32[]{:S(2)}, u32[]{:S(2)}) collective-permute-start(bf16[2,1536,256]{2,1,0:T(8,128)(2,1)} %get-tuple-element.254), channel_id=1, source_target_pairs={{0,1},{1,0},{2,3},{3,2},{4,5},{5,4},{6,7},{7,6},{8,9},{9,8},{10,11... | collective-permute-start | bytes 4718600 | tf_op jit(solution)/shard_map/ppermute | solution.py:643
  547.8 20.2 %collective-permute-start.64 = (bf16[256,1536]{1,0:T(8,128)(2,1)}, bf16[256,1536]{1,0:T(8,128)(2,1)}, u32[]{:S(2)}, u32[]{:S(2)}) collective-permute-start(bf16[256,1536]{1,0:T(8,128)(2,1)} %fusion.30), channel_id=1, source_target_pairs={{0,2},{1,3},{2,0},{3,1},{4,6},{5,7},{6,4},{7,5},{8,10},{9,11},{10,... | collective-permute-start | bytes 2359304 | tf_op jit(solution)/shard_map/ppermute | solution.py:643
  585.4 106.8 %collective-permute-start.70 = (bf16[384,1024]{1,0:T(8,128)(2,1)}, bf16[384,1024]{1,0:T(8,128)(2,1)}, u32[]{:S(2)}, u32[]{:S(2)}) collective-permute-start(bf16[384,1024]{1,0:T(8,128)(2,1)} %pad_maximum_fusion.2), channel_id=1, source_target_pairs={{0,1},{1,0},{2,3},{3,2},{4,5},{5,4},{6,7},{7,6},{8,9},{9,8},{10,11... | collective-permute-start | bytes 2359304 | tf_op jit(solution)/shard_map/ppermute | solution.py:643
  586.7 26.0 %all-to-all-start.12 = ((bf16[8,192,128]{2,1,0:T(8,128)(2,1)}), bf16[8,192,128]{2,1,0:T(8,128)(2,1)}, u32[]{:S(2)}, u32[]{:S(2)}) async-start(bf16[8,192,128]{2,1,0:T(8,128)(2,1)} %bitcast.297), calls=%async_computation.12 | async-start | bytes 786432 | tf_op jit(solution)/shard_map/all_to_all | solution.py:707
  595.5 31.8 %collective-permute-start.74 = (bf16[1536,256]{1,0:T(8,128)(2,1)}, bf16[1536,256]{1,0:T(8,128)(2,1)}, u32[]{:S(2)}, u32[]{:S(2)}) collective-permute-start(bf16[1536,256]{1,0:T(8,128)(2,1)} %get-tuple-element.309), channel_id=1, source_target_pairs={{0,2},{1,3},{2,0},{3,1},{4,6},{5,7},{6,4},{7,5},{8,10},{9,11},{10,... | collective-permute-start | bytes 2359304 | tf_op jit(solution)/shard_map/ppermute | solution.py:643
  597.0 35.6 %collective-permute-start.75 = (bf16[1536,256]{1,0:T(8,128)(2,1)}, bf16[1536,256]{1,0:T(8,128)(2,1)}, u32[]{:S(2)}, u32[]{:S(2)}) collective-permute-start(bf16[1536,256]{1,0:T(8,128)(2,1)} %get-tuple-element.308), channel_id=1, source_target_pairs={{0,2},{1,3},{2,0},{3,1},{4,6},{5,7},{6,4},{7,5},{8,10},{9,11},{10,... | collective-permute-start | bytes 2359304 | tf_op jit(solution)/shard_map/ppermute | solution.py:643
  598.9 94.9 %collective-permute-start.69 = (bf16[384,1536]{1,0:T(8,128)(2,1)}, bf16[384,1536]{1,0:T(8,128)(2,1)}, u32[]{:S(2)}, u32[]{:S(2)}) collective-permute-start(bf16[384,1536]{1,0:T(8,128)(2,1)} %get-tuple-element.312.refs_10_), channel_id=1, source_target_pairs={{0,1},{1,0},{2,3},{3,2},{4,5},{5,4},{6,7},{7,6},{8,9},{9,8},{10,11... | collective-permute-start | bytes 3538952 | tf_op jit(solution)/shard_map/ppermute | solution.py:643
  612.7 44.2 %all-to-all-start.13 = ((bf16[8,48,1536]{2,1,0:T(8,128)(2,1)}), bf16[8,48,1536]{2,1,0:T(8,128)(2,1)}, u32[]{:S(2)}, u32[]{:S(2)}) async-start(bf16[8,48,1536]{2,1,0:T(8,128)(2,1)} %bitcast.281), calls=%async_computation.13 | async-start | bytes 2359296 | tf_op jit(solution)/shard_map/all_to_all | solution.py:707
  618.6 24.8 %collective-permute-start.68 = (bf16[2,1536,256]{2,1,0:T(8,128)(2,1)}, bf16[2,1536,256]{2,1,0:T(8,128)(2,1)S(1)}, u32[]{:S(2)}, u32[]{:S(2)}) collective-permute-start(bf16[2,1536,256]{2,1,0:T(8,128)(2,1)} %get-tuple-element.238), channel_id=1, source_target_pairs={{0,1},{1,0},{2,3},{3,2},{4,5},{5,4},{6,7},{7,6},{8,9},{9,8},{10,11... | collective-permute-start | bytes 4718600 | tf_op jit(solution)/shard_map/ppermute | solution.py:643
  637.2 33.3 %collective-permute-start.84 = (bf16[2,256,1536]{2,1,0:T(8,128)(2,1)}, bf16[2,256,1536]{2,1,0:T(8,128)(2,1)}, u32[]{:S(2)}, u32[]{:S(2)}) collective-permute-start(bf16[2,256,1536]{2,1,0:T(8,128)(2,1)} %get-tuple-element.269), channel_id=1, source_target_pairs={{0,1},{1,0},{2,3},{3,2},{4,5},{5,4},{6,7},{7,6},{8,9},{9,8},{10,11... | collective-permute-start | bytes 4718600 | tf_op jit(solution)/shard_map/ppermute | solution.py:643
  643.4 30.5 %collective-permute-start.88 = (bf16[2,1536,256]{2,1,0:T(8,128)(2,1)}, bf16[2,1536,256]{2,1,0:T(8,128)(2,1)}, u32[]{:S(2)}, u32[]{:S(2)}) collective-permute-start(bf16[2,1536,256]{2,1,0:T(8,128)(2,1)} %get-tuple-element.274), channel_id=1, source_target_pairs={{0,1},{1,0},{2,3},{3,2},{4,5},{5,4},{6,7},{7,6},{8,9},{9,8},{10,11... | collective-permute-start | bytes 4718600 | tf_op jit(solution)/shard_map/ppermute | solution.py:643
  657.0 30.7 %all-to-all-start.14 = ((bf16[8,320,128]{2,1,0:T(8,128)(2,1)}), bf16[8,320,128]{2,1,0:T(8,128)(2,1)}, u32[]{:S(2)}, u32[]{:S(2)}) async-start(bf16[8,320,128]{2,1,0:T(8,128)(2,1)} %get-tuple-element.245), calls=%async_computation.14 | async-start | bytes 1310720 | tf_op jit(solution)/shard_map/all_to_all | solution.py:707
  670.5 17.1 %collective-permute-start.79 = (bf16[528,384]{1,0:T(8,128)(2,1)S(1)}, bf16[528,384]{1,0:T(8,128)(2,1)}, u32[]{:S(2)}, u32[]{:S(2)}) collective-permute-start(bf16[528,384]{1,0:T(8,128)(2,1)S(1)} %slice_dynamic-update-slice_fusion.4.refs_1_), channel_id=1, source_target_pairs={{8,0},{16,8},{24,16},{28,24},{20,28},{12,20},{4,12},{0,4},{9,1},{1... | collective-permute-start | bytes 1216520 | tf_op jit(solution)/shard_map/ppermute | solution.py:687
  673.9 30.7 %collective-permute-start.71 = (bf16[384,1536]{1,0:T(8,128)(2,1)}, bf16[384,1536]{1,0:T(8,128)(2,1)}, u32[]{:S(2)}, u32[]{:S(2)}) collective-permute-start(bf16[384,1536]{1,0:T(8,128)(2,1)} %collective-permute-done.49), channel_id=1, source_target_pairs={{0,1},{1,0},{2,3},{3,2},{4,5},{5,4},{6,7},{7,6},{8,9},{9,8},{10,11... | collective-permute-start | bytes 3538952 | tf_op jit(solution)/shard_map/ppermute | solution.py:643
  693.9 20.0 %collective-permute-start.85 = (bf16[256,1536]{1,0:T(8,128)(2,1)S(1)}, bf16[256,1536]{1,0:T(8,128)(2,1)S(1)}, u32[]{:S(2)}, u32[]{:S(2)}) collective-permute-start(bf16[256,1536]{1,0:T(8,128)(2,1)S(1)} %bitcast.286), channel_id=1, source_target_pairs={{0,2},{1,3},{2,0},{3,1},{4,6},{5,7},{6,4},{7,5},{8,10},{9,11},{10,... | collective-permute-start | bytes 2359304 | tf_op jit(solution)/shard_map/ppermute | solution.py:643
  696.3 17.6 %collective-permute-start.82 = (bf16[528,384]{1,0:T(8,128)(2,1)}, bf16[528,384]{1,0:T(8,128)(2,1)S(1)}, u32[]{:S(2)}, u32[]{:S(2)}) collective-permute-start(bf16[528,384]{1,0:T(8,128)(2,1)} %collective-permute-done.80.refs_4_), channel_id=1, source_target_pairs={{0,8},{8,16},{16,24},{24,28},{28,20},{20,12},{12,4},{4,0},{1,9},{9... | collective-permute-start | bytes 1216520 | tf_op jit(solution)/shard_map/ppermute | solution.py:697
  (173 other events, 1777.0 us)
Sparse Core Ops, SparseCore 0:
  427.2 86.4 reduce-scatter.1
  537.6 79.8 all-gather.2

commit v4 on v3

--- a/solution.py
+++ b/solution.py
@@ -978,7 +978,8 @@
             merged = merge(head_sum, out_rows)
             merged, *head_done = tie(merged, *head_done)
             down_last = [swap(tie(down_sum, head_last)[0][0], 2)]
-            sources, down_last = ring_blocks(merged, ring_start(merged, ring), ring, down_last)
+            sources = ring_blocks(merged, ring_start(merged, ring), ring)
+            *sources[-2:], down_last[0] = tie(*sources[-2:], down_last[0])
             pair_done = finish(layer, layers, pair_own, pair_near, pair_last, expert_done[:2])
             down_done = finish(layer, layers, down_kept, down_near, down_last, expert_done[2:])
             expert_done = [*pair_done, *down_done]

time: 754 us -> 748 us (level)
    unnamed x273 -> x271, local copies, waits for them, and re-layouts: 19.6 us -> 18.3 us
  transfers between devices with their start and end apart: 106 -> 106, of which waited for: 45 -> 47; matrix products, arithmetic and copies ran while one was open for 15% -> 15% of each run, Pallas kernels for 17% -> 17%
where the time goes in v4:
time: 748 us; the launch traced here: 736 us
  waiting for transfers between devices  294 us (39%)
  Pallas kernels  158 us (21%)
  starting transfers between devices  143 us (19%)
  local copies, waits for them, and re-layouts  49 us (7%)
  other arithmetic  40.8 us (5%)
  matrix products  34.7 us (5%)
  between operations  16.4 us (2%)
    ppermute x65, waiting for transfers between devices, swap(): return lax.ppermute(x, 'wt', [(i, i ^ mask) for i in range(4)])  139 us
    all_to_all x15, waiting for transfers between devices, all_to_all(): return lax.all_to_all(x, 'ctx', split_axis=0, concat_axis=0, tiled=True)  78.2 us
    all_to_all x15, starting transfers between devices, all_to_all(): return lax.all_to_all(x, 'ctx', split_axis=0, concat_axis=0, tiled=True)  74.5 us
    ppermute x65, starting transfers between devices, swap(): return lax.ppermute(x, 'wt', [(i, i ^ mask) for i in range(4)])  38 us
    dot_general x26, matrix products, times(): lax.dot_general(left, right, (((a,), (b,)), ((), ())), preferred_element_...  34.4 us
    ppermute x6, waiting for transfers between devices, ring_blocks(): lax.ppermute(ahead, 'ctx', right)  26.1 us
    reduce_scatter x1, waiting for transfers between devices, local_heads(): lax.psum_scatter(out_part, 'ctx', scatter_dimension=0, tiled=True)  23 us
    pallas_call x2, Pallas kernels, front(): pl.pallas_call(functools.partial(front_kernel, raw, rep, head, span, base...  22.8 us
  transfers between devices with their start and end apart: 106, of which 47 were waited for; matrix products, arithmetic and copies ran while one was open for 15% of the time, Pallas kernels for 17%

profile of v4, /device:TPU:0, one launch (start us, length us, event | category | flops | bytes accessed | tf_op | source)
XLA Modules:
  0.0 736.5 jit_solution(11213991720415021863)
XLA Ops:
  22.5 7.5 %collective-permute-done.7.refs_12_ = bf16[672,384]{1,0:T(8,128)(2,1)} collective-permute-done((bf16[672,384]{1,0:T(8,128)(2,1)}, bf16[672,384]{1,0:T(8,128)(2,1)}, u32[]{:S(2)}, u32[]{:S(2)}) %collective-permute-start.7) | collective-permute-done | bytes 516128 | tf_op jit(solution)/shard_map/ppermute | solution.py:643
  34.0 8.7 %collective-permute-done.4.refs_5_ = bf16[128,1536]{1,0:T(8,128)(2,1)S(1)} collective-permute-done((bf16[128,1536]{1,0:T(8,128)(2,1)}, bf16[128,1536]{1,0:T(8,128)(2,1)S(1)}, u32[]{:S(2)}, u32[]{:S(2)}) %collective-permute-start.4) | collective-permute-done | bytes 393248 | tf_op jit(solution)/shard_map/ppermute | solution.py:697
  51.8 4.3 all-to-all-start
  65.5 12.0 %front.2 = (bf16[8,128,1536]{2,1,0:T(8,128)(2,1)}, bf16[320,1024]{1,0:T(8,128)(2,1)}, bf16[8,192,128]{2,1,0:T(8,128)(2,1)}, f32[192,1024]{1,0:T(8,128)}, f32[3,1024]{1,0:T(4,128)}) custom-call(s32[8]{0:T(128)} %get-tuple-element.301.spot_ref, s32[8]{0:T(128)} %get-tuple-element.300.owner_ref, s32[4]{0:T(128)} %xor_convert_fusion.at_ref, ...), custom_call_target="tpu_custom_call" | custom-call | flops 1509949440 | bytes 9437184 | tf_op jit(solution)/shard_map/front/pallas_call | solution.py:130
  77.5 8.1 %all-to-all-done = bf16[8,48,1664]{2,1,0:T(8,128)(2,1)} async-done(((bf16[8,48,1664]{2,1,0:T(8,128)(2,1)}), bf16[8,48,1664]{2,1,0:T(8,128)(2,1)}, u32[]{:S(2)}, u32[]{:S(2)}) %all-to-all-start) | async-done | bytes 1277984 | tf_op jit(solution)/shard_map/all_to_all | solution.py:707
  85.6 3.7 all-to-all-start.1
  93.3 7.8 %all-to-all-done.1 = bf16[8,192,128]{2,1,0:T(8,128)(2,1)S(1)} async-done(((bf16[8,192,128]{2,1,0:T(8,128)(2,1)}), bf16[8,192,128]{2,1,0:T(8,128)(2,1)S(1)}, u32[]{:S(2)}, u32[]{:S(2)}) %all-to-all-start.1) | async-done | bytes 393248 | tf_op jit(solution)/shard_map/all_to_all | solution.py:707
  108.9 5.4 middle_forward.2
  114.3 4.3 all-to-all-start.2
  122.6 6.5 collective-permute-done.18.refs_7_.refs_9_
  129.1 16.3 %collective-permute-done.19.refs_8_.refs_10_ = bf16[256,1536]{1,0:T(8,128)(2,1)S(1)} collective-permute-done((bf16[256,1536]{1,0:T(8,128)(2,1)S(1)}, bf16[256,1536]{1,0:T(8,128)(2,1)S(1)}, u32[]{:S(2)}, u32[]{:S(2)}) %collective-permute-start.19) | collective-permute-done | bytes 786464 | tf_op jit(solution)/shard_map/ppermute | solution.py:643
  149.9 10.1 %expert_forward.1 = (bf16[384,1536]{1,0:T(8,128)(2,1)}, f32[4,384,256]{2,1,0:T(8,128)}, f32[4,384,256]{2,1,0:T(8,128)}, bf16[4,384,256]{2,1,0:T(8,128)(2,1)}) custom-call(bf16[384,1536]{1,0:T(8,128)(2,1)} %bitcast.30.rows_ref, bf16[1536,256]{1,0:T(8,128)(2,1)} %copy-done.22, bf16[1536,256]{1,0:T(8,128)(2,1)} %get-tuple-element.327.refs_1_.refs_3_, ...), custom_call_target="tpu_custom_call" | custom-call | flops 3623878656 | bytes 16777216 | tf_op jit(solution)/shard_map/expert_forward/pallas_call | solution.py:251
  160.1 6.2 all-to-all-start.3
  170.0 15.9 %collective-permute-done.23.refs_6_ = bf16[1536,256]{1,0:T(8,128)(2,1)} collective-permute-done((bf16[1536,256]{1,0:T(8,128)(2,1)}, bf16[1536,256]{1,0:T(8,128)(2,1)}, u32[]{:S(2)}, u32[]{:S(2)}) %collective-permute-start.23) | collective-permute-done | bytes 786464 | tf_op jit(solution)/shard_map/ppermute | solution.py:643
  185.9 9.3 %all-to-all-done.3 = bf16[8,48,1536]{2,1,0:T(8,128)(2,1)S(1)} async-done(((bf16[8,48,1536]{2,1,0:T(8,128)(2,1)}), bf16[8,48,1536]{2,1,0:T(8,128)(2,1)S(1)}, u32[]{:S(2)}, u32[]{:S(2)}) %all-to-all-start.3) | async-done | bytes 1179680 | tf_op jit(solution)/shard_map/all_to_all | solution.py:707
  201.7 6.5 collective-permute-done.24.refs_1_
  211.8 5.7 collective-permute-done.26.refs_3_
  219.6 6.2 collective-permute-done.28.refs_5_
  235.0 10.8 %front.3 = (bf16[8,128,1536]{2,1,0:T(8,128)(2,1)}, bf16[320,1024]{1,0:T(8,128)(2,1)}, bf16[8,192,128]{2,1,0:T(8,128)(2,1)}, f32[192,1024]{1,0:T(8,128)}, f32[3,1024]{1,0:T(4,128)}) custom-call(s32[8]{0:T(128)} %get-tuple-element.301.spot_ref, s32[8]{0:T(128)} %get-tuple-element.300.owner_ref, s32[4]{0:T(128)} %xor_convert_fusion.at_ref, ...), custom_call_target="tpu_custom_call" | custom-call | flops 1509949440 | bytes 9437184 | tf_op jit(solution)/shard_map/front/pallas_call | solution.py:130
  248.9 6.1 all-to-all-start.4
  257.9 8.8 %all-to-all-done.4 = bf16[8,192,128]{2,1,0:T(8,128)(2,1)S(1)} async-done(((bf16[8,192,128]{2,1,0:T(8,128)(2,1)}), bf16[8,192,128]{2,1,0:T(8,128)(2,1)S(1)}, u32[]{:S(2)}, u32[]{:S(2)}) %all-to-all-start.4) | async-done | bytes 393248 | tf_op jit(solution)/shard_map/all_to_all | solution.py:707
  267.4 5.3 middle_forward.3
  272.8 4.6 all-to-all-start.5
  284.1 22.4 %collective-permute-done.39 = bf16[384,1536]{1,0:T(8,128)(2,1)} collective-permute-done((bf16[384,1536]{1,0:T(8,128)(2,1)}, bf16[384,1536]{1,0:T(8,128)(2,1)}, u32[]{:S(2)}, u32[]{:S(2)}) %collective-permute-start.39) | collective-permute-done | bytes 1179680 | tf_op jit(solution)/shard_map/ppermute | solution.py:643
  309.1 14.5 %expert_both.1 = (bf16[384,1536]{1,0:T(8,128)(2,1)}, bf16[384,1664]{1,0:T(8,128)(2,1)}, bf16[384,1536]{1,0:T(8,128)(2,1)}, bf16[4,384,256]{2,1,0:T(8,128)(2,1)},...) custom-call(s32[1]{0:T(128)} %bitcast.3.at_ref.mine_ref, bf16[384,1536]{1,0:T(8,128)(2,1)} %bitcast.279, ...), custom_call_target="tpu_custom_call" | custom-call | flops 7247757312 | bytes 18874368 | tf_op jit(solution)/shard_map/expert_both/pallas_call | solution.py:350
  323.7 5.7 all-to-all-start.6
  337.0 14.6 %collective-permute-done.46 = bf16[384,1024]{1,0:T(8,128)(2,1)} collective-permute-done((bf16[384,1024]{1,0:T(8,128)(2,1)S(1)}, bf16[384,1024]{1,0:T(8,128)(2,1)}, u32[]{:S(2)}, u32[]{:S(2)}) %collective-permute-start.46) | collective-permute-done | bytes 786464 | tf_op jit(solution)/shard_map/ppermute | solution.py:643
  351.6 9.1 %all-to-all-done.6 = bf16[8,48,1664]{2,1,0:T(8,128)(2,1)} async-done(((bf16[8,48,1664]{2,1,0:T(8,128)(2,1)}), bf16[8,48,1664]{2,1,0:T(8,128)(2,1)}, u32[]{:S(2)}, u32[]{:S(2)}) %all-to-all-start.6) | async-done | bytes 1277984 | tf_op jit(solution)/shard_map/all_to_all | solution.py:707
  360.7 7.6 %middle_back.2 = (f32[128,1536]{1,0:T(8,128)}, bf16[128,1536]{1,0:T(8,128)(2,1)}, bf16[1536,128]{1,0:T(8,128)(2,1)}, f32[16,1536]{1,0:T(8,128)}) custom-call(s32[4]{0:T(128)} %xor_convert_fusion.at_ref, bf16[2,128,384]{2,1,0:T(8,128)(2,1)} %get-tuple-element.348.place_ref, bf16[384,1664]{1,0:T(8,128)(2,1)} %bitcast.58.back_ref, ...), custom_call_target="tpu_custom_call" | custom-call | flops 754974720 | bytes 10485760 | tf_op jit(solution)/shard_map/middle_back/pallas_call | solution.py:626
  368.3 3.9 all-to-all-start.7
  373.7 7.4 %collective-permute-done.47 = bf16[2,384,128]{2,1,0:T(8,128)(2,1)} collective-permute-done((bf16[2,384,128]{2,1,0:T(8,128)(2,1)}, bf16[2,384,128]{2,1,0:T(8,128)(2,1)}, u32[]{:S(2)}, u32[]{:S(2)}) %collective-permute-start.47) | collective-permute-done | bytes 196640 | tf_op jit(solution)/shard_map/ppermute | solution.py:643
  384.2 4.4 collective-permute-done.51
  390.6 8.7 %attend_back.2 = (bf16[320,1024]{1,0:T(8,128)(2,1)}, bf16[8,320,128]{2,1,0:T(8,128)(2,1)}) custom-call(s32[8]{0:T(128)} %get-tuple-element.300.owner_ref, bf16[320,1024]{1,0:T(8,128)(2,1)} %get-tuple-element.189.qkv_ref, f32[192,1024]{1,0:T(8,128)} %get-tuple-element.190.exact_ref, f32[3,1024]{1,0:T(4,128)} %get-tuple-element.191.log_ref, ...), custom_call_target="tpu_custom_call" | custom-call | flops 1258291200 | bytes 6291456 | tf_op jit(solution)/shard_map/attend_back/pallas_call | solution.py:195
  399.3 4.6 head_grads.2
  404.4 3.1 convolution_convert_fusion.1
  407.5 5.9 all-to-all-start.8
  417.8 9.3 %expert_grads.2 = (bf16[2,1536,256]{2,1,0:T(8,128)(2,1)}, bf16[2,1536,256]{2,1,0:T(8,128)(2,1)}, bf16[2,1536,256]{2,1,0:T(8,128)(2,1)}, bf16[2,1536,256]{2,1,0:T...) custom-call(bf16[384,1536]{1,0:T(8,128)(2,1)} %bitcast.280, ...), custom_call_target="tpu_custom_call" | custom-call | flops 3623878656 | bytes 14680064 | tf_op jit(solution)/shard_map/expert_grads/pallas_call | solution.py:388
  427.1 12.5 %collective-permute-done.58 = bf16[336,384]{1,0:T(8,128)(2,1)S(1)} collective-permute-done((bf16[336,384]{1,0:T(8,128)(2,1)S(1)}, bf16[336,384]{1,0:T(8,128)(2,1)S(1)}, u32[]{:S(2)}, u32[]{:S(2)}) %collective-permute-start.58) | collective-permute-done | bytes 258080 | tf_op jit(solution)/shard_map/ppermute | solution.py:643
  441.3 5.7 all-to-all-start.9
  463.5 16.2 %all-to-all-done.9 = bf16[8,48,1536]{2,1,0:T(8,128)(2,1)S(1)} async-done(((bf16[8,48,1536]{2,1,0:T(8,128)(2,1)}), bf16[8,48,1536]{2,1,0:T(8,128)(2,1)S(1)}, u32[]{:S(2)}, u32[]{:S(2)}) %all-to-all-start.9) | async-done | bytes 1179680 | tf_op jit(solution)/shard_map/all_to_all | solution.py:707
  479.7 4.7 all-to-all-start.10
  484.5 3.4 fusion.29
  490.7 23.0 %reduce-scatter.2.cloned.1.call-done = bf16[48,1536]{1,0:T(8,128)(2,1)} async-done(((bf16[384,1536]{1,0:T(8,128)(2,1)}), bf16[48,1536]{1,0:T(8,128)(2,1)}) %reduce-scatter.2.cloned.1.call-update) | async-done | bytes 147472 | tf_op jit(solution)/shard_map/reduce_scatter | solution.py:957
  518.0 12.4 %expert_backward.1 = (bf16[384,1536]{1,0:T(8,128)(2,1)}, bf16[4,384,256]{2,1,0:T(8,128)(2,1)}, bf16[4,384,256]{2,1,0:T(8,128)(2,1)}) custom-call(bf16[384,1536]{1,0:T(8,128)(2,1)} %bitcast.82.grad_ref, f32[4,384,256]{2,1,0:T(8,128)} %get-tuple-element.213.refs_0_, f32[4,384,256]{2,1,0:T(8,128)} %get-tuple-element.214.refs_1_, bf16[1536,256]{1,0:T(8,128)(2,1)} %copy-done.22, ...), custom_call_target="tpu_custom_call" | custom-call | flops 3623878656 | bytes 16777216 | tf_op jit(solution)/shard_map/expert_backward/pallas_call | solution.py:289
  530.3 4.3 all-to-all-start.11
  536.3 9.3 %expert_grads.3 = (bf16[2,1536,256]{2,1,0:T(8,128)(2,1)}, bf16[2,1536,256]{2,1,0:T(8,128)(2,1)}, bf16[2,1536,256]{2,1,0:T(8,128)(2,1)}, bf16[2,1536,256]{2,1,0:T...) custom-call(bf16[384,1536]{1,0:T(8,128)(2,1)} %bitcast.30.rows_ref, ...), custom_call_target="tpu_custom_call" | custom-call | flops 3623878656 | bytes 14680064 | tf_op jit(solution)/shard_map/expert_grads/pallas_call | solution.py:388
  551.6 16.5 %collective-permute-done.64.refs_2_ = bf16[256,1536]{1,0:T(8,128)(2,1)} collective-permute-done((bf16[256,1536]{1,0:T(8,128)(2,1)}, bf16[256,1536]{1,0:T(8,128)(2,1)}, u32[]{:S(2)}, u32[]{:S(2)}) %collective-permute-start.64) | collective-permute-done | bytes 786464 | tf_op jit(solution)/shard_map/ppermute | solution.py:643
  568.1 7.9 %all-to-all-done.11 = bf16[8,48,1536]{2,1,0:T(8,128)(2,1)} async-done(((bf16[8,48,1536]{2,1,0:T(8,128)(2,1)}), bf16[8,48,1536]{2,1,0:T(8,128)(2,1)}, u32[]{:S(2)}, u32[]{:S(2)}) %all-to-all-start.11) | async-done | bytes 1179680 | tf_op jit(solution)/shard_map/all_to_all | solution.py:707
  576.0 7.9 %middle_back.3 = (f32[128,1536]{1,0:T(8,128)}, bf16[128,1536]{1,0:T(8,128)(2,1)}, bf16[1536,128]{1,0:T(8,128)(2,1)}, f32[16,1536]{1,0:T(8,128)}) custom-call(s32[4]{0:T(128)} %xor_convert_fusion.at_ref, bf16[2,128,384]{2,1,0:T(8,128)(2,1)} %get-tuple-element.349.place_ref, bf16[384,1536]{1,0:T(8,128)(2,1)} %bitcast.86.back_ref, f32[128,1536]{1,0:T(8,128)} %copy-done.5, ...), custom_call_target="tpu_custom_call" | custom-call | flops 754974720 | bytes 10485760 | tf_op jit(solution)/shard_map/middle_back/pallas_call | solution.py:626
  586.7 4.1 all-to-all-start.12
  592.1 3.4 fusion.32
  601.9 10.9 %all-to-all-done.12.grad_ref = bf16[8,192,128]{2,1,0:T(8,128)(2,1)} async-done(((bf16[8,192,128]{2,1,0:T(8,128)(2,1)}), bf16[8,192,128]{2,1,0:T(8,128)(2,1)}, u32[]{:S(2)}, u32[]{:S(2)}) %all-to-all-start.12) | async-done | bytes 393248 | tf_op jit(solution)/shard_map/all_to_all | solution.py:707
  612.7 4.5 all-to-all-start.13
  617.9 8.7 %attend_back.3 = (bf16[320,1024]{1,0:T(8,128)(2,1)}, bf16[8,320,128]{2,1,0:T(8,128)(2,1)}) custom-call(s32[8]{0:T(128)} %get-tuple-element.300.owner_ref, bf16[320,1024]{1,0:T(8,128)(2,1)} %get-tuple-element.227.qkv_ref, f32[192,1024]{1,0:T(8,128)} %get-tuple-element.228.exact_ref, f32[3,1024]{1,0:T(4,128)} %get-tuple-element.229.log_ref, ...), custom_call_target="tpu_custom_call" | custom-call | flops 1258291200 | bytes 6291456 | tf_op jit(solution)/shard_map/attend_back/pallas_call | solution.py:195
  626.6 6.0 collective-permute-done.75.refs_3_
  632.6 4.5 head_grads.3
  644.5 3.6 finish.4
  651.0 6.0 spread.2
  656.9 6.7 all-to-all-start.14
  674.6 3.7 finish.6
  678.3 4.7 collective-permute-done.78.refs_2_
  683.0 5.0 collective-permute-start.80
  692.4 4.3 collective-permute-done.80.refs_4_
  718.5 6.4 spread.3
  (580 shorter events, 212.9 us)
Async XLA Ops:
  15.3 18.6 %collective-permute-start.6 = (bf16[672,384]{1,0:T(8,128)(2,1)}, bf16[672,384]{1,0:T(8,128)(2,1)S(1)}, u32[]{:S(2)}, u32[]{:S(2)}) collective-permute-start(bf16[672,384]{1,0:T(8,128)(2,1)} %bitcast.287), channel_id=1, source_target_pairs={{0,1},{1,0},{2,3},{3,2},{4,5},{5,4},{6,7},{7,6},{8,9},{9,8},{10,11... | collective-permute-start | bytes 1548296 | tf_op jit(solution)/shard_map/ppermute | solution.py:643
  51.8 33.8 %all-to-all-start = ((bf16[8,48,1664]{2,1,0:T(8,128)(2,1)}), bf16[8,48,1664]{2,1,0:T(8,128)(2,1)}, u32[]{:S(2)}, u32[]{:S(2)}) async-start(bf16[8,48,1664]{2,1,0:T(8,128)(2,1)} %bitcast.17), calls=%async_computation | async-start | bytes 2555904 | tf_op jit(solution)/shard_map/all_to_all | solution.py:707
  58.0 35.3 %collective-permute-start.11 = (bf16[384,1536]{1,0:T(8,128)(2,1)S(1)}, bf16[384,1536]{1,0:T(8,128)(2,1)}, u32[]{:S(2)}, u32[]{:S(2)}) collective-permute-start(bf16[384,1536]{1,0:T(8,128)(2,1)S(1)} %get-tuple-element.315.refs_0_.refs_2_), channel_id=1, source_target_pairs={{0,2},{1,3},{2,0},{3,1},{4,6},{5,7},{6,4},{7,5},{8,10},{9,11},{10,... | collective-permute-start | bytes 3538952 | tf_op jit(solution)/shard_map/ppermute | solution.py:643
  89.3 18.6 %collective-permute-start.12 = (bf16[384,1536]{1,0:T(8,128)(2,1)S(1)}, bf16[384,1536]{1,0:T(8,128)(2,1)}, u32[]{:S(2)}, u32[]{:S(2)}) collective-permute-start(bf16[384,1536]{1,0:T(8,128)(2,1)S(1)} %get-tuple-element.315.refs_0_.refs_2_), channel_id=1, source_target_pairs={{0,1},{1,0},{2,3},{3,2},{4,5},{5,4},{6,7},{7,6},{8,9},{9,8},{10,11... | collective-permute-start | bytes 3538952 | tf_op jit(solution)/shard_map/ppermute | solution.py:643
  91.8 22.5 %collective-permute-start.14 = (bf16[1536,256]{1,0:T(8,128)(2,1)S(1)}, bf16[1536,256]{1,0:T(8,128)(2,1)}, u32[]{:S(2)}, u32[]{:S(2)}) collective-permute-start(bf16[1536,256]{1,0:T(8,128)(2,1)S(1)} %get-tuple-element.329.refs_0_.refs_2_), channel_id=1, source_target_pairs={{0,2},{1,3},{2,0},{3,1},{4,6},{5,7},{6,4},{7,5},{8,10},{9,11},{10,... | collective-permute-start | bytes 2359304 | tf_op jit(solution)/shard_map/ppermute | solution.py:643
  104.0 25.1 %collective-permute-start.18 = (bf16[1536,256]{1,0:T(8,128)(2,1)}, bf16[1536,256]{1,0:T(8,128)(2,1)}, u32[]{:S(2)}, u32[]{:S(2)}) collective-permute-start(bf16[1536,256]{1,0:T(8,128)(2,1)} %get-tuple-element.327.refs_1_.refs_3_), channel_id=1, source_target_pairs={{0,2},{1,3},{2,0},{3,1},{4,6},{5,7},{6,4},{7,5},{8,10},{9,11},{10,... | collective-permute-start | bytes 2359304 | tf_op jit(solution)/shard_map/ppermute | solution.py:643
  114.3 34.8 %all-to-all-start.2 = ((bf16[8,48,1536]{2,1,0:T(8,128)(2,1)}), bf16[8,48,1536]{2,1,0:T(8,128)(2,1)}, u32[]{:S(2)}, u32[]{:S(2)}) async-start(bf16[8,48,1536]{2,1,0:T(8,128)(2,1)} %bitcast.283), calls=%async_computation.2 | async-start | bytes 2359296 | tf_op jit(solution)/shard_map/all_to_all | solution.py:707
  120.9 24.5 %collective-permute-start.19 = (bf16[256,1536]{1,0:T(8,128)(2,1)S(1)}, bf16[256,1536]{1,0:T(8,128)(2,1)S(1)}, u32[]{:S(2)}, u32[]{:S(2)}) collective-permute-start(bf16[256,1536]{1,0:T(8,128)(2,1)S(1)} %get-tuple-element.325.refs_2_.refs_4_), channel_id=1, source_target_pairs={{0,2},{1,3},{2,0},{3,1},{4,6},{5,7},{6,4},{7,5},{8,10},{9,11},{10,... | collective-permute-start | bytes 2359304 | tf_op jit(solution)/shard_map/ppermute | solution.py:643
  122.1 23.4 %collective-permute-start.15 = (bf16[1536,256]{1,0:T(8,128)(2,1)S(1)}, bf16[1536,256]{1,0:T(8,128)(2,1)S(1)}, u32[]{:S(2)}, u32[]{:S(2)}) collective-permute-start(bf16[1536,256]{1,0:T(8,128)(2,1)S(1)} %get-tuple-element.329.refs_0_.refs_2_), channel_id=1, source_target_pairs={{0,1},{1,0},{2,3},{3,2},{4,5},{5,4},{6,7},{7,6},{8,9},{9,8},{10,11... | collective-permute-start | bytes 2359304 | tf_op jit(solution)/shard_map/ppermute | solution.py:643
  122.1 23.9 %collective-permute-start.16 = (bf16[1536,256]{1,0:T(8,128)(2,1)}, bf16[1536,256]{1,0:T(8,128)(2,1)S(1)}, u32[]{:S(2)}, u32[]{:S(2)}) collective-permute-start(bf16[1536,256]{1,0:T(8,128)(2,1)} %get-tuple-element.327.refs_1_.refs_3_), channel_id=1, source_target_pairs={{0,1},{1,0},{2,3},{3,2},{4,5},{5,4},{6,7},{7,6},{8,9},{9,8},{10,11... | collective-permute-start | bytes 2359304 | tf_op jit(solution)/shard_map/ppermute | solution.py:643
  122.6 23.4 %collective-permute-start.17 = (bf16[256,1536]{1,0:T(8,128)(2,1)S(1)}, bf16[256,1536]{1,0:T(8,128)(2,1)S(1)}, u32[]{:S(2)}, u32[]{:S(2)}) collective-permute-start(bf16[256,1536]{1,0:T(8,128)(2,1)S(1)} %get-tuple-element.325.refs_2_.refs_4_), channel_id=1, source_target_pairs={{0,1},{1,0},{2,3},{3,2},{4,5},{5,4},{6,7},{7,6},{8,9},{9,8},{10,11... | collective-permute-start | bytes 2359304 | tf_op jit(solution)/shard_map/ppermute | solution.py:643
  129.1 17.3 %collective-permute-start.21 = (bf16[1536,256]{1,0:T(8,128)(2,1)}, bf16[1536,256]{1,0:T(8,128)(2,1)S(1)}, u32[]{:S(2)}, u32[]{:S(2)}) collective-permute-start(bf16[1536,256]{1,0:T(8,128)(2,1)} %collective-permute-done.18.refs_7_.refs_9_), channel_id=1, source_target_pairs={{0,1},{1,0},{2,3},{3,2},{4,5},{5,4},{6,7},{7,6},{8,9},{9,8},{10,11... | collective-permute-start | bytes 2359304 | tf_op jit(solution)/shard_map/ppermute | solution.py:643
  160.1 35.0 %all-to-all-start.3 = ((bf16[8,48,1536]{2,1,0:T(8,128)(2,1)}), bf16[8,48,1536]{2,1,0:T(8,128)(2,1)S(1)}, u32[]{:S(2)}, u32[]{:S(2)}) async-start(bf16[8,48,1536]{2,1,0:T(8,128)(2,1)} %bitcast.285), calls=%async_computation.3 | async-start | bytes 2359296 | tf_op jit(solution)/shard_map/all_to_all | solution.py:707
  166.2 19.6 %collective-permute-start.23 = (bf16[1536,256]{1,0:T(8,128)(2,1)}, bf16[1536,256]{1,0:T(8,128)(2,1)}, u32[]{:S(2)}, u32[]{:S(2)}) collective-permute-start(bf16[1536,256]{1,0:T(8,128)(2,1)} %get-tuple-element.328.refs_0_), channel_id=1, source_target_pairs={{0,2},{1,3},{2,0},{3,1},{4,6},{5,7},{6,4},{7,5},{8,10},{9,11},{10,... | collective-permute-start | bytes 2359304 | tf_op jit(solution)/shard_map/ppermute | solution.py:643
  200.3 45.6 %collective-permute-start.32 = (bf16[384,1536]{1,0:T(8,128)(2,1)S(1)}, bf16[384,1536]{1,0:T(8,128)(2,1)S(1)}, u32[]{:S(2)}, u32[]{:S(2)}) collective-permute-start(bf16[384,1536]{1,0:T(8,128)(2,1)S(1)} %get-tuple-element.314.refs_0_), channel_id=1, source_target_pairs={{0,2},{1,3},{2,0},{3,1},{4,6},{5,7},{6,4},{7,5},{8,10},{9,11},{10,... | collective-permute-start | bytes 3538952 | tf_op jit(solution)/shard_map/ppermute | solution.py:643
  210.3 35.5 %collective-permute-start.33 = (bf16[1536,256]{1,0:T(8,128)(2,1)}, bf16[1536,256]{1,0:T(8,128)(2,1)}, u32[]{:S(2)}, u32[]{:S(2)}) collective-permute-start(bf16[1536,256]{1,0:T(8,128)(2,1)} %get-tuple-element.326.refs_1_), channel_id=1, source_target_pairs={{0,2},{1,3},{2,0},{3,1},{4,6},{5,7},{6,4},{7,5},{8,10},{9,11},{10,... | collective-permute-start | bytes 2359304 | tf_op jit(solution)/shard_map/ppermute | solution.py:643
  230.4 27.5 %collective-permute-start.34 = (bf16[384,1536]{1,0:T(8,128)(2,1)S(1)}, bf16[384,1536]{1,0:T(8,128)(2,1)}, u32[]{:S(2)}, u32[]{:S(2)}) collective-permute-start(bf16[384,1536]{1,0:T(8,128)(2,1)S(1)} %get-tuple-element.314.refs_0_), channel_id=1, source_target_pairs={{0,1},{1,0},{2,3},{3,2},{4,5},{5,4},{6,7},{7,6},{8,9},{9,8},{10,11... | collective-permute-start | bytes 3538952 | tf_op jit(solution)/shard_map/ppermute | solution.py:643
  245.9 20.8 %collective-permute-start.35 = (bf16[384,1536]{1,0:T(8,128)(2,1)S(1)}, bf16[384,1536]{1,0:T(8,128)(2,1)}, u32[]{:S(2)}, u32[]{:S(2)}) collective-permute-start(bf16[384,1536]{1,0:T(8,128)(2,1)S(1)} %collective-permute-done.32.refs_2_), channel_id=1, source_target_pairs={{0,1},{1,0},{2,3},{3,2},{4,5},{5,4},{6,7},{7,6},{8,9},{9,8},{10,11... | collective-permute-start | bytes 3538952 | tf_op jit(solution)/shard_map/ppermute | solution.py:643
  248.4 24.4 %collective-permute-start.36 = (bf16[256,1536]{1,0:T(8,128)(2,1)}, bf16[256,1536]{1,0:T(8,128)(2,1)}, u32[]{:S(2)}, u32[]{:S(2)}) collective-permute-start(bf16[256,1536]{1,0:T(8,128)(2,1)} %get-tuple-element.324.refs_2_), channel_id=1, source_target_pairs={{0,2},{1,3},{2,0},{3,1},{4,6},{5,7},{6,4},{7,5},{8,10},{9,11},{10,... | collective-permute-start | bytes 2359304 | tf_op jit(solution)/shard_map/ppermute | solution.py:643
  248.9 17.8 %all-to-all-start.4 = ((bf16[8,192,128]{2,1,0:T(8,128)(2,1)}), bf16[8,192,128]{2,1,0:T(8,128)(2,1)S(1)}, u32[]{:S(2)}, u32[]{:S(2)}) async-start(bf16[8,192,128]{2,1,0:T(8,128)(2,1)} %get-tuple-element.175), calls=%async_computation.4 | async-start | bytes 786432 | tf_op jit(solution)/shard_map/all_to_all | solution.py:707
  272.8 35.2 %all-to-all-start.5 = ((bf16[8,48,1536]{2,1,0:T(8,128)(2,1)}), bf16[8,48,1536]{2,1,0:T(8,128)(2,1)S(1)}, u32[]{:S(2)}, u32[]{:S(2)}) async-start(bf16[8,48,1536]{2,1,0:T(8,128)(2,1)} %bitcast.284), calls=%async_computation.5 | async-start | bytes 2359296 | tf_op jit(solution)/shard_map/all_to_all | solution.py:707
  279.1 27.4 %collective-permute-start.39 = (bf16[384,1536]{1,0:T(8,128)(2,1)}, bf16[384,1536]{1,0:T(8,128)(2,1)}, u32[]{:S(2)}, u32[]{:S(2)}) collective-permute-start(bf16[384,1536]{1,0:T(8,128)(2,1)} %get-tuple-element.313.refs_1_), channel_id=1, source_target_pairs={{0,2},{1,3},{2,0},{3,1},{4,6},{5,7},{6,4},{7,5},{8,10},{9,11},{10,... | collective-permute-start | bytes 3538952 | tf_op jit(solution)/shard_map/ppermute | solution.py:643
  280.6 27.4 %collective-permute-start.41 = (bf16[1536,256]{1,0:T(8,128)(2,1)}, bf16[1536,256]{1,0:T(8,128)(2,1)}, u32[]{:S(2)}, u32[]{:S(2)}) collective-permute-start(bf16[1536,256]{1,0:T(8,128)(2,1)} %get-tuple-element.326.refs_1_), channel_id=1, source_target_pairs={{0,1},{1,0},{2,3},{3,2},{4,5},{5,4},{6,7},{7,6},{8,9},{9,8},{10,11... | collective-permute-start | bytes 2359304 | tf_op jit(solution)/shard_map/ppermute | solution.py:643
  281.1 26.9 %collective-permute-start.42 = (bf16[256,1536]{1,0:T(8,128)(2,1)}, bf16[256,1536]{1,0:T(8,128)(2,1)}, u32[]{:S(2)}, u32[]{:S(2)}) collective-permute-start(bf16[256,1536]{1,0:T(8,128)(2,1)} %get-tuple-element.324.refs_2_), channel_id=1, source_target_pairs={{0,1},{1,0},{2,3},{3,2},{4,5},{5,4},{6,7},{7,6},{8,9},{9,8},{10,11... | collective-permute-start | bytes 2359304 | tf_op jit(solution)/shard_map/ppermute | solution.py:643
  281.1 26.9 %collective-permute-start.43 = (bf16[1536,256]{1,0:T(8,128)(2,1)}, bf16[1536,256]{1,0:T(8,128)(2,1)}, u32[]{:S(2)}, u32[]{:S(2)}) collective-permute-start(bf16[1536,256]{1,0:T(8,128)(2,1)} %collective-permute-done.23.refs_6_), channel_id=1, source_target_pairs={{0,1},{1,0},{2,3},{3,2},{4,5},{5,4},{6,7},{7,6},{8,9},{9,8},{10,11... | collective-permute-start | bytes 2359304 | tf_op jit(solution)/shard_map/ppermute | solution.py:643
  283.9 24.0 %collective-permute-start.44 = (bf16[1536,256]{1,0:T(8,128)(2,1)}, bf16[1536,256]{1,0:T(8,128)(2,1)}, u32[]{:S(2)}, u32[]{:S(2)}) collective-permute-start(bf16[1536,256]{1,0:T(8,128)(2,1)} %collective-permute-done.33.refs_7_), channel_id=1, source_target_pairs={{0,1},{1,0},{2,3},{3,2},{4,5},{5,4},{6,7},{7,6},{8,9},{9,8},{10,11... | collective-permute-start | bytes 2359304 | tf_op jit(solution)/shard_map/ppermute | solution.py:643
  323.7 37.0 %all-to-all-start.6 = ((bf16[8,48,1664]{2,1,0:T(8,128)(2,1)}), bf16[8,48,1664]{2,1,0:T(8,128)(2,1)}, u32[]{:S(2)}, u32[]{:S(2)}) async-start(bf16[8,48,1664]{2,1,0:T(8,128)(2,1)} %bitcast.277), calls=%async_computation.6 | async-start | bytes 2555904 | tf_op jit(solution)/shard_map/all_to_all | solution.py:707
  331.0 20.6 %collective-permute-start.46 = (bf16[384,1024]{1,0:T(8,128)(2,1)S(1)}, bf16[384,1024]{1,0:T(8,128)(2,1)}, u32[]{:S(2)}, u32[]{:S(2)}) collective-permute-start(bf16[384,1024]{1,0:T(8,128)(2,1)S(1)} %pad_maximum_fusion.1), channel_id=1, source_target_pairs={{0,2},{1,3},{2,0},{3,1},{4,6},{5,7},{6,4},{7,5},{8,10},{9,11},{10,... | collective-permute-start | bytes 2359304 | tf_op jit(solution)/shard_map/ppermute | solution.py:643
  332.6 74.9 %collective-permute-start.49 = (bf16[384,1536]{1,0:T(8,128)(2,1)}, bf16[384,1536]{1,0:T(8,128)(2,1)}, u32[]{:S(2)}, u32[]{:S(2)}) collective-permute-start(bf16[384,1536]{1,0:T(8,128)(2,1)} %get-tuple-element.312.refs_10_), channel_id=1, source_target_pairs={{0,2},{1,3},{2,0},{3,1},{4,6},{5,7},{6,4},{7,5},{8,10},{9,11},{10,... | collective-permute-start | bytes 3538952 | tf_op jit(solution)/shard_map/ppermute | solution.py:643
  334.5 46.6 %collective-permute-start.47 = (bf16[2,384,128]{2,1,0:T(8,128)(2,1)}, bf16[2,384,128]{2,1,0:T(8,128)(2,1)}, u32[]{:S(2)}, u32[]{:S(2)}) collective-permute-start(bf16[2,384,128]{2,1,0:T(8,128)(2,1)} %pad_maximum_fusion.7), channel_id=1, source_target_pairs={{0,2},{1,3},{2,0},{3,1},{4,6},{5,7},{6,4},{7,5},{8,10},{9,11},{10,... | collective-permute-start | bytes 589832 | tf_op jit(solution)/shard_map/ppermute | solution.py:643
  368.3 21.6 %all-to-all-start.7 = ((bf16[8,192,128]{2,1,0:T(8,128)(2,1)}), bf16[8,192,128]{2,1,0:T(8,128)(2,1)S(1)}, u32[]{:S(2)}, u32[]{:S(2)}) async-start(bf16[8,192,128]{2,1,0:T(8,128)(2,1)} %bitcast.298), calls=%async_computation.7 | async-start | bytes 786432 | tf_op jit(solution)/shard_map/all_to_all | solution.py:707
  372.1 16.5 %collective-permute-start.51 = (bf16[128,1536]{1,0:T(8,128)(2,1)}, bf16[128,1536]{1,0:T(8,128)(2,1)}, u32[]{:S(2)}, u32[]{:S(2)}) collective-permute-start(bf16[128,1536]{1,0:T(8,128)(2,1)} %get-tuple-element.199), channel_id=1, source_target_pairs={{0,2},{1,3},{2,0},{3,1},{4,6},{5,7},{6,4},{7,5},{8,10},{9,11},{10,... | collective-permute-start | bytes 1179656 | tf_op jit(solution)/shard_map/ppermute | solution.py:643
  383.7 20.2 %collective-permute-start.50 = (bf16[128,1536]{1,0:T(8,128)(2,1)}, bf16[128,1536]{1,0:T(8,128)(2,1)}, u32[]{:S(2)}, u32[]{:S(2)}) collective-permute-start(bf16[128,1536]{1,0:T(8,128)(2,1)} %get-tuple-element.199), channel_id=1, source_target_pairs={{0,1},{1,0},{2,3},{3,2},{4,5},{5,4},{6,7},{7,6},{8,9},{9,8},{10,11... | collective-permute-start | bytes 1179656 | tf_op jit(solution)/shard_map/ppermute | solution.py:643
  388.6 64.1 %collective-permute-start.54 = (bf16[384,1024]{1,0:T(8,128)(2,1)}, bf16[384,1024]{1,0:T(8,128)(2,1)}, u32[]{:S(2)}, u32[]{:S(2)}) collective-permute-start(bf16[384,1024]{1,0:T(8,128)(2,1)} %copy-done.41), channel_id=1, source_target_pairs={{0,1},{1,0},{2,3},{3,2},{4,5},{5,4},{6,7},{7,6},{8,9},{9,8},{10,11... | collective-permute-start | bytes 2359304 | tf_op jit(solution)/shard_map/ppermute | solution.py:643
  389.1 65.4 %collective-permute-start.53 = (bf16[384,1536]{1,0:T(8,128)(2,1)}, bf16[384,1536]{1,0:T(8,128)(2,1)}, u32[]{:S(2)}, u32[]{:S(2)}) collective-permute-start(bf16[384,1536]{1,0:T(8,128)(2,1)} %get-tuple-element.313.refs_1_), channel_id=1, source_target_pairs={{0,1},{1,0},{2,3},{3,2},{4,5},{5,4},{6,7},{7,6},{8,9},{9,8},{10,11... | collective-permute-start | bytes 3538952 | tf_op jit(solution)/shard_map/ppermute | solution.py:643
  407.5 33.8 %all-to-all-start.8 = ((bf16[8,320,128]{2,1,0:T(8,128)(2,1)}), bf16[8,320,128]{2,1,0:T(8,128)(2,1)}, u32[]{:S(2)}, u32[]{:S(2)}) async-start(bf16[8,320,128]{2,1,0:T(8,128)(2,1)} %get-tuple-element.200), calls=%async_computation.8 | async-start | bytes 1310720 | tf_op jit(solution)/shard_map/all_to_all | solution.py:707
  413.3 100.3 %reduce-scatter.2.cloned.1.call-start = ((), (), s32[]{:S(2)}) async-start(), calls=%async_computation.16 | async-start | bytes 1327104 | tf_op jit(solution)/shard_map/reduce_scatter | solution.py:957
  414.6 48.9 %collective-permute-start.59 = (bf16[384,1024]{1,0:T(8,128)(2,1)}, bf16[384,1024]{1,0:T(8,128)(2,1)}, u32[]{:S(2)}, u32[]{:S(2)}) collective-permute-start(bf16[384,1024]{1,0:T(8,128)(2,1)} %pad_maximum_fusion.2), channel_id=1, source_target_pairs={{0,2},{1,3},{2,0},{3,1},{4,6},{5,7},{6,4},{7,5},{8,10},{9,11},{10,... | collective-permute-start | bytes 2359304 | tf_op jit(solution)/shard_map/ppermute | solution.py:643
  416.1 42.4 %collective-permute-start.55 = (bf16[384,1536]{1,0:T(8,128)(2,1)}, bf16[384,1536]{1,0:T(8,128)(2,1)}, u32[]{:S(2)}, u32[]{:S(2)}) collective-permute-start(bf16[384,1536]{1,0:T(8,128)(2,1)} %collective-permute-done.39), channel_id=1, source_target_pairs={{0,1},{1,0},{2,3},{3,2},{4,5},{5,4},{6,7},{7,6},{8,9},{9,8},{10,11... | collective-permute-start | bytes 3538952 | tf_op jit(solution)/shard_map/ppermute | solution.py:643
  417.2 22.4 %collective-permute-start.58 = (bf16[336,384]{1,0:T(8,128)(2,1)S(1)}, bf16[336,384]{1,0:T(8,128)(2,1)S(1)}, u32[]{:S(2)}, u32[]{:S(2)}) collective-permute-start(bf16[336,384]{1,0:T(8,128)(2,1)S(1)} %fusion.50), channel_id=1, source_target_pairs={{0,2},{1,3},{2,0},{3,1},{4,6},{5,7},{6,4},{7,5},{8,10},{9,11},{10,... | collective-permute-start | bytes 774152 | tf_op jit(solution)/shard_map/ppermute | solution.py:643
  439.6 44.9 %collective-permute-start.60 = (bf16[2,1536,256]{2,1,0:T(8,128)(2,1)}, bf16[2,1536,256]{2,1,0:T(8,128)(2,1)}, u32[]{:S(2)}, u32[]{:S(2)}) collective-permute-start(bf16[2,1536,256]{2,1,0:T(8,128)(2,1)} %get-tuple-element.221), channel_id=1, source_target_pairs={{0,1},{1,0},{2,3},{3,2},{4,5},{5,4},{6,7},{7,6},{8,9},{9,8},{10,11... | collective-permute-start | bytes 4718600 | tf_op jit(solution)/shard_map/ppermute | solution.py:643
  441.3 38.3 %all-to-all-start.9 = ((bf16[8,48,1536]{2,1,0:T(8,128)(2,1)}), bf16[8,48,1536]{2,1,0:T(8,128)(2,1)S(1)}, u32[]{:S(2)}, u32[]{:S(2)}) async-start(bf16[8,48,1536]{2,1,0:T(8,128)(2,1)} %bitcast.278), calls=%async_computation.9 | async-start | bytes 2359296 | tf_op jit(solution)/shard_map/all_to_all | solution.py:707
  479.7 38.3 %all-to-all-start.10 = ((bf16[8,48,1536]{2,1,0:T(8,128)(2,1)}), bf16[8,48,1536]{2,1,0:T(8,128)(2,1)}, u32[]{:S(2)}, u32[]{:S(2)}) async-start(bf16[8,48,1536]{2,1,0:T(8,128)(2,1)} %bitcast.251), calls=%async_computation.10 | async-start | bytes 2359296 | tf_op jit(solution)/shard_map/all_to_all | solution.py:707
  484.4 61.2 %collective-permute-start.63 = (bf16[2,256,1536]{2,1,0:T(8,128)(2,1)}, bf16[2,256,1536]{2,1,0:T(8,128)(2,1)}, u32[]{:S(2)}, u32[]{:S(2)}) collective-permute-start(bf16[2,256,1536]{2,1,0:T(8,128)(2,1)} %get-tuple-element.224), channel_id=1, source_target_pairs={{0,1},{1,0},{2,3},{3,2},{4,5},{5,4},{6,7},{7,6},{8,9},{9,8},{10,11... | collective-permute-start | bytes 4718600 | tf_op jit(solution)/shard_map/ppermute | solution.py:643
  487.9 42.4 %collective-permute-start.61 = (bf16[1536,256]{1,0:T(8,128)(2,1)}, bf16[1536,256]{1,0:T(8,128)(2,1)}, u32[]{:S(2)}, u32[]{:S(2)}) collective-permute-start(bf16[1536,256]{1,0:T(8,128)(2,1)} %get-tuple-element.311), channel_id=1, source_target_pairs={{0,2},{1,3},{2,0},{3,1},{4,6},{5,7},{6,4},{7,5},{8,10},{9,11},{10,... | collective-permute-start | bytes 2359304 | tf_op jit(solution)/shard_map/ppermute | solution.py:643
  489.4 40.9 %collective-permute-start.62 = (bf16[1536,256]{1,0:T(8,128)(2,1)}, bf16[1536,256]{1,0:T(8,128)(2,1)}, u32[]{:S(2)}, u32[]{:S(2)}) collective-permute-start(bf16[1536,256]{1,0:T(8,128)(2,1)} %get-tuple-element.310), channel_id=1, source_target_pairs={{0,2},{1,3},{2,0},{3,1},{4,6},{5,7},{6,4},{7,5},{8,10},{9,11},{10,... | collective-permute-start | bytes 2359304 | tf_op jit(solution)/shard_map/ppermute | solution.py:643
  530.3 45.6 %all-to-all-start.11 = ((bf16[8,48,1536]{2,1,0:T(8,128)(2,1)}), bf16[8,48,1536]{2,1,0:T(8,128)(2,1)}, u32[]{:S(2)}, u32[]{:S(2)}) async-start(bf16[8,48,1536]{2,1,0:T(8,128)(2,1)} %bitcast.282), calls=%async_computation.11 | async-start | bytes 2359296 | tf_op jit(solution)/shard_map/all_to_all | solution.py:707
  534.6 116.3 %all-gather.3.cloned.1.call-start = ((), (), s32[]{:S(2)}) async-start(), calls=%async_computation.17 | async-start | bytes 3649536 | tf_op jit(solution)/shard_map/all_gather | solution.py:905
  545.5 46.4 %collective-permute-start.73 = (bf16[2,1536,256]{2,1,0:T(8,128)(2,1)}, bf16[2,1536,256]{2,1,0:T(8,128)(2,1)}, u32[]{:S(2)}, u32[]{:S(2)}) collective-permute-start(bf16[2,1536,256]{2,1,0:T(8,128)(2,1)} %get-tuple-element.254), channel_id=1, source_target_pairs={{0,1},{1,0},{2,3},{3,2},{4,5},{5,4},{6,7},{7,6},{8,9},{9,8},{10,11... | collective-permute-start | bytes 4718600 | tf_op jit(solution)/shard_map/ppermute | solution.py:643
  547.8 20.2 %collective-permute-start.64 = (bf16[256,1536]{1,0:T(8,128)(2,1)}, bf16[256,1536]{1,0:T(8,128)(2,1)}, u32[]{:S(2)}, u32[]{:S(2)}) collective-permute-start(bf16[256,1536]{1,0:T(8,128)(2,1)} %fusion.30), channel_id=1, source_target_pairs={{0,2},{1,3},{2,0},{3,1},{4,6},{5,7},{6,4},{7,5},{8,10},{9,11},{10,... | collective-permute-start | bytes 2359304 | tf_op jit(solution)/shard_map/ppermute | solution.py:643
  585.4 104.3 %collective-permute-start.70 = (bf16[384,1024]{1,0:T(8,128)(2,1)}, bf16[384,1024]{1,0:T(8,128)(2,1)}, u32[]{:S(2)}, u32[]{:S(2)}) collective-permute-start(bf16[384,1024]{1,0:T(8,128)(2,1)} %pad_maximum_fusion.2), channel_id=1, source_target_pairs={{0,1},{1,0},{2,3},{3,2},{4,5},{5,4},{6,7},{7,6},{8,9},{9,8},{10,11... | collective-permute-start | bytes 2359304 | tf_op jit(solution)/shard_map/ppermute | solution.py:643
  586.7 26.0 %all-to-all-start.12 = ((bf16[8,192,128]{2,1,0:T(8,128)(2,1)}), bf16[8,192,128]{2,1,0:T(8,128)(2,1)}, u32[]{:S(2)}, u32[]{:S(2)}) async-start(bf16[8,192,128]{2,1,0:T(8,128)(2,1)} %bitcast.297), calls=%async_computation.12 | async-start | bytes 786432 | tf_op jit(solution)/shard_map/all_to_all | solution.py:707
  595.5 31.1 %collective-permute-start.74 = (bf16[1536,256]{1,0:T(8,128)(2,1)}, bf16[1536,256]{1,0:T(8,128)(2,1)}, u32[]{:S(2)}, u32[]{:S(2)}) collective-permute-start(bf16[1536,256]{1,0:T(8,128)(2,1)} %get-tuple-element.309), channel_id=1, source_target_pairs={{0,2},{1,3},{2,0},{3,1},{4,6},{5,7},{6,4},{7,5},{8,10},{9,11},{10,... | collective-permute-start | bytes 2359304 | tf_op jit(solution)/shard_map/ppermute | solution.py:643
  597.0 35.6 %collective-permute-start.75 = (bf16[1536,256]{1,0:T(8,128)(2,1)}, bf16[1536,256]{1,0:T(8,128)(2,1)}, u32[]{:S(2)}, u32[]{:S(2)}) collective-permute-start(bf16[1536,256]{1,0:T(8,128)(2,1)} %get-tuple-element.308), channel_id=1, source_target_pairs={{0,2},{1,3},{2,0},{3,1},{4,6},{5,7},{6,4},{7,5},{8,10},{9,11},{10,... | collective-permute-start | bytes 2359304 | tf_op jit(solution)/shard_map/ppermute | solution.py:643
  598.9 104.2 %collective-permute-start.69 = (bf16[384,1536]{1,0:T(8,128)(2,1)}, bf16[384,1536]{1,0:T(8,128)(2,1)}, u32[]{:S(2)}, u32[]{:S(2)}) collective-permute-start(bf16[384,1536]{1,0:T(8,128)(2,1)} %get-tuple-element.312.refs_10_), channel_id=1, source_target_pairs={{0,1},{1,0},{2,3},{3,2},{4,5},{5,4},{6,7},{7,6},{8,9},{9,8},{10,11... | collective-permute-start | bytes 3538952 | tf_op jit(solution)/shard_map/ppermute | solution.py:643
  612.7 44.2 %all-to-all-start.13 = ((bf16[8,48,1536]{2,1,0:T(8,128)(2,1)}), bf16[8,48,1536]{2,1,0:T(8,128)(2,1)}, u32[]{:S(2)}, u32[]{:S(2)}) async-start(bf16[8,48,1536]{2,1,0:T(8,128)(2,1)} %bitcast.281), calls=%async_computation.13 | async-start | bytes 2359296 | tf_op jit(solution)/shard_map/all_to_all | solution.py:707
  617.9 25.5 %collective-permute-start.68 = (bf16[2,1536,256]{2,1,0:T(8,128)(2,1)}, bf16[2,1536,256]{2,1,0:T(8,128)(2,1)S(1)}, u32[]{:S(2)}, u32[]{:S(2)}) collective-permute-start(bf16[2,1536,256]{2,1,0:T(8,128)(2,1)} %get-tuple-element.238), channel_id=1, source_target_pairs={{0,1},{1,0},{2,3},{3,2},{4,5},{5,4},{6,7},{7,6},{8,9},{9,8},{10,11... | collective-permute-start | bytes 4718600 | tf_op jit(solution)/shard_map/ppermute | solution.py:643
  637.2 33.8 %collective-permute-start.86 = (bf16[2,256,1536]{2,1,0:T(8,128)(2,1)}, bf16[2,256,1536]{2,1,0:T(8,128)(2,1)}, u32[]{:S(2)}, u32[]{:S(2)}) collective-permute-start(bf16[2,256,1536]{2,1,0:T(8,128)(2,1)} %get-tuple-element.269), channel_id=1, source_target_pairs={{0,1},{1,0},{2,3},{3,2},{4,5},{5,4},{6,7},{7,6},{8,9},{9,8},{10,11... | collective-permute-start | bytes 4718600 | tf_op jit(solution)/shard_map/ppermute | solution.py:643
  643.4 31.2 %collective-permute-start.88 = (bf16[2,1536,256]{2,1,0:T(8,128)(2,1)}, bf16[2,1536,256]{2,1,0:T(8,128)(2,1)}, u32[]{:S(2)}, u32[]{:S(2)}) collective-permute-start(bf16[2,1536,256]{2,1,0:T(8,128)(2,1)} %get-tuple-element.274), channel_id=1, source_target_pairs={{0,1},{1,0},{2,3},{3,2},{4,5},{5,4},{6,7},{7,6},{8,9},{9,8},{10,11... | collective-permute-start | bytes 4718600 | tf_op jit(solution)/shard_map/ppermute | solution.py:643
  656.9 31.1 %all-to-all-start.14 = ((bf16[8,320,128]{2,1,0:T(8,128)(2,1)}), bf16[8,320,128]{2,1,0:T(8,128)(2,1)S(1)}, u32[]{:S(2)}, u32[]{:S(2)}) async-start(bf16[8,320,128]{2,1,0:T(8,128)(2,1)} %get-tuple-element.245), calls=%async_computation.14 | async-start | bytes 1310720 | tf_op jit(solution)/shard_map/all_to_all | solution.py:707
  671.0 17.1 %collective-permute-start.79 = (bf16[528,384]{1,0:T(8,128)(2,1)S(1)}, bf16[528,384]{1,0:T(8,128)(2,1)}, u32[]{:S(2)}, u32[]{:S(2)}) collective-permute-start(bf16[528,384]{1,0:T(8,128)(2,1)S(1)} %slice_dynamic-update-slice_fusion.4.refs_1_), channel_id=1, source_target_pairs={{8,0},{16,8},{24,16},{28,24},{20,28},{12,20},{4,12},{0,4},{9,1},{1... | collective-permute-start | bytes 1216520 | tf_op jit(solution)/shard_map/ppermute | solution.py:687
  674.6 17.3 %collective-permute-start.72 = (bf16[384,1024]{1,0:T(8,128)(2,1)}, bf16[384,1024]{1,0:T(8,128)(2,1)}, u32[]{:S(2)}, u32[]{:S(2)}) collective-permute-start(bf16[384,1024]{1,0:T(8,128)(2,1)} %collective-permute-done.59), channel_id=1, source_target_pairs={{0,1},{1,0},{2,3},{3,2},{4,5},{5,4},{6,7},{7,6},{8,9},{9,8},{10,11... | collective-permute-start | bytes 2359304 | tf_op jit(solution)/shard_map/ppermute | solution.py:643
  689.8 17.0 %collective-permute-start.71 = (bf16[384,1536]{1,0:T(8,128)(2,1)}, bf16[384,1536]{1,0:T(8,128)(2,1)S(1)}, u32[]{:S(2)}, u32[]{:S(2)}) collective-permute-start(bf16[384,1536]{1,0:T(8,128)(2,1)} %collective-permute-done.49), channel_id=1, source_target_pairs={{0,1},{1,0},{2,3},{3,2},{4,5},{5,4},{6,7},{7,6},{8,9},{9,8},{10,11... | collective-permute-start | bytes 3538952 | tf_op jit(solution)/shard_map/ppermute | solution.py:643
  691.8 20.4 %collective-permute-start.87 = (bf16[256,1536]{1,0:T(8,128)(2,1)S(1)}, bf16[256,1536]{1,0:T(8,128)(2,1)S(1)}, u32[]{:S(2)}, u32[]{:S(2)}) collective-permute-start(bf16[256,1536]{1,0:T(8,128)(2,1)S(1)} %bitcast.286), channel_id=1, source_target_pairs={{0,2},{1,3},{2,0},{3,1},{4,6},{5,7},{6,4},{7,5},{8,10},{9,11},{10,... | collective-permute-start | bytes 2359304 | tf_op jit(solution)/shard_map/ppermute | solution.py:643
  (172 other events, 1714.8 us)
Sparse Core Ops, SparseCore 0:
  427.2 86.4 reduce-scatter.1
  537.6 79.8 all-gather.2

commit v5 on v4

--- a/solution.py
+++ b/solution.py
@@ -901,7 +901,7 @@
             arrived, inner = k["arrived"], k["inner"]
             back_rows = (gates * upstream[None]).astype(jnp.bfloat16).reshape(2 * rows, width)
             outgoing = times(place[layer].reshape(2 * rows, slot_count), back_rows, 0, 0).astype(jnp.bfloat16)
-            outgoing, returned, head_sum, key_far[layer] = tie(outgoing, returned, sources[0], key_far[layer])
+            outgoing, returned, head_sum, query_far[layer] = tie(outgoing, returned, sources[0], query_far[layer])
             sources = [lax.all_gather(merge(head_sum, sources[1]), "ctx", axis=0)]
             arrived_grad = all_to_all(outgoing.reshape(experts, capacity, width)).reshape(slot_count, width)
             state = saved[last]["middle"] + sum(
@@ -953,7 +953,7 @@
             out_rows = all_to_all(out_part.reshape(n_ctx, part // n_ctx, width))
             grad_sent, out_rows, *expert_done = tie(grad_sent, out_rows, *expert_done)
         else:
-            grad_sent, query_far[0], out_part = tie(grad_sent, query_far[0], out_part)
+            grad_sent, out_part = tie(grad_sent, out_part)
             out_rows = lax.psum_scatter(out_part, "ctx", scatter_dimension=0, tiled=True)
         grad_own = all_to_all(grad_sent)
         if layer == 0:

time: 748 us -> 755 us (level)
  waiting for transfers between devices: 294 us -> 302 us
    ppermute x65, waiting for transfers between devices: 139 us -> 156 us  [swap(): return lax.ppermute(x, 'wt', [(i, i ^ mask) for i in range(4)])]
    reduce_scatter x1, waiting for transfers between devices: 23 us -> 5.93 us  [local_heads(): lax.psum_scatter(out_part, 'ctx', scatter_dimension=0, tiled=True)]
    all_to_all x15, waiting for transfers between devices: 78.2 us -> 89.6 us  [all_to_all(): return lax.all_to_all(x, 'ctx', split_axis=0, concat_axis=0, tiled=True)]
    unnamed x271 -> x267, local copies, waits for them, and re-layouts: 18.3 us -> 19.6 us
  transfers between devices with their start and end apart: 106 -> 106, of which waited for: 47 -> 48; matrix products, arithmetic and copies ran while one was open for 15% -> 14% of each run, Pallas kernels for 17% -> 17%
where the time goes in v5:
time: 755 us; the launch traced here: 744 us
  waiting for transfers between devices  302 us (40%)
  Pallas kernels  158 us (21%)
  starting transfers between devices  144 us (19%)
  local copies, waits for them, and re-layouts  49.3 us (7%)
  other arithmetic  40.2 us (5%)
  matrix products  33.4 us (4%)
  between operations  16.4 us (2%)
    ppermute x65, waiting for transfers between devices, swap(): return lax.ppermute(x, 'wt', [(i, i ^ mask) for i in range(4)])  156 us
    all_to_all x15, waiting for transfers between devices, all_to_all(): return lax.all_to_all(x, 'ctx', split_axis=0, concat_axis=0, tiled=True)  89.6 us
    all_to_all x15, starting transfers between devices, all_to_all(): return lax.all_to_all(x, 'ctx', split_axis=0, concat_axis=0, tiled=True)  77.5 us
    ppermute x65, starting transfers between devices, swap(): return lax.ppermute(x, 'wt', [(i, i ^ mask) for i in range(4)])  36.6 us
    dot_general x26, matrix products, times(): lax.dot_general(left, right, (((a,), (b,)), ((), ())), preferred_element_...  33.2 us
    ppermute x6, waiting for transfers between devices, ring_blocks(): lax.ppermute(ahead, 'ctx', right)  26.7 us
    pallas_call x2, Pallas kernels, front(): pl.pallas_call(functools.partial(front_kernel, raw, rep, head, span, base...  22.8 us
    unnamed x267, local copies, waits for them, and re-layouts  19.6 us
  transfers between devices with their start and end apart: 106, of which 48 were waited for; matrix products, arithmetic and copies ran while one was open for 14% of the time, Pallas kernels for 17%

profile of v5, /device:TPU:0, one launch (start us, length us, event | category | flops | bytes accessed | tf_op | source)
XLA Modules:
  0.0 744.0 jit_solution(4236602921168708378)
XLA Ops:
  22.5 7.4 %collective-permute-done.7.refs_12_ = bf16[672,384]{1,0:T(8,128)(2,1)} collective-permute-done((bf16[672,384]{1,0:T(8,128)(2,1)}, bf16[672,384]{1,0:T(8,128)(2,1)}, u32[]{:S(2)}, u32[]{:S(2)}) %collective-permute-start.7) | collective-permute-done | bytes 516128 | tf_op jit(solution)/shard_map/ppermute | solution.py:643
  34.0 8.7 %collective-permute-done.4.refs_5_ = bf16[128,1536]{1,0:T(8,128)(2,1)S(1)} collective-permute-done((bf16[128,1536]{1,0:T(8,128)(2,1)}, bf16[128,1536]{1,0:T(8,128)(2,1)S(1)}, u32[]{:S(2)}, u32[]{:S(2)}) %collective-permute-start.4) | collective-permute-done | bytes 393248 | tf_op jit(solution)/shard_map/ppermute | solution.py:697
  51.8 4.3 all-to-all-start
  65.6 12.0 %front.2 = (bf16[8,128,1536]{2,1,0:T(8,128)(2,1)}, bf16[320,1024]{1,0:T(8,128)(2,1)}, bf16[8,192,128]{2,1,0:T(8,128)(2,1)}, f32[192,1024]{1,0:T(8,128)}, f32[3,1024]{1,0:T(4,128)}) custom-call(s32[8]{0:T(128)} %get-tuple-element.299.spot_ref, s32[8]{0:T(128)} %get-tuple-element.298.owner_ref, s32[4]{0:T(128)} %xor_convert_fusion.at_ref, ...), custom_call_target="tpu_custom_call" | custom-call | flops 1509949440 | bytes 9437184 | tf_op jit(solution)/shard_map/front/pallas_call | solution.py:130
  77.6 8.0 %all-to-all-done = bf16[8,48,1664]{2,1,0:T(8,128)(2,1)} async-done(((bf16[8,48,1664]{2,1,0:T(8,128)(2,1)}), bf16[8,48,1664]{2,1,0:T(8,128)(2,1)}, u32[]{:S(2)}, u32[]{:S(2)}) %all-to-all-start) | async-done | bytes 1277984 | tf_op jit(solution)/shard_map/all_to_all | solution.py:707
  85.6 3.7 all-to-all-start.1
  93.2 7.9 %all-to-all-done.1 = bf16[8,192,128]{2,1,0:T(8,128)(2,1)S(1)} async-done(((bf16[8,192,128]{2,1,0:T(8,128)(2,1)}), bf16[8,192,128]{2,1,0:T(8,128)(2,1)S(1)}, u32[]{:S(2)}, u32[]{:S(2)}) %all-to-all-start.1) | async-done | bytes 393248 | tf_op jit(solution)/shard_map/all_to_all | solution.py:707
  108.9 5.3 middle_forward.2
  114.3 4.3 all-to-all-start.2
  122.6 6.4 collective-permute-done.18.refs_7_.refs_9_
  129.0 16.3 %collective-permute-done.19.refs_8_.refs_10_ = bf16[256,1536]{1,0:T(8,128)(2,1)S(1)} collective-permute-done((bf16[256,1536]{1,0:T(8,128)(2,1)S(1)}, bf16[256,1536]{1,0:T(8,128)(2,1)S(1)}, u32[]{:S(2)}, u32[]{:S(2)}) %collective-permute-start.19) | collective-permute-done | bytes 786464 | tf_op jit(solution)/shard_map/ppermute | solution.py:643
  150.0 10.1 %expert_forward.1 = (bf16[384,1536]{1,0:T(8,128)(2,1)}, f32[4,384,256]{2,1,0:T(8,128)}, f32[4,384,256]{2,1,0:T(8,128)}, bf16[4,384,256]{2,1,0:T(8,128)(2,1)}) custom-call(bf16[384,1536]{1,0:T(8,128)(2,1)} %bitcast.30.rows_ref, bf16[1536,256]{1,0:T(8,128)(2,1)} %copy-done.23, bf16[1536,256]{1,0:T(8,128)(2,1)} %get-tuple-element.325.refs_1_.refs_3_, ...), custom_call_target="tpu_custom_call" | custom-call | flops 3623878656 | bytes 16777216 | tf_op jit(solution)/shard_map/expert_forward/pallas_call | solution.py:251
  160.1 6.1 all-to-all-start.3
  170.0 15.9 %collective-permute-done.23.refs_6_ = bf16[1536,256]{1,0:T(8,128)(2,1)} collective-permute-done((bf16[1536,256]{1,0:T(8,128)(2,1)}, bf16[1536,256]{1,0:T(8,128)(2,1)}, u32[]{:S(2)}, u32[]{:S(2)}) %collective-permute-start.23) | collective-permute-done | bytes 786464 | tf_op jit(solution)/shard_map/ppermute | solution.py:643
  185.9 9.3 %all-to-all-done.3 = bf16[8,48,1536]{2,1,0:T(8,128)(2,1)S(1)} async-done(((bf16[8,48,1536]{2,1,0:T(8,128)(2,1)}), bf16[8,48,1536]{2,1,0:T(8,128)(2,1)S(1)}, u32[]{:S(2)}, u32[]{:S(2)}) %all-to-all-start.3) | async-done | bytes 1179680 | tf_op jit(solution)/shard_map/all_to_all | solution.py:707
  201.8 6.5 collective-permute-done.24.refs_1_
  211.8 5.7 collective-permute-done.26.refs_3_
  219.6 6.2 collective-permute-done.28.refs_5_
  235.1 10.8 %front.3 = (bf16[8,128,1536]{2,1,0:T(8,128)(2,1)}, bf16[320,1024]{1,0:T(8,128)(2,1)}, bf16[8,192,128]{2,1,0:T(8,128)(2,1)}, f32[192,1024]{1,0:T(8,128)}, f32[3,1024]{1,0:T(4,128)}) custom-call(s32[8]{0:T(128)} %get-tuple-element.299.spot_ref, s32[8]{0:T(128)} %get-tuple-element.298.owner_ref, s32[4]{0:T(128)} %xor_convert_fusion.at_ref, ...), custom_call_target="tpu_custom_call" | custom-call | flops 1509949440 | bytes 9437184 | tf_op jit(solution)/shard_map/front/pallas_call | solution.py:130
  248.9 6.1 all-to-all-start.4
  257.9 8.8 %all-to-all-done.4 = bf16[8,192,128]{2,1,0:T(8,128)(2,1)S(1)} async-done(((bf16[8,192,128]{2,1,0:T(8,128)(2,1)}), bf16[8,192,128]{2,1,0:T(8,128)(2,1)S(1)}, u32[]{:S(2)}, u32[]{:S(2)}) %all-to-all-start.4) | async-done | bytes 393248 | tf_op jit(solution)/shard_map/all_to_all | solution.py:707
  267.4 5.3 middle_forward.3
  272.8 4.6 all-to-all-start.5
  284.0 22.6 %collective-permute-done.39 = bf16[384,1536]{1,0:T(8,128)(2,1)} collective-permute-done((bf16[384,1536]{1,0:T(8,128)(2,1)}, bf16[384,1536]{1,0:T(8,128)(2,1)}, u32[]{:S(2)}, u32[]{:S(2)}) %collective-permute-start.39) | collective-permute-done | bytes 1179680 | tf_op jit(solution)/shard_map/ppermute | solution.py:643
  309.2 14.6 %expert_both.1 = (bf16[384,1536]{1,0:T(8,128)(2,1)}, bf16[384,1664]{1,0:T(8,128)(2,1)}, bf16[384,1536]{1,0:T(8,128)(2,1)}, bf16[4,384,256]{2,1,0:T(8,128)(2,1)},...) custom-call(s32[1]{0:T(128)} %bitcast.3.at_ref.mine_ref, bf16[384,1536]{1,0:T(8,128)(2,1)} %bitcast.279, ...), custom_call_target="tpu_custom_call" | custom-call | flops 7247757312 | bytes 18874368 | tf_op jit(solution)/shard_map/expert_both/pallas_call | solution.py:350
  323.8 5.9 all-to-all-start.6
  336.2 16.2 %collective-permute-done.46 = bf16[384,1024]{1,0:T(8,128)(2,1)} collective-permute-done((bf16[384,1024]{1,0:T(8,128)(2,1)S(1)}, bf16[384,1024]{1,0:T(8,128)(2,1)}, u32[]{:S(2)}, u32[]{:S(2)}) %collective-permute-start.46) | collective-permute-done | bytes 786464 | tf_op jit(solution)/shard_map/ppermute | solution.py:643
  352.5 8.4 %all-to-all-done.6 = bf16[8,48,1664]{2,1,0:T(8,128)(2,1)} async-done(((bf16[8,48,1664]{2,1,0:T(8,128)(2,1)}), bf16[8,48,1664]{2,1,0:T(8,128)(2,1)}, u32[]{:S(2)}, u32[]{:S(2)}) %all-to-all-start.6) | async-done | bytes 1277984 | tf_op jit(solution)/shard_map/all_to_all | solution.py:707
  360.9 7.6 %middle_back.2 = (f32[128,1536]{1,0:T(8,128)}, bf16[128,1536]{1,0:T(8,128)(2,1)}, bf16[1536,128]{1,0:T(8,128)(2,1)}, f32[16,1536]{1,0:T(8,128)}) custom-call(s32[4]{0:T(128)} %xor_convert_fusion.at_ref, bf16[2,128,384]{2,1,0:T(8,128)(2,1)} %get-tuple-element.346.place_ref, bf16[384,1664]{1,0:T(8,128)(2,1)} %bitcast.58.back_ref, ...), custom_call_target="tpu_custom_call" | custom-call | flops 754974720 | bytes 10485760 | tf_op jit(solution)/shard_map/middle_back/pallas_call | solution.py:626
  368.4 3.9 all-to-all-start.7
  375.1 8.3 %collective-permute-done.50 = bf16[128,1536]{1,0:T(8,128)(2,1)} collective-permute-done((bf16[128,1536]{1,0:T(8,128)(2,1)}, bf16[128,1536]{1,0:T(8,128)(2,1)}, u32[]{:S(2)}, u32[]{:S(2)}) %collective-permute-start.50) | collective-permute-done | bytes 393248 | tf_op jit(solution)/shard_map/ppermute | solution.py:643
  384.9 8.7 %attend_back.2 = (bf16[320,1024]{1,0:T(8,128)(2,1)}, bf16[8,320,128]{2,1,0:T(8,128)(2,1)}) custom-call(s32[8]{0:T(128)} %get-tuple-element.298.owner_ref, bf16[320,1024]{1,0:T(8,128)(2,1)} %get-tuple-element.188.qkv_ref, f32[192,1024]{1,0:T(8,128)} %get-tuple-element.189.exact_ref, f32[3,1024]{1,0:T(4,128)} %get-tuple-element.190.log_ref, ...), custom_call_target="tpu_custom_call" | custom-call | flops 1258291200 | bytes 6291456 | tf_op jit(solution)/shard_map/attend_back/pallas_call | solution.py:195
  393.6 4.5 head_grads.2
  401.2 5.6 all-to-all-start.8
  411.4 9.2 %expert_grads.2 = (bf16[2,1536,256]{2,1,0:T(8,128)(2,1)}, bf16[2,1536,256]{2,1,0:T(8,128)(2,1)}, bf16[2,1536,256]{2,1,0:T(8,128)(2,1)}, bf16[2,1536,256]{2,1,0:T...) custom-call(bf16[384,1536]{1,0:T(8,128)(2,1)} %bitcast.280, ...), custom_call_target="tpu_custom_call" | custom-call | flops 3623878656 | bytes 14680064 | tf_op jit(solution)/shard_map/expert_grads/pallas_call | solution.py:388
  420.6 20.8 %collective-permute-done.57 = bf16[336,384]{1,0:T(8,128)(2,1)} collective-permute-done((bf16[336,384]{1,0:T(8,128)(2,1)}, bf16[336,384]{1,0:T(8,128)(2,1)}, u32[]{:S(2)}, u32[]{:S(2)}) %collective-permute-start.57) | collective-permute-done | bytes 258080 | tf_op jit(solution)/shard_map/ppermute | solution.py:643
  444.1 5.9 all-to-all-start.9
  466.5 12.8 %all-to-all-done.9 = bf16[8,48,1536]{2,1,0:T(8,128)(2,1)S(1)} async-done(((bf16[8,48,1536]{2,1,0:T(8,128)(2,1)}), bf16[8,48,1536]{2,1,0:T(8,128)(2,1)S(1)}, u32[]{:S(2)}, u32[]{:S(2)}) %all-to-all-start.9) | async-done | bytes 1179680 | tf_op jit(solution)/shard_map/all_to_all | solution.py:707
  479.4 4.7 all-to-all-start.10
  484.2 3.4 fusion.29
  490.4 5.9 reduce-scatter.2.cloned.1.call-done
  500.4 15.1 %all-to-all-done.10 = bf16[8,48,1536]{2,1,0:T(8,128)(2,1)} async-done(((bf16[8,48,1536]{2,1,0:T(8,128)(2,1)}), bf16[8,48,1536]{2,1,0:T(8,128)(2,1)}, u32[]{:S(2)}, u32[]{:S(2)}) %all-to-all-start.10) | async-done | bytes 1179680 | tf_op jit(solution)/shard_map/all_to_all | solution.py:707
  515.6 12.4 %expert_backward.1 = (bf16[384,1536]{1,0:T(8,128)(2,1)}, bf16[4,384,256]{2,1,0:T(8,128)(2,1)}, bf16[4,384,256]{2,1,0:T(8,128)(2,1)}) custom-call(bf16[384,1536]{1,0:T(8,128)(2,1)} %bitcast.80.grad_ref, f32[4,384,256]{2,1,0:T(8,128)} %get-tuple-element.212.refs_0_, f32[4,384,256]{2,1,0:T(8,128)} %get-tuple-element.213.refs_1_, bf16[1536,256]{1,0:T(8,128)(2,1)} %copy-done.23, ...), custom_call_target="tpu_custom_call" | custom-call | flops 3623878656 | bytes 16777216 | tf_op jit(solution)/shard_map/expert_backward/pallas_call | solution.py:289
  527.9 4.3 all-to-all-start.11
  533.9 9.3 %expert_grads.3 = (bf16[2,1536,256]{2,1,0:T(8,128)(2,1)}, bf16[2,1536,256]{2,1,0:T(8,128)(2,1)}, bf16[2,1536,256]{2,1,0:T(8,128)(2,1)}, bf16[2,1536,256]{2,1,0:T...) custom-call(bf16[384,1536]{1,0:T(8,128)(2,1)} %bitcast.30.rows_ref, ...), custom_call_target="tpu_custom_call" | custom-call | flops 3623878656 | bytes 14680064 | tf_op jit(solution)/shard_map/expert_grads/pallas_call | solution.py:388
  549.2 16.5 %collective-permute-done.63.refs_2_ = bf16[256,1536]{1,0:T(8,128)(2,1)} collective-permute-done((bf16[256,1536]{1,0:T(8,128)(2,1)}, bf16[256,1536]{1,0:T(8,128)(2,1)}, u32[]{:S(2)}, u32[]{:S(2)}) %collective-permute-start.63) | collective-permute-done | bytes 786464 | tf_op jit(solution)/shard_map/ppermute | solution.py:643
  565.7 7.9 %all-to-all-done.11 = bf16[8,48,1536]{2,1,0:T(8,128)(2,1)} async-done(((bf16[8,48,1536]{2,1,0:T(8,128)(2,1)}), bf16[8,48,1536]{2,1,0:T(8,128)(2,1)}, u32[]{:S(2)}, u32[]{:S(2)}) %all-to-all-start.11) | async-done | bytes 1179680 | tf_op jit(solution)/shard_map/all_to_all | solution.py:707
  573.6 8.0 %middle_back.3 = (f32[128,1536]{1,0:T(8,128)}, bf16[128,1536]{1,0:T(8,128)(2,1)}, bf16[1536,128]{1,0:T(8,128)(2,1)}, f32[16,1536]{1,0:T(8,128)}) custom-call(s32[4]{0:T(128)} %xor_convert_fusion.at_ref, bf16[2,128,384]{2,1,0:T(8,128)(2,1)} %get-tuple-element.347.place_ref, bf16[384,1536]{1,0:T(8,128)(2,1)} %bitcast.84.back_ref, f32[128,1536]{1,0:T(8,128)} %copy-done.5, ...), custom_call_target="tpu_custom_call" | custom-call | flops 754974720 | bytes 10485760 | tf_op jit(solution)/shard_map/middle_back/pallas_call | solution.py:626
  585.4 4.1 all-to-all-start.12
  589.5 4.5 collective-permute-done.65
  594.1 3.4 fusion.32
  604.0 6.6 all-to-all-done.12.grad_ref
  610.6 5.8 all-to-all-start.13
  617.2 8.7 %attend_back.3 = (bf16[320,1024]{1,0:T(8,128)(2,1)}, bf16[8,320,128]{2,1,0:T(8,128)(2,1)}) custom-call(s32[8]{0:T(128)} %get-tuple-element.298.owner_ref, bf16[320,1024]{1,0:T(8,128)(2,1)} %get-tuple-element.226.qkv_ref, f32[192,1024]{1,0:T(8,128)} %get-tuple-element.227.exact_ref, f32[3,1024]{1,0:T(4,128)} %get-tuple-element.228.log_ref, ...), custom_call_target="tpu_custom_call" | custom-call | flops 1258291200 | bytes 6291456 | tf_op jit(solution)/shard_map/attend_back/pallas_call | solution.py:195
  626.7 12.4 %collective-permute-done.75.refs_3_ = bf16[1536,256]{1,0:T(8,128)(2,1)} collective-permute-done((bf16[1536,256]{1,0:T(8,128)(2,1)}, bf16[1536,256]{1,0:T(8,128)(2,1)}, u32[]{:S(2)}, u32[]{:S(2)}) %collective-permute-start.75) | collective-permute-done | bytes 786464 | tf_op jit(solution)/shard_map/ppermute | solution.py:643
  639.1 4.5 head_grads.3
  650.7 3.6 finish.4
  657.1 6.0 spread.2
  663.1 8.3 %all-to-all-start.14 = ((bf16[8,320,128]{2,1,0:T(8,128)(2,1)}), bf16[8,320,128]{2,1,0:T(8,128)(2,1)S(1)}, u32[]{:S(2)}, u32[]{:S(2)}) async-start(bf16[8,320,128]{2,1,0:T(8,128)(2,1)} %get-tuple-element.244), calls=%async_computation.14 | async-start | bytes 1310720 | tf_op jit(solution)/shard_map/all_to_all | solution.py:707
  682.3 3.7 finish.6
  686.0 4.1 all-to-all-done.14
  690.7 5.0 collective-permute-start.80
  713.0 3.3 collective-permute-done.82.refs_6_
  726.0 6.4 spread.3
  (576 shorter events, 215.0 us)
Async XLA Ops:
  15.3 18.6 %collective-permute-start.6 = (bf16[672,384]{1,0:T(8,128)(2,1)}, bf16[672,384]{1,0:T(8,128)(2,1)S(1)}, u32[]{:S(2)}, u32[]{:S(2)}) collective-permute-start(bf16[672,384]{1,0:T(8,128)(2,1)} %bitcast.287), channel_id=1, source_target_pairs={{0,1},{1,0},{2,3},{3,2},{4,5},{5,4},{6,7},{7,6},{8,9},{9,8},{10,11... | collective-permute-start | bytes 1548296 | tf_op jit(solution)/shard_map/ppermute | solution.py:643
  51.8 33.8 %all-to-all-start = ((bf16[8,48,1664]{2,1,0:T(8,128)(2,1)}), bf16[8,48,1664]{2,1,0:T(8,128)(2,1)}, u32[]{:S(2)}, u32[]{:S(2)}) async-start(bf16[8,48,1664]{2,1,0:T(8,128)(2,1)} %bitcast.17), calls=%async_computation | async-start | bytes 2555904 | tf_op jit(solution)/shard_map/all_to_all | solution.py:707
  58.0 35.3 %collective-permute-start.11 = (bf16[384,1536]{1,0:T(8,128)(2,1)S(1)}, bf16[384,1536]{1,0:T(8,128)(2,1)}, u32[]{:S(2)}, u32[]{:S(2)}) collective-permute-start(bf16[384,1536]{1,0:T(8,128)(2,1)S(1)} %get-tuple-element.313.refs_0_.refs_2_), channel_id=1, source_target_pairs={{0,2},{1,3},{2,0},{3,1},{4,6},{5,7},{6,4},{7,5},{8,10},{9,11},{10,... | collective-permute-start | bytes 3538952 | tf_op jit(solution)/shard_map/ppermute | solution.py:643
  85.6 15.5 %all-to-all-start.1 = ((bf16[8,192,128]{2,1,0:T(8,128)(2,1)}), bf16[8,192,128]{2,1,0:T(8,128)(2,1)S(1)}, u32[]{:S(2)}, u32[]{:S(2)}) async-start(bf16[8,192,128]{2,1,0:T(8,128)(2,1)} %get-tuple-element.163), calls=%async_computation.1 | async-start | bytes 786432 | tf_op jit(solution)/shard_map/all_to_all | solution.py:707
  89.3 18.6 %collective-permute-start.12 = (bf16[384,1536]{1,0:T(8,128)(2,1)S(1)}, bf16[384,1536]{1,0:T(8,128)(2,1)}, u32[]{:S(2)}, u32[]{:S(2)}) collective-permute-start(bf16[384,1536]{1,0:T(8,128)(2,1)S(1)} %get-tuple-element.313.refs_0_.refs_2_), channel_id=1, source_target_pairs={{0,1},{1,0},{2,3},{3,2},{4,5},{5,4},{6,7},{7,6},{8,9},{9,8},{10,11... | collective-permute-start | bytes 3538952 | tf_op jit(solution)/shard_map/ppermute | solution.py:643
  91.7 22.5 %collective-permute-start.14 = (bf16[1536,256]{1,0:T(8,128)(2,1)S(1)}, bf16[1536,256]{1,0:T(8,128)(2,1)}, u32[]{:S(2)}, u32[]{:S(2)}) collective-permute-start(bf16[1536,256]{1,0:T(8,128)(2,1)S(1)} %get-tuple-element.327.refs_0_.refs_2_), channel_id=1, source_target_pairs={{0,2},{1,3},{2,0},{3,1},{4,6},{5,7},{6,4},{7,5},{8,10},{9,11},{10,... | collective-permute-start | bytes 2359304 | tf_op jit(solution)/shard_map/ppermute | solution.py:643
  104.0 25.1 %collective-permute-start.18 = (bf16[1536,256]{1,0:T(8,128)(2,1)}, bf16[1536,256]{1,0:T(8,128)(2,1)}, u32[]{:S(2)}, u32[]{:S(2)}) collective-permute-start(bf16[1536,256]{1,0:T(8,128)(2,1)} %get-tuple-element.325.refs_1_.refs_3_), channel_id=1, source_target_pairs={{0,2},{1,3},{2,0},{3,1},{4,6},{5,7},{6,4},{7,5},{8,10},{9,11},{10,... | collective-permute-start | bytes 2359304 | tf_op jit(solution)/shard_map/ppermute | solution.py:643
  114.3 34.8 %all-to-all-start.2 = ((bf16[8,48,1536]{2,1,0:T(8,128)(2,1)}), bf16[8,48,1536]{2,1,0:T(8,128)(2,1)}, u32[]{:S(2)}, u32[]{:S(2)}) async-start(bf16[8,48,1536]{2,1,0:T(8,128)(2,1)} %bitcast.283), calls=%async_computation.2 | async-start | bytes 2359296 | tf_op jit(solution)/shard_map/all_to_all | solution.py:707
  121.0 24.4 %collective-permute-start.19 = (bf16[256,1536]{1,0:T(8,128)(2,1)S(1)}, bf16[256,1536]{1,0:T(8,128)(2,1)S(1)}, u32[]{:S(2)}, u32[]{:S(2)}) collective-permute-start(bf16[256,1536]{1,0:T(8,128)(2,1)S(1)} %get-tuple-element.323.refs_2_.refs_4_), channel_id=1, source_target_pairs={{0,2},{1,3},{2,0},{3,1},{4,6},{5,7},{6,4},{7,5},{8,10},{9,11},{10,... | collective-permute-start | bytes 2359304 | tf_op jit(solution)/shard_map/ppermute | solution.py:643
  122.1 23.3 %collective-permute-start.15 = (bf16[1536,256]{1,0:T(8,128)(2,1)S(1)}, bf16[1536,256]{1,0:T(8,128)(2,1)S(1)}, u32[]{:S(2)}, u32[]{:S(2)}) collective-permute-start(bf16[1536,256]{1,0:T(8,128)(2,1)S(1)} %get-tuple-element.327.refs_0_.refs_2_), channel_id=1, source_target_pairs={{0,1},{1,0},{2,3},{3,2},{4,5},{5,4},{6,7},{7,6},{8,9},{9,8},{10,11... | collective-permute-start | bytes 2359304 | tf_op jit(solution)/shard_map/ppermute | solution.py:643
  122.1 23.8 %collective-permute-start.16 = (bf16[1536,256]{1,0:T(8,128)(2,1)}, bf16[1536,256]{1,0:T(8,128)(2,1)S(1)}, u32[]{:S(2)}, u32[]{:S(2)}) collective-permute-start(bf16[1536,256]{1,0:T(8,128)(2,1)} %get-tuple-element.325.refs_1_.refs_3_), channel_id=1, source_target_pairs={{0,1},{1,0},{2,3},{3,2},{4,5},{5,4},{6,7},{7,6},{8,9},{9,8},{10,11... | collective-permute-start | bytes 2359304 | tf_op jit(solution)/shard_map/ppermute | solution.py:643
  122.6 23.3 %collective-permute-start.17 = (bf16[256,1536]{1,0:T(8,128)(2,1)S(1)}, bf16[256,1536]{1,0:T(8,128)(2,1)S(1)}, u32[]{:S(2)}, u32[]{:S(2)}) collective-permute-start(bf16[256,1536]{1,0:T(8,128)(2,1)S(1)} %get-tuple-element.323.refs_2_.refs_4_), channel_id=1, source_target_pairs={{0,1},{1,0},{2,3},{3,2},{4,5},{5,4},{6,7},{7,6},{8,9},{9,8},{10,11... | collective-permute-start | bytes 2359304 | tf_op jit(solution)/shard_map/ppermute | solution.py:643
  129.0 17.2 %collective-permute-start.21 = (bf16[1536,256]{1,0:T(8,128)(2,1)}, bf16[1536,256]{1,0:T(8,128)(2,1)S(1)}, u32[]{:S(2)}, u32[]{:S(2)}) collective-permute-start(bf16[1536,256]{1,0:T(8,128)(2,1)} %collective-permute-done.18.refs_7_.refs_9_), channel_id=1, source_target_pairs={{0,1},{1,0},{2,3},{3,2},{4,5},{5,4},{6,7},{7,6},{8,9},{9,8},{10,11... | collective-permute-start | bytes 2359304 | tf_op jit(solution)/shard_map/ppermute | solution.py:643
  160.1 35.0 %all-to-all-start.3 = ((bf16[8,48,1536]{2,1,0:T(8,128)(2,1)}), bf16[8,48,1536]{2,1,0:T(8,128)(2,1)S(1)}, u32[]{:S(2)}, u32[]{:S(2)}) async-start(bf16[8,48,1536]{2,1,0:T(8,128)(2,1)} %bitcast.285), calls=%async_computation.3 | async-start | bytes 2359296 | tf_op jit(solution)/shard_map/all_to_all | solution.py:707
  166.3 19.6 %collective-permute-start.23 = (bf16[1536,256]{1,0:T(8,128)(2,1)}, bf16[1536,256]{1,0:T(8,128)(2,1)}, u32[]{:S(2)}, u32[]{:S(2)}) collective-permute-start(bf16[1536,256]{1,0:T(8,128)(2,1)} %get-tuple-element.326.refs_0_), channel_id=1, source_target_pairs={{0,2},{1,3},{2,0},{3,1},{4,6},{5,7},{6,4},{7,5},{8,10},{9,11},{10,... | collective-permute-start | bytes 2359304 | tf_op jit(solution)/shard_map/ppermute | solution.py:643
  200.3 45.6 %collective-permute-start.32 = (bf16[384,1536]{1,0:T(8,128)(2,1)S(1)}, bf16[384,1536]{1,0:T(8,128)(2,1)S(1)}, u32[]{:S(2)}, u32[]{:S(2)}) collective-permute-start(bf16[384,1536]{1,0:T(8,128)(2,1)S(1)} %get-tuple-element.312.refs_0_), channel_id=1, source_target_pairs={{0,2},{1,3},{2,0},{3,1},{4,6},{5,7},{6,4},{7,5},{8,10},{9,11},{10,... | collective-permute-start | bytes 3538952 | tf_op jit(solution)/shard_map/ppermute | solution.py:643
  210.3 35.6 %collective-permute-start.33 = (bf16[1536,256]{1,0:T(8,128)(2,1)}, bf16[1536,256]{1,0:T(8,128)(2,1)}, u32[]{:S(2)}, u32[]{:S(2)}) collective-permute-start(bf16[1536,256]{1,0:T(8,128)(2,1)} %get-tuple-element.324.refs_1_), channel_id=1, source_target_pairs={{0,2},{1,3},{2,0},{3,1},{4,6},{5,7},{6,4},{7,5},{8,10},{9,11},{10,... | collective-permute-start | bytes 2359304 | tf_op jit(solution)/shard_map/ppermute | solution.py:643
  230.4 27.5 %collective-permute-start.34 = (bf16[384,1536]{1,0:T(8,128)(2,1)S(1)}, bf16[384,1536]{1,0:T(8,128)(2,1)}, u32[]{:S(2)}, u32[]{:S(2)}) collective-permute-start(bf16[384,1536]{1,0:T(8,128)(2,1)S(1)} %get-tuple-element.312.refs_0_), channel_id=1, source_target_pairs={{0,1},{1,0},{2,3},{3,2},{4,5},{5,4},{6,7},{7,6},{8,9},{9,8},{10,11... | collective-permute-start | bytes 3538952 | tf_op jit(solution)/shard_map/ppermute | solution.py:643
  245.9 20.8 %collective-permute-start.35 = (bf16[384,1536]{1,0:T(8,128)(2,1)S(1)}, bf16[384,1536]{1,0:T(8,128)(2,1)}, u32[]{:S(2)}, u32[]{:S(2)}) collective-permute-start(bf16[384,1536]{1,0:T(8,128)(2,1)S(1)} %collective-permute-done.32.refs_2_), channel_id=1, source_target_pairs={{0,1},{1,0},{2,3},{3,2},{4,5},{5,4},{6,7},{7,6},{8,9},{9,8},{10,11... | collective-permute-start | bytes 3538952 | tf_op jit(solution)/shard_map/ppermute | solution.py:643
  248.4 24.3 %collective-permute-start.36 = (bf16[256,1536]{1,0:T(8,128)(2,1)}, bf16[256,1536]{1,0:T(8,128)(2,1)}, u32[]{:S(2)}, u32[]{:S(2)}) collective-permute-start(bf16[256,1536]{1,0:T(8,128)(2,1)} %get-tuple-element.322.refs_2_), channel_id=1, source_target_pairs={{0,2},{1,3},{2,0},{3,1},{4,6},{5,7},{6,4},{7,5},{8,10},{9,11},{10,... | collective-permute-start | bytes 2359304 | tf_op jit(solution)/shard_map/ppermute | solution.py:643
  248.9 17.7 %all-to-all-start.4 = ((bf16[8,192,128]{2,1,0:T(8,128)(2,1)}), bf16[8,192,128]{2,1,0:T(8,128)(2,1)S(1)}, u32[]{:S(2)}, u32[]{:S(2)}) async-start(bf16[8,192,128]{2,1,0:T(8,128)(2,1)} %get-tuple-element.174), calls=%async_computation.4 | async-start | bytes 786432 | tf_op jit(solution)/shard_map/all_to_all | solution.py:707
  272.8 35.2 %all-to-all-start.5 = ((bf16[8,48,1536]{2,1,0:T(8,128)(2,1)}), bf16[8,48,1536]{2,1,0:T(8,128)(2,1)S(1)}, u32[]{:S(2)}, u32[]{:S(2)}) async-start(bf16[8,48,1536]{2,1,0:T(8,128)(2,1)} %bitcast.284), calls=%async_computation.5 | async-start | bytes 2359296 | tf_op jit(solution)/shard_map/all_to_all | solution.py:707
  279.1 27.4 %collective-permute-start.39 = (bf16[384,1536]{1,0:T(8,128)(2,1)}, bf16[384,1536]{1,0:T(8,128)(2,1)}, u32[]{:S(2)}, u32[]{:S(2)}) collective-permute-start(bf16[384,1536]{1,0:T(8,128)(2,1)} %get-tuple-element.311.refs_1_), channel_id=1, source_target_pairs={{0,2},{1,3},{2,0},{3,1},{4,6},{5,7},{6,4},{7,5},{8,10},{9,11},{10,... | collective-permute-start | bytes 3538952 | tf_op jit(solution)/shard_map/ppermute | solution.py:643
  280.5 27.5 %collective-permute-start.41 = (bf16[1536,256]{1,0:T(8,128)(2,1)}, bf16[1536,256]{1,0:T(8,128)(2,1)}, u32[]{:S(2)}, u32[]{:S(2)}) collective-permute-start(bf16[1536,256]{1,0:T(8,128)(2,1)} %get-tuple-element.324.refs_1_), channel_id=1, source_target_pairs={{0,1},{1,0},{2,3},{3,2},{4,5},{5,4},{6,7},{7,6},{8,9},{9,8},{10,11... | collective-permute-start | bytes 2359304 | tf_op jit(solution)/shard_map/ppermute | solution.py:643
  281.0 27.0 %collective-permute-start.42 = (bf16[256,1536]{1,0:T(8,128)(2,1)}, bf16[256,1536]{1,0:T(8,128)(2,1)}, u32[]{:S(2)}, u32[]{:S(2)}) collective-permute-start(bf16[256,1536]{1,0:T(8,128)(2,1)} %get-tuple-element.322.refs_2_), channel_id=1, source_target_pairs={{0,1},{1,0},{2,3},{3,2},{4,5},{5,4},{6,7},{7,6},{8,9},{9,8},{10,11... | collective-permute-start | bytes 2359304 | tf_op jit(solution)/shard_map/ppermute | solution.py:643
  281.0 27.0 %collective-permute-start.43 = (bf16[1536,256]{1,0:T(8,128)(2,1)}, bf16[1536,256]{1,0:T(8,128)(2,1)}, u32[]{:S(2)}, u32[]{:S(2)}) collective-permute-start(bf16[1536,256]{1,0:T(8,128)(2,1)} %collective-permute-done.23.refs_6_), channel_id=1, source_target_pairs={{0,1},{1,0},{2,3},{3,2},{4,5},{5,4},{6,7},{7,6},{8,9},{9,8},{10,11... | collective-permute-start | bytes 2359304 | tf_op jit(solution)/shard_map/ppermute | solution.py:643
  283.8 24.2 %collective-permute-start.44 = (bf16[1536,256]{1,0:T(8,128)(2,1)}, bf16[1536,256]{1,0:T(8,128)(2,1)}, u32[]{:S(2)}, u32[]{:S(2)}) collective-permute-start(bf16[1536,256]{1,0:T(8,128)(2,1)} %collective-permute-done.33.refs_7_), channel_id=1, source_target_pairs={{0,1},{1,0},{2,3},{3,2},{4,5},{5,4},{6,7},{7,6},{8,9},{9,8},{10,11... | collective-permute-start | bytes 2359304 | tf_op jit(solution)/shard_map/ppermute | solution.py:643
  323.8 37.1 %all-to-all-start.6 = ((bf16[8,48,1664]{2,1,0:T(8,128)(2,1)}), bf16[8,48,1664]{2,1,0:T(8,128)(2,1)}, u32[]{:S(2)}, u32[]{:S(2)}) async-start(bf16[8,48,1664]{2,1,0:T(8,128)(2,1)} %bitcast.277), calls=%async_computation.6 | async-start | bytes 2555904 | tf_op jit(solution)/shard_map/all_to_all | solution.py:707
  331.9 20.6 %collective-permute-start.46 = (bf16[384,1024]{1,0:T(8,128)(2,1)S(1)}, bf16[384,1024]{1,0:T(8,128)(2,1)}, u32[]{:S(2)}, u32[]{:S(2)}) collective-permute-start(bf16[384,1024]{1,0:T(8,128)(2,1)S(1)} %pad_maximum_fusion.1), channel_id=1, source_target_pairs={{0,2},{1,3},{2,0},{3,1},{4,6},{5,7},{6,4},{7,5},{8,10},{9,11},{10,... | collective-permute-start | bytes 2359304 | tf_op jit(solution)/shard_map/ppermute | solution.py:643
  334.1 39.8 %collective-permute-start.47 = (bf16[2,384,128]{2,1,0:T(8,128)(2,1)S(1)}, bf16[2,384,128]{2,1,0:T(8,128)(2,1)S(1)}, u32[]{:S(2)}, u32[]{:S(2)}) collective-permute-start(bf16[2,384,128]{2,1,0:T(8,128)(2,1)S(1)} %pad_maximum_fusion.7), channel_id=1, source_target_pairs={{0,2},{1,3},{2,0},{3,1},{4,6},{5,7},{6,4},{7,5},{8,10},{9,11},{10,... | collective-permute-start | bytes 589832 | tf_op jit(solution)/shard_map/ppermute | solution.py:643
  368.4 15.7 %all-to-all-start.7 = ((bf16[8,192,128]{2,1,0:T(8,128)(2,1)}), bf16[8,192,128]{2,1,0:T(8,128)(2,1)S(1)}, u32[]{:S(2)}, u32[]{:S(2)}) async-start(bf16[8,192,128]{2,1,0:T(8,128)(2,1)} %bitcast.298), calls=%async_computation.7 | async-start | bytes 786432 | tf_op jit(solution)/shard_map/all_to_all | solution.py:707
  374.6 23.5 %collective-permute-start.49 = (bf16[128,1536]{1,0:T(8,128)(2,1)}, bf16[128,1536]{1,0:T(8,128)(2,1)}, u32[]{:S(2)}, u32[]{:S(2)}) collective-permute-start(bf16[128,1536]{1,0:T(8,128)(2,1)} %get-tuple-element.198), channel_id=1, source_target_pairs={{0,1},{1,0},{2,3},{3,2},{4,5},{5,4},{6,7},{7,6},{8,9},{9,8},{10,11... | collective-permute-start | bytes 1179656 | tf_op jit(solution)/shard_map/ppermute | solution.py:643
  401.2 42.1 %all-to-all-start.8 = ((bf16[8,320,128]{2,1,0:T(8,128)(2,1)}), bf16[8,320,128]{2,1,0:T(8,128)(2,1)S(1)}, u32[]{:S(2)}, u32[]{:S(2)}) async-start(bf16[8,320,128]{2,1,0:T(8,128)(2,1)} %get-tuple-element.199), calls=%async_computation.8 | async-start | bytes 1310720 | tf_op jit(solution)/shard_map/all_to_all | solution.py:707
  406.7 89.6 %reduce-scatter.2.cloned.1.call-start = ((), (), s32[]{:S(2)}) async-start(), calls=%async_computation.16 | async-start | bytes 1327104 | tf_op jit(solution)/shard_map/reduce_scatter | solution.py:957
  407.0 48.7 %collective-permute-start.53 = (bf16[384,1024]{1,0:T(8,128)(2,1)}, bf16[384,1024]{1,0:T(8,128)(2,1)}, u32[]{:S(2)}, u32[]{:S(2)}) collective-permute-start(bf16[384,1024]{1,0:T(8,128)(2,1)} %copy-done.43), channel_id=1, source_target_pairs={{0,1},{1,0},{2,3},{3,2},{4,5},{5,4},{6,7},{7,6},{8,9},{9,8},{10,11... | collective-permute-start | bytes 2359304 | tf_op jit(solution)/shard_map/ppermute | solution.py:643
  407.1 50.4 %collective-permute-start.52 = (bf16[384,1536]{1,0:T(8,128)(2,1)}, bf16[384,1536]{1,0:T(8,128)(2,1)}, u32[]{:S(2)}, u32[]{:S(2)}) collective-permute-start(bf16[384,1536]{1,0:T(8,128)(2,1)} %get-tuple-element.311.refs_1_), channel_id=1, source_target_pairs={{0,1},{1,0},{2,3},{3,2},{4,5},{5,4},{6,7},{7,6},{8,9},{9,8},{10,11... | collective-permute-start | bytes 3538952 | tf_op jit(solution)/shard_map/ppermute | solution.py:643
  407.6 58.9 %collective-permute-start.58 = (bf16[384,1536]{1,0:T(8,128)(2,1)}, bf16[384,1536]{1,0:T(8,128)(2,1)}, u32[]{:S(2)}, u32[]{:S(2)}) collective-permute-start(bf16[384,1536]{1,0:T(8,128)(2,1)} %get-tuple-element.310.refs_10_), channel_id=1, source_target_pairs={{0,2},{1,3},{2,0},{3,1},{4,6},{5,7},{6,4},{7,5},{8,10},{9,11},{10,... | collective-permute-start | bytes 3538952 | tf_op jit(solution)/shard_map/ppermute | solution.py:643
  409.1 52.5 %collective-permute-start.54 = (bf16[384,1536]{1,0:T(8,128)(2,1)}, bf16[384,1536]{1,0:T(8,128)(2,1)}, u32[]{:S(2)}, u32[]{:S(2)}) collective-permute-start(bf16[384,1536]{1,0:T(8,128)(2,1)} %collective-permute-done.39), channel_id=1, source_target_pairs={{0,1},{1,0},{2,3},{3,2},{4,5},{5,4},{6,7},{7,6},{8,9},{9,8},{10,11... | collective-permute-start | bytes 3538952 | tf_op jit(solution)/shard_map/ppermute | solution.py:643
  410.8 30.6 %collective-permute-start.57 = (bf16[336,384]{1,0:T(8,128)(2,1)}, bf16[336,384]{1,0:T(8,128)(2,1)}, u32[]{:S(2)}, u32[]{:S(2)}) collective-permute-start(bf16[336,384]{1,0:T(8,128)(2,1)} %fusion.50), channel_id=1, source_target_pairs={{0,2},{1,3},{2,0},{3,1},{4,6},{5,7},{6,4},{7,5},{8,10},{9,11},{10,... | collective-permute-start | bytes 774152 | tf_op jit(solution)/shard_map/ppermute | solution.py:643
  441.4 42.7 %collective-permute-start.59 = (bf16[2,1536,256]{2,1,0:T(8,128)(2,1)}, bf16[2,1536,256]{2,1,0:T(8,128)(2,1)}, u32[]{:S(2)}, u32[]{:S(2)}) collective-permute-start(bf16[2,1536,256]{2,1,0:T(8,128)(2,1)} %get-tuple-element.220), channel_id=1, source_target_pairs={{0,1},{1,0},{2,3},{3,2},{4,5},{5,4},{6,7},{7,6},{8,9},{9,8},{10,11... | collective-permute-start | bytes 4718600 | tf_op jit(solution)/shard_map/ppermute | solution.py:643
  444.1 35.2 %all-to-all-start.9 = ((bf16[8,48,1536]{2,1,0:T(8,128)(2,1)}), bf16[8,48,1536]{2,1,0:T(8,128)(2,1)S(1)}, u32[]{:S(2)}, u32[]{:S(2)}) async-start(bf16[8,48,1536]{2,1,0:T(8,128)(2,1)} %bitcast.278), calls=%async_computation.9 | async-start | bytes 2359296 | tf_op jit(solution)/shard_map/all_to_all | solution.py:707
  479.4 36.2 %all-to-all-start.10 = ((bf16[8,48,1536]{2,1,0:T(8,128)(2,1)}), bf16[8,48,1536]{2,1,0:T(8,128)(2,1)}, u32[]{:S(2)}, u32[]{:S(2)}) async-start(bf16[8,48,1536]{2,1,0:T(8,128)(2,1)} %bitcast.251), calls=%async_computation.10 | async-start | bytes 2359296 | tf_op jit(solution)/shard_map/all_to_all | solution.py:707
  484.1 59.1 %collective-permute-start.62 = (bf16[2,256,1536]{2,1,0:T(8,128)(2,1)}, bf16[2,256,1536]{2,1,0:T(8,128)(2,1)}, u32[]{:S(2)}, u32[]{:S(2)}) collective-permute-start(bf16[2,256,1536]{2,1,0:T(8,128)(2,1)} %get-tuple-element.223), channel_id=1, source_target_pairs={{0,1},{1,0},{2,3},{3,2},{4,5},{5,4},{6,7},{7,6},{8,9},{9,8},{10,11... | collective-permute-start | bytes 4718600 | tf_op jit(solution)/shard_map/ppermute | solution.py:643
  487.6 40.3 %collective-permute-start.60 = (bf16[1536,256]{1,0:T(8,128)(2,1)}, bf16[1536,256]{1,0:T(8,128)(2,1)}, u32[]{:S(2)}, u32[]{:S(2)}) collective-permute-start(bf16[1536,256]{1,0:T(8,128)(2,1)} %get-tuple-element.309), channel_id=1, source_target_pairs={{0,2},{1,3},{2,0},{3,1},{4,6},{5,7},{6,4},{7,5},{8,10},{9,11},{10,... | collective-permute-start | bytes 2359304 | tf_op jit(solution)/shard_map/ppermute | solution.py:643
  489.1 38.8 %collective-permute-start.61 = (bf16[1536,256]{1,0:T(8,128)(2,1)}, bf16[1536,256]{1,0:T(8,128)(2,1)}, u32[]{:S(2)}, u32[]{:S(2)}) collective-permute-start(bf16[1536,256]{1,0:T(8,128)(2,1)} %get-tuple-element.308), channel_id=1, source_target_pairs={{0,2},{1,3},{2,0},{3,1},{4,6},{5,7},{6,4},{7,5},{8,10},{9,11},{10,... | collective-permute-start | bytes 2359304 | tf_op jit(solution)/shard_map/ppermute | solution.py:643
  527.9 45.7 %all-to-all-start.11 = ((bf16[8,48,1536]{2,1,0:T(8,128)(2,1)}), bf16[8,48,1536]{2,1,0:T(8,128)(2,1)}, u32[]{:S(2)}, u32[]{:S(2)}) async-start(bf16[8,48,1536]{2,1,0:T(8,128)(2,1)} %bitcast.282), calls=%async_computation.11 | async-start | bytes 2359296 | tf_op jit(solution)/shard_map/all_to_all | solution.py:707
  532.2 124.9 %all-gather.3.cloned.1.call-start = ((), (), s32[]{:S(2)}) async-start(), calls=%async_computation.17 | async-start | bytes 3649536 | tf_op jit(solution)/shard_map/all_gather | solution.py:905
  543.2 50.8 %collective-permute-start.73 = (bf16[2,1536,256]{2,1,0:T(8,128)(2,1)}, bf16[2,1536,256]{2,1,0:T(8,128)(2,1)}, u32[]{:S(2)}, u32[]{:S(2)}) collective-permute-start(bf16[2,1536,256]{2,1,0:T(8,128)(2,1)} %get-tuple-element.252), channel_id=1, source_target_pairs={{0,1},{1,0},{2,3},{3,2},{4,5},{5,4},{6,7},{7,6},{8,9},{9,8},{10,11... | collective-permute-start | bytes 4718600 | tf_op jit(solution)/shard_map/ppermute | solution.py:643
  545.5 20.3 %collective-permute-start.63 = (bf16[256,1536]{1,0:T(8,128)(2,1)}, bf16[256,1536]{1,0:T(8,128)(2,1)}, u32[]{:S(2)}, u32[]{:S(2)}) collective-permute-start(bf16[256,1536]{1,0:T(8,128)(2,1)} %fusion.30), channel_id=1, source_target_pairs={{0,2},{1,3},{2,0},{3,1},{4,6},{5,7},{6,4},{7,5},{8,10},{9,11},{10,... | collective-permute-start | bytes 2359304 | tf_op jit(solution)/shard_map/ppermute | solution.py:643
  584.1 106.0 %collective-permute-start.70 = (bf16[384,1024]{1,0:T(8,128)(2,1)}, bf16[384,1024]{1,0:T(8,128)(2,1)}, u32[]{:S(2)}, u32[]{:S(2)}) collective-permute-start(bf16[384,1024]{1,0:T(8,128)(2,1)} %pad_maximum_fusion.2), channel_id=1, source_target_pairs={{0,2},{1,3},{2,0},{3,1},{4,6},{5,7},{6,4},{7,5},{8,10},{9,11},{10,... | collective-permute-start | bytes 2359304 | tf_op jit(solution)/shard_map/ppermute | solution.py:643
  585.4 25.2 %all-to-all-start.12 = ((bf16[8,192,128]{2,1,0:T(8,128)(2,1)}), bf16[8,192,128]{2,1,0:T(8,128)(2,1)}, u32[]{:S(2)}, u32[]{:S(2)}) async-start(bf16[8,192,128]{2,1,0:T(8,128)(2,1)} %bitcast.297), calls=%async_computation.12 | async-start | bytes 786432 | tf_op jit(solution)/shard_map/all_to_all | solution.py:707
  597.5 29.2 %collective-permute-start.74 = (bf16[1536,256]{1,0:T(8,128)(2,1)}, bf16[1536,256]{1,0:T(8,128)(2,1)}, u32[]{:S(2)}, u32[]{:S(2)}) collective-permute-start(bf16[1536,256]{1,0:T(8,128)(2,1)} %get-tuple-element.307), channel_id=1, source_target_pairs={{0,2},{1,3},{2,0},{3,1},{4,6},{5,7},{6,4},{7,5},{8,10},{9,11},{10,... | collective-permute-start | bytes 2359304 | tf_op jit(solution)/shard_map/ppermute | solution.py:643
  598.9 40.2 %collective-permute-start.75 = (bf16[1536,256]{1,0:T(8,128)(2,1)}, bf16[1536,256]{1,0:T(8,128)(2,1)}, u32[]{:S(2)}, u32[]{:S(2)}) collective-permute-start(bf16[1536,256]{1,0:T(8,128)(2,1)} %get-tuple-element.306), channel_id=1, source_target_pairs={{0,2},{1,3},{2,0},{3,1},{4,6},{5,7},{6,4},{7,5},{8,10},{9,11},{10,... | collective-permute-start | bytes 2359304 | tf_op jit(solution)/shard_map/ppermute | solution.py:643
  610.6 52.5 %all-to-all-start.13 = ((bf16[8,48,1536]{2,1,0:T(8,128)(2,1)}), bf16[8,48,1536]{2,1,0:T(8,128)(2,1)}, u32[]{:S(2)}, u32[]{:S(2)}) async-start(bf16[8,48,1536]{2,1,0:T(8,128)(2,1)} %bitcast.281), calls=%async_computation.13 | async-start | bytes 2359296 | tf_op jit(solution)/shard_map/all_to_all | solution.py:707
  617.1 32.4 %collective-permute-start.67 = (bf16[2,1536,256]{2,1,0:T(8,128)(2,1)}, bf16[2,1536,256]{2,1,0:T(8,128)(2,1)S(1)}, u32[]{:S(2)}, u32[]{:S(2)}) collective-permute-start(bf16[2,1536,256]{2,1,0:T(8,128)(2,1)} %get-tuple-element.237), channel_id=1, source_target_pairs={{0,1},{1,0},{2,3},{3,2},{4,5},{5,4},{6,7},{7,6},{8,9},{9,8},{10,11... | collective-permute-start | bytes 4718600 | tf_op jit(solution)/shard_map/ppermute | solution.py:643
  643.7 46.5 %collective-permute-start.71 = (bf16[384,1536]{1,0:T(8,128)(2,1)}, bf16[384,1536]{1,0:T(8,128)(2,1)}, u32[]{:S(2)}, u32[]{:S(2)}) collective-permute-start(bf16[384,1536]{1,0:T(8,128)(2,1)} %collective-permute-done.58), channel_id=1, source_target_pairs={{0,1},{1,0},{2,3},{3,2},{4,5},{5,4},{6,7},{7,6},{8,9},{9,8},{10,11... | collective-permute-start | bytes 3538952 | tf_op jit(solution)/shard_map/ppermute | solution.py:643
  644.2 34.4 %collective-permute-start.86 = (bf16[2,256,1536]{2,1,0:T(8,128)(2,1)}, bf16[2,256,1536]{2,1,0:T(8,128)(2,1)}, u32[]{:S(2)}, u32[]{:S(2)}) collective-permute-start(bf16[2,256,1536]{2,1,0:T(8,128)(2,1)} %get-tuple-element.267), channel_id=1, source_target_pairs={{0,1},{1,0},{2,3},{3,2},{4,5},{5,4},{6,7},{7,6},{8,9},{9,8},{10,11... | collective-permute-start | bytes 4718600 | tf_op jit(solution)/shard_map/ppermute | solution.py:643
  649.5 32.7 %collective-permute-start.88 = (bf16[2,1536,256]{2,1,0:T(8,128)(2,1)}, bf16[2,1536,256]{2,1,0:T(8,128)(2,1)}, u32[]{:S(2)}, u32[]{:S(2)}) collective-permute-start(bf16[2,1536,256]{2,1,0:T(8,128)(2,1)} %get-tuple-element.272), channel_id=1, source_target_pairs={{0,1},{1,0},{2,3},{3,2},{4,5},{5,4},{6,7},{7,6},{8,9},{9,8},{10,11... | collective-permute-start | bytes 4718600 | tf_op jit(solution)/shard_map/ppermute | solution.py:643
  663.1 27.0 %all-to-all-start.14 = ((bf16[8,320,128]{2,1,0:T(8,128)(2,1)}), bf16[8,320,128]{2,1,0:T(8,128)(2,1)S(1)}, u32[]{:S(2)}, u32[]{:S(2)}) async-start(bf16[8,320,128]{2,1,0:T(8,128)(2,1)} %get-tuple-element.244), calls=%async_computation.14 | async-start | bytes 1310720 | tf_op jit(solution)/shard_map/all_to_all | solution.py:707
  678.7 17.1 %collective-permute-start.79 = (bf16[528,384]{1,0:T(8,128)(2,1)S(1)}, bf16[528,384]{1,0:T(8,128)(2,1)}, u32[]{:S(2)}, u32[]{:S(2)}) collective-permute-start(bf16[528,384]{1,0:T(8,128)(2,1)S(1)} %slice_dynamic-update-slice_fusion.4.refs_1_), channel_id=1, source_target_pairs={{8,0},{16,8},{24,16},{28,24},{20,28},{12,20},{4,12},{0,4},{9,1},{1... | collective-permute-start | bytes 1216520 | tf_op jit(solution)/shard_map/ppermute | solution.py:687
  682.3 18.2 %collective-permute-start.69 = (bf16[384,1024]{1,0:T(8,128)(2,1)}, bf16[384,1024]{1,0:T(8,128)(2,1)}, u32[]{:S(2)}, u32[]{:S(2)}) collective-permute-start(bf16[384,1024]{1,0:T(8,128)(2,1)} %pad_maximum_fusion.2), channel_id=1, source_target_pairs={{0,1},{1,0},{2,3},{3,2},{4,5},{5,4},{6,7},{7,6},{8,9},{9,8},{10,11... | collective-permute-start | bytes 2359304 | tf_op jit(solution)/shard_map/ppermute | solution.py:643
  690.1 19.7 %collective-permute-start.68 = (bf16[384,1536]{1,0:T(8,128)(2,1)}, bf16[384,1536]{1,0:T(8,128)(2,1)S(1)}, u32[]{:S(2)}, u32[]{:S(2)}) collective-permute-start(bf16[384,1536]{1,0:T(8,128)(2,1)} %get-tuple-element.310.refs_10_), channel_id=1, source_target_pairs={{0,1},{1,0},{2,3},{3,2},{4,5},{5,4},{6,7},{7,6},{8,9},{9,8},{10,11... | collective-permute-start | bytes 3538952 | tf_op jit(solution)/shard_map/ppermute | solution.py:643
  690.2 22.1 %collective-permute-start.72 = (bf16[384,1024]{1,0:T(8,128)(2,1)}, bf16[384,1024]{1,0:T(8,128)(2,1)S(1)}, u32[]{:S(2)}, u32[]{:S(2)}) collective-permute-start(bf16[384,1024]{1,0:T(8,128)(2,1)} %collective-permute-done.70), channel_id=1, source_target_pairs={{0,1},{1,0},{2,3},{3,2},{4,5},{5,4},{6,7},{7,6},{8,9},{9,8},{10,11... | collective-permute-start | bytes 2359304 | tf_op jit(solution)/shard_map/ppermute | solution.py:643
  700.9 18.7 %collective-permute-start.87 = (bf16[256,1536]{1,0:T(8,128)(2,1)S(1)}, bf16[256,1536]{1,0:T(8,128)(2,1)S(1)}, u32[]{:S(2)}, u32[]{:S(2)}) collective-permute-start(bf16[256,1536]{1,0:T(8,128)(2,1)S(1)} %bitcast.286), channel_id=1, source_target_pairs={{0,2},{1,3},{2,0},{3,1},{4,6},{5,7},{6,4},{7,5},{8,10},{9,11},{10,... | collective-permute-start | bytes 2359304 | tf_op jit(solution)/shard_map/ppermute | solution.py:643
  (170 other events, 1519.8 us)
Sparse Core Ops, SparseCore 0:
  420.7 75.5 reduce-scatter.1
  535.2 79.9 all-gather.2

commit v6 on v4

--- a/solution.py
+++ b/solution.py
@@ -976,10 +976,10 @@
             *head_done, smalls[last], gain_sums[last] = columns(last, None, sources, None)
             out_rows = jnp.sum(out_rows.astype(jnp.float32), axis=0).astype(jnp.bfloat16)
             merged = merge(head_sum, out_rows)
-            merged, *head_done = tie(merged, *head_done)
             down_last = [swap(tie(down_sum, head_last)[0][0], 2)]
             sources = ring_blocks(merged, ring_start(merged, ring), ring)
-            *sources[-2:], down_last[0] = tie(*sources[-2:], down_last[0])
+            *tied, down_last[0] = tie(*sources[-2:], *head_done, down_last[0])
+            sources[-2:], head_done = tied[:2], tied[2:]
             pair_done = finish(layer, layers, pair_own, pair_near, pair_last, expert_done[:2])
             down_done = finish(layer, layers, down_kept, down_near, down_last, expert_done[2:])
             expert_done = [*pair_done, *down_done]

time: 748 us -> 757 us (1.012)
  waiting for transfers between devices: 294 us -> 309 us
    all_to_all x15, waiting for transfers between devices: 78.2 us -> 93.5 us  [all_to_all(): return lax.all_to_all(x, 'ctx', split_axis=0, concat_axis=0, tiled=True)]
  transfers between devices with their start and end apart: 106 -> 106, of which waited for: 47 -> 45; matrix products, arithmetic and copies ran while one was open for 15% -> 14% of each run, Pallas kernels for 17% -> 17%
where the time goes in v6:
time: 757 us; the launch traced here: 746 us
  waiting for transfers between devices  309 us (41%)
  Pallas kernels  158 us (21%)
  starting transfers between devices  140 us (18%)
  local copies, waits for them, and re-layouts  46.6 us (6%)
  other arithmetic  41.1 us (5%)
  matrix products  34.6 us (5%)
  between operations  16.4 us (2%)
    ppermute x65, waiting for transfers between devices, swap(): return lax.ppermute(x, 'wt', [(i, i ^ mask) for i in range(4)])  136 us
    all_to_all x15, waiting for transfers between devices, all_to_all(): return lax.all_to_all(x, 'ctx', split_axis=0, concat_axis=0, tiled=True)  93.5 us
    all_to_all x15, starting transfers between devices, all_to_all(): return lax.all_to_all(x, 'ctx', split_axis=0, concat_axis=0, tiled=True)  71.8 us
    ppermute x65, starting transfers between devices, swap(): return lax.ppermute(x, 'wt', [(i, i ^ mask) for i in range(4)])  38.9 us
    dot_general x26, matrix products, times(): lax.dot_general(left, right, (((a,), (b,)), ((), ())), preferred_element_...  34.3 us
    reduce_scatter x1, waiting for transfers between devices, local_heads(): lax.psum_scatter(out_part, 'ctx', scatter_dimension=0, tiled=True)  29.5 us
    ppermute x6, waiting for transfers between devices, ring_blocks(): lax.ppermute(ahead, 'ctx', right)  25.5 us
    pallas_call x2, Pallas kernels, front(): pl.pallas_call(functools.partial(front_kernel, raw, rep, head, span, base...  22.8 us
  transfers between devices with their start and end apart: 106, of which 45 were waited for; matrix products, arithmetic and copies ran while one was open for 14% of the time, Pallas kernels for 17%

profile of v6, /device:TPU:0, one launch (start us, length us, event | category | flops | bytes accessed | tf_op | source)
XLA Modules:
  0.0 746.0 jit_solution(13038228646528435352)
XLA Ops:
  7.2 3.1 collective-permute-start
  22.5 7.5 collective-permute-done.7.refs_12_
  34.0 8.7 %collective-permute-done.4.refs_5_ = bf16[128,1536]{1,0:T(8,128)(2,1)S(1)} collective-permute-done((bf16[128,1536]{1,0:T(8,128)(2,1)}, bf16[128,1536]{1,0:T(8,128)(2,1)S(1)}, u32[]{:S(2)}, u32[]{:S(2)}) %collective-permute-start.4) | collective-permute-done | bytes 393248 | tf_op jit(solution)/shard_map/ppermute | solution.py:697
  51.8 4.3 all-to-all-start
  65.6 12.0 %front.2 = (bf16[8,128,1536]{2,1,0:T(8,128)(2,1)}, bf16[320,1024]{1,0:T(8,128)(2,1)}, bf16[8,192,128]{2,1,0:T(8,128)(2,1)}, f32[192,1024]{1,0:T(8,128)}, f32[3,1024]{1,0:T(4,128)}) custom-call(s32[8]{0:T(128)} %get-tuple-element.299.spot_ref, s32[8]{0:T(128)} %get-tuple-element.298.owner_ref, s32[4]{0:T(128)} %xor_convert_fusion.at_ref, ...), custom_call_target="tpu_custom_call" | custom-call | flops 1509949440 | bytes 9437184 | tf_op jit(solution)/shard_map/front/pallas_call | solution.py:130
  77.6 8.1 %all-to-all-done = bf16[8,48,1664]{2,1,0:T(8,128)(2,1)} async-done(((bf16[8,48,1664]{2,1,0:T(8,128)(2,1)}), bf16[8,48,1664]{2,1,0:T(8,128)(2,1)}, u32[]{:S(2)}, u32[]{:S(2)}) %all-to-all-start) | async-done | bytes 1277984 | tf_op jit(solution)/shard_map/all_to_all | solution.py:707
  85.6 3.7 all-to-all-start.1
  93.3 7.8 %all-to-all-done.1 = bf16[8,192,128]{2,1,0:T(8,128)(2,1)S(1)} async-done(((bf16[8,192,128]{2,1,0:T(8,128)(2,1)}), bf16[8,192,128]{2,1,0:T(8,128)(2,1)S(1)}, u32[]{:S(2)}, u32[]{:S(2)}) %all-to-all-start.1) | async-done | bytes 393248 | tf_op jit(solution)/shard_map/all_to_all | solution.py:707
  108.9 5.3 middle_forward.2
  114.3 4.2 all-to-all-start.2
  122.6 6.5 collective-permute-done.18.refs_7_.refs_9_
  129.1 16.3 %collective-permute-done.19.refs_8_.refs_10_ = bf16[256,1536]{1,0:T(8,128)(2,1)S(1)} collective-permute-done((bf16[256,1536]{1,0:T(8,128)(2,1)S(1)}, bf16[256,1536]{1,0:T(8,128)(2,1)S(1)}, u32[]{:S(2)}, u32[]{:S(2)}) %collective-permute-start.19) | collective-permute-done | bytes 786464 | tf_op jit(solution)/shard_map/ppermute | solution.py:643
  149.9 10.1 %expert_forward.1 = (bf16[384,1536]{1,0:T(8,128)(2,1)}, f32[4,384,256]{2,1,0:T(8,128)}, f32[4,384,256]{2,1,0:T(8,128)}, bf16[4,384,256]{2,1,0:T(8,128)(2,1)}) custom-call(bf16[384,1536]{1,0:T(8,128)(2,1)} %bitcast.30.rows_ref, bf16[1536,256]{1,0:T(8,128)(2,1)} %copy-done.22, bf16[1536,256]{1,0:T(8,128)(2,1)} %get-tuple-element.325.refs_1_.refs_3_, ...), custom_call_target="tpu_custom_call" | custom-call | flops 3623878656 | bytes 16777216 | tf_op jit(solution)/shard_map/expert_forward/pallas_call | solution.py:251
  160.1 6.1 all-to-all-start.3
  170.0 15.9 %collective-permute-done.23.refs_6_ = bf16[1536,256]{1,0:T(8,128)(2,1)} collective-permute-done((bf16[1536,256]{1,0:T(8,128)(2,1)}, bf16[1536,256]{1,0:T(8,128)(2,1)}, u32[]{:S(2)}, u32[]{:S(2)}) %collective-permute-start.23) | collective-permute-done | bytes 786464 | tf_op jit(solution)/shard_map/ppermute | solution.py:643
  185.9 9.3 %all-to-all-done.3 = bf16[8,48,1536]{2,1,0:T(8,128)(2,1)S(1)} async-done(((bf16[8,48,1536]{2,1,0:T(8,128)(2,1)}), bf16[8,48,1536]{2,1,0:T(8,128)(2,1)S(1)}, u32[]{:S(2)}, u32[]{:S(2)}) %all-to-all-start.3) | async-done | bytes 1179680 | tf_op jit(solution)/shard_map/all_to_all | solution.py:707
  201.7 6.5 collective-permute-done.24.refs_1_
  211.8 5.8 collective-permute-done.26.refs_3_
  219.6 6.2 collective-permute-done.28.refs_5_
  235.1 10.8 %front.3 = (bf16[8,128,1536]{2,1,0:T(8,128)(2,1)}, bf16[320,1024]{1,0:T(8,128)(2,1)}, bf16[8,192,128]{2,1,0:T(8,128)(2,1)}, f32[192,1024]{1,0:T(8,128)}, f32[3,1024]{1,0:T(4,128)}) custom-call(s32[8]{0:T(128)} %get-tuple-element.299.spot_ref, s32[8]{0:T(128)} %get-tuple-element.298.owner_ref, s32[4]{0:T(128)} %xor_convert_fusion.at_ref, ...), custom_call_target="tpu_custom_call" | custom-call | flops 1509949440 | bytes 9437184 | tf_op jit(solution)/shard_map/front/pallas_call | solution.py:130
  248.9 6.1 all-to-all-start.4
  257.8 8.8 %all-to-all-done.4 = bf16[8,192,128]{2,1,0:T(8,128)(2,1)S(1)} async-done(((bf16[8,192,128]{2,1,0:T(8,128)(2,1)}), bf16[8,192,128]{2,1,0:T(8,128)(2,1)S(1)}, u32[]{:S(2)}, u32[]{:S(2)}) %all-to-all-start.4) | async-done | bytes 393248 | tf_op jit(solution)/shard_map/all_to_all | solution.py:707
  267.4 5.4 middle_forward.3
  272.8 4.6 all-to-all-start.5
  284.1 22.4 %collective-permute-done.39 = bf16[384,1536]{1,0:T(8,128)(2,1)} collective-permute-done((bf16[384,1536]{1,0:T(8,128)(2,1)}, bf16[384,1536]{1,0:T(8,128)(2,1)}, u32[]{:S(2)}, u32[]{:S(2)}) %collective-permute-start.39) | collective-permute-done | bytes 1179680 | tf_op jit(solution)/shard_map/ppermute | solution.py:643
  309.1 14.5 %expert_both.1 = (bf16[384,1536]{1,0:T(8,128)(2,1)}, bf16[384,1664]{1,0:T(8,128)(2,1)}, bf16[384,1536]{1,0:T(8,128)(2,1)}, bf16[4,384,256]{2,1,0:T(8,128)(2,1)},...) custom-call(s32[1]{0:T(128)} %bitcast.3.at_ref.mine_ref, bf16[384,1536]{1,0:T(8,128)(2,1)} %bitcast.279, ...), custom_call_target="tpu_custom_call" | custom-call | flops 7247757312 | bytes 18874368 | tf_op jit(solution)/shard_map/expert_both/pallas_call | solution.py:350
  323.7 5.7 all-to-all-start.6
  337.0 14.6 %collective-permute-done.46 = bf16[384,1024]{1,0:T(8,128)(2,1)} collective-permute-done((bf16[384,1024]{1,0:T(8,128)(2,1)S(1)}, bf16[384,1024]{1,0:T(8,128)(2,1)}, u32[]{:S(2)}, u32[]{:S(2)}) %collective-permute-start.46) | collective-permute-done | bytes 786464 | tf_op jit(solution)/shard_map/ppermute | solution.py:643
  351.6 9.0 %all-to-all-done.6 = bf16[8,48,1664]{2,1,0:T(8,128)(2,1)} async-done(((bf16[8,48,1664]{2,1,0:T(8,128)(2,1)}), bf16[8,48,1664]{2,1,0:T(8,128)(2,1)}, u32[]{:S(2)}, u32[]{:S(2)}) %all-to-all-start.6) | async-done | bytes 1277984 | tf_op jit(solution)/shard_map/all_to_all | solution.py:707
  360.7 7.6 %middle_back.2 = (f32[128,1536]{1,0:T(8,128)}, bf16[128,1536]{1,0:T(8,128)(2,1)}, bf16[1536,128]{1,0:T(8,128)(2,1)}, f32[16,1536]{1,0:T(8,128)}) custom-call(s32[4]{0:T(128)} %xor_convert_fusion.at_ref, bf16[2,128,384]{2,1,0:T(8,128)(2,1)} %get-tuple-element.346.place_ref, bf16[384,1664]{1,0:T(8,128)(2,1)} %bitcast.58.back_ref, ...), custom_call_target="tpu_custom_call" | custom-call | flops 754974720 | bytes 10485760 | tf_op jit(solution)/shard_map/middle_back/pallas_call | solution.py:626
  368.2 3.9 all-to-all-start.7
  373.7 7.4 collective-permute-done.47
  384.2 4.4 collective-permute-done.51
  390.5 8.7 %attend_back.2 = (bf16[320,1024]{1,0:T(8,128)(2,1)}, bf16[8,320,128]{2,1,0:T(8,128)(2,1)}) custom-call(s32[8]{0:T(128)} %get-tuple-element.298.owner_ref, bf16[320,1024]{1,0:T(8,128)(2,1)} %get-tuple-element.188.qkv_ref, f32[192,1024]{1,0:T(8,128)} %get-tuple-element.189.exact_ref, f32[3,1024]{1,0:T(4,128)} %get-tuple-element.190.log_ref, ...), custom_call_target="tpu_custom_call" | custom-call | flops 1258291200 | bytes 6291456 | tf_op jit(solution)/shard_map/attend_back/pallas_call | solution.py:195
  399.2 4.5 head_grads.2
  404.4 3.0 convolution_convert_fusion.1
  407.4 6.2 all-to-all-start.8
  417.7 9.3 %expert_grads.2 = (bf16[2,1536,256]{2,1,0:T(8,128)(2,1)}, bf16[2,1536,256]{2,1,0:T(8,128)(2,1)}, bf16[2,1536,256]{2,1,0:T(8,128)(2,1)}, bf16[2,1536,256]{2,1,0:T...) custom-call(bf16[384,1536]{1,0:T(8,128)(2,1)} %bitcast.280, ...), custom_call_target="tpu_custom_call" | custom-call | flops 3623878656 | bytes 14680064 | tf_op jit(solution)/shard_map/expert_grads/pallas_call | solution.py:388
  427.0 12.5 %collective-permute-done.58 = bf16[336,384]{1,0:T(8,128)(2,1)S(1)} collective-permute-done((bf16[336,384]{1,0:T(8,128)(2,1)S(1)}, bf16[336,384]{1,0:T(8,128)(2,1)S(1)}, u32[]{:S(2)}, u32[]{:S(2)}) %collective-permute-start.58) | collective-permute-done | bytes 258080 | tf_op jit(solution)/shard_map/ppermute | solution.py:643
  441.3 5.7 all-to-all-start.9
  463.4 12.8 %all-to-all-done.9 = bf16[8,48,1536]{2,1,0:T(8,128)(2,1)S(1)} async-done(((bf16[8,48,1536]{2,1,0:T(8,128)(2,1)}), bf16[8,48,1536]{2,1,0:T(8,128)(2,1)S(1)}, u32[]{:S(2)}, u32[]{:S(2)}) %all-to-all-start.9) | async-done | bytes 1179680 | tf_op jit(solution)/shard_map/all_to_all | solution.py:707
  476.2 4.3 all-to-all-start.10
  481.3 3.4 fusion.29
  486.7 27.2 %all-to-all-done.10 = bf16[8,48,1536]{2,1,0:T(8,128)(2,1)} async-done(((bf16[8,48,1536]{2,1,0:T(8,128)(2,1)}), bf16[8,48,1536]{2,1,0:T(8,128)(2,1)}, u32[]{:S(2)}, u32[]{:S(2)}) %all-to-all-start.10) | async-done | bytes 1179680 | tf_op jit(solution)/shard_map/all_to_all | solution.py:707
  514.0 12.5 %expert_backward.1 = (bf16[384,1536]{1,0:T(8,128)(2,1)}, bf16[4,384,256]{2,1,0:T(8,128)(2,1)}, bf16[4,384,256]{2,1,0:T(8,128)(2,1)}) custom-call(bf16[384,1536]{1,0:T(8,128)(2,1)} %bitcast.82.grad_ref, f32[4,384,256]{2,1,0:T(8,128)} %get-tuple-element.212.refs_0_, f32[4,384,256]{2,1,0:T(8,128)} %get-tuple-element.213.refs_1_, bf16[1536,256]{1,0:T(8,128)(2,1)} %copy-done.22, ...), custom_call_target="tpu_custom_call" | custom-call | flops 3623878656 | bytes 16777216 | tf_op jit(solution)/shard_map/expert_backward/pallas_call | solution.py:289
  526.5 4.9 all-to-all-start.11
  536.3 29.5 %reduce-scatter.2.cloned.1.call-done = bf16[48,1536]{1,0:T(8,128)(2,1)} async-done(((bf16[384,1536]{1,0:T(8,128)(2,1)}), bf16[48,1536]{1,0:T(8,128)(2,1)}) %reduce-scatter.2.cloned.1.call-update) | async-done | bytes 147472 | tf_op jit(solution)/shard_map/reduce_scatter | solution.py:957
  567.2 9.2 %expert_grads.3 = (bf16[2,1536,256]{2,1,0:T(8,128)(2,1)}, bf16[2,1536,256]{2,1,0:T(8,128)(2,1)}, bf16[2,1536,256]{2,1,0:T(8,128)(2,1)}, bf16[2,1536,256]{2,1,0:T...) custom-call(bf16[384,1536]{1,0:T(8,128)(2,1)} %bitcast.30.rows_ref, ...), custom_call_target="tpu_custom_call" | custom-call | flops 3623878656 | bytes 14680064 | tf_op jit(solution)/shard_map/expert_grads/pallas_call | solution.py:388
  580.6 7.9 %middle_back.3 = (f32[128,1536]{1,0:T(8,128)}, bf16[128,1536]{1,0:T(8,128)(2,1)}, bf16[1536,128]{1,0:T(8,128)(2,1)}, f32[16,1536]{1,0:T(8,128)}) custom-call(s32[4]{0:T(128)} %xor_convert_fusion.at_ref, bf16[2,128,384]{2,1,0:T(8,128)(2,1)} %get-tuple-element.347.place_ref, bf16[384,1536]{1,0:T(8,128)(2,1)} %bitcast.86.back_ref, f32[128,1536]{1,0:T(8,128)} %copy-done.5, ...), custom_call_target="tpu_custom_call" | custom-call | flops 754974720 | bytes 10485760 | tf_op jit(solution)/shard_map/middle_back/pallas_call | solution.py:626
  591.3 4.1 all-to-all-start.12
  595.4 5.0 collective-permute-done.66
  600.5 3.4 fusion.32
  611.4 4.5 all-to-all-start.13
  616.6 8.7 %attend_back.3 = (bf16[320,1024]{1,0:T(8,128)(2,1)}, bf16[8,320,128]{2,1,0:T(8,128)(2,1)}) custom-call(s32[8]{0:T(128)} %get-tuple-element.298.owner_ref, bf16[320,1024]{1,0:T(8,128)(2,1)} %get-tuple-element.226.qkv_ref, f32[192,1024]{1,0:T(8,128)} %get-tuple-element.227.exact_ref, f32[3,1024]{1,0:T(4,128)} %get-tuple-element.228.log_ref, ...), custom_call_target="tpu_custom_call" | custom-call | flops 1258291200 | bytes 6291456 | tf_op jit(solution)/shard_map/attend_back/pallas_call | solution.py:195
  625.3 15.7 %collective-permute-done.75.refs_3_ = bf16[1536,256]{1,0:T(8,128)(2,1)} collective-permute-done((bf16[1536,256]{1,0:T(8,128)(2,1)}, bf16[1536,256]{1,0:T(8,128)(2,1)}, u32[]{:S(2)}, u32[]{:S(2)}) %collective-permute-start.75) | collective-permute-done | bytes 786464 | tf_op jit(solution)/shard_map/ppermute | solution.py:643
  641.0 4.5 head_grads.3
  652.9 3.6 finish.4
  659.3 9.4 %all-to-all-done.13 = bf16[8,48,1536]{2,1,0:T(8,128)(2,1)} async-done(((bf16[8,48,1536]{2,1,0:T(8,128)(2,1)}), bf16[8,48,1536]{2,1,0:T(8,128)(2,1)}, u32[]{:S(2)}, u32[]{:S(2)}) %all-to-all-start.13) | async-done | bytes 1179680 | tf_op jit(solution)/shard_map/all_to_all | solution.py:707
  668.7 3.6 all-to-all-start.14
  682.2 6.0 spread.2
  689.3 3.7 finish.6
  693.0 4.0 collective-permute-start.80
  702.3 3.6 collective-permute-done.80.refs_4_
  728.0 6.4 spread.3
  (580 shorter events, 209.1 us)
Async XLA Ops:
  15.3 18.6 %collective-permute-start.6 = (bf16[672,384]{1,0:T(8,128)(2,1)}, bf16[672,384]{1,0:T(8,128)(2,1)S(1)}, u32[]{:S(2)}, u32[]{:S(2)}) collective-permute-start(bf16[672,384]{1,0:T(8,128)(2,1)} %bitcast.287), channel_id=1, source_target_pairs={{0,1},{1,0},{2,3},{3,2},{4,5},{5,4},{6,7},{7,6},{8,9},{9,8},{10,11... | collective-permute-start | bytes 1548296 | tf_op jit(solution)/shard_map/ppermute | solution.py:643
  51.8 33.8 %all-to-all-start = ((bf16[8,48,1664]{2,1,0:T(8,128)(2,1)}), bf16[8,48,1664]{2,1,0:T(8,128)(2,1)}, u32[]{:S(2)}, u32[]{:S(2)}) async-start(bf16[8,48,1664]{2,1,0:T(8,128)(2,1)} %bitcast.17), calls=%async_computation | async-start | bytes 2555904 | tf_op jit(solution)/shard_map/all_to_all | solution.py:707
  58.0 35.3 %collective-permute-start.11 = (bf16[384,1536]{1,0:T(8,128)(2,1)S(1)}, bf16[384,1536]{1,0:T(8,128)(2,1)}, u32[]{:S(2)}, u32[]{:S(2)}) collective-permute-start(bf16[384,1536]{1,0:T(8,128)(2,1)S(1)} %get-tuple-element.313.refs_0_.refs_2_), channel_id=1, source_target_pairs={{0,2},{1,3},{2,0},{3,1},{4,6},{5,7},{6,4},{7,5},{8,10},{9,11},{10,... | collective-permute-start | bytes 3538952 | tf_op jit(solution)/shard_map/ppermute | solution.py:643
  89.3 18.5 %collective-permute-start.12 = (bf16[384,1536]{1,0:T(8,128)(2,1)S(1)}, bf16[384,1536]{1,0:T(8,128)(2,1)}, u32[]{:S(2)}, u32[]{:S(2)}) collective-permute-start(bf16[384,1536]{1,0:T(8,128)(2,1)S(1)} %get-tuple-element.313.refs_0_.refs_2_), channel_id=1, source_target_pairs={{0,1},{1,0},{2,3},{3,2},{4,5},{5,4},{6,7},{7,6},{8,9},{9,8},{10,11... | collective-permute-start | bytes 3538952 | tf_op jit(solution)/shard_map/ppermute | solution.py:643
  91.8 22.5 %collective-permute-start.14 = (bf16[1536,256]{1,0:T(8,128)(2,1)S(1)}, bf16[1536,256]{1,0:T(8,128)(2,1)}, u32[]{:S(2)}, u32[]{:S(2)}) collective-permute-start(bf16[1536,256]{1,0:T(8,128)(2,1)S(1)} %get-tuple-element.327.refs_0_.refs_2_), channel_id=1, source_target_pairs={{0,2},{1,3},{2,0},{3,1},{4,6},{5,7},{6,4},{7,5},{8,10},{9,11},{10,... | collective-permute-start | bytes 2359304 | tf_op jit(solution)/shard_map/ppermute | solution.py:643
  103.9 25.1 %collective-permute-start.18 = (bf16[1536,256]{1,0:T(8,128)(2,1)}, bf16[1536,256]{1,0:T(8,128)(2,1)}, u32[]{:S(2)}, u32[]{:S(2)}) collective-permute-start(bf16[1536,256]{1,0:T(8,128)(2,1)} %get-tuple-element.325.refs_1_.refs_3_), channel_id=1, source_target_pairs={{0,2},{1,3},{2,0},{3,1},{4,6},{5,7},{6,4},{7,5},{8,10},{9,11},{10,... | collective-permute-start | bytes 2359304 | tf_op jit(solution)/shard_map/ppermute | solution.py:643
  114.3 34.8 %all-to-all-start.2 = ((bf16[8,48,1536]{2,1,0:T(8,128)(2,1)}), bf16[8,48,1536]{2,1,0:T(8,128)(2,1)}, u32[]{:S(2)}, u32[]{:S(2)}) async-start(bf16[8,48,1536]{2,1,0:T(8,128)(2,1)} %bitcast.283), calls=%async_computation.2 | async-start | bytes 2359296 | tf_op jit(solution)/shard_map/all_to_all | solution.py:707
  120.9 24.5 %collective-permute-start.19 = (bf16[256,1536]{1,0:T(8,128)(2,1)S(1)}, bf16[256,1536]{1,0:T(8,128)(2,1)S(1)}, u32[]{:S(2)}, u32[]{:S(2)}) collective-permute-start(bf16[256,1536]{1,0:T(8,128)(2,1)S(1)} %get-tuple-element.323.refs_2_.refs_4_), channel_id=1, source_target_pairs={{0,2},{1,3},{2,0},{3,1},{4,6},{5,7},{6,4},{7,5},{8,10},{9,11},{10,... | collective-permute-start | bytes 2359304 | tf_op jit(solution)/shard_map/ppermute | solution.py:643
  122.1 23.4 %collective-permute-start.15 = (bf16[1536,256]{1,0:T(8,128)(2,1)S(1)}, bf16[1536,256]{1,0:T(8,128)(2,1)S(1)}, u32[]{:S(2)}, u32[]{:S(2)}) collective-permute-start(bf16[1536,256]{1,0:T(8,128)(2,1)S(1)} %get-tuple-element.327.refs_0_.refs_2_), channel_id=1, source_target_pairs={{0,1},{1,0},{2,3},{3,2},{4,5},{5,4},{6,7},{7,6},{8,9},{9,8},{10,11... | collective-permute-start | bytes 2359304 | tf_op jit(solution)/shard_map/ppermute | solution.py:643
  122.1 23.9 %collective-permute-start.16 = (bf16[1536,256]{1,0:T(8,128)(2,1)}, bf16[1536,256]{1,0:T(8,128)(2,1)S(1)}, u32[]{:S(2)}, u32[]{:S(2)}) collective-permute-start(bf16[1536,256]{1,0:T(8,128)(2,1)} %get-tuple-element.325.refs_1_.refs_3_), channel_id=1, source_target_pairs={{0,1},{1,0},{2,3},{3,2},{4,5},{5,4},{6,7},{7,6},{8,9},{9,8},{10,11... | collective-permute-start | bytes 2359304 | tf_op jit(solution)/shard_map/ppermute | solution.py:643
  122.6 23.4 %collective-permute-start.17 = (bf16[256,1536]{1,0:T(8,128)(2,1)S(1)}, bf16[256,1536]{1,0:T(8,128)(2,1)S(1)}, u32[]{:S(2)}, u32[]{:S(2)}) collective-permute-start(bf16[256,1536]{1,0:T(8,128)(2,1)S(1)} %get-tuple-element.323.refs_2_.refs_4_), channel_id=1, source_target_pairs={{0,1},{1,0},{2,3},{3,2},{4,5},{5,4},{6,7},{7,6},{8,9},{9,8},{10,11... | collective-permute-start | bytes 2359304 | tf_op jit(solution)/shard_map/ppermute | solution.py:643
  129.1 17.3 %collective-permute-start.21 = (bf16[1536,256]{1,0:T(8,128)(2,1)}, bf16[1536,256]{1,0:T(8,128)(2,1)S(1)}, u32[]{:S(2)}, u32[]{:S(2)}) collective-permute-start(bf16[1536,256]{1,0:T(8,128)(2,1)} %collective-permute-done.18.refs_7_.refs_9_), channel_id=1, source_target_pairs={{0,1},{1,0},{2,3},{3,2},{4,5},{5,4},{6,7},{7,6},{8,9},{9,8},{10,11... | collective-permute-start | bytes 2359304 | tf_op jit(solution)/shard_map/ppermute | solution.py:643
  160.1 35.0 %all-to-all-start.3 = ((bf16[8,48,1536]{2,1,0:T(8,128)(2,1)}), bf16[8,48,1536]{2,1,0:T(8,128)(2,1)S(1)}, u32[]{:S(2)}, u32[]{:S(2)}) async-start(bf16[8,48,1536]{2,1,0:T(8,128)(2,1)} %bitcast.285), calls=%async_computation.3 | async-start | bytes 2359296 | tf_op jit(solution)/shard_map/all_to_all | solution.py:707
  166.2 19.6 %collective-permute-start.23 = (bf16[1536,256]{1,0:T(8,128)(2,1)}, bf16[1536,256]{1,0:T(8,128)(2,1)}, u32[]{:S(2)}, u32[]{:S(2)}) collective-permute-start(bf16[1536,256]{1,0:T(8,128)(2,1)} %get-tuple-element.326.refs_0_), channel_id=1, source_target_pairs={{0,2},{1,3},{2,0},{3,1},{4,6},{5,7},{6,4},{7,5},{8,10},{9,11},{10,... | collective-permute-start | bytes 2359304 | tf_op jit(solution)/shard_map/ppermute | solution.py:643
  200.3 45.6 %collective-permute-start.32 = (bf16[384,1536]{1,0:T(8,128)(2,1)S(1)}, bf16[384,1536]{1,0:T(8,128)(2,1)S(1)}, u32[]{:S(2)}, u32[]{:S(2)}) collective-permute-start(bf16[384,1536]{1,0:T(8,128)(2,1)S(1)} %get-tuple-element.312.refs_0_), channel_id=1, source_target_pairs={{0,2},{1,3},{2,0},{3,1},{4,6},{5,7},{6,4},{7,5},{8,10},{9,11},{10,... | collective-permute-start | bytes 3538952 | tf_op jit(solution)/shard_map/ppermute | solution.py:643
  210.3 35.5 %collective-permute-start.33 = (bf16[1536,256]{1,0:T(8,128)(2,1)}, bf16[1536,256]{1,0:T(8,128)(2,1)}, u32[]{:S(2)}, u32[]{:S(2)}) collective-permute-start(bf16[1536,256]{1,0:T(8,128)(2,1)} %get-tuple-element.324.refs_1_), channel_id=1, source_target_pairs={{0,2},{1,3},{2,0},{3,1},{4,6},{5,7},{6,4},{7,5},{8,10},{9,11},{10,... | collective-permute-start | bytes 2359304 | tf_op jit(solution)/shard_map/ppermute | solution.py:643
  230.4 27.5 %collective-permute-start.34 = (bf16[384,1536]{1,0:T(8,128)(2,1)S(1)}, bf16[384,1536]{1,0:T(8,128)(2,1)}, u32[]{:S(2)}, u32[]{:S(2)}) collective-permute-start(bf16[384,1536]{1,0:T(8,128)(2,1)S(1)} %get-tuple-element.312.refs_0_), channel_id=1, source_target_pairs={{0,1},{1,0},{2,3},{3,2},{4,5},{5,4},{6,7},{7,6},{8,9},{9,8},{10,11... | collective-permute-start | bytes 3538952 | tf_op jit(solution)/shard_map/ppermute | solution.py:643
  245.9 20.7 %collective-permute-start.35 = (bf16[384,1536]{1,0:T(8,128)(2,1)S(1)}, bf16[384,1536]{1,0:T(8,128)(2,1)}, u32[]{:S(2)}, u32[]{:S(2)}) collective-permute-start(bf16[384,1536]{1,0:T(8,128)(2,1)S(1)} %collective-permute-done.32.refs_2_), channel_id=1, source_target_pairs={{0,1},{1,0},{2,3},{3,2},{4,5},{5,4},{6,7},{7,6},{8,9},{9,8},{10,11... | collective-permute-start | bytes 3538952 | tf_op jit(solution)/shard_map/ppermute | solution.py:643
  248.4 24.4 %collective-permute-start.36 = (bf16[256,1536]{1,0:T(8,128)(2,1)}, bf16[256,1536]{1,0:T(8,128)(2,1)}, u32[]{:S(2)}, u32[]{:S(2)}) collective-permute-start(bf16[256,1536]{1,0:T(8,128)(2,1)} %get-tuple-element.322.refs_2_), channel_id=1, source_target_pairs={{0,2},{1,3},{2,0},{3,1},{4,6},{5,7},{6,4},{7,5},{8,10},{9,11},{10,... | collective-permute-start | bytes 2359304 | tf_op jit(solution)/shard_map/ppermute | solution.py:643
  248.9 17.7 %all-to-all-start.4 = ((bf16[8,192,128]{2,1,0:T(8,128)(2,1)}), bf16[8,192,128]{2,1,0:T(8,128)(2,1)S(1)}, u32[]{:S(2)}, u32[]{:S(2)}) async-start(bf16[8,192,128]{2,1,0:T(8,128)(2,1)} %get-tuple-element.174), calls=%async_computation.4 | async-start | bytes 786432 | tf_op jit(solution)/shard_map/all_to_all | solution.py:707
  272.8 35.2 %all-to-all-start.5 = ((bf16[8,48,1536]{2,1,0:T(8,128)(2,1)}), bf16[8,48,1536]{2,1,0:T(8,128)(2,1)S(1)}, u32[]{:S(2)}, u32[]{:S(2)}) async-start(bf16[8,48,1536]{2,1,0:T(8,128)(2,1)} %bitcast.284), calls=%async_computation.5 | async-start | bytes 2359296 | tf_op jit(solution)/shard_map/all_to_all | solution.py:707
  279.1 27.5 %collective-permute-start.39 = (bf16[384,1536]{1,0:T(8,128)(2,1)}, bf16[384,1536]{1,0:T(8,128)(2,1)}, u32[]{:S(2)}, u32[]{:S(2)}) collective-permute-start(bf16[384,1536]{1,0:T(8,128)(2,1)} %get-tuple-element.311.refs_1_), channel_id=1, source_target_pairs={{0,2},{1,3},{2,0},{3,1},{4,6},{5,7},{6,4},{7,5},{8,10},{9,11},{10,... | collective-permute-start | bytes 3538952 | tf_op jit(solution)/shard_map/ppermute | solution.py:643
  280.6 27.4 %collective-permute-start.41 = (bf16[1536,256]{1,0:T(8,128)(2,1)}, bf16[1536,256]{1,0:T(8,128)(2,1)}, u32[]{:S(2)}, u32[]{:S(2)}) collective-permute-start(bf16[1536,256]{1,0:T(8,128)(2,1)} %get-tuple-element.324.refs_1_), channel_id=1, source_target_pairs={{0,1},{1,0},{2,3},{3,2},{4,5},{5,4},{6,7},{7,6},{8,9},{9,8},{10,11... | collective-permute-start | bytes 2359304 | tf_op jit(solution)/shard_map/ppermute | solution.py:643
  281.1 26.9 %collective-permute-start.42 = (bf16[256,1536]{1,0:T(8,128)(2,1)}, bf16[256,1536]{1,0:T(8,128)(2,1)}, u32[]{:S(2)}, u32[]{:S(2)}) collective-permute-start(bf16[256,1536]{1,0:T(8,128)(2,1)} %get-tuple-element.322.refs_2_), channel_id=1, source_target_pairs={{0,1},{1,0},{2,3},{3,2},{4,5},{5,4},{6,7},{7,6},{8,9},{9,8},{10,11... | collective-permute-start | bytes 2359304 | tf_op jit(solution)/shard_map/ppermute | solution.py:643
  281.1 26.9 %collective-permute-start.43 = (bf16[1536,256]{1,0:T(8,128)(2,1)}, bf16[1536,256]{1,0:T(8,128)(2,1)}, u32[]{:S(2)}, u32[]{:S(2)}) collective-permute-start(bf16[1536,256]{1,0:T(8,128)(2,1)} %collective-permute-done.23.refs_6_), channel_id=1, source_target_pairs={{0,1},{1,0},{2,3},{3,2},{4,5},{5,4},{6,7},{7,6},{8,9},{9,8},{10,11... | collective-permute-start | bytes 2359304 | tf_op jit(solution)/shard_map/ppermute | solution.py:643
  283.9 24.0 %collective-permute-start.44 = (bf16[1536,256]{1,0:T(8,128)(2,1)}, bf16[1536,256]{1,0:T(8,128)(2,1)}, u32[]{:S(2)}, u32[]{:S(2)}) collective-permute-start(bf16[1536,256]{1,0:T(8,128)(2,1)} %collective-permute-done.33.refs_7_), channel_id=1, source_target_pairs={{0,1},{1,0},{2,3},{3,2},{4,5},{5,4},{6,7},{7,6},{8,9},{9,8},{10,11... | collective-permute-start | bytes 2359304 | tf_op jit(solution)/shard_map/ppermute | solution.py:643
  323.7 37.0 %all-to-all-start.6 = ((bf16[8,48,1664]{2,1,0:T(8,128)(2,1)}), bf16[8,48,1664]{2,1,0:T(8,128)(2,1)}, u32[]{:S(2)}, u32[]{:S(2)}) async-start(bf16[8,48,1664]{2,1,0:T(8,128)(2,1)} %bitcast.277), calls=%async_computation.6 | async-start | bytes 2555904 | tf_op jit(solution)/shard_map/all_to_all | solution.py:707
  331.0 20.6 %collective-permute-start.46 = (bf16[384,1024]{1,0:T(8,128)(2,1)S(1)}, bf16[384,1024]{1,0:T(8,128)(2,1)}, u32[]{:S(2)}, u32[]{:S(2)}) collective-permute-start(bf16[384,1024]{1,0:T(8,128)(2,1)S(1)} %pad_maximum_fusion.1), channel_id=1, source_target_pairs={{0,2},{1,3},{2,0},{3,1},{4,6},{5,7},{6,4},{7,5},{8,10},{9,11},{10,... | collective-permute-start | bytes 2359304 | tf_op jit(solution)/shard_map/ppermute | solution.py:643
  332.6 74.8 %collective-permute-start.49 = (bf16[384,1536]{1,0:T(8,128)(2,1)}, bf16[384,1536]{1,0:T(8,128)(2,1)}, u32[]{:S(2)}, u32[]{:S(2)}) collective-permute-start(bf16[384,1536]{1,0:T(8,128)(2,1)} %get-tuple-element.310.refs_10_), channel_id=1, source_target_pairs={{0,2},{1,3},{2,0},{3,1},{4,6},{5,7},{6,4},{7,5},{8,10},{9,11},{10,... | collective-permute-start | bytes 3538952 | tf_op jit(solution)/shard_map/ppermute | solution.py:643
  334.5 46.6 %collective-permute-start.47 = (bf16[2,384,128]{2,1,0:T(8,128)(2,1)}, bf16[2,384,128]{2,1,0:T(8,128)(2,1)}, u32[]{:S(2)}, u32[]{:S(2)}) collective-permute-start(bf16[2,384,128]{2,1,0:T(8,128)(2,1)} %pad_maximum_fusion.7), channel_id=1, source_target_pairs={{0,2},{1,3},{2,0},{3,1},{4,6},{5,7},{6,4},{7,5},{8,10},{9,11},{10,... | collective-permute-start | bytes 589832 | tf_op jit(solution)/shard_map/ppermute | solution.py:643
  368.2 21.6 %all-to-all-start.7 = ((bf16[8,192,128]{2,1,0:T(8,128)(2,1)}), bf16[8,192,128]{2,1,0:T(8,128)(2,1)S(1)}, u32[]{:S(2)}, u32[]{:S(2)}) async-start(bf16[8,192,128]{2,1,0:T(8,128)(2,1)} %bitcast.298), calls=%async_computation.7 | async-start | bytes 786432 | tf_op jit(solution)/shard_map/all_to_all | solution.py:707
  372.1 16.5 %collective-permute-start.51 = (bf16[128,1536]{1,0:T(8,128)(2,1)}, bf16[128,1536]{1,0:T(8,128)(2,1)}, u32[]{:S(2)}, u32[]{:S(2)}) collective-permute-start(bf16[128,1536]{1,0:T(8,128)(2,1)} %get-tuple-element.198), channel_id=1, source_target_pairs={{0,2},{1,3},{2,0},{3,1},{4,6},{5,7},{6,4},{7,5},{8,10},{9,11},{10,... | collective-permute-start | bytes 1179656 | tf_op jit(solution)/shard_map/ppermute | solution.py:643
  383.7 20.1 %collective-permute-start.50 = (bf16[128,1536]{1,0:T(8,128)(2,1)}, bf16[128,1536]{1,0:T(8,128)(2,1)}, u32[]{:S(2)}, u32[]{:S(2)}) collective-permute-start(bf16[128,1536]{1,0:T(8,128)(2,1)} %get-tuple-element.198), channel_id=1, source_target_pairs={{0,1},{1,0},{2,3},{3,2},{4,5},{5,4},{6,7},{7,6},{8,9},{9,8},{10,11... | collective-permute-start | bytes 1179656 | tf_op jit(solution)/shard_map/ppermute | solution.py:643
  388.6 64.0 %collective-permute-start.54 = (bf16[384,1024]{1,0:T(8,128)(2,1)}, bf16[384,1024]{1,0:T(8,128)(2,1)}, u32[]{:S(2)}, u32[]{:S(2)}) collective-permute-start(bf16[384,1024]{1,0:T(8,128)(2,1)} %copy-done.41), channel_id=1, source_target_pairs={{0,1},{1,0},{2,3},{3,2},{4,5},{5,4},{6,7},{7,6},{8,9},{9,8},{10,11... | collective-permute-start | bytes 2359304 | tf_op jit(solution)/shard_map/ppermute | solution.py:643
  389.1 65.4 %collective-permute-start.53 = (bf16[384,1536]{1,0:T(8,128)(2,1)}, bf16[384,1536]{1,0:T(8,128)(2,1)}, u32[]{:S(2)}, u32[]{:S(2)}) collective-permute-start(bf16[384,1536]{1,0:T(8,128)(2,1)} %get-tuple-element.311.refs_1_), channel_id=1, source_target_pairs={{0,1},{1,0},{2,3},{3,2},{4,5},{5,4},{6,7},{7,6},{8,9},{9,8},{10,11... | collective-permute-start | bytes 3538952 | tf_op jit(solution)/shard_map/ppermute | solution.py:643
  407.4 33.9 %all-to-all-start.8 = ((bf16[8,320,128]{2,1,0:T(8,128)(2,1)}), bf16[8,320,128]{2,1,0:T(8,128)(2,1)}, u32[]{:S(2)}, u32[]{:S(2)}) async-start(bf16[8,320,128]{2,1,0:T(8,128)(2,1)} %get-tuple-element.199), calls=%async_computation.8 | async-start | bytes 1310720 | tf_op jit(solution)/shard_map/all_to_all | solution.py:707
  414.6 48.8 %collective-permute-start.59 = (bf16[384,1024]{1,0:T(8,128)(2,1)}, bf16[384,1024]{1,0:T(8,128)(2,1)}, u32[]{:S(2)}, u32[]{:S(2)}) collective-permute-start(bf16[384,1024]{1,0:T(8,128)(2,1)} %pad_maximum_fusion.2), channel_id=1, source_target_pairs={{0,2},{1,3},{2,0},{3,1},{4,6},{5,7},{6,4},{7,5},{8,10},{9,11},{10,... | collective-permute-start | bytes 2359304 | tf_op jit(solution)/shard_map/ppermute | solution.py:643
  416.1 42.4 %collective-permute-start.55 = (bf16[384,1536]{1,0:T(8,128)(2,1)}, bf16[384,1536]{1,0:T(8,128)(2,1)}, u32[]{:S(2)}, u32[]{:S(2)}) collective-permute-start(bf16[384,1536]{1,0:T(8,128)(2,1)} %collective-permute-done.39), channel_id=1, source_target_pairs={{0,1},{1,0},{2,3},{3,2},{4,5},{5,4},{6,7},{7,6},{8,9},{9,8},{10,11... | collective-permute-start | bytes 3538952 | tf_op jit(solution)/shard_map/ppermute | solution.py:643
  417.1 22.4 %collective-permute-start.58 = (bf16[336,384]{1,0:T(8,128)(2,1)S(1)}, bf16[336,384]{1,0:T(8,128)(2,1)S(1)}, u32[]{:S(2)}, u32[]{:S(2)}) collective-permute-start(bf16[336,384]{1,0:T(8,128)(2,1)S(1)} %fusion.50), channel_id=1, source_target_pairs={{0,2},{1,3},{2,0},{3,1},{4,6},{5,7},{6,4},{7,5},{8,10},{9,11},{10,... | collective-permute-start | bytes 774152 | tf_op jit(solution)/shard_map/ppermute | solution.py:643
  439.5 41.8 %collective-permute-start.60 = (bf16[2,1536,256]{2,1,0:T(8,128)(2,1)}, bf16[2,1536,256]{2,1,0:T(8,128)(2,1)}, u32[]{:S(2)}, u32[]{:S(2)}) collective-permute-start(bf16[2,1536,256]{2,1,0:T(8,128)(2,1)} %get-tuple-element.220), channel_id=1, source_target_pairs={{0,1},{1,0},{2,3},{3,2},{4,5},{5,4},{6,7},{7,6},{8,9},{9,8},{10,11... | collective-permute-start | bytes 4718600 | tf_op jit(solution)/shard_map/ppermute | solution.py:643
  441.3 35.0 %all-to-all-start.9 = ((bf16[8,48,1536]{2,1,0:T(8,128)(2,1)}), bf16[8,48,1536]{2,1,0:T(8,128)(2,1)S(1)}, u32[]{:S(2)}, u32[]{:S(2)}) async-start(bf16[8,48,1536]{2,1,0:T(8,128)(2,1)} %bitcast.278), calls=%async_computation.9 | async-start | bytes 2359296 | tf_op jit(solution)/shard_map/all_to_all | solution.py:707
  476.2 37.7 %all-to-all-start.10 = ((bf16[8,48,1536]{2,1,0:T(8,128)(2,1)}), bf16[8,48,1536]{2,1,0:T(8,128)(2,1)}, u32[]{:S(2)}, u32[]{:S(2)}) async-start(bf16[8,48,1536]{2,1,0:T(8,128)(2,1)} %bitcast.251), calls=%async_computation.10 | async-start | bytes 2359296 | tf_op jit(solution)/shard_map/all_to_all | solution.py:707
  480.5 85.4 %reduce-scatter.2.cloned.1.call-start = ((), (), s32[]{:S(2)}) async-start(), calls=%async_computation.16 | async-start | bytes 1327104 | tf_op jit(solution)/shard_map/reduce_scatter | solution.py:957
  481.2 50.3 %collective-permute-start.63 = (bf16[2,256,1536]{2,1,0:T(8,128)(2,1)}, bf16[2,256,1536]{2,1,0:T(8,128)(2,1)}, u32[]{:S(2)}, u32[]{:S(2)}) collective-permute-start(bf16[2,256,1536]{2,1,0:T(8,128)(2,1)} %get-tuple-element.223), channel_id=1, source_target_pairs={{0,1},{1,0},{2,3},{3,2},{4,5},{5,4},{6,7},{7,6},{8,9},{9,8},{10,11... | collective-permute-start | bytes 4718600 | tf_op jit(solution)/shard_map/ppermute | solution.py:643
  484.7 41.7 %collective-permute-start.61 = (bf16[1536,256]{1,0:T(8,128)(2,1)}, bf16[1536,256]{1,0:T(8,128)(2,1)}, u32[]{:S(2)}, u32[]{:S(2)}) collective-permute-start(bf16[1536,256]{1,0:T(8,128)(2,1)} %get-tuple-element.309), channel_id=1, source_target_pairs={{0,2},{1,3},{2,0},{3,1},{4,6},{5,7},{6,4},{7,5},{8,10},{9,11},{10,... | collective-permute-start | bytes 2359304 | tf_op jit(solution)/shard_map/ppermute | solution.py:643
  486.2 40.2 %collective-permute-start.62 = (bf16[1536,256]{1,0:T(8,128)(2,1)}, bf16[1536,256]{1,0:T(8,128)(2,1)}, u32[]{:S(2)}, u32[]{:S(2)}) collective-permute-start(bf16[1536,256]{1,0:T(8,128)(2,1)} %get-tuple-element.308), channel_id=1, source_target_pairs={{0,2},{1,3},{2,0},{3,1},{4,6},{5,7},{6,4},{7,5},{8,10},{9,11},{10,... | collective-permute-start | bytes 2359304 | tf_op jit(solution)/shard_map/ppermute | solution.py:643
  526.5 54.2 %all-to-all-start.11 = ((bf16[8,48,1536]{2,1,0:T(8,128)(2,1)}), bf16[8,48,1536]{2,1,0:T(8,128)(2,1)}, u32[]{:S(2)}, u32[]{:S(2)}) async-start(bf16[8,48,1536]{2,1,0:T(8,128)(2,1)} %bitcast.282), calls=%async_computation.11 | async-start | bytes 2359296 | tf_op jit(solution)/shard_map/all_to_all | solution.py:707
  531.3 150.8 %all-gather.3.cloned.1.call-start = ((), (), s32[]{:S(2)}) async-start(), calls=%async_computation.17 | async-start | bytes 3649536 | tf_op jit(solution)/shard_map/all_gather | solution.py:905
  534.1 46.5 %collective-permute-start.64 = (bf16[256,1536]{1,0:T(8,128)(2,1)}, bf16[256,1536]{1,0:T(8,128)(2,1)}, u32[]{:S(2)}, u32[]{:S(2)}) collective-permute-start(bf16[256,1536]{1,0:T(8,128)(2,1)} %fusion.30), channel_id=1, source_target_pairs={{0,2},{1,3},{2,0},{3,1},{4,6},{5,7},{6,4},{7,5},{8,10},{9,11},{10,... | collective-permute-start | bytes 2359304 | tf_op jit(solution)/shard_map/ppermute | solution.py:643
  576.5 23.9 %collective-permute-start.73 = (bf16[2,1536,256]{2,1,0:T(8,128)(2,1)}, bf16[2,1536,256]{2,1,0:T(8,128)(2,1)}, u32[]{:S(2)}, u32[]{:S(2)}) collective-permute-start(bf16[2,1536,256]{2,1,0:T(8,128)(2,1)} %get-tuple-element.253), channel_id=1, source_target_pairs={{0,1},{1,0},{2,3},{3,2},{4,5},{5,4},{6,7},{7,6},{8,9},{9,8},{10,11... | collective-permute-start | bytes 4718600 | tf_op jit(solution)/shard_map/ppermute | solution.py:643
  590.1 108.6 %collective-permute-start.70 = (bf16[384,1024]{1,0:T(8,128)(2,1)}, bf16[384,1024]{1,0:T(8,128)(2,1)}, u32[]{:S(2)}, u32[]{:S(2)}) collective-permute-start(bf16[384,1024]{1,0:T(8,128)(2,1)} %pad_maximum_fusion.2), channel_id=1, source_target_pairs={{0,1},{1,0},{2,3},{3,2},{4,5},{5,4},{6,7},{7,6},{8,9},{9,8},{10,11... | collective-permute-start | bytes 2359304 | tf_op jit(solution)/shard_map/ppermute | solution.py:643
  591.0 16.3 %collective-permute-start.65 = (bf16[128,1536]{1,0:T(8,128)(2,1)}, bf16[128,1536]{1,0:T(8,128)(2,1)}, u32[]{:S(2)}, u32[]{:S(2)}) collective-permute-start(bf16[128,1536]{1,0:T(8,128)(2,1)} %get-tuple-element.235), channel_id=1, source_target_pairs={{0,1},{1,0},{2,3},{3,2},{4,5},{5,4},{6,7},{7,6},{8,9},{9,8},{10,11... | collective-permute-start | bytes 1179656 | tf_op jit(solution)/shard_map/ppermute | solution.py:643
  591.3 20.1 %all-to-all-start.12 = ((bf16[8,192,128]{2,1,0:T(8,128)(2,1)}), bf16[8,192,128]{2,1,0:T(8,128)(2,1)}, u32[]{:S(2)}, u32[]{:S(2)}) async-start(bf16[8,192,128]{2,1,0:T(8,128)(2,1)} %bitcast.297), calls=%async_computation.12 | async-start | bytes 786432 | tf_op jit(solution)/shard_map/all_to_all | solution.py:707
  603.9 21.4 %collective-permute-start.74 = (bf16[1536,256]{1,0:T(8,128)(2,1)}, bf16[1536,256]{1,0:T(8,128)(2,1)}, u32[]{:S(2)}, u32[]{:S(2)}) collective-permute-start(bf16[1536,256]{1,0:T(8,128)(2,1)} %get-tuple-element.307), channel_id=1, source_target_pairs={{0,2},{1,3},{2,0},{3,1},{4,6},{5,7},{6,4},{7,5},{8,10},{9,11},{10,... | collective-permute-start | bytes 2359304 | tf_op jit(solution)/shard_map/ppermute | solution.py:643
  605.4 35.6 %collective-permute-start.75 = (bf16[1536,256]{1,0:T(8,128)(2,1)}, bf16[1536,256]{1,0:T(8,128)(2,1)}, u32[]{:S(2)}, u32[]{:S(2)}) collective-permute-start(bf16[1536,256]{1,0:T(8,128)(2,1)} %get-tuple-element.306), channel_id=1, source_target_pairs={{0,2},{1,3},{2,0},{3,1},{4,6},{5,7},{6,4},{7,5},{8,10},{9,11},{10,... | collective-permute-start | bytes 2359304 | tf_op jit(solution)/shard_map/ppermute | solution.py:643
  607.3 104.7 %collective-permute-start.69 = (bf16[384,1536]{1,0:T(8,128)(2,1)}, bf16[384,1536]{1,0:T(8,128)(2,1)}, u32[]{:S(2)}, u32[]{:S(2)}) collective-permute-start(bf16[384,1536]{1,0:T(8,128)(2,1)} %get-tuple-element.310.refs_10_), channel_id=1, source_target_pairs={{0,1},{1,0},{2,3},{3,2},{4,5},{5,4},{6,7},{7,6},{8,9},{9,8},{10,11... | collective-permute-start | bytes 3538952 | tf_op jit(solution)/shard_map/ppermute | solution.py:643
  611.4 57.4 %all-to-all-start.13 = ((bf16[8,48,1536]{2,1,0:T(8,128)(2,1)}), bf16[8,48,1536]{2,1,0:T(8,128)(2,1)}, u32[]{:S(2)}, u32[]{:S(2)}) async-start(bf16[8,48,1536]{2,1,0:T(8,128)(2,1)} %bitcast.281), calls=%async_computation.13 | async-start | bytes 2359296 | tf_op jit(solution)/shard_map/all_to_all | solution.py:707
  616.6 35.2 %collective-permute-start.68 = (bf16[2,1536,256]{2,1,0:T(8,128)(2,1)}, bf16[2,1536,256]{2,1,0:T(8,128)(2,1)S(1)}, u32[]{:S(2)}, u32[]{:S(2)}) collective-permute-start(bf16[2,1536,256]{2,1,0:T(8,128)(2,1)} %get-tuple-element.237), channel_id=1, source_target_pairs={{0,1},{1,0},{2,3},{3,2},{4,5},{5,4},{6,7},{7,6},{8,9},{9,8},{10,11... | collective-permute-start | bytes 4718600 | tf_op jit(solution)/shard_map/ppermute | solution.py:643
  645.6 34.0 %collective-permute-start.86 = (bf16[2,256,1536]{2,1,0:T(8,128)(2,1)}, bf16[2,256,1536]{2,1,0:T(8,128)(2,1)}, u32[]{:S(2)}, u32[]{:S(2)}) collective-permute-start(bf16[2,256,1536]{2,1,0:T(8,128)(2,1)} %get-tuple-element.267), channel_id=1, source_target_pairs={{0,1},{1,0},{2,3},{3,2},{4,5},{5,4},{6,7},{7,6},{8,9},{9,8},{10,11... | collective-permute-start | bytes 4718600 | tf_op jit(solution)/shard_map/ppermute | solution.py:643
  651.8 37.4 %collective-permute-start.88 = (bf16[2,1536,256]{2,1,0:T(8,128)(2,1)}, bf16[2,1536,256]{2,1,0:T(8,128)(2,1)}, u32[]{:S(2)}, u32[]{:S(2)}) collective-permute-start(bf16[2,1536,256]{2,1,0:T(8,128)(2,1)} %get-tuple-element.272), channel_id=1, source_target_pairs={{0,1},{1,0},{2,3},{3,2},{4,5},{5,4},{6,7},{7,6},{8,9},{9,8},{10,11... | collective-permute-start | bytes 4718600 | tf_op jit(solution)/shard_map/ppermute | solution.py:643
  668.7 28.2 %all-to-all-start.14 = ((bf16[8,320,128]{2,1,0:T(8,128)(2,1)}), bf16[8,320,128]{2,1,0:T(8,128)(2,1)S(1)}, u32[]{:S(2)}, u32[]{:S(2)}) async-start(bf16[8,320,128]{2,1,0:T(8,128)(2,1)} %get-tuple-element.244), calls=%async_computation.14 | async-start | bytes 1310720 | tf_op jit(solution)/shard_map/all_to_all | solution.py:707
  679.6 17.3 %collective-permute-start.79 = (bf16[528,384]{1,0:T(8,128)(2,1)S(1)}, bf16[528,384]{1,0:T(8,128)(2,1)}, u32[]{:S(2)}, u32[]{:S(2)}) collective-permute-start(bf16[528,384]{1,0:T(8,128)(2,1)S(1)} %slice_dynamic-update-slice_fusion.4.refs_1_), channel_id=1, source_target_pairs={{8,0},{16,8},{24,16},{28,24},{20,28},{12,20},{4,12},{0,4},{9,1},{1... | collective-permute-start | bytes 1216520 | tf_op jit(solution)/shard_map/ppermute | solution.py:687
  698.7 17.1 %collective-permute-start.71 = (bf16[384,1536]{1,0:T(8,128)(2,1)}, bf16[384,1536]{1,0:T(8,128)(2,1)S(1)}, u32[]{:S(2)}, u32[]{:S(2)}) collective-permute-start(bf16[384,1536]{1,0:T(8,128)(2,1)} %collective-permute-done.49), channel_id=1, source_target_pairs={{0,1},{1,0},{2,3},{3,2},{4,5},{5,4},{6,7},{7,6},{8,9},{9,8},{10,11... | collective-permute-start | bytes 3538952 | tf_op jit(solution)/shard_map/ppermute | solution.py:643
  700.7 20.5 %collective-permute-start.87 = (bf16[256,1536]{1,0:T(8,128)(2,1)S(1)}, bf16[256,1536]{1,0:T(8,128)(2,1)S(1)}, u32[]{:S(2)}, u32[]{:S(2)}) collective-permute-start(bf16[256,1536]{1,0:T(8,128)(2,1)S(1)} %bitcast.286), channel_id=1, source_target_pairs={{0,2},{1,3},{2,0},{3,1},{4,6},{5,7},{6,4},{7,5},{8,10},{9,11},{10,... | collective-permute-start | bytes 2359304 | tf_op jit(solution)/shard_map/ppermute | solution.py:643
  (172 other events, 1715.5 us)
Sparse Core Ops, SparseCore 0:
  484.7 81.0 reduce-scatter.1
  578.5 89.8 all-gather.2
